TPU v7x, 32 devices: a whole 2x2x4 slice. The times are simulated.
32 devices in a mesh: shot: 2 (over y), gx: 4 (over x, core), gy: 4 (over z).
Axes of the slice: x: 2, y: 2, z: 4, core: 2. Of those that a mesh axis runs over, the one named last changes fastest.
Arguments:
- src_p_prev: float32 [128, 64, 128], P(('shot', 'gx'), 'gy'), parts along dimension 0, may hold values from -6 to 6
- src_p_now: float32 [128, 64, 128], P(('shot', 'gx'), 'gy'), parts along dimension 0, may hold values from -6 to 6
- src_q_prev: float32 [128, 64, 128], P(('shot', 'gx'), 'gy'), parts along dimension 0, may hold values from -6 to 6
- src_q_now: float32 [128, 64, 128], P(('shot', 'gx'), 'gy'), parts along dimension 0, may hold values from -6 to 6
- rec_p_next: float32 [128, 64, 128], P(('shot', 'gx'), 'gy'), parts along dimension 0, may hold values from -6 to 6
- rec_p_now: float32 [128, 64, 128], P(('shot', 'gx'), 'gy'), parts along dimension 0, may hold values from -6 to 6
- rec_q_next: float32 [128, 64, 128], P(('shot', 'gx'), 'gy'), parts along dimension 0, may hold values from -6 to 6
- rec_q_now: float32 [128, 64, 128], P(('shot', 'gx'), 'gy'), parts along dimension 0, may hold values from -6 to 6
- velocity_term: float32 [64, 64, 128], P('gx', 'gy'), may hold values from 0.12 to 0.16
- epsilon: float32 [64, 64, 128], P('gx', 'gy'), may hold values from 0.2 to 0.4
- delta: float32 [64, 64, 128], P('gx', 'gy'), may hold values from 0 to 0.2
- tilt: float32 [64, 64, 128], P('gx', 'gy'), may hold values from 0 to 1.2
- azimuth: float32 [64, 64, 128], P('gx', 'gy'), may hold values from -3.140625 to 3.140625
- traces: float32 [32, 1024], P('shot', ('gx', 'gy')), parts along dimension 0, may hold values from -6 to 6
- receiver_x: int32 [1024], replicated, may hold values from 0 to 63
- receiver_y: int32 [1024], replicated, may hold values from 0 to 63
- segment_start: int32 [1], replicated, may hold values from 0 to 12
Outputs:
- image: float32 [128, 64, 128], P(('shot', 'gx'), 'gy'), parts along dimension 0
- rec_p_last: float32 [128, 64, 128], P(('shot', 'gx'), 'gy'), parts along dimension 0
- rec_q_last: float32 [128, 64, 128], P(('shot', 'gx'), 'gy'), parts along dimension 0
There are 2 independent parts, one for each index of `shot`. A program takes and returns all parts, laid end to end along the dimension named above; an argument that names none is the same for every part. Nothing has to cross between parts.
All inputs are finite; a program needn't handle non-finite values.
Results may differ from a plain program's by a relative error of at most 0.00021.
Values sent between devices are 32-bit elements; how exact they have to be, the bound alone decides.
No kernel may reach another device: no remote copies, remote signals or barrier semaphores. Data moves between devices by JAX's collectives and lax.ppermute only.
A program may use at most 64 MiB of HBM per device.

v0:
```python
import jax
import jax.numpy as jnp
from jax import lax
from jax.sharding import PartitionSpec as P

STEPS = 4
REC_DEPTH = 4


def padded_2(value, sides, width):
    for axis, dim in sides:
        devices, length = (lax.axis_size(axis), value.shape[dim])
        up = [(i, (i + 1) % devices) for i in range(devices - 1)]
        down = [(j, i) for i, j in up]
        last = lax.slice_in_dim(value, length - width, length, axis=dim)
        initial = lax.slice_in_dim(value, 0, width, axis=dim)
        before = lax.ppermute(last, axis, up)
        after = lax.ppermute(initial, axis, down)
        value = jnp.concatenate([before, value, after], axis=dim)
    return value


def factors_of(velocity_term, epsilon, delta, tilt, azimuth):
    sin_tilt = jnp.sin(tilt)
    cos_tilt = jnp.cos(tilt)
    sin_azim = jnp.sin(azimuth)
    cos_azim = jnp.cos(azimuth)
    sin_square = sin_tilt * sin_tilt
    double_tilt = 2.0 * sin_tilt * cos_tilt
    return (
        velocity_term,
        1.0 + 2.0 * epsilon,
        jnp.sqrt(1.0 + 2.0 * delta),
        sin_square * cos_azim * cos_azim,
        sin_square * sin_azim * sin_azim,
        cos_tilt * cos_tilt,
        2.0 * sin_square * sin_azim * cos_azim,
        double_tilt * cos_azim,
        double_tilt * sin_azim,
    )


def rotated(padded, factors):
    center = padded[1:-1, 1:-1, 1:-1]
    d_xx = padded[2:, 1:-1, 1:-1] - 2.0 * center + padded[:-2, 1:-1, 1:-1]
    d_yy = padded[1:-1, 2:, 1:-1] - 2.0 * center + padded[1:-1, :-2, 1:-1]
    d_zz = padded[1:-1, 1:-1, 2:] - 2.0 * center + padded[1:-1, 1:-1, :-2]
    d_xy = 0.25 * (
        padded[2:, 2:, 1:-1]
        - padded[2:, :-2, 1:-1]
        - padded[:-2, 2:, 1:-1]
        + padded[:-2, :-2, 1:-1]
    )
    d_xz = 0.25 * (
        padded[2:, 1:-1, 2:]
        - padded[2:, 1:-1, :-2]
        - padded[:-2, 1:-1, 2:]
        + padded[:-2, 1:-1, :-2]
    )
    d_yz = 0.25 * (
        padded[1:-1, 2:, 2:]
        - padded[1:-1, 2:, :-2]
        - padded[1:-1, :-2, 2:]
        + padded[1:-1, :-2, :-2]
    )
    along_axis = (
        factors[3] * d_xx
        + factors[4] * d_yy
        + factors[5] * d_zz
        + factors[6] * d_xy
        + factors[7] * d_xz
        + factors[8] * d_yz
    )
    return (along_axis, d_xx + d_yy + d_zz)


def advance(wave_state, factors):
    p_prev, p_now, q_prev, q_now = wave_state
    p_axis, p_laplace = rotated(jnp.pad(p_now, 1), factors)
    q_axis = rotated(jnp.pad(q_now, 1), factors)[0]
    p_across = p_laplace - p_axis
    p_next = 2.0 * p_now - p_prev + factors[0] * (factors[1] * p_across + factors[2] * q_axis)
    q_next = 2.0 * q_now - q_prev + factors[0] * (factors[2] * p_across + q_axis)
    return (p_next, q_next)


def side_pad(array, margin):
    return jnp.pad(array, ((margin, margin), (margin, margin), (0, 0)))


def core_of(array, margin):
    return array[margin:-margin, margin:-margin]


def split_depth(stacked, count):
    return jnp.split(stacked, count, axis=2)


def exchange_rims(groups):
    nows = [member for wave_state in groups for member in (wave_state[1], wave_state[3])]
    stacked = jnp.concatenate(nows, axis=2)
    widened = split_depth(padded_2(stacked, (("gx", 0), ("gy", 1)), 1), len(nows))
    return [
        (
            side_pad(wave_state[0], 1),
            widened[2 * number],
            side_pad(wave_state[2], 1),
            widened[2 * number + 1],
        )
        for number, wave_state in enumerate(groups)
    ]


def run_round(records, factors, inside, planes, margin):
    widened = exchange_rims([record["state"] for record in records])
    for number, record in enumerate(records):
        wave_state = widened[number]
        p_next, q_next = advance(wave_state, factors)
        if record["backward"]:
            sample = STEPS - 1 - record["done"]
            p_next = p_next.at[:, :, REC_DEPTH].add(planes[sample])
        p_next = p_next * inside
        q_next = q_next * inside
        wave_state = (wave_state[1], p_next, wave_state[3], q_next)
        record["done"] = record["done"] + 1
        record["snaps"].append(core_of(p_next, margin))
        record["state"] = tuple((core_of(member, margin) for member in wave_state))


def per_device(
    src_p_prev,
    src_p_now,
    src_q_prev,
    src_q_now,
    rec_p_next,
    rec_p_now,
    rec_q_next,
    rec_q_now,
    velocity_term,
    epsilon,
    delta,
    tilt,
    azimuth,
    traces,
    receiver_x,
    receiver_y,
    segment_start,
):
    cells_x = src_p_now.shape[0]
    cells_y = src_p_now.shape[1]
    margin = 1
    earth_model = tuple(
        (side_pad(member, 1) for member in (velocity_term, epsilon, delta, tilt, azimuth))
    )
    factors = factors_of(
        earth_model[0], earth_model[1], earth_model[2], earth_model[3], earth_model[4]
    )
    x_global = (
        lax.axis_index("gx") * cells_x - margin + jnp.arange(cells_x + 2 * margin, dtype=jnp.int32)
    )
    y_global = (
        lax.axis_index("gy") * cells_y - margin + jnp.arange(cells_y + 2 * margin, dtype=jnp.int32)
    )
    inside_x = (x_global >= 0) & (x_global < cells_x * lax.axis_size("gx"))
    inside_y = (y_global >= 0) & (y_global < cells_y * lax.axis_size("gy"))
    inside = (inside_x[:, None, None] & inside_y[None, :, None]).astype(jnp.float32)
    window = lax.dynamic_slice_in_dim(traces, segment_start[0], STEPS, 0)
    everyone = lax.all_gather(window, ("gx", "gy"), axis=1, tiled=True)
    pick_x = (receiver_x[:, None] == x_global[None, :]).astype(jnp.float32)
    pick_y = (receiver_y[:, None] == y_global[None, :]).astype(jnp.float32)
    weighted = everyone[:, :, None] * pick_x[None, :, :]
    planes = jnp.einsum("krx,ry->kxy", weighted, pick_y, precision=lax.Precision.HIGHEST)
    source = {
        "state": (src_p_prev, src_p_now, src_q_prev, src_q_now),
        "backward": False,
        "done": 0,
        "snaps": [src_p_now],
    }
    receiver = {
        "state": (rec_p_next, rec_p_now, rec_q_next, rec_q_now),
        "backward": True,
        "done": 0,
        "snaps": [rec_p_now],
    }
    rounds = STEPS // margin
    for turn_index in range(rounds):
        run_round([source, receiver], factors, inside, planes, margin)
    image_sum = source["snaps"][STEPS] * receiver["snaps"][0]
    for back_index in range(1, STEPS + 1):
        image_sum = image_sum + source["snaps"][STEPS - back_index] * receiver["snaps"][back_index]
    return (image_sum, receiver["state"][1], receiver["state"][3])


def solution(mesh):
    return jax.shard_map(
        per_device,
        mesh=mesh,
        in_specs=(
            P(("shot", "gx"), "gy", None),
            P(("shot", "gx"), "gy", None),
            P(("shot", "gx"), "gy", None),
            P(("shot", "gx"), "gy", None),
            P(("shot", "gx"), "gy", None),
            P(("shot", "gx"), "gy", None),
            P(("shot", "gx"), "gy", None),
            P(("shot", "gx"), "gy", None),
            P("gx", "gy", None),
            P("gx", "gy", None),
            P("gx", "gy", None),
            P("gx", "gy", None),
            P("gx", "gy", None),
            P("shot", ("gx", "gy")),
            P(),
            P(),
            P(),
        ),
        out_specs=(
            P(("shot", "gx"), "gy", None),
            P(("shot", "gx"), "gy", None),
            P(("shot", "gx"), "gy", None),
        ),
        check_vma=False,
    )
```

profile of v0, /device:TPU:1, one launch (start us, length us, event | category | flops | bytes accessed | tf_op | source)
XLA Modules:
  0.0 141.3 jit_solution(2109060058614045298)
XLA Ops:
  0.7 1.0 constant_dynamic-update-slice_fusion.3
  1.7 0.9 copy-done.7
  2.5 0.9 copy-done.24
  3.5 4.5 %collective-permute-start = (f32[1,16,512]{2,1,0:T(8,128)S(1)}, f32[1,16,512]{2,1,0:T(8,128)S(1)}, u32[]{:S(2)}, u32[]{:S(2)}) collective-permute-start(f32[1,16,512]{2,1,0:T(8,128)S(1)} %get-tuple-element.137), channel_id=1, source_target_pairs={{0,4},{4,8},{8,12},{1,5},{5,9},{9,13},{2,6},{6,10},{10,14},{3,7},{... | collective-permute-start | bytes 98312 | tf_op jit(solution)/shard_map/ppermute | solution.py:17
  8.0 1.9 %collective-permute-start.1 = (f32[1,16,512]{2,1,0:T(8,128)S(1)}, f32[1,16,512]{2,1,0:T(8,128)S(1)}, u32[]{:S(2)}, u32[]{:S(2)}) collective-permute-start(f32[1,16,512]{2,1,0:T(8,128)S(1)} %get-tuple-element.138), channel_id=1, source_target_pairs={{4,0},{8,4},{12,8},{5,1},{9,5},{13,9},{6,2},{10,6},{14,10},{7,3},{... | collective-permute-start | bytes 98312 | tf_op jit(solution)/shard_map/ppermute | solution.py:18
  10.6 28.7 %all-gather = f32[16,64,4]{1,2,0:T(4,128)S(1)} all-gather(f32[1,64,4]{1,2,0:T(4,128)S(1)} %dynamic-slice_bitcast_fusion), channel_id=1, replica_groups=mesh['shot'=2,'gx'=4,'gy'=4] {'gx','gy'}, dimensions={0}, use_global_device_ids=true | all-gather | bytes 17408 | tf_op jit(solution)/shard_map/all_gather | solution.py:168
  39.4 0.6 copy-done.31
  40.1 0.6 copy-done.32
  40.7 0.4 fusion
  41.2 1.3 collective-permute-start.2
  42.5 1.3 collective-permute-start.3
  43.9 3.2 %collective-permute-done.3 = f32[18,1,512]{2,1,0:T(1,128)S(1)} collective-permute-done((f32[18,1,512]{2,1,0:T(1,128)S(1)}, f32[18,1,512]{2,1,0:T(1,128)S(1)}, u32[]{:S(2)}, u32[]{:S(2)}) %collective-permute-start.3) | collective-permute-done | bytes 36896 | tf_op jit(solution)/shard_map/ppermute | solution.py:18
  47.4 0.8 copy-done.1
  48.5 3.0 %broadcast_multiply_fusion.10 = (f32[18,18,128]{2,1,0:T(8,128)S(1)}, f32[18,18,128]{2,1,0:T(8,128)S(1)}, f32[18,18,128]{2,1,0:T(8,128)S(1)}, f32[18,18,128]{2,1,...) fusion(f32[18,18,512]{2,1,0:T(8,128)S(1)} %pad_maximum_fusion, ...), kind=kLoop, calls=%fused_computation.842 | loop fusion | flops 3732480 | bytes 3440640 | tf_op jit(solution)/shard_map/mul | solution.py:82
  51.7 1.4 %scatter-add.14 = f32[18,18,128]{2,1,0:T(8,128)S(1)} dynamic-update-slice(f32[18,18,128]{2,1,0:T(8,128)S(1)} %get-tuple-element.109, f32[18,18,1]{2,1,0:T(8,128)S(1)} %slice_add_fusion.3, s32[]{:T(128)} %constant.111.clone.1, s32[]{:T(128)} %constant.111.clone.1, s32[]{:T(128)} %constant.113.clone.1) | dynamic-update-slice | bytes 2596 | tf_op jit(solution)/shard_map/scatter-add | solution.py:121
  53.2 2.8 %fusion.31 = (f32[18,18,128]{2,1,0:T(8,128)S(1)}, f32[18,18,128]{2,1,0:T(8,128)S(1)}) fusion(f32[16,16,128]{2,1,0:T(8,128)S(1)} %copy-done.3, f32[18,18,128]{2,1,0:T(8,128)S(1)} %get-tuple-element.114, f32[16,16,128]{2,1,0:T(8,128)S(1)} %copy-done.2, f32[18,18,128]{2,1,0:T(8,128)S(1)} %get-tuple-element.113), kind=kLoop, calls=%fused_computation.333 | loop fusion | flops 3151872 | bytes 925696 | tf_op jit(solution)/shard_map/sub | solution.py:81
  56.2 0.8 copy-done.29
  57.2 7.8 %collective-permute-start.4 = (f32[1,16,512]{2,1,0:T(8,128)S(1)}, f32[1,16,512]{2,1,0:T(8,128)S(1)}, u32[]{:S(2)}, u32[]{:S(2)}) collective-permute-start(f32[1,16,512]{2,1,0:T(8,128)S(1)} %get-tuple-element.135), channel_id=1, source_target_pairs={{0,4},{4,8},{8,12},{1,5},{5,9},{9,13},{2,6},{6,10},{10,14},{3,7},{... | collective-permute-start | bytes 98312 | tf_op jit(solution)/shard_map/ppermute | solution.py:17
  65.0 1.9 %collective-permute-start.5 = (f32[1,16,512]{2,1,0:T(8,128)S(1)}, f32[1,16,512]{2,1,0:T(8,128)S(1)}, u32[]{:S(2)}, u32[]{:S(2)}) collective-permute-start(f32[1,16,512]{2,1,0:T(8,128)S(1)} %get-tuple-element.136), channel_id=1, source_target_pairs={{4,0},{8,4},{12,8},{5,1},{9,5},{13,9},{6,2},{10,6},{14,10},{7,3},{... | collective-permute-start | bytes 98312 | tf_op jit(solution)/shard_map/ppermute | solution.py:18
  66.9 3.3 %collective-permute-done.5 = f32[1,16,512]{2,1,0:T(8,128)S(1)} collective-permute-done((f32[1,16,512]{2,1,0:T(8,128)S(1)}, f32[1,16,512]{2,1,0:T(8,128)S(1)}, u32[]{:S(2)}, u32[]{:S(2)}) %collective-permute-start.5) | collective-permute-done | bytes 32800 | tf_op jit(solution)/shard_map/ppermute | solution.py:18
  70.3 2.4 %collective-permute-start.6 = (f32[18,1,512]{2,1,0:T(1,128)S(1)}, f32[18,1,512]{2,1,0:T(1,128)S(1)}, u32[]{:S(2)}, u32[]{:S(2)}) collective-permute-start(f32[18,1,512]{2,1,0:T(1,128)S(1)} %get-tuple-element.127), channel_id=1, source_target_pairs={{0,1},{1,2},{2,3},{4,5},{5,6},{6,7},{8,9},{9,10},{10,11},{12,13},{... | collective-permute-start | bytes 110600 | tf_op jit(solution)/shard_map/ppermute | solution.py:17
  72.7 1.3 collective-permute-start.7
  74.0 3.4 %collective-permute-done.7 = f32[18,1,512]{2,1,0:T(1,128)S(1)} collective-permute-done((f32[18,1,512]{2,1,0:T(1,128)S(1)}, f32[18,1,512]{2,1,0:T(1,128)S(1)}, u32[]{:S(2)}, u32[]{:S(2)}) %collective-permute-start.7) | collective-permute-done | bytes 36896 | tf_op jit(solution)/shard_map/ppermute | solution.py:18
  77.6 3.8 %broadcast_multiply_fusion.6 = (f32[18,18,128]{2,1,0:T(8,128)}, f32[18,18,128]{2,1,0:T(8,128)}, f32[18,18,128]{2,1,0:T(8,128)S(1)}, f32[18,18,128]{2,1,0:T(8,128...) fusion(f32[18,18,512]{2,1,0:T(8,128)S(1)} %pad_maximum_fusion.1, ...), kind=kLoop, calls=%fused_computation.838 | loop fusion | flops 3732480 | bytes 3108864 | tf_op jit(solution)/shard_map/mul | solution.py:45
  81.6 1.4 %scatter-add.15 = f32[18,18,128]{2,1,0:T(8,128)S(1)} dynamic-update-slice(f32[18,18,128]{2,1,0:T(8,128)S(1)} %get-tuple-element.99, f32[18,18,1]{2,1,0:T(8,128)S(1)} %slice_add_fusion.2, s32[]{:T(128)} %constant.111.clone.1, s32[]{:T(128)} %constant.111.clone.1, s32[]{:T(128)} %constant.113.clone.1) | dynamic-update-slice | bytes 2596 | tf_op jit(solution)/shard_map/scatter-add | solution.py:121
  83.0 2.8 %fusion.49 = (f32[18,18,128]{2,1,0:T(8,128)S(1)}, f32[18,18,128]{2,1,0:T(8,128)S(1)}) fusion(f32[16,16,128]{2,1,0:T(8,128)S(1)} %copy-done.3, f32[18,18,128]{2,1,0:T(8,128)S(1)} %get-tuple-element.104, f32[16,16,128]{2,1,0:T(8,128)S(1)} %copy-done.2, f32[18,18,128]{2,1,0:T(8,128)S(1)} %get-tuple-element.103), kind=kLoop, calls=%fused_computation.351 | loop fusion | flops 3151872 | bytes 925696 | tf_op jit(solution)/shard_map/sub | solution.py:81
  86.0 0.7 copy-done.6
  87.2 3.3 %collective-permute-start.8 = (f32[1,16,512]{2,1,0:T(8,128)S(1)}, f32[1,16,512]{2,1,0:T(8,128)S(1)}, u32[]{:S(2)}, u32[]{:S(2)}) collective-permute-start(f32[1,16,512]{2,1,0:T(8,128)S(1)} %get-tuple-element.133), channel_id=1, source_target_pairs={{0,4},{4,8},{8,12},{1,5},{5,9},{9,13},{2,6},{6,10},{10,14},{3,7},{... | collective-permute-start | bytes 98312 | tf_op jit(solution)/shard_map/ppermute | solution.py:17
  90.6 1.9 %collective-permute-start.9 = (f32[1,16,512]{2,1,0:T(8,128)S(1)}, f32[1,16,512]{2,1,0:T(8,128)S(1)}, u32[]{:S(2)}, u32[]{:S(2)}) collective-permute-start(f32[1,16,512]{2,1,0:T(8,128)S(1)} %get-tuple-element.134), channel_id=1, source_target_pairs={{4,0},{8,4},{12,8},{5,1},{9,5},{13,9},{6,2},{10,6},{14,10},{7,3},{... | collective-permute-start | bytes 98312 | tf_op jit(solution)/shard_map/ppermute | solution.py:18
  92.5 3.3 %collective-permute-done.9 = f32[1,16,512]{2,1,0:T(8,128)S(1)} collective-permute-done((f32[1,16,512]{2,1,0:T(8,128)S(1)}, f32[1,16,512]{2,1,0:T(8,128)S(1)}, u32[]{:S(2)}, u32[]{:S(2)}) %collective-permute-start.9) | collective-permute-done | bytes 32800 | tf_op jit(solution)/shard_map/ppermute | solution.py:18
  95.9 1.6 %collective-permute-start.10 = (f32[18,1,512]{2,1,0:T(1,128)S(1)}, f32[18,1,512]{2,1,0:T(1,128)S(1)}, u32[]{:S(2)}, u32[]{:S(2)}) collective-permute-start(f32[18,1,512]{2,1,0:T(1,128)S(1)} %get-tuple-element.125), channel_id=1, source_target_pairs={{0,1},{1,2},{2,3},{4,5},{5,6},{6,7},{8,9},{9,10},{10,11},{12,13},{... | collective-permute-start | bytes 110600 | tf_op jit(solution)/shard_map/ppermute | solution.py:17
  97.5 1.3 collective-permute-start.11
  98.8 3.4 %collective-permute-done.11 = f32[18,1,512]{2,1,0:T(1,128)S(1)} collective-permute-done((f32[18,1,512]{2,1,0:T(1,128)S(1)}, f32[18,1,512]{2,1,0:T(1,128)S(1)}, u32[]{:S(2)}, u32[]{:S(2)}) %collective-permute-start.11) | collective-permute-done | bytes 36896 | tf_op jit(solution)/shard_map/ppermute | solution.py:18
  102.4 3.8 %broadcast_multiply_fusion.4 = (f32[18,18,128]{2,1,0:T(8,128)}, f32[18,18,128]{2,1,0:T(8,128)}, f32[18,18,128]{2,1,0:T(8,128)S(1)}, f32[18,18,128]{2,1,0:T(8,128...) fusion(f32[18,18,512]{2,1,0:T(8,128)S(1)} %pad_maximum_fusion.2, ...), kind=kLoop, calls=%fused_computation.836 | loop fusion | flops 3732480 | bytes 3108864 | tf_op jit(solution)/shard_map/mul | solution.py:82
  106.4 1.4 %scatter-add.16 = f32[18,18,128]{2,1,0:T(8,128)S(1)} dynamic-update-slice(f32[18,18,128]{2,1,0:T(8,128)S(1)} %get-tuple-element.89, f32[18,18,1]{2,1,0:T(8,128)S(1)} %slice_add_fusion.1, s32[]{:T(128)} %constant.111.clone.1, s32[]{:T(128)} %constant.111.clone.1, s32[]{:T(128)} %constant.113.clone.1) | dynamic-update-slice | bytes 2596 | tf_op jit(solution)/shard_map/scatter-add | solution.py:121
  107.9 6.6 %fusion.67 = (f32[18,18,128]{2,1,0:T(8,128)S(1)}, f32[18,18,128]{2,1,0:T(8,128)S(1)}) fusion(f32[16,16,128]{2,1,0:T(8,128)S(1)} %copy-done.3, f32[18,18,128]{2,1,0:T(8,128)} %get-tuple-element.94, f32[16,16,128]{2,1,0:T(8,128)S(1)} %copy-done.2, f32[18,18,128]{2,1,0:T(8,128)S(1)} %get-tuple-element.93), kind=kLoop, calls=%fused_computation.369 | loop fusion | flops 3151872 | bytes 925696 | tf_op jit(solution)/shard_map/sub | solution.py:81
  114.6 0.8 copy-done.20
  115.7 3.3 %collective-permute-start.12 = (f32[1,16,512]{2,1,0:T(8,128)S(1)}, f32[1,16,512]{2,1,0:T(8,128)S(1)}, u32[]{:S(2)}, u32[]{:S(2)}) collective-permute-start(f32[1,16,512]{2,1,0:T(8,128)S(1)} %get-tuple-element.131), channel_id=1, source_target_pairs={{0,4},{4,8},{8,12},{1,5},{5,9},{9,13},{2,6},{6,10},{10,14},{3,7},{... | collective-permute-start | bytes 98312 | tf_op jit(solution)/shard_map/ppermute | solution.py:17
  119.1 1.9 %collective-permute-start.13 = (f32[1,16,512]{2,1,0:T(8,128)S(1)}, f32[1,16,512]{2,1,0:T(8,128)S(1)}, u32[]{:S(2)}, u32[]{:S(2)}) collective-permute-start(f32[1,16,512]{2,1,0:T(8,128)S(1)} %get-tuple-element.132), channel_id=1, source_target_pairs={{4,0},{8,4},{12,8},{5,1},{9,5},{13,9},{6,2},{10,6},{14,10},{7,3},{... | collective-permute-start | bytes 98312 | tf_op jit(solution)/shard_map/ppermute | solution.py:18
  121.0 3.3 %collective-permute-done.13 = f32[1,16,512]{2,1,0:T(8,128)S(1)} collective-permute-done((f32[1,16,512]{2,1,0:T(8,128)S(1)}, f32[1,16,512]{2,1,0:T(8,128)S(1)}, u32[]{:S(2)}, u32[]{:S(2)}) %collective-permute-start.13) | collective-permute-done | bytes 32800 | tf_op jit(solution)/shard_map/ppermute | solution.py:18
  124.4 1.6 %collective-permute-start.14 = (f32[18,1,512]{2,1,0:T(1,128)S(1)}, f32[18,1,512]{2,1,0:T(1,128)S(1)}, u32[]{:S(2)}, u32[]{:S(2)}) collective-permute-start(f32[18,1,512]{2,1,0:T(1,128)S(1)} %get-tuple-element.123), channel_id=1, source_target_pairs={{0,1},{1,2},{2,3},{4,5},{5,6},{6,7},{8,9},{9,10},{10,11},{12,13},{... | collective-permute-start | bytes 110600 | tf_op jit(solution)/shard_map/ppermute | solution.py:17
  126.0 1.5 %collective-permute-start.15 = (f32[18,1,512]{2,1,0:T(1,128)S(1)}, f32[18,1,512]{2,1,0:T(1,128)S(1)}, u32[]{:S(2)}, u32[]{:S(2)}) collective-permute-start(f32[18,1,512]{2,1,0:T(1,128)S(1)} %get-tuple-element.124), channel_id=1, source_target_pairs={{1,0},{2,1},{3,2},{5,4},{6,5},{7,6},{9,8},{10,9},{11,10},{13,12},{... | collective-permute-start | bytes 110600 | tf_op jit(solution)/shard_map/ppermute | solution.py:18
  127.5 3.2 %collective-permute-done.15 = f32[18,1,512]{2,1,0:T(1,128)S(1)} collective-permute-done((f32[18,1,512]{2,1,0:T(1,128)S(1)}, f32[18,1,512]{2,1,0:T(1,128)S(1)}, u32[]{:S(2)}, u32[]{:S(2)}) %collective-permute-start.15) | collective-permute-done | bytes 36896 | tf_op jit(solution)/shard_map/ppermute | solution.py:18
  130.9 4.3 %broadcast_multiply_fusion = (f32[18,18,128]{2,1,0:T(8,128)}, f32[18,18,128]{2,1,0:T(8,128)}, f32[18,18,128]{2,1,0:T(8,128)}, f32[18,18,128]{2,1,0:T(8,128)}, f3...) fusion(f32[18,18,512]{2,1,0:T(8,128)S(1)} %pad_maximum_fusion.3, ...), kind=kLoop, calls=%fused_computation.832 | loop fusion | flops 5225472 | bytes 2942976 | tf_op jit(solution)/shard_map/mul | solution.py:45
  135.4 1.4 %scatter-add.19 = f32[18,18,128]{2,1,0:T(8,128)S(1)} dynamic-update-slice(f32[18,18,128]{2,1,0:T(8,128)S(1)} %get-tuple-element.80, f32[18,18,1]{2,1,0:T(8,128)S(1)} %slice_add_fusion, s32[]{:T(128)} %constant.111.clone.1, s32[]{:T(128)} %constant.111.clone.1, s32[]{:T(128)} %constant.113.clone.1) | dynamic-update-slice | bytes 2596 | tf_op jit(solution)/shard_map/scatter-add | solution.py:121
  136.9 2.3 %fusion.87 = (f32[18,18,128]{2,1,0:T(8,128)S(1)}, f32[18,18,128]{2,1,0:T(8,128)S(1)}) fusion(f32[16,16,128]{2,1,0:T(8,128)S(1)} %copy-done.3, f32[18,18,128]{2,1,0:T(8,128)S(1)} %get-tuple-element.85, f32[16,16,128]{2,1,0:T(8,128)S(1)} %copy-done.2), kind=kLoop, calls=%fused_computation.389 | loop fusion | flops 1741824 | bytes 759808 | tf_op jit(solution)/shard_map/add | solution.py:67
  139.2 0.8 fusion.464
  140.4 1.0 fusion.472
  (106 shorter events, 4.2 us)
Async XLA Ops:
  0.6 10.0 %copy-start = (f32[16,64]{1,0:T(8,128)S(1)}, f32[16,64]{1,0:T(8,128)}, u32[]{:S(2)}) copy-start(f32[16,64]{1,0:T(8,128)} %param.38) | copy-start | bytes 12292
  0.6 1.0 copy-start.25
  1.6 0.9 copy-start.7
  2.5 0.9 copy-start.24
  3.5 37.6 %collective-permute-start = (f32[1,16,512]{2,1,0:T(8,128)S(1)}, f32[1,16,512]{2,1,0:T(8,128)S(1)}, u32[]{:S(2)}, u32[]{:S(2)}) collective-permute-start(f32[1,16,512]{2,1,0:T(8,128)S(1)} %get-tuple-element.137), channel_id=1, source_target_pairs={{0,4},{4,8},{8,12},{1,5},{5,9},{9,13},{2,6},{6,10},{10,14},{3,7},{... | collective-permute-start | bytes 98312 | tf_op jit(solution)/shard_map/ppermute | solution.py:17
  8.0 33.1 %collective-permute-start.1 = (f32[1,16,512]{2,1,0:T(8,128)S(1)}, f32[1,16,512]{2,1,0:T(8,128)S(1)}, u32[]{:S(2)}, u32[]{:S(2)}) collective-permute-start(f32[1,16,512]{2,1,0:T(8,128)S(1)} %get-tuple-element.138), channel_id=1, source_target_pairs={{4,0},{8,4},{12,8},{5,1},{9,5},{13,9},{6,2},{10,6},{14,10},{7,3},{... | collective-permute-start | bytes 98312 | tf_op jit(solution)/shard_map/ppermute | solution.py:18
  39.3 0.7 copy-start.31
  41.2 2.8 %collective-permute-start.2 = (f32[18,1,512]{2,1,0:T(1,128)S(1)}, f32[18,1,512]{2,1,0:T(1,128)S(1)}, u32[]{:S(2)}, u32[]{:S(2)}) collective-permute-start(f32[18,1,512]{2,1,0:T(1,128)S(1)} %get-tuple-element.129), channel_id=1, source_target_pairs={{0,1},{1,2},{2,3},{4,5},{5,6},{6,7},{8,9},{9,10},{10,11},{12,13},{... | collective-permute-start | bytes 110600 | tf_op jit(solution)/shard_map/ppermute | solution.py:17
  42.5 4.7 %collective-permute-start.3 = (f32[18,1,512]{2,1,0:T(1,128)S(1)}, f32[18,1,512]{2,1,0:T(1,128)S(1)}, u32[]{:S(2)}, u32[]{:S(2)}) collective-permute-start(f32[18,1,512]{2,1,0:T(1,128)S(1)} %get-tuple-element.130), channel_id=1, source_target_pairs={{1,0},{2,1},{3,2},{5,4},{6,5},{7,6},{9,8},{10,9},{11,10},{13,12},{... | collective-permute-start | bytes 110600 | tf_op jit(solution)/shard_map/ppermute | solution.py:18
  47.3 0.9 copy-start.1
  47.3 1.0 copy-start.2
  47.3 1.0 copy-start.3
  47.4 1.1 copy-start.4
  47.4 1.1 copy-start.5
  47.4 1.2 copy-start.27
  53.2 2.8 %copy-start.28 = (f32[16,16,128]{2,1,0:T(8,128)S(1)}, f32[16,16,128]{2,1,0:T(8,128)}, u32[]{:S(2)}) copy-start(f32[16,16,128]{2,1,0:T(8,128)} %param.31) | copy-start | bytes 393220
  56.0 0.9 copy-start.29
  56.0 1.0 copy-start.30
  57.2 9.8 %collective-permute-start.4 = (f32[1,16,512]{2,1,0:T(8,128)S(1)}, f32[1,16,512]{2,1,0:T(8,128)S(1)}, u32[]{:S(2)}, u32[]{:S(2)}) collective-permute-start(f32[1,16,512]{2,1,0:T(8,128)S(1)} %get-tuple-element.135), channel_id=1, source_target_pairs={{0,4},{4,8},{8,12},{1,5},{5,9},{9,13},{2,6},{6,10},{10,14},{3,7},{... | collective-permute-start | bytes 98312 | tf_op jit(solution)/shard_map/ppermute | solution.py:17
  65.0 5.2 %collective-permute-start.5 = (f32[1,16,512]{2,1,0:T(8,128)S(1)}, f32[1,16,512]{2,1,0:T(8,128)S(1)}, u32[]{:S(2)}, u32[]{:S(2)}) collective-permute-start(f32[1,16,512]{2,1,0:T(8,128)S(1)} %get-tuple-element.136), channel_id=1, source_target_pairs={{4,0},{8,4},{12,8},{5,1},{9,5},{13,9},{6,2},{10,6},{14,10},{7,3},{... | collective-permute-start | bytes 98312 | tf_op jit(solution)/shard_map/ppermute | solution.py:18
  70.3 3.7 %collective-permute-start.6 = (f32[18,1,512]{2,1,0:T(1,128)S(1)}, f32[18,1,512]{2,1,0:T(1,128)S(1)}, u32[]{:S(2)}, u32[]{:S(2)}) collective-permute-start(f32[18,1,512]{2,1,0:T(1,128)S(1)} %get-tuple-element.127), channel_id=1, source_target_pairs={{0,1},{1,2},{2,3},{4,5},{5,6},{6,7},{8,9},{9,10},{10,11},{12,13},{... | collective-permute-start | bytes 110600 | tf_op jit(solution)/shard_map/ppermute | solution.py:17
  72.7 4.7 %collective-permute-start.7 = (f32[18,1,512]{2,1,0:T(1,128)S(1)}, f32[18,1,512]{2,1,0:T(1,128)S(1)}, u32[]{:S(2)}, u32[]{:S(2)}) collective-permute-start(f32[18,1,512]{2,1,0:T(1,128)S(1)} %get-tuple-element.128), channel_id=1, source_target_pairs={{1,0},{2,1},{3,2},{5,4},{6,5},{7,6},{9,8},{10,9},{11,10},{13,12},{... | collective-permute-start | bytes 110600 | tf_op jit(solution)/shard_map/ppermute | solution.py:18
  83.0 2.8 %copy-start.17 = (f32[18,18,128]{2,1,0:T(8,128)S(1)}, f32[18,18,128]{2,1,0:T(8,128)}, u32[]{:S(2)}) copy-start(f32[18,18,128]{2,1,0:T(8,128)} %get-tuple-element.100) | copy-start | bytes 497668
  83.0 2.8 %copy-start.18 = (f32[18,18,128]{2,1,0:T(8,128)S(1)}, f32[18,18,128]{2,1,0:T(8,128)}, u32[]{:S(2)}) copy-start(f32[18,18,128]{2,1,0:T(8,128)} %get-tuple-element.101) | copy-start | bytes 497668
  83.0 2.8 %copy-start.19 = (f32[18,18,128]{2,1,0:T(8,128)S(1)}, f32[18,18,128]{2,1,0:T(8,128)}, u32[]{:S(2)}) copy-start(f32[18,18,128]{2,1,0:T(8,128)} %get-tuple-element.102) | copy-start | bytes 497668
  85.9 0.9 copy-start.6
  85.9 1.0 copy-start.22
  85.9 1.1 copy-start.23
  85.9 1.2 copy-start.26
  87.2 5.3 %collective-permute-start.8 = (f32[1,16,512]{2,1,0:T(8,128)S(1)}, f32[1,16,512]{2,1,0:T(8,128)S(1)}, u32[]{:S(2)}, u32[]{:S(2)}) collective-permute-start(f32[1,16,512]{2,1,0:T(8,128)S(1)} %get-tuple-element.133), channel_id=1, source_target_pairs={{0,4},{4,8},{8,12},{1,5},{5,9},{9,13},{2,6},{6,10},{10,14},{3,7},{... | collective-permute-start | bytes 98312 | tf_op jit(solution)/shard_map/ppermute | solution.py:17
  90.6 5.2 %collective-permute-start.9 = (f32[1,16,512]{2,1,0:T(8,128)S(1)}, f32[1,16,512]{2,1,0:T(8,128)S(1)}, u32[]{:S(2)}, u32[]{:S(2)}) collective-permute-start(f32[1,16,512]{2,1,0:T(8,128)S(1)} %get-tuple-element.134), channel_id=1, source_target_pairs={{4,0},{8,4},{12,8},{5,1},{9,5},{13,9},{6,2},{10,6},{14,10},{7,3},{... | collective-permute-start | bytes 98312 | tf_op jit(solution)/shard_map/ppermute | solution.py:18
  95.9 3.0 %collective-permute-start.10 = (f32[18,1,512]{2,1,0:T(1,128)S(1)}, f32[18,1,512]{2,1,0:T(1,128)S(1)}, u32[]{:S(2)}, u32[]{:S(2)}) collective-permute-start(f32[18,1,512]{2,1,0:T(1,128)S(1)} %get-tuple-element.125), channel_id=1, source_target_pairs={{0,1},{1,2},{2,3},{4,5},{5,6},{6,7},{8,9},{9,10},{10,11},{12,13},{... | collective-permute-start | bytes 110600 | tf_op jit(solution)/shard_map/ppermute | solution.py:17
  97.5 4.7 %collective-permute-start.11 = (f32[18,1,512]{2,1,0:T(1,128)S(1)}, f32[18,1,512]{2,1,0:T(1,128)S(1)}, u32[]{:S(2)}, u32[]{:S(2)}) collective-permute-start(f32[18,1,512]{2,1,0:T(1,128)S(1)} %get-tuple-element.126), channel_id=1, source_target_pairs={{1,0},{2,1},{3,2},{5,4},{6,5},{7,6},{9,8},{10,9},{11,10},{13,12},{... | collective-permute-start | bytes 110600 | tf_op jit(solution)/shard_map/ppermute | solution.py:18
  107.9 6.6 %copy-start.14 = (f32[18,18,128]{2,1,0:T(8,128)S(1)}, f32[18,18,128]{2,1,0:T(8,128)}, u32[]{:S(2)}) copy-start(f32[18,18,128]{2,1,0:T(8,128)} %get-tuple-element.90) | copy-start | bytes 497668
  107.9 6.6 %copy-start.15 = (f32[18,18,128]{2,1,0:T(8,128)S(1)}, f32[18,18,128]{2,1,0:T(8,128)}, u32[]{:S(2)}) copy-start(f32[18,18,128]{2,1,0:T(8,128)} %get-tuple-element.91) | copy-start | bytes 497668
  107.9 6.6 %copy-start.16 = (f32[18,18,128]{2,1,0:T(8,128)S(1)}, f32[18,18,128]{2,1,0:T(8,128)}, u32[]{:S(2)}) copy-start(f32[18,18,128]{2,1,0:T(8,128)} %get-tuple-element.92) | copy-start | bytes 497668
  114.5 0.9 copy-start.20
  114.5 1.0 copy-start.21
  115.7 5.3 %collective-permute-start.12 = (f32[1,16,512]{2,1,0:T(8,128)S(1)}, f32[1,16,512]{2,1,0:T(8,128)S(1)}, u32[]{:S(2)}, u32[]{:S(2)}) collective-permute-start(f32[1,16,512]{2,1,0:T(8,128)S(1)} %get-tuple-element.131), channel_id=1, source_target_pairs={{0,4},{4,8},{8,12},{1,5},{5,9},{9,13},{2,6},{6,10},{10,14},{3,7},{... | collective-permute-start | bytes 98312 | tf_op jit(solution)/shard_map/ppermute | solution.py:17
  119.1 5.2 %collective-permute-start.13 = (f32[1,16,512]{2,1,0:T(8,128)S(1)}, f32[1,16,512]{2,1,0:T(8,128)S(1)}, u32[]{:S(2)}, u32[]{:S(2)}) collective-permute-start(f32[1,16,512]{2,1,0:T(8,128)S(1)} %get-tuple-element.132), channel_id=1, source_target_pairs={{4,0},{8,4},{12,8},{5,1},{9,5},{13,9},{6,2},{10,6},{14,10},{7,3},{... | collective-permute-start | bytes 98312 | tf_op jit(solution)/shard_map/ppermute | solution.py:18
  124.4 3.1 %collective-permute-start.14 = (f32[18,1,512]{2,1,0:T(1,128)S(1)}, f32[18,1,512]{2,1,0:T(1,128)S(1)}, u32[]{:S(2)}, u32[]{:S(2)}) collective-permute-start(f32[18,1,512]{2,1,0:T(1,128)S(1)} %get-tuple-element.123), channel_id=1, source_target_pairs={{0,1},{1,2},{2,3},{4,5},{5,6},{6,7},{8,9},{9,10},{10,11},{12,13},{... | collective-permute-start | bytes 110600 | tf_op jit(solution)/shard_map/ppermute | solution.py:17
  126.0 4.7 %collective-permute-start.15 = (f32[18,1,512]{2,1,0:T(1,128)S(1)}, f32[18,1,512]{2,1,0:T(1,128)S(1)}, u32[]{:S(2)}, u32[]{:S(2)}) collective-permute-start(f32[18,1,512]{2,1,0:T(1,128)S(1)} %get-tuple-element.124), channel_id=1, source_target_pairs={{1,0},{2,1},{3,2},{5,4},{6,5},{7,6},{9,8},{10,9},{11,10},{13,12},{... | collective-permute-start | bytes 110600 | tf_op jit(solution)/shard_map/ppermute | solution.py:18
  136.9 2.3 %copy-start.11 = (f32[18,18,128]{2,1,0:T(8,128)S(1)}, f32[18,18,128]{2,1,0:T(8,128)}, u32[]{:S(2)}) copy-start(f32[18,18,128]{2,1,0:T(8,128)} %get-tuple-element.76) | copy-start | bytes 497668
  136.9 2.3 %copy-start.12 = (f32[18,18,128]{2,1,0:T(8,128)S(1)}, f32[18,18,128]{2,1,0:T(8,128)}, u32[]{:S(2)}) copy-start(f32[18,18,128]{2,1,0:T(8,128)} %get-tuple-element.81) | copy-start | bytes 497668
  136.9 2.3 %copy-start.13 = (f32[18,18,128]{2,1,0:T(8,128)S(1)}, f32[18,18,128]{2,1,0:T(8,128)}, u32[]{:S(2)}) copy-start(f32[18,18,128]{2,1,0:T(8,128)} %get-tuple-element.82) | copy-start | bytes 497668
  139.2 0.9 copy-start.8
  139.2 1.1 copy-start.9
  139.2 1.2 copy-start.10
  (1 other events, 0.7 us)
where the time goes:
time: 142 us; the launch traced here: 141 us
  starting transfers between devices  39 us (27%)
  other arithmetic  33.5 us (24%)
  blocking collectives  28.7 us (20%)
  waiting for transfers between devices  23.2 us (16%)
  local copies, waits for them, and re-layouts  14.5 us (10%)
  between operations  2.13 us (2%)
    all_gather x1, blocking collectives, per_device(): everyone = lax.all_gather(window, ('gx', 'gy'), axis=1, tiled=True)  28.7 us
    ppermute x8, starting transfers between devices, padded_2(): before = lax.ppermute(last, axis, up)  26 us
    ppermute x8, waiting for transfers between devices, padded_2(): after = lax.ppermute(initial, axis, down)  23.1 us
    ppermute x8, starting transfers between devices, padded_2(): after = lax.ppermute(initial, axis, down)  13 us
    sub x3, other arithmetic, advance(): p_across = p_laplace - p_axis  12.1 us
    unnamed x71, local copies, waits for them, and re-layouts  8.43 us
    mul x2, other arithmetic, rotated(): d_xx = padded[2:, 1:-1, 1:-1] - 2.0 * center + padded[:-2, 1:-1, 1:-1]  8.05 us
    mul x2, other arithmetic, advance(): 2.0 * p_now - p_prev  6.82 us
  transfers between devices with their start and end apart: 16, of which 7 were waited for; matrix products, arithmetic and copies ran while one was open for 1% of the time, Pallas kernels for 0%

commit v1 on v0

v1 whole, which is shorter than its diff:
```python
import functools

import jax
import jax.numpy as jnp
from jax import lax
from jax.experimental import pallas as pl
from jax.experimental.pallas import tpu as pltpu
from jax.sharding import PartitionSpec as P

STEPS = 4
REC_DEPTH = 4
RIM = STEPS
FIELDS = 8
VMEM_LIMIT = 48 * 1024 * 1024
HIGH = 1
LOW = -1


def whole_vmem(count):
    return [pl.BlockSpec(memory_space=pltpu.VMEM)] * count


DIRECTIONS = ((0, HIGH), (0, LOW), (HIGH, 0), (LOW, 0), (HIGH, HIGH), (HIGH, LOW), (LOW, HIGH), (LOW, LOW))


def rim_range(direction, length):
    if direction == 0:
        return slice(0, length)
    return slice(length - RIM, length) if direction == HIGH else slice(0, RIM)


def pack_kernel(count, *refs):
    blocks, packed = refs[:count], refs[count:]
    cells_x, cells_y = blocks[0].shape[:2]
    for out, (dir_x, dir_y) in zip(packed, DIRECTIONS):
        for number, block in enumerate(blocks):
            out[number] = block[rim_range(dir_x, cells_x), rim_range(dir_y, cells_y), :]


def pack(blocks):
    cells_x, cells_y, depth = blocks[0].shape
    count = len(blocks)
    shapes = [
        jax.ShapeDtypeStruct(
            (count, RIM if dir_x else cells_x, RIM if dir_y else cells_y, depth), jnp.float32
        )
        for dir_x, dir_y in DIRECTIONS
    ]
    return pl.pallas_call(
        functools.partial(pack_kernel, count),
        out_shape=shapes,
        in_specs=whole_vmem(count),
        out_specs=whole_vmem(len(shapes)),
        compiler_params=pltpu.CompilerParams(vmem_limit_bytes=VMEM_LIMIT),
        name="pack_rims",
    )(*blocks)


def send(value, direction):
    dir_x, dir_y = direction
    size_x, size_y = lax.axis_size("gx"), lax.axis_size("gy")
    pairs = [
        (x * size_y + y, (x + dir_x) * size_y + y + dir_y)
        for x in range(size_x)
        for y in range(size_y)
        if 0 <= x + dir_x < size_x and 0 <= y + dir_y < size_y
    ]
    return lax.ppermute(value, ("gx", "gy"), pairs)


def shifted_z(plane, lane):
    depth = plane.shape[-1]
    above = jnp.where(lane < depth - 1, pltpu.roll(plane, depth - 1, 1), 0.0)
    below = jnp.where(lane > 0, pltpu.roll(plane, 1, 1), 0.0)
    return above, below


def shifted_y(plane):
    rows = plane.shape[0]
    return pltpu.roll(plane, rows - 1, 0), pltpu.roll(plane, 1, 0)


def slopes(plane, lane):
    above, below = shifted_z(plane, lane)
    after, before = shifted_y(plane)
    return after - before, above - below, after + before, above + below


def main_kernel(count, cells_x, cells_y, *refs):
    blocks = refs[:count]
    rims = refs[count : count + len(DIRECTIONS)]
    planes = refs[count + len(DIRECTIONS)]
    image, p_last, q_last = refs[count + len(DIRECTIONS) + 1 : count + len(DIRECTIONS) + 4]
    scratch = refs[count + len(DIRECTIONS) + 4 :]
    waves, model, factors = scratch
    span_x = cells_x + 2 * RIM
    rows = cells_y + 2 * RIM
    depth = blocks[0].shape[-1]

    def place_x(direction):
        if direction == 0:
            return slice(RIM, RIM + cells_x)
        return slice(0, RIM) if direction == HIGH else slice(RIM + cells_x, span_x)

    def place_y(direction):
        if direction == 0:
            return slice(0, cells_y)
        return slice(cells_y + RIM, rows) if direction == HIGH else slice(cells_y, cells_y + RIM)

    targets = [waves.at[number, slot] for number in range(4) for slot in range(2)]
    targets += [model.at[number] for number in range(count - FIELDS)]
    for number, target in enumerate(targets):
        target[place_x(0), place_y(0), :] = blocks[number][...]
        for (dir_x, dir_y), rim in zip(DIRECTIONS, rims):
            target[place_x(dir_x), place_y(dir_y), :] = rim[number]

    lane = lax.broadcasted_iota(jnp.int32, (rows, depth), 1)

    def make_factors(x, carry):
        velocity = model[0, x]
        f_e = 1.0 + 2.0 * model[1, x]
        f_d = jnp.sqrt(1.0 + 2.0 * model[2, x])
        tilt = model[3, x]
        azimuth = model[4, x]
        sin_tilt, cos_tilt = jnp.sin(tilt), jnp.cos(tilt)
        sin_azim, cos_azim = jnp.sin(azimuth), jnp.cos(azimuth)
        sin_square = sin_tilt * sin_tilt
        double_tilt = 0.5 * sin_tilt * cos_tilt
        factors[0, x] = velocity
        factors[1, x] = velocity * f_e
        factors[2, x] = velocity * f_d
        factors[3, x] = sin_square * cos_azim * cos_azim
        factors[4, x] = sin_square * sin_azim * sin_azim
        factors[5, x] = cos_tilt * cos_tilt
        factors[6, x] = 0.5 * sin_square * sin_azim * cos_azim
        factors[7, x] = double_tilt * cos_azim
        factors[8, x] = double_tilt * sin_azim
        return carry

    lax.fori_loop(1, span_x - 1, make_factors, 0)

    def step(pair, turn, plane_ref):
        p_number, q_number = 2 * pair, 2 * pair + 1
        first, last = turn + 1, span_x - 1 - turn

        def stencil(number, x, before, now):
            u_now = waves[number, turn + 1, x]
            u_after = waves[number, turn + 1, x + 1]
            u_before = waves[number, turn + 1, x - 1]
            dy_after, dz_after, sy_after, sz_after = slopes(u_after, lane)
            dy_now, dz_now, sy_now, sz_now = now
            dy_before, dz_before = before
            double = 2.0 * u_now
            d_xx = (u_after + u_before) - double
            d_yy = sy_now - double
            d_zz = sz_now - double
            d_xy = dy_after - dy_before
            d_xz = dz_after - dz_before
            dz_up, dz_down = shifted_y(dz_now)
            d_yz = dz_up - dz_down
            along = (
                factors[3, x] * d_xx
                + factors[4, x] * d_yy
                + factors[5, x] * d_zz
                + factors[6, x] * d_xy
                + factors[7, x] * d_xz
                + factors[8, x] * d_yz
            )
            return (
                along,
                (d_xx + d_yy) + d_zz,
                double,
                (dy_now, dz_now),
                (dy_after, dz_after, sy_after, sz_after),
            )

        def body(x, carry):
            p_before, p_now, q_before, q_now = carry
            p_axis, p_laplace, p_double, p_before, p_now = stencil(p_number, x, p_before, p_now)
            q_axis, _, q_double, q_before, q_now = stencil(q_number, x, q_before, q_now)
            across = p_laplace - p_axis
            p_next = (p_double - waves[p_number, turn, x]) + (
                factors[1, x] * across + factors[2, x] * q_axis
            )
            q_next = (q_double - waves[q_number, turn, x]) + (
                factors[2, x] * across + factors[0, x] * q_axis
            )
            if plane_ref is not None:
                moved = pltpu.roll(plane_ref[...], lax.rem(REC_DEPTH - x + depth, depth), 1)
                p_next = p_next + jnp.where(lane == REC_DEPTH, moved, 0.0)
            waves[p_number, turn + 2, x] = p_next
            waves[q_number, turn + 2, x] = q_next
            return p_before, p_now, q_before, q_now

        def start(number):
            before = slopes(waves[number, turn + 1, first - 1], lane)
            now = slopes(waves[number, turn + 1, first], lane)
            return before[:2], now

        p_before, p_now = start(p_number)
        q_before, q_now = start(q_number)
        lax.fori_loop(first, last, body, (p_before, p_now, q_before, q_now))

    for turn in range(STEPS):
        step(0, turn, None)
    for turn in range(STEPS):
        step(1, turn, planes.at[STEPS - 1 - turn])

    def finish(x, carry):
        total = waves[0, 1 + STEPS, x, :cells_y] * waves[2, 1, x, :cells_y]
        for back in range(1, STEPS + 1):
            total = total + waves[0, 1 + STEPS - back, x, :cells_y] * waves[2, 1 + back, x, :cells_y]
        image[x - RIM] = total
        p_last[x - RIM] = waves[2, 1 + STEPS, x, :cells_y]
        q_last[x - RIM] = waves[3, 1 + STEPS, x, :cells_y]
        return carry

    lax.fori_loop(RIM, RIM + cells_x, finish, 0)


def migrate(blocks, rims, planes):
    cells_x, cells_y, depth = blocks[0].shape
    count = len(blocks)
    span_x, rows = cells_x + 2 * RIM, cells_y + 2 * RIM
    out = jax.ShapeDtypeStruct((cells_x, cells_y, depth), jnp.float32)
    return pl.pallas_call(
        functools.partial(main_kernel, count, cells_x, cells_y),
        out_shape=[out] * 3,
        in_specs=whole_vmem(count + len(rims) + 1),
        out_specs=whole_vmem(3),
        scratch_shapes=[
            pltpu.VMEM((4, STEPS + 2, span_x, rows, depth), jnp.float32),
            pltpu.VMEM((count - FIELDS, span_x, rows, depth), jnp.float32),
            pltpu.VMEM((9, span_x, rows, depth), jnp.float32),
        ],
        compiler_params=pltpu.CompilerParams(vmem_limit_bytes=VMEM_LIMIT),
        name="migrate",
    )(*blocks, *rims, planes)


def gathered(window):
    devices = lax.axis_size("gx") * lax.axis_size("gy")
    copies = jnp.broadcast_to(window[None], (devices,) + window.shape)
    everyone = lax.all_to_all(copies, ("gx", "gy"), 0, 0)
    return everyone.transpose(1, 0, 2).reshape(window.shape[0], -1)


def injected(everyone, receiver_x, receiver_y, cells_x, cells_y, depth):
    x_global = lax.axis_index("gx") * cells_x - RIM + jnp.arange(depth, dtype=jnp.int32)
    y_local = jnp.arange(cells_y + 2 * RIM, dtype=jnp.int32)
    y_local = jnp.where(y_local < cells_y + RIM, y_local, y_local - cells_y - 2 * RIM)
    y_global = lax.axis_index("gy") * cells_y + y_local
    pick_x = (receiver_x[None, :] == x_global[:, None]).astype(jnp.float32)
    pick_y = (receiver_y[None, :] == y_global[:, None]).astype(jnp.float32)
    weighted = everyone[:, None, :] * pick_y[None, :, :]
    return jnp.einsum("kyr,xr->kyx", weighted, pick_x, precision=lax.Precision.HIGHEST)


def per_device(
    src_p_prev,
    src_p_now,
    src_q_prev,
    src_q_now,
    rec_p_next,
    rec_p_now,
    rec_q_next,
    rec_q_now,
    velocity_term,
    epsilon,
    delta,
    tilt,
    azimuth,
    traces,
    receiver_x,
    receiver_y,
    segment_start,
):
    blocks = (
        src_p_prev,
        src_p_now,
        src_q_prev,
        src_q_now,
        rec_p_next,
        rec_p_now,
        rec_q_next,
        rec_q_now,
        velocity_term,
        epsilon,
        delta,
        tilt,
        azimuth,
    )
    cells_x, cells_y, depth = src_p_now.shape
    window = lax.dynamic_slice_in_dim(traces, segment_start[0], STEPS, 0)
    everyone = gathered(window)
    rims = [send(packed, direction) for packed, direction in zip(pack(blocks), DIRECTIONS)]
    planes = injected(everyone, receiver_x, receiver_y, cells_x, cells_y, depth)
    return tuple(migrate(blocks, rims, planes))


def solution(mesh):
    state = P(("shot", "gx"), "gy", None)
    earth = P("gx", "gy", None)
    return jax.shard_map(
        per_device,
        mesh=mesh,
        in_specs=(state,) * FIELDS + (earth,) * 5 + (P("shot", ("gx", "gy")), P(), P(), P()),
        out_specs=(state,) * 3,
        check_vma=False,
    )
```

time: 142 us -> 78 us (0.55)
  other arithmetic: 33.5 us -> 1.37 us
  blocking collectives: 28.7 us -> 0 us
  Pallas kernels: 0 us -> 19.8 us
  starting transfers between devices: 39 us -> 25.6 us
  waiting for transfers between devices: 23.2 us -> 13.5 us
    all_gather x1 -> x0, blocking collectives: 28.7 us -> none  [per_device(): everyone = lax.all_gather(window, ('gx', 'gy'), axis=1, tiled=True)]
    pallas_call x0 -> x2, Pallas kernels: none -> 19.8 us  [the longest x1 18.3 us: migrate(): pl.pallas_call(functools.partial(main_kernel, count, cells_x, cells_y), o...]
    ppermute x16 -> x8, starting transfers between devices: 39 us -> 21.5 us  [send(): return lax.ppermute(value, ('gx', 'gy'), pairs)]
    mul x11 -> x0, other arithmetic: 16.5 us -> none  [the longest x2 8.05 us: rotated(): d_xx = padded[2:, 1:-1, 1:-1] - 2.0 * center + padded[:-2, 1:-1, 1:-1]]
    sub x3 -> x0, other arithmetic: 12.1 us -> none  [advance(): p_across = p_laplace - p_axis]
    ppermute x16 -> x8, waiting for transfers between devices: 23.2 us -> 13.5 us  [send(): return lax.ppermute(value, ('gx', 'gy'), pairs)]
    scatter-add x4 -> x0, local copies, waits for them, and re-layouts: 5.78 us -> none  [run_round(): p_next = p_next.at[:, :, REC_DEPTH].add(planes[sample])]
    unnamed x71 -> x62, local copies, waits for them, and re-layouts: 8.43 us -> 13.2 us
  transfers between devices with their start and end apart: 16 -> 9, of which waited for: 7 -> 3; matrix products, arithmetic and copies ran while one was open for 1% -> 5% of each run, Pallas kernels for 0% -> 0%
where the time goes in v1:
time: 78 us; the launch traced here: 77.2 us
  starting transfers between devices  25.6 us (33%)
  Pallas kernels  19.8 us (25%)
  local copies, waits for them, and re-layouts  13.9 us (18%)
  waiting for transfers between devices  13.5 us (17%)
  between operations  1.65 us (2%)
  other arithmetic  1.37 us (2%)
  matrix products  1.36 us (2%)
    ppermute x8, starting transfers between devices, send(): return lax.ppermute(value, ('gx', 'gy'), pairs)  21.5 us
    pallas_call x1, Pallas kernels, migrate(): pl.pallas_call(functools.partial(main_kernel, count, cells_x, cells_y), o...  18.3 us
    ppermute x8, waiting for transfers between devices, send(): return lax.ppermute(value, ('gx', 'gy'), pairs)  13.5 us
    unnamed x62, local copies, waits for them, and re-layouts  13.2 us
    all_to_all x1, starting transfers between devices, gathered(): everyone = lax.all_to_all(copies, ('gx', 'gy'), 0, 0)  4.12 us
  transfers between devices with their start and end apart: 9, of which 3 were waited for; matrix products, arithmetic and copies ran while one was open for 5% of the time, Pallas kernels for 0%

profile of v1, /device:TPU:1, one launch (start us, length us, event | category | flops | bytes accessed | tf_op | source)
XLA Modules:
  0.0 77.2 jit_solution(12884205873235829466)
XLA Ops:
  0.6 0.0 copy-start
  0.6 0.0 copy-start.1
  0.7 0.9 %copy-done.1 = f32[16,16,128]{2,1,0:T(8,128)S(1)} copy-done((f32[16,16,128]{2,1,0:T(8,128)S(1)}, f32[16,16,128]{2,1,0:T(8,128)}, u32[]{:S(2)}) %copy-start.1) | copy-done | bytes 131096
  1.6 0.9 %copy-done.3 = f32[16,16,128]{2,1,0:T(8,128)S(1)} copy-done((f32[16,16,128]{2,1,0:T(8,128)S(1)}, f32[16,16,128]{2,1,0:T(8,128)}, u32[]{:S(2)}) %copy-start.3) | copy-done | bytes 131096
  2.5 0.9 %copy-done.5 = f32[16,16,128]{2,1,0:T(8,128)S(1)} copy-done((f32[16,16,128]{2,1,0:T(8,128)S(1)}, f32[16,16,128]{2,1,0:T(8,128)}, u32[]{:S(2)}) %copy-start.5) | copy-done | bytes 131096
  3.4 0.9 %copy-done.7 = f32[16,16,128]{2,1,0:T(8,128)S(1)} copy-done((f32[16,16,128]{2,1,0:T(8,128)S(1)}, f32[16,16,128]{2,1,0:T(8,128)}, u32[]{:S(2)}) %copy-start.7) | copy-done | bytes 131096
  4.3 0.9 %copy-done.9 = f32[16,16,128]{2,1,0:T(8,128)S(1)} copy-done((f32[16,16,128]{2,1,0:T(8,128)S(1)}, f32[16,16,128]{2,1,0:T(8,128)}, u32[]{:S(2)}) %copy-start.9) | copy-done | bytes 131096
  5.2 0.9 %copy-done.11 = f32[16,16,128]{2,1,0:T(8,128)S(1)} copy-done((f32[16,16,128]{2,1,0:T(8,128)S(1)}, f32[16,16,128]{2,1,0:T(8,128)}, u32[]{:S(2)}) %copy-start.11) | copy-done | bytes 131096
  6.1 0.9 %copy-done.13 = f32[16,16,128]{2,1,0:T(8,128)S(1)} copy-done((f32[16,16,128]{2,1,0:T(8,128)S(1)}, f32[16,16,128]{2,1,0:T(8,128)}, u32[]{:S(2)}) %copy-start.13) | copy-done | bytes 131096
  7.0 0.9 %copy-done.15 = f32[16,16,128]{2,1,0:T(8,128)S(1)} copy-done((f32[16,16,128]{2,1,0:T(8,128)S(1)}, f32[16,16,128]{2,1,0:T(8,128)}, u32[]{:S(2)}) %copy-start.15) | copy-done | bytes 131096
  7.9 0.9 %copy-done.17 = f32[16,16,128]{2,1,0:T(8,128)S(1)} copy-done((f32[16,16,128]{2,1,0:T(8,128)S(1)}, f32[16,16,128]{2,1,0:T(8,128)}, u32[]{:S(2)}) %copy-start.17) | copy-done | bytes 131096
  8.8 0.9 %copy-done.19 = f32[16,16,128]{2,1,0:T(8,128)S(1)} copy-done((f32[16,16,128]{2,1,0:T(8,128)S(1)}, f32[16,16,128]{2,1,0:T(8,128)}, u32[]{:S(2)}) %copy-start.19) | copy-done | bytes 131096
  9.7 0.9 %copy-done.21 = f32[16,16,128]{2,1,0:T(8,128)S(1)} copy-done((f32[16,16,128]{2,1,0:T(8,128)S(1)}, f32[16,16,128]{2,1,0:T(8,128)}, u32[]{:S(2)}) %copy-start.21) | copy-done | bytes 131096
  10.6 0.9 %copy-done.23 = f32[16,16,128]{2,1,0:T(8,128)S(1)} copy-done((f32[16,16,128]{2,1,0:T(8,128)S(1)}, f32[16,16,128]{2,1,0:T(8,128)}, u32[]{:S(2)}) %copy-start.23) | copy-done | bytes 131096
  11.5 0.9 %copy-done.25 = f32[16,16,128]{2,1,0:T(8,128)S(1)} copy-done((f32[16,16,128]{2,1,0:T(8,128)S(1)}, f32[16,16,128]{2,1,0:T(8,128)}, u32[]{:S(2)}) %copy-start.25) | copy-done | bytes 131096
  12.5 1.5 %pack_rims.1 = (f32[13,16,4,128]{3,2,1,0:T(4,128)}, f32[13,16,4,128]{3,2,1,0:T(4,128)}, f32[13,4,16,128]{3,2,1,0:T(8,128)}, f32[13,4,16,128]{3,2,1,0:T(8,128)}, ...) custom-call(f32[16,16,128]{2,1,0:T(8,128)S(1)} %copy-done.1, ...), custom_call_target="tpu_custom_call" | custom-call | tf_op jit(solution)/shard_map/pack_rims/pallas_call | solution.py:49
  13.9 0.6 copy-done.27
  14.6 4.0 %collective-permute-start = (f32[13,16,4,128]{3,2,1,0:T(4,128)}, f32[13,16,4,128]{3,2,1,0:T(4,128)S(1)}, u32[]{:S(2)}, u32[]{:S(2)}) collective-permute-start(f32[13,16,4,128]{3,2,1,0:T(4,128)} %get-tuple-element.11), channel_id=1, source_target_pairs={{0,1},{1,2},{2,3},{4,5},{5,6},{6,7},{8,9},{9,10},{10,11},{12,13},{... | collective-permute-start | bytes 1277960 | tf_op jit(solution)/shard_map/ppermute | solution.py:68
  18.6 0.0 copy-start.12
  18.6 1.4 %collective-permute-start.1 = (f32[13,16,4,128]{3,2,1,0:T(4,128)}, f32[13,16,4,128]{3,2,1,0:T(4,128)S(1)}, u32[]{:S(2)}, u32[]{:S(2)}) collective-permute-start(f32[13,16,4,128]{3,2,1,0:T(4,128)} %get-tuple-element.12), channel_id=1, source_target_pairs={{1,0},{2,1},{3,2},{5,4},{6,5},{7,6},{9,8},{10,9},{11,10},{13,12},{... | collective-permute-start | bytes 1277960 | tf_op jit(solution)/shard_map/ppermute | solution.py:68
  20.1 4.0 %collective-permute-start.2 = (f32[13,4,16,128]{3,2,1,0:T(8,128)}, f32[13,4,16,128]{3,2,1,0:T(8,128)S(1)}, u32[]{:S(2)}, u32[]{:S(2)}) collective-permute-start(f32[13,4,16,128]{3,2,1,0:T(8,128)} %get-tuple-element.13), channel_id=1, source_target_pairs={{0,4},{1,5},{2,6},{3,7},{4,8},{5,9},{6,10},{7,11},{8,12},{9,13},{1... | collective-permute-start | bytes 1277960 | tf_op jit(solution)/shard_map/ppermute | solution.py:68
  24.0 1.9 %collective-permute-start.3 = (f32[13,4,16,128]{3,2,1,0:T(8,128)}, f32[13,4,16,128]{3,2,1,0:T(8,128)S(1)}, u32[]{:S(2)}, u32[]{:S(2)}) collective-permute-start(f32[13,4,16,128]{3,2,1,0:T(8,128)} %get-tuple-element.14), channel_id=1, source_target_pairs={{4,0},{5,1},{6,2},{7,3},{8,4},{9,5},{10,6},{11,7},{12,8},{13,9},{1... | collective-permute-start | bytes 1277960 | tf_op jit(solution)/shard_map/ppermute | solution.py:68
  26.0 5.7 %collective-permute-start.4 = (f32[13,4,4,128]{3,2,1,0:T(4,128)S(1)}, f32[13,4,4,128]{3,2,1,0:T(4,128)S(1)}, u32[]{:S(2)}, u32[]{:S(2)}) collective-permute-start(f32[13,4,4,128]{3,2,1,0:T(4,128)S(1)} %get-tuple-element.15), channel_id=1, source_target_pairs={{0,5},{1,6},{2,7},{4,9},{5,10},{6,11},{8,13},{9,14},{10,15},{16,21... | collective-permute-start | bytes 319496 | tf_op jit(solution)/shard_map/ppermute | solution.py:68
  32.4 0.7 reshape.52
  33.1 4.1 %all-to-all-start = ((f32[16,1,256]{2,1,0:T(1,128)}), f32[16,1,256]{2,1,0:T(1,128)S(1)}, u32[]{:S(2)}, u32[]{:S(2)}) async-start(f32[16,1,256]{2,1,0:T(1,128)} %reshape.52), calls=%async_computation | async-start | bytes 32768 | tf_op jit(solution)/shard_map/all_to_all | solution.py:244
  37.2 0.0 collective-permute-done.4.refs_17_
  37.2 1.3 %collective-permute-start.5 = (f32[13,4,4,128]{3,2,1,0:T(4,128)S(1)}, f32[13,4,4,128]{3,2,1,0:T(4,128)S(1)}, u32[]{:S(2)}, u32[]{:S(2)}) collective-permute-start(f32[13,4,4,128]{3,2,1,0:T(4,128)S(1)} %get-tuple-element.16), channel_id=1, source_target_pairs={{1,4},{2,5},{3,6},{5,8},{6,9},{7,10},{9,12},{10,13},{11,14},{17,20... | collective-permute-start | bytes 319496 | tf_op jit(solution)/shard_map/ppermute | solution.py:68
  38.5 0.0 copy-start.8
  38.5 0.7 compare_convert_fusion
  39.3 4.5 %collective-permute-done.5.refs_18_ = f32[13,4,4,128]{3,2,1,0:T(4,128)S(1)} collective-permute-done((f32[13,4,4,128]{3,2,1,0:T(4,128)S(1)}, f32[13,4,4,128]{3,2,1,0:T(4,128)S(1)}, u32[]{:S(2)}, u32[]{:S(2)}) %collective-permute-start.5) | collective-permute-done | bytes 106528 | tf_op jit(solution)/shard_map/ppermute | solution.py:68
  43.7 1.7 %collective-permute-start.6 = (f32[13,4,4,128]{3,2,1,0:T(4,128)}, f32[13,4,4,128]{3,2,1,0:T(4,128)S(1)}, u32[]{:S(2)}, u32[]{:S(2)}) collective-permute-start(f32[13,4,4,128]{3,2,1,0:T(4,128)} %get-tuple-element.17), channel_id=1, source_target_pairs={{4,1},{5,2},{6,3},{8,5},{9,6},{10,7},{12,9},{13,10},{14,11},{20,17... | collective-permute-start | bytes 319496 | tf_op jit(solution)/shard_map/ppermute | solution.py:68
  45.5 0.0 all-to-all-done
  45.5 0.5 broadcast.48
  46.0 0.6 reduce
  46.7 0.1 reshape.53
  46.8 0.0 copy-start.6
  46.8 0.1 mul.21
  46.9 0.6 collective-permute-done.6.refs_19_
  47.5 1.4 %collective-permute-start.7 = (f32[13,4,4,128]{3,2,1,0:T(4,128)}, f32[13,4,4,128]{3,2,1,0:T(4,128)S(1)}, u32[]{:S(2)}, u32[]{:S(2)}) collective-permute-start(f32[13,4,4,128]{3,2,1,0:T(4,128)} %copy-done.27), channel_id=1, source_target_pairs={{5,0},{6,1},{7,2},{9,4},{10,5},{11,6},{13,8},{14,9},{15,10},{21,16... | collective-permute-start | bytes 319496 | tf_op jit(solution)/shard_map/ppermute | solution.py:68
  48.9 1.4 %fusion.refs_21_ = f32[4,24,128]{2,1,0:T(8,128)S(1)} fusion(s32[1024]{0:T(1024)S(1)} %copy-done.29, s32[128]{0:T(128)S(1)} %iota_add_fusion, f32[24,1024]{1,0:T(8,128)} %compare_convert_fusion, f32[4,1024]{1,0:T(4,128)S(1)} %mul.21), kind=kOutput, calls=%fused_computation | convolution fusion | flops 151224320 | bytes 168448 | tf_op jit(solution)/shard_map/kyr,xr->kyx/dot_general | solution.py:256
  50.3 8.4 %collective-permute-done.7.refs_20_ = f32[13,4,4,128]{3,2,1,0:T(4,128)S(1)} collective-permute-done((f32[13,4,4,128]{3,2,1,0:T(4,128)}, f32[13,4,4,128]{3,2,1,0:T(4,128)S(1)}, u32[]{:S(2)}, u32[]{:S(2)}) %collective-permute-start.7) | collective-permute-done | bytes 106528 | tf_op jit(solution)/shard_map/ppermute | solution.py:68
  58.7 0.0 collective-permute-done.refs_13_
  58.7 0.0 collective-permute-done.1.refs_14_
  58.7 0.0 collective-permute-done.2.refs_15_
  58.7 0.0 collective-permute-done.3.refs_16_
  58.7 0.0 copy-done.14
  58.8 0.0 copy-done.16
  58.9 18.3 %migrate.1 = (f32[16,16,128]{2,1,0:T(8,128)}, f32[16,16,128]{2,1,0:T(8,128)}, f32[16,16,128]{2,1,0:T(8,128)}) custom-call(f32[16,16,128]{2,1,0:T(8,128)S(1)} %copy-done.2, f32[16,16,128]{2,1,0:T(8,128)S(1)} %copy-done.4, f32[16,16,128]{2,1,0:T(8,128)S(1)} %copy-done.6, f32[16,16,128]{2,1,0:T(8,128)S(1)} %copy-done.8, f32[16,16,128]{2,1,0:T(8,128)S(1)} %copy-done.10, ...), custom_call_target="tpu_custom_call" | custom-call | tf_op jit(solution)/shard_map/migrate/pallas_call | solution.py:226
  (44 shorter events, 0.1 us)
Async XLA Ops:
  0.6 31.7 %copy-start = (f32[16,64]{1,0:T(8,128)S(1)}, f32[16,64]{1,0:T(8,128)}, u32[]{:S(2)}) copy-start(f32[16,64]{1,0:T(8,128)} %param.30) | copy-start | bytes 12292
  0.6 0.9 %copy-start.1 = (f32[16,16,128]{2,1,0:T(8,128)S(1)}, f32[16,16,128]{2,1,0:T(8,128)}, u32[]{:S(2)}) copy-start(f32[16,16,128]{2,1,0:T(8,128)} %refs_0_.3) | copy-start | bytes 393220
  1.6 0.9 %copy-start.3 = (f32[16,16,128]{2,1,0:T(8,128)S(1)}, f32[16,16,128]{2,1,0:T(8,128)}, u32[]{:S(2)}) copy-start(f32[16,16,128]{2,1,0:T(8,128)} %refs_1_.3) | copy-start | bytes 393220
  2.5 0.9 %copy-start.5 = (f32[16,16,128]{2,1,0:T(8,128)S(1)}, f32[16,16,128]{2,1,0:T(8,128)}, u32[]{:S(2)}) copy-start(f32[16,16,128]{2,1,0:T(8,128)} %refs_2_.3) | copy-start | bytes 393220
  3.4 0.9 %copy-start.7 = (f32[16,16,128]{2,1,0:T(8,128)S(1)}, f32[16,16,128]{2,1,0:T(8,128)}, u32[]{:S(2)}) copy-start(f32[16,16,128]{2,1,0:T(8,128)} %refs_3_.3) | copy-start | bytes 393220
  4.3 0.9 %copy-start.9 = (f32[16,16,128]{2,1,0:T(8,128)S(1)}, f32[16,16,128]{2,1,0:T(8,128)}, u32[]{:S(2)}) copy-start(f32[16,16,128]{2,1,0:T(8,128)} %refs_4_.3) | copy-start | bytes 393220
  5.2 0.9 %copy-start.11 = (f32[16,16,128]{2,1,0:T(8,128)S(1)}, f32[16,16,128]{2,1,0:T(8,128)}, u32[]{:S(2)}) copy-start(f32[16,16,128]{2,1,0:T(8,128)} %refs_5_.3) | copy-start | bytes 393220
  6.1 0.9 %copy-start.13 = (f32[16,16,128]{2,1,0:T(8,128)S(1)}, f32[16,16,128]{2,1,0:T(8,128)}, u32[]{:S(2)}) copy-start(f32[16,16,128]{2,1,0:T(8,128)} %refs_6_.3) | copy-start | bytes 393220
  7.0 0.9 %copy-start.15 = (f32[16,16,128]{2,1,0:T(8,128)S(1)}, f32[16,16,128]{2,1,0:T(8,128)}, u32[]{:S(2)}) copy-start(f32[16,16,128]{2,1,0:T(8,128)} %refs_7_.3) | copy-start | bytes 393220
  7.9 0.9 %copy-start.17 = (f32[16,16,128]{2,1,0:T(8,128)S(1)}, f32[16,16,128]{2,1,0:T(8,128)}, u32[]{:S(2)}) copy-start(f32[16,16,128]{2,1,0:T(8,128)} %refs_8_.3) | copy-start | bytes 393220
  8.8 0.9 %copy-start.19 = (f32[16,16,128]{2,1,0:T(8,128)S(1)}, f32[16,16,128]{2,1,0:T(8,128)}, u32[]{:S(2)}) copy-start(f32[16,16,128]{2,1,0:T(8,128)} %refs_9_.3) | copy-start | bytes 393220
  9.7 0.9 %copy-start.21 = (f32[16,16,128]{2,1,0:T(8,128)S(1)}, f32[16,16,128]{2,1,0:T(8,128)}, u32[]{:S(2)}) copy-start(f32[16,16,128]{2,1,0:T(8,128)} %refs_10_.3) | copy-start | bytes 393220
  10.6 0.9 %copy-start.23 = (f32[16,16,128]{2,1,0:T(8,128)S(1)}, f32[16,16,128]{2,1,0:T(8,128)}, u32[]{:S(2)}) copy-start(f32[16,16,128]{2,1,0:T(8,128)} %refs_11_.3) | copy-start | bytes 393220
  11.5 0.9 %copy-start.25 = (f32[16,16,128]{2,1,0:T(8,128)S(1)}, f32[16,16,128]{2,1,0:T(8,128)}, u32[]{:S(2)}) copy-start(f32[16,16,128]{2,1,0:T(8,128)} %refs_12_.3) | copy-start | bytes 393220
  12.4 26.1 %copy-start.28 = (s32[1024]{0:T(1024)S(1)}, s32[1024]{0:T(1024)}, u32[]{:S(2)}) copy-start(s32[1024]{0:T(1024)} %param.32) | copy-start | bytes 12292
  12.4 36.5 %copy-start.29 = (s32[1024]{0:T(1024)S(1)}, s32[1024]{0:T(1024)}, u32[]{:S(2)}) copy-start(s32[1024]{0:T(1024)} %param.31) | copy-start | bytes 12292
  12.4 46.3 %copy-start.14 = (f32[16,16,128]{2,1,0:T(8,128)S(1)}, f32[16,16,128]{2,1,0:T(8,128)}, u32[]{:S(2)}) copy-start(f32[16,16,128]{2,1,0:T(8,128)} %refs_6_.3) | copy-start | bytes 393220
  12.4 46.3 %copy-start.16 = (f32[16,16,128]{2,1,0:T(8,128)S(1)}, f32[16,16,128]{2,1,0:T(8,128)}, u32[]{:S(2)}) copy-start(f32[16,16,128]{2,1,0:T(8,128)} %refs_7_.3) | copy-start | bytes 393220
  12.4 46.3 %copy-start.18 = (f32[16,16,128]{2,1,0:T(8,128)S(1)}, f32[16,16,128]{2,1,0:T(8,128)}, u32[]{:S(2)}) copy-start(f32[16,16,128]{2,1,0:T(8,128)} %refs_8_.3) | copy-start | bytes 393220
  12.4 46.3 %copy-start.20 = (f32[16,16,128]{2,1,0:T(8,128)S(1)}, f32[16,16,128]{2,1,0:T(8,128)}, u32[]{:S(2)}) copy-start(f32[16,16,128]{2,1,0:T(8,128)} %refs_9_.3) | copy-start | bytes 393220
  12.4 46.3 %copy-start.22 = (f32[16,16,128]{2,1,0:T(8,128)S(1)}, f32[16,16,128]{2,1,0:T(8,128)}, u32[]{:S(2)}) copy-start(f32[16,16,128]{2,1,0:T(8,128)} %refs_10_.3) | copy-start | bytes 393220
  12.5 46.3 %copy-start.24 = (f32[16,16,128]{2,1,0:T(8,128)S(1)}, f32[16,16,128]{2,1,0:T(8,128)}, u32[]{:S(2)}) copy-start(f32[16,16,128]{2,1,0:T(8,128)} %refs_11_.3) | copy-start | bytes 393220
  12.5 46.3 %copy-start.26 = (f32[16,16,128]{2,1,0:T(8,128)S(1)}, f32[16,16,128]{2,1,0:T(8,128)}, u32[]{:S(2)}) copy-start(f32[16,16,128]{2,1,0:T(8,128)} %refs_12_.3) | copy-start | bytes 393220
  13.9 0.6 copy-start.27
  14.6 44.1 %collective-permute-start = (f32[13,16,4,128]{3,2,1,0:T(4,128)}, f32[13,16,4,128]{3,2,1,0:T(4,128)S(1)}, u32[]{:S(2)}, u32[]{:S(2)}) collective-permute-start(f32[13,16,4,128]{3,2,1,0:T(4,128)} %get-tuple-element.11), channel_id=1, source_target_pairs={{0,1},{1,2},{2,3},{4,5},{5,6},{6,7},{8,9},{9,10},{10,11},{12,13},{... | collective-permute-start | bytes 1277960 | tf_op jit(solution)/shard_map/ppermute | solution.py:68
  18.6 40.2 %copy-start.12 = (f32[16,16,128]{2,1,0:T(8,128)S(1)}, f32[16,16,128]{2,1,0:T(8,128)}, u32[]{:S(2)}) copy-start(f32[16,16,128]{2,1,0:T(8,128)} %refs_5_.3) | copy-start | bytes 393220
  18.6 40.1 %collective-permute-start.1 = (f32[13,16,4,128]{3,2,1,0:T(4,128)}, f32[13,16,4,128]{3,2,1,0:T(4,128)S(1)}, u32[]{:S(2)}, u32[]{:S(2)}) collective-permute-start(f32[13,16,4,128]{3,2,1,0:T(4,128)} %get-tuple-element.12), channel_id=1, source_target_pairs={{1,0},{2,1},{3,2},{5,4},{6,5},{7,6},{9,8},{10,9},{11,10},{13,12},{... | collective-permute-start | bytes 1277960 | tf_op jit(solution)/shard_map/ppermute | solution.py:68
  20.1 38.7 %collective-permute-start.2 = (f32[13,4,16,128]{3,2,1,0:T(8,128)}, f32[13,4,16,128]{3,2,1,0:T(8,128)S(1)}, u32[]{:S(2)}, u32[]{:S(2)}) collective-permute-start(f32[13,4,16,128]{3,2,1,0:T(8,128)} %get-tuple-element.13), channel_id=1, source_target_pairs={{0,4},{1,5},{2,6},{3,7},{4,8},{5,9},{6,10},{7,11},{8,12},{9,13},{1... | collective-permute-start | bytes 1277960 | tf_op jit(solution)/shard_map/ppermute | solution.py:68
  24.0 34.7 %collective-permute-start.3 = (f32[13,4,16,128]{3,2,1,0:T(8,128)}, f32[13,4,16,128]{3,2,1,0:T(8,128)S(1)}, u32[]{:S(2)}, u32[]{:S(2)}) collective-permute-start(f32[13,4,16,128]{3,2,1,0:T(8,128)} %get-tuple-element.14), channel_id=1, source_target_pairs={{4,0},{5,1},{6,2},{7,3},{8,4},{9,5},{10,6},{11,7},{12,8},{13,9},{1... | collective-permute-start | bytes 1277960 | tf_op jit(solution)/shard_map/ppermute | solution.py:68
  26.0 11.3 %collective-permute-start.4 = (f32[13,4,4,128]{3,2,1,0:T(4,128)S(1)}, f32[13,4,4,128]{3,2,1,0:T(4,128)S(1)}, u32[]{:S(2)}, u32[]{:S(2)}) collective-permute-start(f32[13,4,4,128]{3,2,1,0:T(4,128)S(1)} %get-tuple-element.15), channel_id=1, source_target_pairs={{0,5},{1,6},{2,7},{4,9},{5,10},{6,11},{8,13},{9,14},{10,15},{16,21... | collective-permute-start | bytes 319496 | tf_op jit(solution)/shard_map/ppermute | solution.py:68
  33.1 25.7 %copy-start.10 = (f32[16,16,128]{2,1,0:T(8,128)S(1)}, f32[16,16,128]{2,1,0:T(8,128)}, u32[]{:S(2)}) copy-start(f32[16,16,128]{2,1,0:T(8,128)} %refs_4_.3) | copy-start | bytes 393220
  33.1 12.4 %all-to-all-start = ((f32[16,1,256]{2,1,0:T(1,128)}), f32[16,1,256]{2,1,0:T(1,128)S(1)}, u32[]{:S(2)}, u32[]{:S(2)}) async-start(f32[16,1,256]{2,1,0:T(1,128)} %reshape.52), calls=%async_computation | async-start | bytes 32768 | tf_op jit(solution)/shard_map/all_to_all | solution.py:244
  37.2 6.5 %collective-permute-start.5 = (f32[13,4,4,128]{3,2,1,0:T(4,128)S(1)}, f32[13,4,4,128]{3,2,1,0:T(4,128)S(1)}, u32[]{:S(2)}, u32[]{:S(2)}) collective-permute-start(f32[13,4,4,128]{3,2,1,0:T(4,128)S(1)} %get-tuple-element.16), channel_id=1, source_target_pairs={{1,4},{2,5},{3,6},{5,8},{6,9},{7,10},{9,12},{10,13},{11,14},{17,20... | collective-permute-start | bytes 319496 | tf_op jit(solution)/shard_map/ppermute | solution.py:68
  38.5 20.3 %copy-start.8 = (f32[16,16,128]{2,1,0:T(8,128)S(1)}, f32[16,16,128]{2,1,0:T(8,128)}, u32[]{:S(2)}) copy-start(f32[16,16,128]{2,1,0:T(8,128)} %refs_3_.3) | copy-start | bytes 393220
  43.7 3.8 %collective-permute-start.6 = (f32[13,4,4,128]{3,2,1,0:T(4,128)}, f32[13,4,4,128]{3,2,1,0:T(4,128)S(1)}, u32[]{:S(2)}, u32[]{:S(2)}) collective-permute-start(f32[13,4,4,128]{3,2,1,0:T(4,128)} %get-tuple-element.17), channel_id=1, source_target_pairs={{4,1},{5,2},{6,3},{8,5},{9,6},{10,7},{12,9},{13,10},{14,11},{20,17... | collective-permute-start | bytes 319496 | tf_op jit(solution)/shard_map/ppermute | solution.py:68
  46.8 12.1 %copy-start.6 = (f32[16,16,128]{2,1,0:T(8,128)S(1)}, f32[16,16,128]{2,1,0:T(8,128)}, u32[]{:S(2)}) copy-start(f32[16,16,128]{2,1,0:T(8,128)} %refs_2_.3) | copy-start | bytes 393220
  47.5 11.4 %copy-start.2 = (f32[16,16,128]{2,1,0:T(8,128)S(1)}, f32[16,16,128]{2,1,0:T(8,128)}, u32[]{:S(2)}) copy-start(f32[16,16,128]{2,1,0:T(8,128)} %refs_0_.3) | copy-start | bytes 393220
  47.5 11.4 %copy-start.4 = (f32[16,16,128]{2,1,0:T(8,128)S(1)}, f32[16,16,128]{2,1,0:T(8,128)}, u32[]{:S(2)}) copy-start(f32[16,16,128]{2,1,0:T(8,128)} %refs_1_.3) | copy-start | bytes 393220
  47.5 11.2 %collective-permute-start.7 = (f32[13,4,4,128]{3,2,1,0:T(4,128)}, f32[13,4,4,128]{3,2,1,0:T(4,128)S(1)}, u32[]{:S(2)}, u32[]{:S(2)}) collective-permute-start(f32[13,4,4,128]{3,2,1,0:T(4,128)} %copy-done.27), channel_id=1, source_target_pairs={{5,0},{6,1},{7,2},{9,4},{10,5},{11,6},{13,8},{14,9},{15,10},{21,16... | collective-permute-start | bytes 319496 | tf_op jit(solution)/shard_map/ppermute | solution.py:68

commit v2 on v1

v2 whole, which is shorter than its diff:
```python
import functools

import jax
import jax.numpy as jnp
from jax import lax
from jax.experimental import pallas as pl
from jax.experimental.pallas import tpu as pltpu
from jax.sharding import PartitionSpec as P

STEPS = 4
REC_DEPTH = 4
RIM = STEPS
FIELDS = 8
SUBLANES = 8
LANES = 128
VMEM_LIMIT = 48 * 1024 * 1024
PARAMS = pltpu.CompilerParams(vmem_limit_bytes=VMEM_LIMIT)


def in_vmem(count):
    return [pl.BlockSpec(memory_space=pltpu.VMEM)] * count


def is_odd(axis):
    return lax.rem(lax.axis_index(axis), 2) == 1


def swap(value, axis, first):
    size = lax.axis_size(axis)
    lower = range(first, size - 1, 2)
    pairs = [(i, i + 1) for i in lower] + [(i + 1, i) for i in lower]
    return lax.ppermute(value, axis, pairs)


def pack_kernel(count, *refs):
    blocks, traces, start = refs[:count], refs[count], refs[count + 1]
    y_a, y_b, x_a, x_b, copies = refs[count + 2 : count + 7]
    held, sems = refs[count + 7 :]
    cells_x, cells_y = blocks[0].shape[:2]
    moves = [
        pltpu.make_async_copy(block, held.at[number], sems.at[number])
        for number, block in enumerate(blocks)
    ]
    for move in moves:
        move.start()
    odd_x, odd_y = is_odd("gx"), is_odd("gy")
    begin = start[0]
    samples = traces.shape[1]
    copies[...] = jnp.zeros_like(copies)
    for sample in range(STEPS):
        row = traces[pl.ds(begin + sample, 1), :]
        for device in range(copies.shape[0]):
            copies[device, sample : sample + 1, :samples] = row
    for move in moves:
        move.wait()

    def put_y(low, high):
        for number in range(count):
            low[number] = held[number, :, :RIM, :]
            high[number] = held[number, :, cells_y - RIM :, :]

    @pl.when(odd_y)
    def _():
        put_y(y_a, y_b)

    @pl.when(jnp.logical_not(odd_y))
    def _():
        put_y(y_b, y_a)

    from_a = jnp.where(odd_x, 0, cells_x - RIM)
    from_b = jnp.where(odd_x, cells_x - RIM, 0)
    for number in range(count):
        x_a[number] = held[number, pl.ds(from_a, RIM)]
        x_b[number] = held[number, pl.ds(from_b, RIM)]


def pack(blocks, traces, segment_start):
    cells_x, cells_y, depth = blocks[0].shape
    count = len(blocks)
    devices = lax.axis_size("gx") * lax.axis_size("gy")
    rim_y = jax.ShapeDtypeStruct((count, cells_x, RIM, depth), jnp.float32)
    rim_x = jax.ShapeDtypeStruct((count, RIM, cells_y, depth), jnp.float32)
    copies = jax.ShapeDtypeStruct((devices, SUBLANES, LANES), jnp.float32)
    return pl.pallas_call(
        functools.partial(pack_kernel, count),
        out_shape=[rim_y, rim_y, rim_x, rim_x, copies],
        in_specs=[pl.BlockSpec(memory_space=pltpu.HBM)] * count
        + in_vmem(1)
        + [pl.BlockSpec(memory_space=pltpu.SMEM)],
        out_specs=in_vmem(5),
        scratch_shapes=[
            pltpu.VMEM((count, cells_x, cells_y, depth), jnp.float32),
            pltpu.SemaphoreType.DMA((count,)),
        ],
        compiler_params=PARAMS,
        name="pack_rims",
    )(*blocks, traces, segment_start)


def corner_kernel(y_a, y_b, c_a, c_b):
    count, cells_x = y_a.shape[:2]
    odd_x, odd_y = is_odd("gx"), is_odd("gy")
    from_a = jnp.where(odd_x, 0, cells_x - RIM)
    from_b = jnp.where(odd_x, cells_x - RIM, 0)

    def put(low, high):
        for number in range(count):
            for begin, out in ((from_a, c_a), (from_b, c_b)):
                out[number, :, :RIM, :] = high[number, pl.ds(begin, RIM)]
                out[number, :, RIM:, :] = low[number, pl.ds(begin, RIM)]

    @pl.when(odd_y)
    def _():
        put(y_a, y_b)

    @pl.when(jnp.logical_not(odd_y))
    def _():
        put(y_b, y_a)


def corners(y_a, y_b):
    count, _, _, depth = y_a.shape
    corner = jax.ShapeDtypeStruct((count, RIM, 2 * RIM, depth), jnp.float32)
    return pl.pallas_call(
        corner_kernel,
        out_shape=[corner, corner],
        in_specs=in_vmem(2),
        out_specs=in_vmem(2),
        compiler_params=PARAMS,
        name="pack_corners",
    )(y_a, y_b)


def sine_cosine(angle):
    square = angle * angle
    sine = 1.0 / 6227020800.0
    for term in (-1.0 / 39916800.0, 1.0 / 362880.0, -1.0 / 5040.0, 1.0 / 120.0, -1.0 / 6.0, 1.0):
        sine = sine * square + term
    cosine = 1.0 / 479001600.0
    for term in (-1.0 / 3628800.0, 1.0 / 40320.0, -1.0 / 720.0, 1.0 / 24.0, -0.5, 1.0):
        cosine = cosine * square + term
    return sine * angle, cosine


def main_kernel(count, cells_x, cells_y, *refs):
    blocks = refs[:count]
    y_a, y_b, x_a, x_b, c_a, c_b, planes = refs[count : count + 7]
    image, p_last, q_last = refs[count + 7 : count + 10]
    wide, waves, factors, local = refs[count + 10 :]
    span_x = cells_x + 2 * RIM
    rows = cells_y + 2 * RIM
    tiles = rows // SUBLANES
    depth = wide.shape[-1]
    odd_x, odd_y = is_odd("gx"), is_odd("gy")

    def place_y(low, high):
        for number in range(count):
            wide[number, RIM : RIM + cells_x, cells_y : cells_y + RIM, :] = high[number]
            wide[number, RIM : RIM + cells_x, cells_y + RIM :, :] = low[number]

    for number in range(count):
        wide[number, RIM : RIM + cells_x, :cells_y, :] = blocks[number][...]

    @pl.when(odd_y)
    def _():
        place_y(y_a, y_b)

    @pl.when(jnp.logical_not(odd_y))
    def _():
        place_y(y_b, y_a)

    to_a = jnp.where(odd_x, 0, RIM + cells_x)
    to_b = jnp.where(odd_x, RIM + cells_x, 0)
    for number in range(count):
        for begin, side, corner in ((to_a, x_a, c_a), (to_b, x_b, c_b)):
            wide[number, pl.ds(begin, RIM), :cells_y, :] = side[number]
            wide[number, pl.ds(begin, RIM), cells_y:, :] = corner[number]

    def wide_tiles(number, x):
        return [wide[number, x, pl.ds(tile, SUBLANES, stride=tiles), :] for tile in range(tiles)]

    def wave_tiles(number, slot, x):
        if slot < 2:
            return wide_tiles(2 * number + slot, x)
        return [waves[number, slot - 2, x, tile] for tile in range(tiles)]

    lane = lax.broadcasted_iota(jnp.int32, (SUBLANES, depth), 1)
    not_last, not_first = lane < depth - 1, lane > 0
    at_depth = lane == REC_DEPTH

    def next_y(value):
        return value[1:] + [pltpu.roll(value[0], SUBLANES - 1, 0)]

    def previous_y(value):
        return [pltpu.roll(value[-1], 1, 0)] + value[:-1]

    def make_factors(i, carry):
        stores = []
        for x in (1 + 2 * i, 2 + 2 * i):
            raw = [wide_tiles(FIELDS + number, x) for number in range(count - FIELDS)]
            for tile in range(tiles):
                velocity, epsilon, delta, tilt, azimuth = [value[tile] for value in raw]
                f_e = 1.0 + 2.0 * epsilon
                f_d = jnp.sqrt(1.0 + 2.0 * delta)
                sin_tilt, cos_tilt = sine_cosine(tilt)
                sin_half, cos_half = sine_cosine(0.5 * azimuth)
                sin_azim = 2.0 * sin_half * cos_half
                cos_azim = 1.0 - 2.0 * sin_half * sin_half
                sin_square = sin_tilt * sin_tilt
                half_tilt = 0.5 * sin_tilt * cos_tilt
                along_x = sin_square * cos_azim
                values = (
                    velocity,
                    velocity * f_e,
                    velocity * f_d,
                    along_x * cos_azim,
                    sin_square * sin_azim * sin_azim,
                    cos_tilt * cos_tilt,
                    0.5 * along_x * sin_azim,
                    half_tilt * cos_azim,
                    half_tilt * sin_azim,
                )
                stores += [(number, x, tile, value) for number, value in enumerate(values)]
        for number, x, tile, value in stores:
            factors[number, x, tile] = value
        return carry

    lax.fori_loop(0, (span_x - 2) // 2, make_factors, 0)

    def plane_part(turn, x, stores):
        ayy = [factors[4, x, tile] for tile in range(tiles)]
        azz = [factors[5, x, tile] for tile in range(tiles)]
        ayz = [factors[8, x, tile] for tile in range(tiles)]
        for number in range(4):
            now = wave_tiles(number, turn + 1, x)
            above = [jnp.where(not_last, pltpu.roll(u, depth - 1, 1), 0.0) for u in now]
            below = [jnp.where(not_first, pltpu.roll(u, 1, 1), 0.0) for u in now]
            slope_z = [a - b for a, b in zip(above, below)]
            after, before = next_y(now), previous_y(now)
            slope_after, slope_before = next_y(slope_z), previous_y(slope_z)
            for tile in range(tiles):
                double = now[tile] + now[tile]
                sum_y = after[tile] + before[tile]
                sum_z = above[tile] + below[tile]
                part = (
                    (ayy[tile] * sum_y + azz[tile] * sum_z)
                    + ayz[tile] * (slope_after[tile] - slope_before[tile])
                ) - double
                stores.append((local, (number, 0, x, tile), part))
                stores.append((local, (number, 1, x, tile), after[tile] - before[tile]))
                stores.append((local, (number, 2, x, tile), slope_z[tile]))
                if number % 2 == 0:
                    rest = (sum_y + sum_z) - 3.0 * double
                    stores.append((local, (number, 3, x, tile), rest))

    def next_part(turn, x, stores):
        held = [wave_tiles(number, turn, x) for number in range(4)]
        now = [wave_tiles(number, turn + 1, x) for number in range(4)]
        after = [wave_tiles(number, turn + 1, x + 1) for number in range(4)]
        before = [wave_tiles(number, turn + 1, x - 1) for number in range(4)]
        for tile in range(tiles):
            velocity, with_e, with_d = [factors[number, x, tile] for number in range(3)]
            axx, axy, axz = [factors[number, x, tile] for number in (3, 6, 7)]
            for pair in range(2):
                sums, axis = [], []
                for number in (2 * pair, 2 * pair + 1):
                    sum_x = after[number][tile] + before[number][tile]
                    d_xy = local[number, 1, x + 1, tile] - local[number, 1, x - 1, tile]
                    d_xz = local[number, 2, x + 1, tile] - local[number, 2, x - 1, tile]
                    sums.append(sum_x)
                    axis.append((local[number, 0, x, tile] + axx * sum_x) + (axy * d_xy + axz * d_xz))
                p_number, q_number = 2 * pair, 2 * pair + 1
                across = (sums[0] + local[p_number, 3, x, tile]) - axis[0]
                p_now, q_now = now[p_number][tile], now[q_number][tile]
                p_next = ((p_now + p_now) - held[p_number][tile]) + (
                    with_e * across + with_d * axis[1]
                )
                q_next = ((q_now + q_now) - held[q_number][tile]) + (
                    with_d * across + velocity * axis[1]
                )
                if pair == 1:
                    shift = lax.rem(REC_DEPTH - x + depth, depth)
                    moved = pltpu.roll(planes[STEPS - 1 - turn, tile], shift, 1)
                    p_next = p_next + jnp.where(at_depth, moved, 0.0)
                stores.append((waves, (p_number, turn, x, tile), p_next))
                stores.append((waves, (q_number, turn, x, tile), q_next))

    def write(stores):
        for ref, index, value in stores:
            ref[index] = value

    for turn in range(STEPS):
        first, last = turn + 1, span_x - 1 - turn
        for x in range(first - 1, first + 3):
            stores = []
            plane_part(turn, x, stores)
            write(stores)

        def body(i, carry, turn=turn, first=first):
            x = first + 2 * i
            stores = []
            next_part(turn, x, stores)
            next_part(turn, x + 1, stores)
            plane_part(turn, x + 3, stores)
            plane_part(turn, x + 4, stores)
            write(stores)
            return carry

        lax.fori_loop(0, (last - first) // 2, body, 0)

    def finish(i, carry):
        x = RIM + i
        total = None
        for back in range(STEPS + 1):
            source = wave_tiles(0, 1 + STEPS - back, x)
            receiver = wave_tiles(2, 1 + back, x)
            product = [a * b for a, b in zip(source, receiver)]
            total = product if total is None else [a + b for a, b in zip(total, product)]
        for out, value in (
            (0, total),
            (1, wave_tiles(2, 1 + STEPS, x)),
            (2, wave_tiles(3, 1 + STEPS, x)),
        ):
            for tile in range(tiles):
                wide[out, x, pl.ds(tile, SUBLANES, stride=tiles), :] = value[tile]
        return carry

    lax.fori_loop(0, cells_x, finish, 0)
    for out, ref in enumerate((image, p_last, q_last)):
        ref[...] = wide[out, RIM : RIM + cells_x, :cells_y, :]


def migrate(blocks, rims, planes):
    cells_x, cells_y, depth = blocks[0].shape
    count = len(blocks)
    planes_x, rows = cells_x + 2 * RIM + 2, cells_y + 2 * RIM
    tile = (rows // SUBLANES, SUBLANES, depth)
    out = jax.ShapeDtypeStruct((cells_x, cells_y, depth), jnp.float32)
    return pl.pallas_call(
        functools.partial(main_kernel, count, cells_x, cells_y),
        out_shape=[out] * 3,
        in_specs=in_vmem(count + len(rims) + 1),
        out_specs=in_vmem(3),
        scratch_shapes=[
            pltpu.VMEM((count, planes_x, rows, depth), jnp.float32),
            pltpu.VMEM((4, STEPS, planes_x) + tile, jnp.float32),
            pltpu.VMEM((9, planes_x) + tile, jnp.float32),
            pltpu.VMEM((4, 4, planes_x) + tile, jnp.float32),
        ],
        compiler_params=PARAMS,
        name="migrate",
    )(*blocks, *rims, planes)


def injected(gathered, receiver_x, receiver_y, samples, cells_x, cells_y, depth):
    everyone = gathered[:, :STEPS, :samples].transpose(1, 0, 2).reshape(STEPS, -1)
    rows = cells_y + 2 * RIM
    tiles = rows // SUBLANES
    x_global = lax.axis_index("gx") * cells_x - RIM + jnp.arange(depth, dtype=jnp.int32)
    place = jnp.arange(rows, dtype=jnp.int32)
    row = tiles * (place % SUBLANES) + place // SUBLANES
    y_local = jnp.where(row < cells_y + RIM, row, row - rows)
    y_global = lax.axis_index("gy") * cells_y + y_local
    pick_x = (receiver_x[None, :] == x_global[:, None]).astype(jnp.float32)
    pick_y = (receiver_y[None, :] == y_global[:, None]).astype(jnp.float32)
    weighted = everyone[:, None, :] * pick_y[None, :, :]
    planes = jnp.einsum("kyr,xr->kyx", weighted, pick_x, precision=lax.Precision.HIGHEST)
    return planes.reshape(STEPS, tiles, SUBLANES, depth)


def per_device(
    src_p_prev,
    src_p_now,
    src_q_prev,
    src_q_now,
    rec_p_next,
    rec_p_now,
    rec_q_next,
    rec_q_now,
    velocity_term,
    epsilon,
    delta,
    tilt,
    azimuth,
    traces,
    receiver_x,
    receiver_y,
    segment_start,
):
    blocks = (
        src_p_prev,
        src_p_now,
        src_q_prev,
        src_q_now,
        rec_p_next,
        rec_p_now,
        rec_q_next,
        rec_q_now,
        velocity_term,
        epsilon,
        delta,
        tilt,
        azimuth,
    )
    cells_x, cells_y, depth = src_p_now.shape
    y_a, y_b, x_a, x_b, copies = pack(blocks, traces, segment_start)
    y_a, y_b = swap(y_a, "gy", 0), swap(y_b, "gy", 1)
    x_a, x_b = swap(x_a, "gx", 0), swap(x_b, "gx", 1)
    gathered = lax.all_to_all(copies, ("gx", "gy"), 0, 0, tiled=True)
    c_a, c_b = corners(y_a, y_b)
    c_a, c_b = swap(c_a, "gx", 0), swap(c_b, "gx", 1)
    planes = injected(
        gathered, receiver_x, receiver_y, traces.shape[1], cells_x, cells_y, depth
    )
    return tuple(migrate(blocks, (y_a, y_b, x_a, x_b, c_a, c_b), planes))


def solution(mesh):
    state = P(("shot", "gx"), "gy", None)
    earth = P("gx", "gy", None)
    return jax.shard_map(
        per_device,
        mesh=mesh,
        in_specs=(state,) * FIELDS + (earth,) * 5 + (P("shot", ("gx", "gy")), P(), P(), P()),
        out_specs=(state,) * 3,
        check_vma=False,
    )
```

time: 78 us -> 52.3 us (0.67)
  the two profiles are of different devices: /device:TPU:1 before, /device:TPU:17 now
where the time goes in v2:
time: 52.3 us; the launch traced here: 51.7 us
  starting transfers between devices  18.2 us (35%)
  local copies, waits for them, and re-layouts  13.8 us (26%)
  Pallas kernels  13.8 us (26%)
  waiting for transfers between devices  3.76 us (7%)
  between operations  1.55 us (3%)
    unnamed x58, local copies, waits for them, and re-layouts  13.7 us
    ppermute x6, starting transfers between devices, swap(): return lax.ppermute(value, axis, pairs)  13.2 us
    pallas_call x1, Pallas kernels, migrate(): pl.pallas_call(functools.partial(main_kernel, count, cells_x, cells_y), o...  9.31 us
    all_to_all x1, starting transfers between devices, per_device(): gathered = lax.all_to_all(copies, ('gx', 'gy'), 0, 0, tiled=True)  5 us
    ppermute x6, waiting for transfers between devices, swap(): return lax.ppermute(value, axis, pairs)  3.76 us
    pallas_call x1, Pallas kernels, pack(): pl.pallas_call(functools.partial(pack_kernel, count), out_shape=[rim_y, r...  3.61 us
  transfers between devices with their start and end apart: 7, of which 2 were waited for; matrix products, arithmetic and copies ran while one was open for 1% of the time, Pallas kernels for 2%

profile of v2, /device:TPU:17, one launch (start us, length us, event | category | flops | bytes accessed | tf_op | source)
XLA Modules:
  0.0 51.7 jit_solution(15473194668798342124)
XLA Ops:
  1.3 0.0 copy-start
  1.3 0.9 %copy-done = f32[16,16,128]{2,1,0:T(8,128)S(1)} copy-done((f32[16,16,128]{2,1,0:T(8,128)S(1)}, f32[16,16,128]{2,1,0:T(8,128)}, u32[]{:S(2)}) %copy-start) | copy-done | bytes 131096
  2.2 0.9 %copy-done.2 = f32[16,16,128]{2,1,0:T(8,128)S(1)} copy-done((f32[16,16,128]{2,1,0:T(8,128)S(1)}, f32[16,16,128]{2,1,0:T(8,128)}, u32[]{:S(2)}) %copy-start.2) | copy-done | bytes 131096
  3.1 0.9 %copy-done.4 = f32[16,16,128]{2,1,0:T(8,128)S(1)} copy-done((f32[16,16,128]{2,1,0:T(8,128)S(1)}, f32[16,16,128]{2,1,0:T(8,128)}, u32[]{:S(2)}) %copy-start.4) | copy-done | bytes 131096
  4.0 0.9 %copy-done.6 = f32[16,16,128]{2,1,0:T(8,128)S(1)} copy-done((f32[16,16,128]{2,1,0:T(8,128)S(1)}, f32[16,16,128]{2,1,0:T(8,128)}, u32[]{:S(2)}) %copy-start.6) | copy-done | bytes 131096
  4.9 0.9 %copy-done.8 = f32[16,16,128]{2,1,0:T(8,128)S(1)} copy-done((f32[16,16,128]{2,1,0:T(8,128)S(1)}, f32[16,16,128]{2,1,0:T(8,128)}, u32[]{:S(2)}) %copy-start.8) | copy-done | bytes 131096
  5.8 0.9 %copy-done.10 = f32[16,16,128]{2,1,0:T(8,128)S(1)} copy-done((f32[16,16,128]{2,1,0:T(8,128)S(1)}, f32[16,16,128]{2,1,0:T(8,128)}, u32[]{:S(2)}) %copy-start.10) | copy-done | bytes 131096
  6.7 0.9 %copy-done.12 = f32[16,16,128]{2,1,0:T(8,128)S(1)} copy-done((f32[16,16,128]{2,1,0:T(8,128)S(1)}, f32[16,16,128]{2,1,0:T(8,128)}, u32[]{:S(2)}) %copy-start.12) | copy-done | bytes 131096
  7.6 0.9 %copy-done.14 = f32[16,16,128]{2,1,0:T(8,128)S(1)} copy-done((f32[16,16,128]{2,1,0:T(8,128)S(1)}, f32[16,16,128]{2,1,0:T(8,128)}, u32[]{:S(2)}) %copy-start.14) | copy-done | bytes 131096
  8.5 0.9 %copy-done.16 = f32[16,16,128]{2,1,0:T(8,128)S(1)} copy-done((f32[16,16,128]{2,1,0:T(8,128)S(1)}, f32[16,16,128]{2,1,0:T(8,128)}, u32[]{:S(2)}) %copy-start.16) | copy-done | bytes 131096
  9.4 0.9 %copy-done.18 = f32[16,16,128]{2,1,0:T(8,128)S(1)} copy-done((f32[16,16,128]{2,1,0:T(8,128)S(1)}, f32[16,16,128]{2,1,0:T(8,128)}, u32[]{:S(2)}) %copy-start.18) | copy-done | bytes 131096
  10.3 0.9 %copy-done.20 = f32[16,16,128]{2,1,0:T(8,128)S(1)} copy-done((f32[16,16,128]{2,1,0:T(8,128)S(1)}, f32[16,16,128]{2,1,0:T(8,128)}, u32[]{:S(2)}) %copy-start.20) | copy-done | bytes 131096
  11.2 0.9 %copy-done.22 = f32[16,16,128]{2,1,0:T(8,128)S(1)} copy-done((f32[16,16,128]{2,1,0:T(8,128)S(1)}, f32[16,16,128]{2,1,0:T(8,128)}, u32[]{:S(2)}) %copy-start.22) | copy-done | bytes 131096
  12.1 0.9 %copy-done.24 = f32[16,16,128]{2,1,0:T(8,128)S(1)} copy-done((f32[16,16,128]{2,1,0:T(8,128)S(1)}, f32[16,16,128]{2,1,0:T(8,128)}, u32[]{:S(2)}) %copy-start.24) | copy-done | bytes 131096
  13.0 0.7 %copy-done.26 = f32[16,64]{1,0:T(8,128)S(1)} copy-done((f32[16,64]{1,0:T(8,128)S(1)}, f32[16,64]{1,0:T(8,128)}, u32[]{:S(2)}) %copy-start.26) | copy-done | bytes 4120
  13.7 3.6 %pack_rims.1 = (f32[13,16,4,128]{3,2,1,0:T(4,128)S(1)}, f32[13,16,4,128]{3,2,1,0:T(4,128)S(1)}, f32[13,4,16,128]{3,2,1,0:T(8,128)}, f32[13,4,16,128]{3,2,1,0:T(8,128)}, f32[16,8,128]{2,1,0:T(8,128)}) custom-call(f32[16,16,128]{2,1,0:T(8,128)S(1)} %copy-done, f32[16,16,128]{2,1,0:T(8,128)S(1)} %copy-done.2, f32[16,16,128]{2,1,0:T(8,128)S(1)} %copy-done.4, ...), custom_call_target="tpu_custom_call" | custom-call | tf_op jit(solution)/shard_map/pack_rims/pallas_call | solution.py:84
  17.4 1.4 %collective-permute-start = (f32[13,16,4,128]{3,2,1,0:T(4,128)S(1)}, f32[13,16,4,128]{3,2,1,0:T(4,128)S(1)}, u32[]{:S(2)}, u32[]{:S(2)}) collective-permute-start(f32[13,16,4,128]{3,2,1,0:T(4,128)S(1)} %get-tuple-element.10), channel_id=1, source_target_pairs={{0,1},{2,3},{1,0},{3,2},{4,5},{6,7},{5,4},{7,6},{8,9},{10,11},{9,8... | collective-permute-start | bytes 1277960 | tf_op jit(solution)/shard_map/ppermute | solution.py:32
  18.7 1.9 %collective-permute-start.1 = (f32[13,16,4,128]{3,2,1,0:T(4,128)S(1)}, f32[13,16,4,128]{3,2,1,0:T(4,128)S(1)}, u32[]{:S(2)}, u32[]{:S(2)}) collective-permute-start(f32[13,16,4,128]{3,2,1,0:T(4,128)S(1)} %get-tuple-element.11), channel_id=1, source_target_pairs={{1,2},{2,1},{5,6},{6,5},{9,10},{10,9},{13,14},{14,13},{17,18},{18,... | collective-permute-start | bytes 1277960 | tf_op jit(solution)/shard_map/ppermute | solution.py:32
  20.6 1.0 %collective-permute-start.2 = (f32[13,4,16,128]{3,2,1,0:T(8,128)}, f32[13,4,16,128]{3,2,1,0:T(8,128)S(1)}, u32[]{:S(2)}, u32[]{:S(2)}) collective-permute-start(f32[13,4,16,128]{3,2,1,0:T(8,128)} %get-tuple-element.12), channel_id=1, source_target_pairs={{0,4},{8,12},{4,0},{12,8},{1,5},{9,13},{5,1},{13,9},{2,6},{10,14},... | collective-permute-start | bytes 1277960 | tf_op jit(solution)/shard_map/ppermute | solution.py:32
  21.7 3.0 %collective-permute-start.3 = (f32[13,4,16,128]{3,2,1,0:T(8,128)}, f32[13,4,16,128]{3,2,1,0:T(8,128)S(1)}, u32[]{:S(2)}, u32[]{:S(2)}) collective-permute-start(f32[13,4,16,128]{3,2,1,0:T(8,128)} %get-tuple-element.13), channel_id=1, source_target_pairs={{4,8},{8,4},{5,9},{9,5},{6,10},{10,6},{7,11},{11,7},{20,24},{24,20... | collective-permute-start | bytes 1277960 | tf_op jit(solution)/shard_map/ppermute | solution.py:32
  24.7 0.0 copy-start.23
  24.7 5.0 %all-to-all-start = ((f32[16,8,128]{2,1,0:T(8,128)}), f32[16,8,128]{2,1,0:T(8,128)S(1)}, u32[]{:S(2)}, u32[]{:S(2)}) async-start(f32[16,8,128]{2,1,0:T(8,128)} %get-tuple-element.16), calls=%async_computation | async-start | bytes 131072 | tf_op jit(solution)/shard_map/all_to_all | solution.py:409
  29.7 0.7 %copy-done.27 = s32[1024]{0:T(1024)S(1)} copy-done((s32[1024]{0:T(1024)S(1)}, s32[1024]{0:T(1024)}, u32[]{:S(2)}) %copy-start.27) | copy-done | bytes 4120
  30.4 0.1 compare_convert_fusion
  30.5 0.0 collective-permute-done.y_a.refs_13_
  30.5 0.5 collective-permute-done.1.y_b.refs_14_
  31.0 0.0 copy-start.15
  31.0 0.0 copy-start.17
  31.0 0.0 copy-start.19
  31.0 0.9 %pack_corners.1 = (f32[13,4,8,128]{3,2,1,0:T(8,128)}, f32[13,4,8,128]{3,2,1,0:T(8,128)}) custom-call(f32[13,16,4,128]{3,2,1,0:T(4,128)S(1)} %collective-permute-done.y_a.refs_13_, f32[13,16,4,128]{3,2,1,0:T(4,128)S(1)} %collective-permute-done.1.y_b.refs_14_), custom_call_target="tpu_custom_call" | custom-call | tf_op jit(solution)/shard_map/pack_corners/pallas_call | solution.py:124
  31.9 2.9 %collective-permute-start.4 = (f32[13,4,8,128]{3,2,1,0:T(8,128)}, f32[13,4,8,128]{3,2,1,0:T(8,128)S(1)}, u32[]{:S(2)}, u32[]{:S(2)}) collective-permute-start(f32[13,4,8,128]{3,2,1,0:T(8,128)} %get-tuple-element.14), channel_id=1, source_target_pairs={{0,4},{8,12},{4,0},{12,8},{1,5},{9,13},{5,1},{13,9},{2,6},{10,14},... | collective-permute-start | bytes 638984 | tf_op jit(solution)/shard_map/ppermute | solution.py:32
  34.8 3.0 %collective-permute-start.5 = (f32[13,4,8,128]{3,2,1,0:T(8,128)}, f32[13,4,8,128]{3,2,1,0:T(8,128)}, u32[]{:S(2)}, u32[]{:S(2)}) collective-permute-start(f32[13,4,8,128]{3,2,1,0:T(8,128)} %get-tuple-element.15), channel_id=1, source_target_pairs={{4,8},{8,4},{5,9},{9,5},{6,10},{10,6},{7,11},{11,7},{20,24},{24,20... | collective-permute-start | bytes 638984 | tf_op jit(solution)/shard_map/ppermute | solution.py:32
  37.8 0.0 all-to-all-done
  37.8 0.0 copy-start.28
  37.8 0.0 copy-start.5
  37.9 0.1 mul.28
  37.9 0.6 %copy-done.28 = s32[1024]{0:T(1024)S(1)} copy-done((s32[1024]{0:T(1024)S(1)}, s32[1024]{0:T(1024)}, u32[]{:S(2)}) %copy-start.28) | copy-done | bytes 4120
  38.5 0.5 convolution_bitcast_fusion.refs_19_
  39.0 0.0 collective-permute-done.2.refs_15_
  39.0 0.0 collective-permute-done.3.refs_16_
  39.0 0.0 collective-permute-done.4.refs_17_
  39.0 3.3 %collective-permute-done.5.refs_18_ = f32[13,4,8,128]{3,2,1,0:T(8,128)} collective-permute-done((f32[13,4,8,128]{3,2,1,0:T(8,128)}, f32[13,4,8,128]{3,2,1,0:T(8,128)}, u32[]{:S(2)}, u32[]{:S(2)}) %collective-permute-start.5) | collective-permute-done | bytes 213024 | tf_op jit(solution)/shard_map/ppermute | solution.py:32
  42.3 0.0 copy-done.25
  42.3 0.0 copy-done.23
  42.3 0.0 copy-done.21
  42.3 0.0 copy-done.7
  42.3 0.0 copy-done.9
  42.4 9.3 %migrate.1 = (f32[16,16,128]{2,1,0:T(8,128)}, f32[16,16,128]{2,1,0:T(8,128)}, f32[16,16,128]{2,1,0:T(8,128)}) custom-call(f32[16,16,128]{2,1,0:T(8,128)S(1)} %copy-done.1, f32[16,16,128]{2,1,0:T(8,128)S(1)} %copy-done.3, f32[16,16,128]{2,1,0:T(8,128)S(1)} %copy-done.5, f32[16,16,128]{2,1,0:T(8,128)S(1)} %copy-done.7, f32[16,16,128]{2,1,0:T(8,128)S(1)} %copy-done.9, ...), custom_call_target="tpu_custom_call" | custom-call | tf_op jit(solution)/shard_map/migrate/pallas_call | solution.py:339
  (34 shorter events, 0.1 us)
Async XLA Ops:
  1.3 0.9 %copy-start = (f32[16,16,128]{2,1,0:T(8,128)S(1)}, f32[16,16,128]{2,1,0:T(8,128)}, u32[]{:S(2)}) copy-start(f32[16,16,128]{2,1,0:T(8,128)} %refs_0_.3) | copy-start | bytes 393220
  2.2 0.9 %copy-start.2 = (f32[16,16,128]{2,1,0:T(8,128)S(1)}, f32[16,16,128]{2,1,0:T(8,128)}, u32[]{:S(2)}) copy-start(f32[16,16,128]{2,1,0:T(8,128)} %refs_1_.3) | copy-start | bytes 393220
  3.1 0.9 %copy-start.4 = (f32[16,16,128]{2,1,0:T(8,128)S(1)}, f32[16,16,128]{2,1,0:T(8,128)}, u32[]{:S(2)}) copy-start(f32[16,16,128]{2,1,0:T(8,128)} %refs_2_.3) | copy-start | bytes 393220
  4.0 0.9 %copy-start.6 = (f32[16,16,128]{2,1,0:T(8,128)S(1)}, f32[16,16,128]{2,1,0:T(8,128)}, u32[]{:S(2)}) copy-start(f32[16,16,128]{2,1,0:T(8,128)} %refs_3_.3) | copy-start | bytes 393220
  4.9 0.9 %copy-start.8 = (f32[16,16,128]{2,1,0:T(8,128)S(1)}, f32[16,16,128]{2,1,0:T(8,128)}, u32[]{:S(2)}) copy-start(f32[16,16,128]{2,1,0:T(8,128)} %refs_4_.3) | copy-start | bytes 393220
  5.8 0.9 %copy-start.10 = (f32[16,16,128]{2,1,0:T(8,128)S(1)}, f32[16,16,128]{2,1,0:T(8,128)}, u32[]{:S(2)}) copy-start(f32[16,16,128]{2,1,0:T(8,128)} %refs_5_.3) | copy-start | bytes 393220
  6.7 0.9 %copy-start.12 = (f32[16,16,128]{2,1,0:T(8,128)S(1)}, f32[16,16,128]{2,1,0:T(8,128)}, u32[]{:S(2)}) copy-start(f32[16,16,128]{2,1,0:T(8,128)} %refs_6_.3) | copy-start | bytes 393220
  7.6 0.9 %copy-start.14 = (f32[16,16,128]{2,1,0:T(8,128)S(1)}, f32[16,16,128]{2,1,0:T(8,128)}, u32[]{:S(2)}) copy-start(f32[16,16,128]{2,1,0:T(8,128)} %refs_7_.3) | copy-start | bytes 393220
  8.5 0.9 %copy-start.16 = (f32[16,16,128]{2,1,0:T(8,128)S(1)}, f32[16,16,128]{2,1,0:T(8,128)}, u32[]{:S(2)}) copy-start(f32[16,16,128]{2,1,0:T(8,128)} %refs_8_.3) | copy-start | bytes 393220
  9.4 0.9 %copy-start.18 = (f32[16,16,128]{2,1,0:T(8,128)S(1)}, f32[16,16,128]{2,1,0:T(8,128)}, u32[]{:S(2)}) copy-start(f32[16,16,128]{2,1,0:T(8,128)} %refs_9_.3) | copy-start | bytes 393220
  10.3 0.9 %copy-start.20 = (f32[16,16,128]{2,1,0:T(8,128)S(1)}, f32[16,16,128]{2,1,0:T(8,128)}, u32[]{:S(2)}) copy-start(f32[16,16,128]{2,1,0:T(8,128)} %refs_10_.3) | copy-start | bytes 393220
  11.2 0.9 %copy-start.22 = (f32[16,16,128]{2,1,0:T(8,128)S(1)}, f32[16,16,128]{2,1,0:T(8,128)}, u32[]{:S(2)}) copy-start(f32[16,16,128]{2,1,0:T(8,128)} %refs_11_.3) | copy-start | bytes 393220
  12.1 0.9 %copy-start.24 = (f32[16,16,128]{2,1,0:T(8,128)S(1)}, f32[16,16,128]{2,1,0:T(8,128)}, u32[]{:S(2)}) copy-start(f32[16,16,128]{2,1,0:T(8,128)} %refs_12_.3) | copy-start | bytes 393220
  13.0 0.7 %copy-start.26 = (f32[16,64]{1,0:T(8,128)S(1)}, f32[16,64]{1,0:T(8,128)}, u32[]{:S(2)}) copy-start(f32[16,64]{1,0:T(8,128)} %refs_13_.1) | copy-start | bytes 12292
  13.7 28.5 %copy-start.25 = (f32[16,16,128]{2,1,0:T(8,128)S(1)}, f32[16,16,128]{2,1,0:T(8,128)}, u32[]{:S(2)}) copy-start(f32[16,16,128]{2,1,0:T(8,128)} %refs_12_.3) | copy-start | bytes 393220
  17.4 13.1 %collective-permute-start = (f32[13,16,4,128]{3,2,1,0:T(4,128)S(1)}, f32[13,16,4,128]{3,2,1,0:T(4,128)S(1)}, u32[]{:S(2)}, u32[]{:S(2)}) collective-permute-start(f32[13,16,4,128]{3,2,1,0:T(4,128)S(1)} %get-tuple-element.10), channel_id=1, source_target_pairs={{0,1},{2,3},{1,0},{3,2},{4,5},{6,7},{5,4},{7,6},{8,9},{10,11},{9,8... | collective-permute-start | bytes 1277960 | tf_op jit(solution)/shard_map/ppermute | solution.py:32
  18.7 12.2 %collective-permute-start.1 = (f32[13,16,4,128]{3,2,1,0:T(4,128)S(1)}, f32[13,16,4,128]{3,2,1,0:T(4,128)S(1)}, u32[]{:S(2)}, u32[]{:S(2)}) collective-permute-start(f32[13,16,4,128]{3,2,1,0:T(4,128)S(1)} %get-tuple-element.11), channel_id=1, source_target_pairs={{1,2},{2,1},{5,6},{6,5},{9,10},{10,9},{13,14},{14,13},{17,18},{18,... | collective-permute-start | bytes 1277960 | tf_op jit(solution)/shard_map/ppermute | solution.py:32
  20.6 18.3 %collective-permute-start.2 = (f32[13,4,16,128]{3,2,1,0:T(8,128)}, f32[13,4,16,128]{3,2,1,0:T(8,128)S(1)}, u32[]{:S(2)}, u32[]{:S(2)}) collective-permute-start(f32[13,4,16,128]{3,2,1,0:T(8,128)} %get-tuple-element.12), channel_id=1, source_target_pairs={{0,4},{8,12},{4,0},{12,8},{1,5},{9,13},{5,1},{13,9},{2,6},{10,14},... | collective-permute-start | bytes 1277960 | tf_op jit(solution)/shard_map/ppermute | solution.py:32
  21.7 17.3 %collective-permute-start.3 = (f32[13,4,16,128]{3,2,1,0:T(8,128)}, f32[13,4,16,128]{3,2,1,0:T(8,128)S(1)}, u32[]{:S(2)}, u32[]{:S(2)}) collective-permute-start(f32[13,4,16,128]{3,2,1,0:T(8,128)} %get-tuple-element.13), channel_id=1, source_target_pairs={{4,8},{8,4},{5,9},{9,5},{6,10},{10,6},{7,11},{11,7},{20,24},{24,20... | collective-permute-start | bytes 1277960 | tf_op jit(solution)/shard_map/ppermute | solution.py:32
  24.7 17.6 %copy-start.23 = (f32[16,16,128]{2,1,0:T(8,128)S(1)}, f32[16,16,128]{2,1,0:T(8,128)}, u32[]{:S(2)}) copy-start(f32[16,16,128]{2,1,0:T(8,128)} %refs_11_.3) | copy-start | bytes 393220
  24.7 13.1 %all-to-all-start = ((f32[16,8,128]{2,1,0:T(8,128)}), f32[16,8,128]{2,1,0:T(8,128)S(1)}, u32[]{:S(2)}, u32[]{:S(2)}) async-start(f32[16,8,128]{2,1,0:T(8,128)} %get-tuple-element.16), calls=%async_computation | async-start | bytes 131072 | tf_op jit(solution)/shard_map/all_to_all | solution.py:409
  29.7 0.7 %copy-start.27 = (s32[1024]{0:T(1024)S(1)}, s32[1024]{0:T(1024)}, u32[]{:S(2)}) copy-start(s32[1024]{0:T(1024)} %param.32) | copy-start | bytes 12292
  30.4 11.9 %copy-start.21 = (f32[16,16,128]{2,1,0:T(8,128)S(1)}, f32[16,16,128]{2,1,0:T(8,128)}, u32[]{:S(2)}) copy-start(f32[16,16,128]{2,1,0:T(8,128)} %refs_10_.3) | copy-start | bytes 393220
  31.0 11.3 %copy-start.7 = (f32[16,16,128]{2,1,0:T(8,128)S(1)}, f32[16,16,128]{2,1,0:T(8,128)}, u32[]{:S(2)}) copy-start(f32[16,16,128]{2,1,0:T(8,128)} %refs_3_.3) | copy-start | bytes 393220
  31.0 11.3 %copy-start.9 = (f32[16,16,128]{2,1,0:T(8,128)S(1)}, f32[16,16,128]{2,1,0:T(8,128)}, u32[]{:S(2)}) copy-start(f32[16,16,128]{2,1,0:T(8,128)} %refs_4_.3) | copy-start | bytes 393220
  31.0 11.3 %copy-start.11 = (f32[16,16,128]{2,1,0:T(8,128)S(1)}, f32[16,16,128]{2,1,0:T(8,128)}, u32[]{:S(2)}) copy-start(f32[16,16,128]{2,1,0:T(8,128)} %refs_5_.3) | copy-start | bytes 393220
  31.0 11.3 %copy-start.13 = (f32[16,16,128]{2,1,0:T(8,128)S(1)}, f32[16,16,128]{2,1,0:T(8,128)}, u32[]{:S(2)}) copy-start(f32[16,16,128]{2,1,0:T(8,128)} %refs_6_.3) | copy-start | bytes 393220
  31.0 11.3 %copy-start.15 = (f32[16,16,128]{2,1,0:T(8,128)S(1)}, f32[16,16,128]{2,1,0:T(8,128)}, u32[]{:S(2)}) copy-start(f32[16,16,128]{2,1,0:T(8,128)} %refs_7_.3) | copy-start | bytes 393220
  31.0 11.3 %copy-start.17 = (f32[16,16,128]{2,1,0:T(8,128)S(1)}, f32[16,16,128]{2,1,0:T(8,128)}, u32[]{:S(2)}) copy-start(f32[16,16,128]{2,1,0:T(8,128)} %refs_8_.3) | copy-start | bytes 393220
  31.0 11.3 %copy-start.19 = (f32[16,16,128]{2,1,0:T(8,128)S(1)}, f32[16,16,128]{2,1,0:T(8,128)}, u32[]{:S(2)}) copy-start(f32[16,16,128]{2,1,0:T(8,128)} %refs_9_.3) | copy-start | bytes 393220
  31.9 7.1 %collective-permute-start.4 = (f32[13,4,8,128]{3,2,1,0:T(8,128)}, f32[13,4,8,128]{3,2,1,0:T(8,128)S(1)}, u32[]{:S(2)}, u32[]{:S(2)}) collective-permute-start(f32[13,4,8,128]{3,2,1,0:T(8,128)} %get-tuple-element.14), channel_id=1, source_target_pairs={{0,4},{8,12},{4,0},{12,8},{1,5},{9,13},{5,1},{13,9},{2,6},{10,14},... | collective-permute-start | bytes 638984 | tf_op jit(solution)/shard_map/ppermute | solution.py:32
  34.8 7.5 %collective-permute-start.5 = (f32[13,4,8,128]{3,2,1,0:T(8,128)}, f32[13,4,8,128]{3,2,1,0:T(8,128)}, u32[]{:S(2)}, u32[]{:S(2)}) collective-permute-start(f32[13,4,8,128]{3,2,1,0:T(8,128)} %get-tuple-element.15), channel_id=1, source_target_pairs={{4,8},{8,4},{5,9},{9,5},{6,10},{10,6},{7,11},{11,7},{20,24},{24,20... | collective-permute-start | bytes 638984 | tf_op jit(solution)/shard_map/ppermute | solution.py:32
  37.8 0.7 %copy-start.28 = (s32[1024]{0:T(1024)S(1)}, s32[1024]{0:T(1024)}, u32[]{:S(2)}) copy-start(s32[1024]{0:T(1024)} %param.31) | copy-start | bytes 12292
  37.8 4.5 %copy-start.5 = (f32[16,16,128]{2,1,0:T(8,128)S(1)}, f32[16,16,128]{2,1,0:T(8,128)}, u32[]{:S(2)}) copy-start(f32[16,16,128]{2,1,0:T(8,128)} %refs_2_.3) | copy-start | bytes 393220
  38.5 3.9 %copy-start.1 = (f32[16,16,128]{2,1,0:T(8,128)S(1)}, f32[16,16,128]{2,1,0:T(8,128)}, u32[]{:S(2)}) copy-start(f32[16,16,128]{2,1,0:T(8,128)} %refs_0_.3) | copy-start | bytes 393220
  38.5 3.9 %copy-start.3 = (f32[16,16,128]{2,1,0:T(8,128)S(1)}, f32[16,16,128]{2,1,0:T(8,128)}, u32[]{:S(2)}) copy-start(f32[16,16,128]{2,1,0:T(8,128)} %refs_1_.3) | copy-start | bytes 393220

commit v3 on v2

--- a/solution.py
+++ b/solution.py
@@ -32,13 +32,59 @@
     return lax.ppermute(value, axis, pairs)
 
 
+NOW = (1, 3, 5, 7)
+REST = (0, 2, 4, 6, 8, 9, 10, 11, 12)
+SLIM = RIM - 1
+
+
+def y_slots():
+    slots = [((number, 0, RIM, 0),) for number in NOW]
+    whole = len(REST) - len(REST) // RIM
+    for place in range(whole):
+        parts = [(REST[place], 0, SLIM, 0)]
+        guest = whole + place // SLIM
+        if guest < len(REST):
+            parts.append((REST[guest], place % SLIM, 1, SLIM))
+        slots.append(tuple(parts))
+    return slots
+
+
+def each_y_part(slots, high):
+    for slot, parts in enumerate(slots):
+        for number, row, rows, place in parts:
+            if not high:
+                yield slot, number, row, place, rows
+            else:
+                width = RIM if number in NOW else SLIM
+                yield slot, number, RIM - width + row, 0 if place else RIM - rows, rows
+
+
+def x_parts():
+    parts, place = [], 0
+    for number in NOW:
+        parts.append((number, RIM, place))
+        place += RIM
+    for number in REST:
+        parts.append((number, SLIM, place))
+        place += SLIM
+    return parts, place
+
+
+def pinned(value, space):
+    return pltpu.with_memory_space_constraint(value, space)
+
+
+def vmem_out(*shape):
+    return pltpu.VMEM(shape, jnp.float32)
+
+
 def pack_kernel(count, *refs):
     blocks, traces, start = refs[:count], refs[count], refs[count + 1]
-    y_a, y_b, x_a, x_b, copies = refs[count + 2 : count + 7]
-    held, sems = refs[count + 7 :]
+    wide, y_a, y_b, x_a, x_b, copies, sems = refs[count + 2 :]
     cells_x, cells_y = blocks[0].shape[:2]
+    core_x = pl.ds(RIM, cells_x)
     moves = [
-        pltpu.make_async_copy(block, held.at[number], sems.at[number])
+        pltpu.make_async_copy(block, wide.at[number, core_x, pl.ds(0, cells_y)], sems.at[number])
         for number, block in enumerate(blocks)
     ]
     for move in moves:
@@ -46,18 +92,19 @@
     odd_x, odd_y = is_odd("gx"), is_odd("gy")
     begin = start[0]
     samples = traces.shape[1]
-    copies[...] = jnp.zeros_like(copies)
-    for sample in range(STEPS):
-        row = traces[pl.ds(begin + sample, 1), :]
-        for device in range(copies.shape[0]):
-            copies[device, sample : sample + 1, :samples] = row
+    rows = [traces[pl.ds(begin + sample, 1), :] for sample in range(STEPS)]
+    for device in range(copies.shape[0]):
+        for sample in range(STEPS):
+            copies[device, sample : sample + 1, :samples] = rows[sample]
     for move in moves:
         move.wait()
 
     def put_y(low, high):
-        for number in range(count):
-            low[number] = held[number, :, :RIM, :]
-            high[number] = held[number, :, cells_y - RIM :, :]
+        for out, is_high, base in ((low, False, 0), (high, True, cells_y - RIM)):
+            for slot, number, row, place, length in each_y_part(y_slots(), is_high):
+                out[slot, :, place : place + length, :] = wide[
+                    number, RIM : RIM + cells_x, base + row : base + row + length, :
+                ]
 
     @pl.when(odd_y)
     def _():
@@ -67,68 +114,69 @@
     def _():
         put_y(y_b, y_a)
 
-    from_a = jnp.where(odd_x, 0, cells_x - RIM)
-    from_b = jnp.where(odd_x, cells_x - RIM, 0)
-    for number in range(count):
-        x_a[number] = held[number, pl.ds(from_a, RIM)]
-        x_b[number] = held[number, pl.ds(from_b, RIM)]
+    for number, width, place in x_parts()[0]:
+        first, last = RIM, RIM + cells_x - width
+        for out, begin in ((x_a, jnp.where(odd_x, first, last)), (x_b, jnp.where(odd_x, last, first))):
+            out[place : place + width] = wide[number, pl.ds(begin, width), :cells_y, :]
 
 
 def pack(blocks, traces, segment_start):
     cells_x, cells_y, depth = blocks[0].shape
     count = len(blocks)
     devices = lax.axis_size("gx") * lax.axis_size("gy")
-    rim_y = jax.ShapeDtypeStruct((count, cells_x, RIM, depth), jnp.float32)
-    rim_x = jax.ShapeDtypeStruct((count, RIM, cells_y, depth), jnp.float32)
-    copies = jax.ShapeDtypeStruct((devices, SUBLANES, LANES), jnp.float32)
+    rim_y = vmem_out(len(y_slots()), cells_x, RIM, depth)
+    rim_x = vmem_out(x_parts()[1], cells_y, depth)
+    wide = vmem_out(count, cells_x + 2 * RIM + 2, cells_y + 2 * RIM, depth)
     return pl.pallas_call(
         functools.partial(pack_kernel, count),
-        out_shape=[rim_y, rim_y, rim_x, rim_x, copies],
+        out_shape=[wide, rim_y, rim_y, rim_x, rim_x, vmem_out(devices, SUBLANES, LANES)],
         in_specs=[pl.BlockSpec(memory_space=pltpu.HBM)] * count
         + in_vmem(1)
         + [pl.BlockSpec(memory_space=pltpu.SMEM)],
-        out_specs=in_vmem(5),
-        scratch_shapes=[
-            pltpu.VMEM((count, cells_x, cells_y, depth), jnp.float32),
-            pltpu.SemaphoreType.DMA((count,)),
-        ],
+        out_specs=in_vmem(6),
+        scratch_shapes=[pltpu.SemaphoreType.DMA((count,))],
         compiler_params=PARAMS,
         name="pack_rims",
-    )(*blocks, traces, segment_start)
-
-
-def corner_kernel(y_a, y_b, c_a, c_b):
-    count, cells_x = y_a.shape[:2]
+    )(*(pinned(block, pltpu.HBM) for block in blocks), traces, segment_start)
+
+
+def corner_kernel(_, y_a, y_b, wide, c_a, c_b):
+    cells_x = y_a.shape[1]
+    cells_y = wide.shape[2] - 2 * RIM
     odd_x, odd_y = is_odd("gx"), is_odd("gy")
-    from_a = jnp.where(odd_x, 0, cells_x - RIM)
-    from_b = jnp.where(odd_x, cells_x - RIM, 0)
-
-    def put(low, high):
-        for number in range(count):
-            for begin, out in ((from_a, c_a), (from_b, c_b)):
-                out[number, :, :RIM, :] = high[number, pl.ds(begin, RIM)]
-                out[number, :, RIM:, :] = low[number, pl.ds(begin, RIM)]
+
+    def place_y(low, high):
+        for rim, is_high, base in ((high, False, cells_y), (low, True, cells_y + RIM)):
+            for slot, number, row, place, length in each_y_part(y_slots(), is_high):
+                wide[number, RIM : RIM + cells_x, base + row : base + row + length, :] = rim[
+                    slot, :, place : place + length, :
+                ]
 
     @pl.when(odd_y)
     def _():
-        put(y_a, y_b)
+        place_y(y_a, y_b)
 
     @pl.when(jnp.logical_not(odd_y))
     def _():
-        put(y_b, y_a)
-
-
-def corners(y_a, y_b):
-    count, _, _, depth = y_a.shape
-    corner = jax.ShapeDtypeStruct((count, RIM, 2 * RIM, depth), jnp.float32)
+        place_y(y_b, y_a)
+
+    for number, width, place in x_parts()[0]:
+        first, last = RIM, RIM + cells_x - width
+        for out, begin in ((c_a, jnp.where(odd_x, first, last)), (c_b, jnp.where(odd_x, last, first))):
+            out[place : place + width] = wide[number, pl.ds(begin, width), cells_y:, :]
+
+
+def corners(wide, y_a, y_b):
+    corner = vmem_out(x_parts()[1], 2 * RIM, wide.shape[-1])
     return pl.pallas_call(
         corner_kernel,
-        out_shape=[corner, corner],
-        in_specs=in_vmem(2),
-        out_specs=in_vmem(2),
+        out_shape=[vmem_out(*wide.shape), corner, corner],
+        in_specs=in_vmem(3),
+        out_specs=in_vmem(3),
+        input_output_aliases={0: 0},
         compiler_params=PARAMS,
         name="pack_corners",
-    )(y_a, y_b)
+    )(pinned(wide, pltpu.VMEM), y_a, y_b)
 
 
 def sine_cosine(angle):
@@ -142,39 +190,20 @@
     return sine * angle, cosine
 
 
-def main_kernel(count, cells_x, cells_y, *refs):
-    blocks = refs[:count]
-    y_a, y_b, x_a, x_b, c_a, c_b, planes = refs[count : count + 7]
-    image, p_last, q_last = refs[count + 7 : count + 10]
-    wide, waves, factors, local = refs[count + 10 :]
+def main_kernel(_, x_a, x_b, c_a, c_b, planes, wide, image, p_last, q_last, waves, factors, local):
+    count = wide.shape[0]
+    cells_x, cells_y, depth = image.shape
     span_x = cells_x + 2 * RIM
-    rows = cells_y + 2 * RIM
-    tiles = rows // SUBLANES
-    depth = wide.shape[-1]
-    odd_x, odd_y = is_odd("gx"), is_odd("gy")
-
-    def place_y(low, high):
-        for number in range(count):
-            wide[number, RIM : RIM + cells_x, cells_y : cells_y + RIM, :] = high[number]
-            wide[number, RIM : RIM + cells_x, cells_y + RIM :, :] = low[number]
-
-    for number in range(count):
-        wide[number, RIM : RIM + cells_x, :cells_y, :] = blocks[number][...]
-
-    @pl.when(odd_y)
-    def _():
-        place_y(y_a, y_b)
-
-    @pl.when(jnp.logical_not(odd_y))
-    def _():
-        place_y(y_b, y_a)
-
-    to_a = jnp.where(odd_x, 0, RIM + cells_x)
-    to_b = jnp.where(odd_x, RIM + cells_x, 0)
-    for number in range(count):
-        for begin, side, corner in ((to_a, x_a, c_a), (to_b, x_b, c_b)):
-            wide[number, pl.ds(begin, RIM), :cells_y, :] = side[number]
-            wide[number, pl.ds(begin, RIM), cells_y:, :] = corner[number]
+    tiles = (cells_y + 2 * RIM) // SUBLANES
+    odd_x = is_odd("gx")
+    for number, width, place in x_parts()[0]:
+        low, high = RIM - width, RIM + cells_x
+        for begin, side, corner in (
+            (jnp.where(odd_x, low, high), x_a, c_a),
+            (jnp.where(odd_x, high, low), x_b, c_b),
+        ):
+            wide[number, pl.ds(begin, width), :cells_y, :] = side[place : place + width]
+            wide[number, pl.ds(begin, width), cells_y:, :] = corner[place : place + width]
 
     def wide_tiles(number, x):
         return [wide[number, x, pl.ds(tile, SUBLANES, stride=tiles), :] for tile in range(tiles)]
@@ -330,26 +359,24 @@
         ref[...] = wide[out, RIM : RIM + cells_x, :cells_y, :]
 
 
-def migrate(blocks, rims, planes):
-    cells_x, cells_y, depth = blocks[0].shape
-    count = len(blocks)
-    planes_x, rows = cells_x + 2 * RIM + 2, cells_y + 2 * RIM
+def migrate(wide, rims, planes, cells_x, cells_y):
+    count, planes_x, rows, depth = wide.shape
     tile = (rows // SUBLANES, SUBLANES, depth)
     out = jax.ShapeDtypeStruct((cells_x, cells_y, depth), jnp.float32)
     return pl.pallas_call(
-        functools.partial(main_kernel, count, cells_x, cells_y),
-        out_shape=[out] * 3,
-        in_specs=in_vmem(count + len(rims) + 1),
-        out_specs=in_vmem(3),
+        main_kernel,
+        out_shape=[vmem_out(*wide.shape)] + [out] * 3,
+        in_specs=in_vmem(len(rims) + 2),
+        out_specs=in_vmem(4),
+        input_output_aliases={0: 0},
         scratch_shapes=[
-            pltpu.VMEM((count, planes_x, rows, depth), jnp.float32),
             pltpu.VMEM((4, STEPS, planes_x) + tile, jnp.float32),
             pltpu.VMEM((9, planes_x) + tile, jnp.float32),
             pltpu.VMEM((4, 4, planes_x) + tile, jnp.float32),
         ],
         compiler_params=PARAMS,
         name="migrate",
-    )(*blocks, *rims, planes)
+    )(pinned(wide, pltpu.VMEM), *rims, planes)[1:]
 
 
 def injected(gathered, receiver_x, receiver_y, samples, cells_x, cells_y, depth):
@@ -403,16 +430,16 @@
         azimuth,
     )
     cells_x, cells_y, depth = src_p_now.shape
-    y_a, y_b, x_a, x_b, copies = pack(blocks, traces, segment_start)
+    wide, y_a, y_b, x_a, x_b, copies = pack(blocks, traces, segment_start)
     y_a, y_b = swap(y_a, "gy", 0), swap(y_b, "gy", 1)
     x_a, x_b = swap(x_a, "gx", 0), swap(x_b, "gx", 1)
     gathered = lax.all_to_all(copies, ("gx", "gy"), 0, 0, tiled=True)
-    c_a, c_b = corners(y_a, y_b)
+    wide, c_a, c_b = corners(wide, y_a, y_b)
     c_a, c_b = swap(c_a, "gx", 0), swap(c_b, "gx", 1)
     planes = injected(
         gathered, receiver_x, receiver_y, traces.shape[1], cells_x, cells_y, depth
     )
-    return tuple(migrate(blocks, (y_a, y_b, x_a, x_b, c_a, c_b), planes))
+    return tuple(migrate(wide, (x_a, x_b, c_a, c_b), planes, cells_x, cells_y))
 
 
 def solution(mesh):

time: 52.3 us -> 49.9 us (0.954)
  waiting for transfers between devices: 3.76 us -> 11.1 us
  local copies, waits for them, and re-layouts: 13.8 us -> 9 us
  Pallas kernels: 13.8 us -> 10.9 us
  starting transfers between devices: 18.2 us -> 15.9 us
  other arithmetic: 0.09 us -> 0.78 us
    ppermute x6, waiting for transfers between devices: 3.76 us -> 11.1 us  [swap(): return lax.ppermute(value, axis, pairs)]
    unnamed x58 -> x12, local copies, waits for them, and re-layouts: 13.7 us -> 8.91 us
    ppermute x6, starting transfers between devices: 13.2 us -> 9.41 us  [swap(): return lax.ppermute(value, axis, pairs)]
    pallas_call x3, Pallas kernels: 13.8 us -> 10.9 us  [the longest x1 8.17 us: migrate(): pl.pallas_call(main_kernel, out_shape=[vmem_out(*wide.shape)] + [out] * 3...]
    all_to_all x1, starting transfers between devices: 5 us -> 6.47 us  [per_device(): gathered = lax.all_to_all(copies, ('gx', 'gy'), 0, 0, tiled=True)]
    convert_element_type x1, other arithmetic: 0.08 us -> 0.76 us  [injected(): pick_y = (receiver_y[None, :] == y_global[:, None]).astype(jnp.float32)]
  transfers between devices with their start and end apart: 7 -> 7, of which waited for: 2 -> 3; matrix products, arithmetic and copies ran while one was open for 1% -> 3% of each run, Pallas kernels for 2% -> 0%
where the time goes in v3:
time: 49.9 us; the launch traced here: 49.5 us
  starting transfers between devices  15.9 us (32%)
  waiting for transfers between devices  11.1 us (22%)
  Pallas kernels  10.9 us (22%)
  local copies, waits for them, and re-layouts  9 us (18%)
  between operations  1.42 us (3%)
  other arithmetic  0.78 us (2%)
    ppermute x6, waiting for transfers between devices, swap(): return lax.ppermute(value, axis, pairs)  11.1 us
    ppermute x6, starting transfers between devices, swap(): return lax.ppermute(value, axis, pairs)  9.41 us
    unnamed x12, local copies, waits for them, and re-layouts  8.91 us
    pallas_call x1, Pallas kernels, migrate(): pl.pallas_call(main_kernel, out_shape=[vmem_out(*wide.shape)] + [out] * 3...  8.17 us
    all_to_all x1, starting transfers between devices, per_device(): gathered = lax.all_to_all(copies, ('gx', 'gy'), 0, 0, tiled=True)  6.47 us
    pallas_call x1, Pallas kernels, pack(): pl.pallas_call(functools.partial(pack_kernel, count), out_shape=[wide, ri...  2.47 us
  transfers between devices with their start and end apart: 7, of which 3 were waited for; matrix products, arithmetic and copies ran while one was open for 3% of the time, Pallas kernels for 0%

profile of v3, /device:TPU:17, one launch (start us, length us, event | category | flops | bytes accessed | tf_op | source)
XLA Modules:
  0.0 49.5 jit_solution(8050492905145334090)
XLA Ops:
  1.3 0.0 copy-start.4
  1.3 0.7 %copy-done.4 = f32[16,64]{1,0:T(8,128)S(1)} copy-done((f32[16,64]{1,0:T(8,128)S(1)}, f32[16,64]{1,0:T(8,128)}, u32[]{:S(2)}) %copy-start.4) | copy-done | bytes 4120
  2.0 0.0 copy-start.5
  2.0 2.5 %pack_rims.1 = (f32[13,26,24,128]{3,2,1,0:T(8,128)S(1)}, f32[11,16,4,128]{3,2,1,0:T(4,128)S(1)}, f32[11,16,4,128]{3,2,1,0:T(4,128)S(1)}, f32[43,16,128]{2,1,0:T(...) custom-call(f32[16,16,128]{2,1,0:T(8,128)} %refs_0_.1, f32[16,16,128]{2,1,0:T(8,128)} %refs_1_.1, ...), custom_call_target="tpu_custom_call" | custom-call | tf_op jit(solution)/shard_map/pack_rims/pallas_call | solution.py:130
  4.5 0.0 copy-start
  4.5 1.9 %copy-done = f32[13,26,24,128]{3,2,1,0:T(8,128)} copy-done((f32[13,26,24,128]{3,2,1,0:T(8,128)}, f32[13,26,24,128]{3,2,1,0:T(8,128)S(1)}, u32[]{:S(2)}) %copy-start) | copy-done | bytes 4153368
  6.4 6.5 %all-to-all-start = ((f32[16,8,128]{2,1,0:T(8,128)}), f32[16,8,128]{2,1,0:T(8,128)S(1)}, u32[]{:S(2)}, u32[]{:S(2)}) async-start(f32[16,8,128]{2,1,0:T(8,128)} %get-tuple-element.23), calls=%async_computation | async-start | bytes 131072 | tf_op jit(solution)/shard_map/all_to_all | solution.py:436
  12.9 0.4 collective-permute-start.2
  13.2 3.1 %collective-permute-start.3 = (f32[43,16,128]{2,1,0:T(8,128)S(1)}, f32[43,16,128]{2,1,0:T(8,128)S(1)}, u32[]{:S(2)}, u32[]{:S(2)}) collective-permute-start(f32[43,16,128]{2,1,0:T(8,128)S(1)} %get-tuple-element.20), channel_id=1, source_target_pairs={{4,8},{8,4},{5,9},{9,5},{6,10},{10,6},{7,11},{11,7},{20,24},{24,20... | collective-permute-start | bytes 1056776 | tf_op jit(solution)/shard_map/ppermute | solution.py:32
  16.4 1.2 %collective-permute-start = (f32[11,16,4,128]{3,2,1,0:T(4,128)S(1)}, f32[11,16,4,128]{3,2,1,0:T(4,128)S(1)}, u32[]{:S(2)}, u32[]{:S(2)}) collective-permute-start(f32[11,16,4,128]{3,2,1,0:T(4,128)S(1)} %get-tuple-element.16), channel_id=1, source_target_pairs={{0,1},{2,3},{1,0},{3,2},{4,5},{6,7},{5,4},{7,6},{8,9},{10,11},{9,8... | collective-permute-start | bytes 1081352 | tf_op jit(solution)/shard_map/ppermute | solution.py:32
  17.6 1.9 %collective-permute-start.1 = (f32[11,16,4,128]{3,2,1,0:T(4,128)S(1)}, f32[11,16,4,128]{3,2,1,0:T(4,128)S(1)}, u32[]{:S(2)}, u32[]{:S(2)}) collective-permute-start(f32[11,16,4,128]{3,2,1,0:T(4,128)S(1)} %get-tuple-element.17), channel_id=1, source_target_pairs={{1,2},{2,1},{5,6},{6,5},{9,10},{10,9},{13,14},{14,13},{17,18},{18,... | collective-permute-start | bytes 1081352 | tf_op jit(solution)/shard_map/ppermute | solution.py:32
  19.5 0.8 %compare_convert_fusion = f32[24,1024]{1,0:T(8,128)S(1)} fusion(s32[1024]{0:T(1024)} %param.32, s32[24]{0:T(128)S(1)} %fusion.9), kind=kLoop, calls=%fused_computation.8 | loop fusion | flops 49152 | bytes 102496 | tf_op jit(solution)/shard_map/convert_element_type | solution.py:392
  20.3 4.7 %collective-permute-done.y_a = f32[11,16,4,128]{3,2,1,0:T(4,128)S(1)} collective-permute-done((f32[11,16,4,128]{3,2,1,0:T(4,128)S(1)}, f32[11,16,4,128]{3,2,1,0:T(4,128)S(1)}, u32[]{:S(2)}, u32[]{:S(2)}) %collective-permute-start) | collective-permute-done | bytes 360480 | tf_op jit(solution)/shard_map/ppermute | solution.py:32
  25.0 3.0 %collective-permute-done.1.y_b = f32[11,16,4,128]{3,2,1,0:T(4,128)S(1)} collective-permute-done((f32[11,16,4,128]{3,2,1,0:T(4,128)S(1)}, f32[11,16,4,128]{3,2,1,0:T(4,128)S(1)}, u32[]{:S(2)}, u32[]{:S(2)}) %collective-permute-start.1) | collective-permute-done | bytes 360480 | tf_op jit(solution)/shard_map/ppermute | solution.py:32
  28.1 0.0 copy-start.1
  28.1 2.2 %copy-done.1 = f32[13,26,24,128]{3,2,1,0:T(8,128)S(1)} copy-done((f32[13,26,24,128]{3,2,1,0:T(8,128)S(1)}, f32[13,26,24,128]{3,2,1,0:T(8,128)}, u32[]{:S(2)}) %copy-start.1) | copy-done | bytes 4153368
  30.2 0.2 pack_corners.1
  30.5 0.0 copy-start.2
  30.5 1.9 %copy-done.2 = f32[13,26,24,128]{3,2,1,0:T(8,128)} copy-done((f32[13,26,24,128]{3,2,1,0:T(8,128)}, f32[13,26,24,128]{3,2,1,0:T(8,128)S(1)}, u32[]{:S(2)}) %copy-start.2) | copy-done | bytes 4153368
  32.4 0.0 collective-permute-start.4
  32.4 2.8 %collective-permute-start.5 = (f32[43,8,128]{2,1,0:T(8,128)S(1)}, f32[43,8,128]{2,1,0:T(8,128)S(1)}, u32[]{:S(2)}, u32[]{:S(2)}) collective-permute-start(f32[43,8,128]{2,1,0:T(8,128)S(1)} %get-tuple-element.22), channel_id=1, source_target_pairs={{4,8},{8,4},{5,9},{9,5},{6,10},{10,6},{7,11},{11,7},{20,24},{24,20... | collective-permute-start | bytes 528392 | tf_op jit(solution)/shard_map/ppermute | solution.py:32
  35.2 0.0 all-to-all-done
  35.2 0.1 mul.28
  35.3 0.0 copy-done.5
  35.3 0.5 convolution_bitcast_fusion.planes
  35.8 0.0 collective-permute-done.2.x_a
  35.8 0.0 collective-permute-done.3.x_b
  35.8 0.0 collective-permute-done.4.c_a
  35.8 3.4 %collective-permute-done.5.c_b = f32[43,8,128]{2,1,0:T(8,128)S(1)} collective-permute-done((f32[43,8,128]{2,1,0:T(8,128)S(1)}, f32[43,8,128]{2,1,0:T(8,128)S(1)}, u32[]{:S(2)}, u32[]{:S(2)}) %collective-permute-start.5) | collective-permute-done | bytes 176160 | tf_op jit(solution)/shard_map/ppermute | solution.py:32
  39.2 0.0 copy-start.3
  39.2 2.2 %copy-done.3 = f32[13,26,24,128]{3,2,1,0:T(8,128)S(1)} copy-done((f32[13,26,24,128]{3,2,1,0:T(8,128)S(1)}, f32[13,26,24,128]{3,2,1,0:T(8,128)}, u32[]{:S(2)}) %copy-start.3) | copy-done | bytes 4153368
  41.3 8.2 %migrate.1 = (f32[13,26,24,128]{3,2,1,0:T(8,128)S(1)}, f32[16,16,128]{2,1,0:T(8,128)}, f32[16,16,128]{2,1,0:T(8,128)}, f32[16,16,128]{2,1,0:T(8,128)}) custom-call(f32[13,26,24,128]{3,2,1,0:T(8,128)S(1)} %copy-done.3, f32[43,16,128]{2,1,0:T(8,128)S(1)} %collective-permute-done.2.x_a, ...), custom_call_target="tpu_custom_call", output_to_operand_aliasing={{0}: (0, {})} | custom-call | tf_op jit(solution)/shard_map/migrate/pallas_call | solution.py:366
  (4 shorter events, 0.0 us)
Async XLA Ops:
  1.3 0.7 %copy-start.4 = (f32[16,64]{1,0:T(8,128)S(1)}, f32[16,64]{1,0:T(8,128)}, u32[]{:S(2)}) copy-start(f32[16,64]{1,0:T(8,128)} %refs_13_.1) | copy-start | bytes 12292
  2.0 33.3 %copy-start.5 = (s32[1024]{0:T(1024)S(1)}, s32[1024]{0:T(1024)}, u32[]{:S(2)}) copy-start(s32[1024]{0:T(1024)} %param.31) | copy-start | bytes 12292
  4.5 1.9 %copy-start = (f32[13,26,24,128]{3,2,1,0:T(8,128)}, f32[13,26,24,128]{3,2,1,0:T(8,128)S(1)}, u32[]{:S(2)}) copy-start(f32[13,26,24,128]{3,2,1,0:T(8,128)S(1)} %get-tuple-element.15._) | copy-start | bytes 12460036
  6.4 28.8 %all-to-all-start = ((f32[16,8,128]{2,1,0:T(8,128)}), f32[16,8,128]{2,1,0:T(8,128)S(1)}, u32[]{:S(2)}, u32[]{:S(2)}) async-start(f32[16,8,128]{2,1,0:T(8,128)} %get-tuple-element.23), calls=%async_computation | async-start | bytes 131072 | tf_op jit(solution)/shard_map/all_to_all | solution.py:436
  12.9 22.9 %collective-permute-start.2 = (f32[43,16,128]{2,1,0:T(8,128)S(1)}, f32[43,16,128]{2,1,0:T(8,128)S(1)}, u32[]{:S(2)}, u32[]{:S(2)}) collective-permute-start(f32[43,16,128]{2,1,0:T(8,128)S(1)} %get-tuple-element.19), channel_id=1, source_target_pairs={{0,4},{8,12},{4,0},{12,8},{1,5},{9,13},{5,1},{13,9},{2,6},{10,14},... | collective-permute-start | bytes 1056776 | tf_op jit(solution)/shard_map/ppermute | solution.py:32
  13.2 22.6 %collective-permute-start.3 = (f32[43,16,128]{2,1,0:T(8,128)S(1)}, f32[43,16,128]{2,1,0:T(8,128)S(1)}, u32[]{:S(2)}, u32[]{:S(2)}) collective-permute-start(f32[43,16,128]{2,1,0:T(8,128)S(1)} %get-tuple-element.20), channel_id=1, source_target_pairs={{4,8},{8,4},{5,9},{9,5},{6,10},{10,6},{7,11},{11,7},{20,24},{24,20... | collective-permute-start | bytes 1056776 | tf_op jit(solution)/shard_map/ppermute | solution.py:32
  16.4 8.7 %collective-permute-start = (f32[11,16,4,128]{3,2,1,0:T(4,128)S(1)}, f32[11,16,4,128]{3,2,1,0:T(4,128)S(1)}, u32[]{:S(2)}, u32[]{:S(2)}) collective-permute-start(f32[11,16,4,128]{3,2,1,0:T(4,128)S(1)} %get-tuple-element.16), channel_id=1, source_target_pairs={{0,1},{2,3},{1,0},{3,2},{4,5},{6,7},{5,4},{7,6},{8,9},{10,11},{9,8... | collective-permute-start | bytes 1081352 | tf_op jit(solution)/shard_map/ppermute | solution.py:32
  17.6 10.5 %collective-permute-start.1 = (f32[11,16,4,128]{3,2,1,0:T(4,128)S(1)}, f32[11,16,4,128]{3,2,1,0:T(4,128)S(1)}, u32[]{:S(2)}, u32[]{:S(2)}) collective-permute-start(f32[11,16,4,128]{3,2,1,0:T(4,128)S(1)} %get-tuple-element.17), channel_id=1, source_target_pairs={{1,2},{2,1},{5,6},{6,5},{9,10},{10,9},{13,14},{14,13},{17,18},{18,... | collective-permute-start | bytes 1081352 | tf_op jit(solution)/shard_map/ppermute | solution.py:32
  28.1 2.2 %copy-start.1 = (f32[13,26,24,128]{3,2,1,0:T(8,128)S(1)}, f32[13,26,24,128]{3,2,1,0:T(8,128)}, u32[]{:S(2)}) copy-start(f32[13,26,24,128]{3,2,1,0:T(8,128)} %copy-done) | copy-start | bytes 12460036
  30.5 1.9 %copy-start.2 = (f32[13,26,24,128]{3,2,1,0:T(8,128)}, f32[13,26,24,128]{3,2,1,0:T(8,128)S(1)}, u32[]{:S(2)}) copy-start(f32[13,26,24,128]{3,2,1,0:T(8,128)S(1)} %get-tuple-element.18._) | copy-start | bytes 12460036
  32.4 3.4 %collective-permute-start.4 = (f32[43,8,128]{2,1,0:T(8,128)S(1)}, f32[43,8,128]{2,1,0:T(8,128)S(1)}, u32[]{:S(2)}, u32[]{:S(2)}) collective-permute-start(f32[43,8,128]{2,1,0:T(8,128)S(1)} %get-tuple-element.21), channel_id=1, source_target_pairs={{0,4},{8,12},{4,0},{12,8},{1,5},{9,13},{5,1},{13,9},{2,6},{10,14},... | collective-permute-start | bytes 528392 | tf_op jit(solution)/shard_map/ppermute | solution.py:32
  32.4 6.8 %collective-permute-start.5 = (f32[43,8,128]{2,1,0:T(8,128)S(1)}, f32[43,8,128]{2,1,0:T(8,128)S(1)}, u32[]{:S(2)}, u32[]{:S(2)}) collective-permute-start(f32[43,8,128]{2,1,0:T(8,128)S(1)} %get-tuple-element.22), channel_id=1, source_target_pairs={{4,8},{8,4},{5,9},{9,5},{6,10},{10,6},{7,11},{11,7},{20,24},{24,20... | collective-permute-start | bytes 528392 | tf_op jit(solution)/shard_map/ppermute | solution.py:32
  39.2 2.2 %copy-start.3 = (f32[13,26,24,128]{3,2,1,0:T(8,128)S(1)}, f32[13,26,24,128]{3,2,1,0:T(8,128)}, u32[]{:S(2)}) copy-start(f32[13,26,24,128]{3,2,1,0:T(8,128)} %copy-done.2) | copy-start | bytes 12460036

commit v4 on v3

--- a/solution.py
+++ b/solution.py
@@ -80,24 +80,24 @@
 
 def pack_kernel(count, *refs):
     blocks, traces, start = refs[:count], refs[count], refs[count + 1]
-    wide, y_a, y_b, x_a, x_b, copies, sems = refs[count + 2 :]
+    wide, y_a, y_b, window, held, sems = refs[count + 2 :]
     cells_x, cells_y = blocks[0].shape[:2]
     core_x = pl.ds(RIM, cells_x)
     moves = [
         pltpu.make_async_copy(block, wide.at[number, core_x, pl.ds(0, cells_y)], sems.at[number])
         for number, block in enumerate(blocks)
     ]
+    moves.append(pltpu.make_async_copy(traces, held, sems.at[count]))
     for move in moves:
         move.start()
-    odd_x, odd_y = is_odd("gx"), is_odd("gy")
+    odd_y = is_odd("gy")
     begin = start[0]
     samples = traces.shape[1]
-    rows = [traces[pl.ds(begin + sample, 1), :] for sample in range(STEPS)]
-    for device in range(copies.shape[0]):
-        for sample in range(STEPS):
-            copies[device, sample : sample + 1, :samples] = rows[sample]
+    window[...] = jnp.zeros_like(window)
     for move in moves:
         move.wait()
+    for sample in range(STEPS):
+        window[0, sample : sample + 1, :samples] = held[pl.ds(begin + sample, 1), :]
 
     def put_y(low, high):
         for out, is_high, base in ((low, False, 0), (high, True, cells_y - RIM)):
@@ -114,30 +114,55 @@
     def _():
         put_y(y_b, y_a)
 
-    for number, width, place in x_parts()[0]:
+
+def pack(blocks, traces, segment_start):
+    cells_x, cells_y, depth = blocks[0].shape
+    count = len(blocks)
+    rim_y = vmem_out(len(y_slots()), cells_x, RIM, depth)
+    wide = vmem_out(count, cells_x + 2 * RIM + 2, cells_y + 2 * RIM, depth)
+    return pl.pallas_call(
+        functools.partial(pack_kernel, count),
+        out_shape=[wide, rim_y, rim_y, vmem_out(1, STEPS, LANES)],
+        in_specs=[pl.BlockSpec(memory_space=pltpu.HBM)] * (count + 1)
+        + [pl.BlockSpec(memory_space=pltpu.SMEM)],
+        out_specs=in_vmem(4),
+        scratch_shapes=[
+            pltpu.VMEM(traces.shape, jnp.float32),
+            pltpu.SemaphoreType.DMA((count + 1,)),
+        ],
+        compiler_params=PARAMS,
+        name="pack_y_rims",
+    )(*(pinned(value, pltpu.HBM) for value in (*blocks, traces)), segment_start)
+
+
+def pack_x_kernel(_, window, wide, x_a, x_b):
+    cells_x, cells_y = wide.shape[1] - 2 * RIM - 2, wide.shape[2] - 2 * RIM
+    odd_x = is_odd("gx")
+    parts, total = x_parts()
+    for number, width, place in parts:
         first, last = RIM, RIM + cells_x - width
         for out, begin in ((x_a, jnp.where(odd_x, first, last)), (x_b, jnp.where(odd_x, last, first))):
             out[place : place + width] = wide[number, pl.ds(begin, width), :cells_y, :]
-
-
-def pack(blocks, traces, segment_start):
-    cells_x, cells_y, depth = blocks[0].shape
-    count = len(blocks)
-    devices = lax.axis_size("gx") * lax.axis_size("gy")
-    rim_y = vmem_out(len(y_slots()), cells_x, RIM, depth)
-    rim_x = vmem_out(x_parts()[1], cells_y, depth)
-    wide = vmem_out(count, cells_x + 2 * RIM + 2, cells_y + 2 * RIM, depth)
+    x_a[total] = jnp.zeros_like(x_a[total])
+    x_a[total, :STEPS, :] = window[0]
+
+
+def pack_x(wide, window):
+    _, _, rows, depth = wide.shape
+    total = x_parts()[1]
     return pl.pallas_call(
-        functools.partial(pack_kernel, count),
-        out_shape=[wide, rim_y, rim_y, rim_x, rim_x, vmem_out(devices, SUBLANES, LANES)],
-        in_specs=[pl.BlockSpec(memory_space=pltpu.HBM)] * count
-        + in_vmem(1)
-        + [pl.BlockSpec(memory_space=pltpu.SMEM)],
-        out_specs=in_vmem(6),
-        scratch_shapes=[pltpu.SemaphoreType.DMA((count,))],
+        pack_x_kernel,
+        out_shape=[
+            vmem_out(*wide.shape),
+            vmem_out(total + 1, rows - 2 * RIM, depth),
+            vmem_out(total, rows - 2 * RIM, depth),
+        ],
+        in_specs=in_vmem(2),
+        out_specs=in_vmem(3),
+        input_output_aliases={0: 0},
         compiler_params=PARAMS,
-        name="pack_rims",
-    )(*(pinned(block, pltpu.HBM) for block in blocks), traces, segment_start)
+        name="pack_x_rims",
+    )(pinned(wide, pltpu.VMEM), window)
 
 
 def corner_kernel(_, y_a, y_b, wide, c_a, c_b):
@@ -379,8 +404,31 @@
     )(pinned(wide, pltpu.VMEM), *rims, planes)[1:]
 
 
+def bits_of(axis):
+    size = lax.axis_size(axis)
+    return [1 << bit for bit in range(size.bit_length() - 1)] if size & (size - 1) == 0 else None
+
+
+def doubled(windows, axis, bit):
+    pairs = [(i, i ^ bit) for i in range(lax.axis_size(axis))]
+    return jnp.concatenate([windows, lax.ppermute(windows, axis, pairs)], axis=0)
+
+
+def in_gathered_order(receivers, samples):
+    size_x, size_y = lax.axis_size("gx"), lax.axis_size("gy")
+    grid = receivers.reshape(size_x, size_y, samples).transpose(1, 0, 2)
+    for dim, axis, size in ((0, "gy", size_y), (1, "gx", size_x)):
+        for bit in bits_of(axis):
+            shape = grid.shape[:dim] + (size // (2 * bit), 2, bit) + grid.shape[dim + 1 :]
+            apart = grid.reshape(shape)
+            swapped = jnp.flip(apart, dim + 1)
+            is_set = (lax.axis_index(axis) // bit) % 2 == 1
+            grid = jnp.where(is_set, swapped, apart).reshape(grid.shape)
+    return grid.reshape(-1)
+
+
 def injected(gathered, receiver_x, receiver_y, samples, cells_x, cells_y, depth):
-    everyone = gathered[:, :STEPS, :samples].transpose(1, 0, 2).reshape(STEPS, -1)
+    everyone = gathered[:, :, :samples].transpose(1, 0, 2).reshape(STEPS, -1)
     rows = cells_y + 2 * RIM
     tiles = rows // SUBLANES
     x_global = lax.axis_index("gx") * cells_x - RIM + jnp.arange(depth, dtype=jnp.int32)
@@ -388,8 +436,10 @@
     row = tiles * (place % SUBLANES) + place // SUBLANES
     y_local = jnp.where(row < cells_y + RIM, row, row - rows)
     y_global = lax.axis_index("gy") * cells_y + y_local
-    pick_x = (receiver_x[None, :] == x_global[:, None]).astype(jnp.float32)
-    pick_y = (receiver_y[None, :] == y_global[:, None]).astype(jnp.float32)
+    order_x = in_gathered_order(receiver_x, samples)
+    order_y = in_gathered_order(receiver_y, samples)
+    pick_x = (order_x[None, :] == x_global[:, None]).astype(jnp.float32)
+    pick_y = (order_y[None, :] == y_global[:, None]).astype(jnp.float32)
     weighted = everyone[:, None, :] * pick_y[None, :, :]
     planes = jnp.einsum("kyr,xr->kyx", weighted, pick_x, precision=lax.Precision.HIGHEST)
     return planes.reshape(STEPS, tiles, SUBLANES, depth)
@@ -430,14 +480,19 @@
         azimuth,
     )
     cells_x, cells_y, depth = src_p_now.shape
-    wide, y_a, y_b, x_a, x_b, copies = pack(blocks, traces, segment_start)
+    wide, y_a, y_b, window = pack(blocks, traces, segment_start)
     y_a, y_b = swap(y_a, "gy", 0), swap(y_b, "gy", 1)
+    wide, x_a, x_b = pack_x(wide, window)
     x_a, x_b = swap(x_a, "gx", 0), swap(x_b, "gx", 1)
-    gathered = lax.all_to_all(copies, ("gx", "gy"), 0, 0, tiled=True)
+    windows = jnp.concatenate([window, x_a[x_parts()[1] :, :STEPS, :]], axis=0)
+    for bit in bits_of("gx")[1:]:
+        windows = doubled(windows, "gx", bit)
+    for bit in bits_of("gy"):
+        windows = doubled(windows, "gy", bit)
     wide, c_a, c_b = corners(wide, y_a, y_b)
     c_a, c_b = swap(c_a, "gx", 0), swap(c_b, "gx", 1)
     planes = injected(
-        gathered, receiver_x, receiver_y, traces.shape[1], cells_x, cells_y, depth
+        windows, receiver_x, receiver_y, traces.shape[1], cells_x, cells_y, depth
     )
     return tuple(migrate(wide, (x_a, x_b, c_a, c_b), planes, cells_x, cells_y))
 

time: 49.9 us -> 43.1 us (0.86)
  the two profiles are of different devices: /device:TPU:17 before, /device:TPU:1 now
where the time goes in v4:
time: 43.1 us; the launch traced here: 42.4 us
  starting transfers between devices  18.3 us (42%)
  Pallas kernels  10.3 us (24%)
  local copies, waits for them, and re-layouts  8.81 us (20%)
  waiting for transfers between devices  2.74 us (6%)
  between operations  1.66 us (4%)
  matrix products  0.47 us (1%)
    ppermute x6, starting transfers between devices, swap(): return lax.ppermute(value, axis, pairs)  11.2 us
    unnamed x15, local copies, waits for them, and re-layouts  8.25 us
    pallas_call x1, Pallas kernels, migrate(): pl.pallas_call(main_kernel, out_shape=[vmem_out(*wide.shape)] + [out] * 3...  8.17 us
    ppermute x3, starting transfers between devices, doubled(): lax.ppermute(windows, axis, pairs)  7.08 us
    ppermute x3, waiting for transfers between devices, doubled(): lax.ppermute(windows, axis, pairs)  2.15 us
    pallas_call x1, Pallas kernels, pack(): pl.pallas_call(functools.partial(pack_kernel, count), out_shape=[wide, ri...  1.8 us
  transfers between devices with their start and end apart: 9, of which 3 were waited for; matrix products, arithmetic and copies ran while one was open for 3% of the time, Pallas kernels for 1%

profile of v4, /device:TPU:1, one launch (start us, length us, event | category | flops | bytes accessed | tf_op | source)
XLA Modules:
  0.0 42.4 jit_solution(5956811291899404654)
XLA Ops:
  0.6 0.0 copy-start.4
  0.6 0.0 copy-start.5
  1.3 1.8 %pack_y_rims.1 = (f32[13,26,24,128]{3,2,1,0:T(8,128)S(1)}, f32[11,16,4,128]{3,2,1,0:T(4,128)S(1)}, f32[11,16,4,128]{3,2,1,0:T(4,128)S(1)}, f32[1,4,128]{2,1,0:T(4,128)S(1)}) custom-call(f32[16,16,128]{2,1,0:T(8,128)} %refs_0_.1, f32[16,16,128]{2,1,0:T(8,128)} %refs_1_.1, f32[16,16,128]{2,1,0:T(8,128)} %refs_2_.1, f32[16,16,128]{2,1,0:T(8,128)} %refs_3_.1, ...), custom_call_target="tpu_custom_call" | custom-call | tf_op jit(solution)/shard_map/pack_y_rims/pallas_call | solution.py:123
  3.1 2.2 %collective-permute-start = (f32[11,16,4,128]{3,2,1,0:T(4,128)S(1)}, f32[11,16,4,128]{3,2,1,0:T(4,128)S(1)}, u32[]{:S(2)}, u32[]{:S(2)}) collective-permute-start(f32[11,16,4,128]{3,2,1,0:T(4,128)S(1)} %get-tuple-element.19), channel_id=1, source_target_pairs={{0,1},{2,3},{1,0},{3,2},{4,5},{6,7},{5,4},{7,6},{8,9},{10,11},{9,8... | collective-permute-start | bytes 1081352 | tf_op jit(solution)/shard_map/ppermute | solution.py:32
  5.3 0.7 %collective-permute-start.1 = (f32[11,16,4,128]{3,2,1,0:T(4,128)S(1)}, f32[11,16,4,128]{3,2,1,0:T(4,128)S(1)}, u32[]{:S(2)}, u32[]{:S(2)}) collective-permute-start(f32[11,16,4,128]{3,2,1,0:T(4,128)S(1)} %get-tuple-element.20), channel_id=1, source_target_pairs={{1,2},{2,1},{5,6},{6,5},{9,10},{10,9},{13,14},{14,13},{17,18},{18,... | collective-permute-start | bytes 1081352 | tf_op jit(solution)/shard_map/ppermute | solution.py:32
  6.0 0.1 pack_x_rims.1
  6.1 0.0 copy-start
  6.1 1.9 %copy-done = f32[13,26,24,128]{3,2,1,0:T(8,128)} copy-done((f32[13,26,24,128]{3,2,1,0:T(8,128)}, f32[13,26,24,128]{3,2,1,0:T(8,128)S(1)}, u32[]{:S(2)}) %copy-start) | copy-done | bytes 4153368
  8.0 1.0 %collective-permute-start.2 = (f32[44,16,128]{2,1,0:T(8,128)S(1)}, f32[44,16,128]{2,1,0:T(8,128)S(1)}, u32[]{:S(2)}, u32[]{:S(2)}) collective-permute-start(f32[44,16,128]{2,1,0:T(8,128)S(1)} %get-tuple-element.22), channel_id=1, source_target_pairs={{0,4},{8,12},{4,0},{12,8},{1,5},{9,13},{5,1},{13,9},{2,6},{10,14},... | collective-permute-start | bytes 1081352 | tf_op jit(solution)/shard_map/ppermute | solution.py:32
  9.0 3.0 %collective-permute-start.3 = (f32[43,16,128]{2,1,0:T(8,128)S(1)}, f32[43,16,128]{2,1,0:T(8,128)S(1)}, u32[]{:S(2)}, u32[]{:S(2)}) collective-permute-start(f32[43,16,128]{2,1,0:T(8,128)S(1)} %get-tuple-element.23), channel_id=1, source_target_pairs={{4,8},{8,4},{5,9},{9,5},{6,10},{10,6},{7,11},{11,7},{20,24},{24,20... | collective-permute-start | bytes 1056776 | tf_op jit(solution)/shard_map/ppermute | solution.py:32
  12.0 0.0 copy-done.4
  12.1 0.1 reshape.87
  12.2 0.0 copy-done.5
  12.2 0.1 reshape.85
  12.5 0.1 eq.65
  12.6 0.1 compare_convert_fusion
  12.7 0.0 collective-permute-done.2.x_a
  12.7 0.1 collective-permute-start.6
  12.8 0.1 eq.69
  12.9 0.6 %collective-permute-done.y_a = f32[11,16,4,128]{3,2,1,0:T(4,128)S(1)} collective-permute-done((f32[11,16,4,128]{3,2,1,0:T(4,128)S(1)}, f32[11,16,4,128]{3,2,1,0:T(4,128)S(1)}, u32[]{:S(2)}, u32[]{:S(2)}) %collective-permute-start) | collective-permute-done | bytes 360480 | tf_op jit(solution)/shard_map/ppermute | solution.py:32
  13.5 0.0 collective-permute-done.1.y_b
  13.5 0.0 copy-start.1
  13.5 2.2 %copy-done.1 = f32[13,26,24,128]{3,2,1,0:T(8,128)S(1)} copy-done((f32[13,26,24,128]{3,2,1,0:T(8,128)S(1)}, f32[13,26,24,128]{3,2,1,0:T(8,128)}, u32[]{:S(2)}) %copy-start.1) | copy-done | bytes 4153368
  15.6 0.2 pack_corners.1
  15.9 0.0 copy-start.2
  15.9 1.9 %copy-done.2 = f32[13,26,24,128]{3,2,1,0:T(8,128)} copy-done((f32[13,26,24,128]{3,2,1,0:T(8,128)}, f32[13,26,24,128]{3,2,1,0:T(8,128)S(1)}, u32[]{:S(2)}) %copy-start.2) | copy-done | bytes 4153368
  17.8 1.2 %collective-permute-start.4 = (f32[43,8,128]{2,1,0:T(8,128)S(1)}, f32[43,8,128]{2,1,0:T(8,128)S(1)}, u32[]{:S(2)}, u32[]{:S(2)}) collective-permute-start(f32[43,8,128]{2,1,0:T(8,128)S(1)} %get-tuple-element.24), channel_id=1, source_target_pairs={{0,4},{8,12},{4,0},{12,8},{1,5},{9,13},{5,1},{13,9},{2,6},{10,14},... | collective-permute-start | bytes 528392 | tf_op jit(solution)/shard_map/ppermute | solution.py:32
  19.0 3.2 %collective-permute-start.5 = (f32[43,8,128]{2,1,0:T(8,128)S(1)}, f32[43,8,128]{2,1,0:T(8,128)S(1)}, u32[]{:S(2)}, u32[]{:S(2)}) collective-permute-start(f32[43,8,128]{2,1,0:T(8,128)S(1)} %get-tuple-element.25), channel_id=1, source_target_pairs={{4,8},{8,4},{5,9},{9,5},{6,10},{10,6},{7,11},{11,7},{20,24},{24,20... | collective-permute-start | bytes 528392 | tf_op jit(solution)/shard_map/ppermute | solution.py:32
  22.2 0.0 collective-permute-done.6
  22.2 4.4 %collective-permute-start.7 = (f32[4,4,128]{2,1,0:T(4,128)S(1)}, f32[4,4,128]{2,1,0:T(4,128)S(1)}, u32[]{:S(2)}, u32[]{:S(2)}) collective-permute-start(f32[4,4,128]{2,1,0:T(4,128)S(1)} %pad_maximum_fusion.1), channel_id=1, source_target_pairs={{0,1},{1,0},{2,3},{3,2},{4,5},{5,4},{6,7},{7,6},{8,9},{9,8},{10,11... | collective-permute-start | bytes 24584 | tf_op jit(solution)/shard_map/ppermute | solution.py:414
  26.6 1.0 %collective-permute-done.7 = f32[4,4,128]{2,1,0:T(4,128)S(1)} collective-permute-done((f32[4,4,128]{2,1,0:T(4,128)S(1)}, f32[4,4,128]{2,1,0:T(4,128)S(1)}, u32[]{:S(2)}, u32[]{:S(2)}) %collective-permute-start.7) | collective-permute-done | bytes 8224 | tf_op jit(solution)/shard_map/ppermute | solution.py:414
  27.7 2.6 %collective-permute-start.8 = (f32[8,4,128]{2,1,0:T(4,128)S(1)}, f32[8,4,128]{2,1,0:T(4,128)S(1)}, u32[]{:S(2)}, u32[]{:S(2)}) collective-permute-start(f32[8,4,128]{2,1,0:T(4,128)S(1)} %pad_maximum_fusion), channel_id=1, source_target_pairs={{0,2},{1,3},{2,0},{3,1},{4,6},{5,7},{6,4},{7,5},{8,10},{9,11},{10,... | collective-permute-start | bytes 49160 | tf_op jit(solution)/shard_map/ppermute | solution.py:414
  30.3 1.1 %collective-permute-done.8 = f32[8,4,128]{2,1,0:T(4,128)S(1)} collective-permute-done((f32[8,4,128]{2,1,0:T(4,128)S(1)}, f32[8,4,128]{2,1,0:T(4,128)S(1)}, u32[]{:S(2)}, u32[]{:S(2)}) %collective-permute-start.8) | collective-permute-done | bytes 16416 | tf_op jit(solution)/shard_map/ppermute | solution.py:414
  31.4 0.1 mul.28
  31.5 0.5 %convolution_bitcast_fusion.planes = f32[4,3,8,128]{3,2,1,0:T(8,128)S(1)} fusion(s32[1024]{0:T(1024)S(1)} %eq.69, s32[128]{0:T(128)S(1)} %iota_add_fusion, f32[24,1024]{1,0:T(8,128)S(1)} %compare_convert_fusion, f32[4,1024]{1,0:T(4,128)S(1)} %mul.28), kind=kOutput, calls=%fused_computation | convolution fusion | flops 151224320 | bytes 168448 | tf_op jit(solution)/shard_map/kyr,xr->kyx/dot_general | solution.py:444
  32.0 0.0 collective-permute-done.3.x_b
  32.0 0.0 collective-permute-done.4.c_a
  32.0 0.0 collective-permute-done.5.c_b
  32.0 0.0 copy-start.3
  32.0 2.2 %copy-done.3 = f32[13,26,24,128]{3,2,1,0:T(8,128)S(1)} copy-done((f32[13,26,24,128]{3,2,1,0:T(8,128)S(1)}, f32[13,26,24,128]{3,2,1,0:T(8,128)}, u32[]{:S(2)}) %copy-start.3) | copy-done | bytes 4153368
  34.2 8.2 %migrate.1 = (f32[13,26,24,128]{3,2,1,0:T(8,128)S(1)}, f32[16,16,128]{2,1,0:T(8,128)}, f32[16,16,128]{2,1,0:T(8,128)}, f32[16,16,128]{2,1,0:T(8,128)}) custom-call(f32[13,26,24,128]{3,2,1,0:T(8,128)S(1)} %copy-done.3, f32[44,16,128]{2,1,0:T(8,128)S(1)} %collective-permute-done.2.x_a, ...), custom_call_target="tpu_custom_call", output_to_operand_aliasing={{0}: (0, {})} | custom-call | tf_op jit(solution)/shard_map/migrate/pallas_call | solution.py:391
  (25 shorter events, 0.3 us)
Async XLA Ops:
  0.6 11.4 %copy-start.4 = (s32[1024]{0:T(1024)S(1)}, s32[1024]{0:T(1024)}, u32[]{:S(2)}) copy-start(s32[1024]{0:T(1024)} %param.31) | copy-start | bytes 12292
  0.6 11.5 %copy-start.5 = (s32[1024]{0:T(1024)S(1)}, s32[1024]{0:T(1024)}, u32[]{:S(2)}) copy-start(s32[1024]{0:T(1024)} %param.32) | copy-start | bytes 12292
  3.1 10.3 %collective-permute-start = (f32[11,16,4,128]{3,2,1,0:T(4,128)S(1)}, f32[11,16,4,128]{3,2,1,0:T(4,128)S(1)}, u32[]{:S(2)}, u32[]{:S(2)}) collective-permute-start(f32[11,16,4,128]{3,2,1,0:T(4,128)S(1)} %get-tuple-element.19), channel_id=1, source_target_pairs={{0,1},{2,3},{1,0},{3,2},{4,5},{6,7},{5,4},{7,6},{8,9},{10,11},{9,8... | collective-permute-start | bytes 1081352 | tf_op jit(solution)/shard_map/ppermute | solution.py:32
  5.3 8.1 %collective-permute-start.1 = (f32[11,16,4,128]{3,2,1,0:T(4,128)S(1)}, f32[11,16,4,128]{3,2,1,0:T(4,128)S(1)}, u32[]{:S(2)}, u32[]{:S(2)}) collective-permute-start(f32[11,16,4,128]{3,2,1,0:T(4,128)S(1)} %get-tuple-element.20), channel_id=1, source_target_pairs={{1,2},{2,1},{5,6},{6,5},{9,10},{10,9},{13,14},{14,13},{17,18},{18,... | collective-permute-start | bytes 1081352 | tf_op jit(solution)/shard_map/ppermute | solution.py:32
  6.1 1.9 %copy-start = (f32[13,26,24,128]{3,2,1,0:T(8,128)}, f32[13,26,24,128]{3,2,1,0:T(8,128)S(1)}, u32[]{:S(2)}) copy-start(f32[13,26,24,128]{3,2,1,0:T(8,128)S(1)} %get-tuple-element.18._) | copy-start | bytes 12460036
  8.0 4.7 %collective-permute-start.2 = (f32[44,16,128]{2,1,0:T(8,128)S(1)}, f32[44,16,128]{2,1,0:T(8,128)S(1)}, u32[]{:S(2)}, u32[]{:S(2)}) collective-permute-start(f32[44,16,128]{2,1,0:T(8,128)S(1)} %get-tuple-element.22), channel_id=1, source_target_pairs={{0,4},{8,12},{4,0},{12,8},{1,5},{9,13},{5,1},{13,9},{2,6},{10,14},... | collective-permute-start | bytes 1081352 | tf_op jit(solution)/shard_map/ppermute | solution.py:32
  9.0 23.0 %collective-permute-start.3 = (f32[43,16,128]{2,1,0:T(8,128)S(1)}, f32[43,16,128]{2,1,0:T(8,128)S(1)}, u32[]{:S(2)}, u32[]{:S(2)}) collective-permute-start(f32[43,16,128]{2,1,0:T(8,128)S(1)} %get-tuple-element.23), channel_id=1, source_target_pairs={{4,8},{8,4},{5,9},{9,5},{6,10},{10,6},{7,11},{11,7},{20,24},{24,20... | collective-permute-start | bytes 1056776 | tf_op jit(solution)/shard_map/ppermute | solution.py:32
  12.7 9.5 %collective-permute-start.6 = (f32[2,4,128]{2,1,0:T(4,128)S(1)}, f32[2,4,128]{2,1,0:T(4,128)S(1)}, u32[]{:S(2)}, u32[]{:S(2)}) collective-permute-start(f32[2,4,128]{2,1,0:T(4,128)S(1)} %pad_maximum_fusion.2), channel_id=1, source_target_pairs={{0,8},{4,12},{8,0},{12,4},{1,9},{5,13},{9,1},{13,5},{2,10},{6,14},... | collective-permute-start | bytes 12296 | tf_op jit(solution)/shard_map/ppermute | solution.py:414
  13.5 2.2 %copy-start.1 = (f32[13,26,24,128]{3,2,1,0:T(8,128)S(1)}, f32[13,26,24,128]{3,2,1,0:T(8,128)}, u32[]{:S(2)}) copy-start(f32[13,26,24,128]{3,2,1,0:T(8,128)} %copy-done) | copy-start | bytes 12460036
  15.9 1.9 %copy-start.2 = (f32[13,26,24,128]{3,2,1,0:T(8,128)}, f32[13,26,24,128]{3,2,1,0:T(8,128)S(1)}, u32[]{:S(2)}) copy-start(f32[13,26,24,128]{3,2,1,0:T(8,128)S(1)} %get-tuple-element.21._) | copy-start | bytes 12460036
  17.8 14.2 %collective-permute-start.4 = (f32[43,8,128]{2,1,0:T(8,128)S(1)}, f32[43,8,128]{2,1,0:T(8,128)S(1)}, u32[]{:S(2)}, u32[]{:S(2)}) collective-permute-start(f32[43,8,128]{2,1,0:T(8,128)S(1)} %get-tuple-element.24), channel_id=1, source_target_pairs={{0,4},{8,12},{4,0},{12,8},{1,5},{9,13},{5,1},{13,9},{2,6},{10,14},... | collective-permute-start | bytes 528392 | tf_op jit(solution)/shard_map/ppermute | solution.py:32
  19.0 13.0 %collective-permute-start.5 = (f32[43,8,128]{2,1,0:T(8,128)S(1)}, f32[43,8,128]{2,1,0:T(8,128)S(1)}, u32[]{:S(2)}, u32[]{:S(2)}) collective-permute-start(f32[43,8,128]{2,1,0:T(8,128)S(1)} %get-tuple-element.25), channel_id=1, source_target_pairs={{4,8},{8,4},{5,9},{9,5},{6,10},{10,6},{7,11},{11,7},{20,24},{24,20... | collective-permute-start | bytes 528392 | tf_op jit(solution)/shard_map/ppermute | solution.py:32
  22.2 5.4 %collective-permute-start.7 = (f32[4,4,128]{2,1,0:T(4,128)S(1)}, f32[4,4,128]{2,1,0:T(4,128)S(1)}, u32[]{:S(2)}, u32[]{:S(2)}) collective-permute-start(f32[4,4,128]{2,1,0:T(4,128)S(1)} %pad_maximum_fusion.1), channel_id=1, source_target_pairs={{0,1},{1,0},{2,3},{3,2},{4,5},{5,4},{6,7},{7,6},{8,9},{9,8},{10,11... | collective-permute-start | bytes 24584 | tf_op jit(solution)/shard_map/ppermute | solution.py:414
  27.7 3.8 %collective-permute-start.8 = (f32[8,4,128]{2,1,0:T(4,128)S(1)}, f32[8,4,128]{2,1,0:T(4,128)S(1)}, u32[]{:S(2)}, u32[]{:S(2)}) collective-permute-start(f32[8,4,128]{2,1,0:T(4,128)S(1)} %pad_maximum_fusion), channel_id=1, source_target_pairs={{0,2},{1,3},{2,0},{3,1},{4,6},{5,7},{6,4},{7,5},{8,10},{9,11},{10,... | collective-permute-start | bytes 49160 | tf_op jit(solution)/shard_map/ppermute | solution.py:414
  32.0 2.2 %copy-start.3 = (f32[13,26,24,128]{3,2,1,0:T(8,128)S(1)}, f32[13,26,24,128]{3,2,1,0:T(8,128)}, u32[]{:S(2)}) copy-start(f32[13,26,24,128]{3,2,1,0:T(8,128)} %copy-done.2) | copy-start | bytes 12460036

commit v5 on v4

--- a/solution.py
+++ b/solution.py
@@ -414,35 +414,85 @@
     return jnp.concatenate([windows, lax.ppermute(windows, axis, pairs)], axis=0)
 
 
-def in_gathered_order(receivers, samples):
-    size_x, size_y = lax.axis_size("gx"), lax.axis_size("gy")
-    grid = receivers.reshape(size_x, size_y, samples).transpose(1, 0, 2)
-    for dim, axis, size in ((0, "gy", size_y), (1, "gx", size_x)):
-        for bit in bits_of(axis):
-            shape = grid.shape[:dim] + (size // (2 * bit), 2, bit) + grid.shape[dim + 1 :]
-            apart = grid.reshape(shape)
-            swapped = jnp.flip(apart, dim + 1)
-            is_set = (lax.axis_index(axis) // bit) % 2 == 1
-            grid = jnp.where(is_set, swapped, apart).reshape(grid.shape)
-    return grid.reshape(-1)
-
-
-def injected(gathered, receiver_x, receiver_y, samples, cells_x, cells_y, depth):
-    everyone = gathered[:, :, :samples].transpose(1, 0, 2).reshape(STEPS, -1)
+def inject_kernel(samples, cells_x, cells_y, gathered, table_x, table_y, planes, weights, picks):
+    size_y = lax.axis_size("gy")
+    own_x, own_y = lax.axis_index("gx"), lax.axis_index("gy")
     rows = cells_y + 2 * RIM
     tiles = rows // SUBLANES
-    x_global = lax.axis_index("gx") * cells_x - RIM + jnp.arange(depth, dtype=jnp.int32)
-    place = jnp.arange(rows, dtype=jnp.int32)
-    row = tiles * (place % SUBLANES) + place // SUBLANES
-    y_local = jnp.where(row < cells_y + RIM, row, row - rows)
-    y_global = lax.axis_index("gy") * cells_y + y_local
-    order_x = in_gathered_order(receiver_x, samples)
-    order_y = in_gathered_order(receiver_y, samples)
-    pick_x = (order_x[None, :] == x_global[:, None]).astype(jnp.float32)
-    pick_y = (order_y[None, :] == y_global[:, None]).astype(jnp.float32)
-    weighted = everyone[:, None, :] * pick_y[None, :, :]
-    planes = jnp.einsum("kyr,xr->kyx", weighted, pick_x, precision=lax.Precision.HIGHEST)
-    return planes.reshape(STEPS, tiles, SUBLANES, depth)
+    wide_x = picks.shape[0]
+    in_row = LANES // samples
+    place = lax.broadcasted_iota(jnp.int32, (rows, LANES), 0)
+    row = tiles * lax.rem(place, SUBLANES) + lax.div(place, SUBLANES)
+    y_global = own_y * cells_y + jnp.where(row < cells_y + RIM, row, row - rows)
+    x_global = own_x * cells_x - RIM + lax.broadcasted_iota(jnp.int32, (wide_x, LANES), 0)
+    lane = lax.broadcasted_iota(jnp.int32, (1, LANES), 1)
+    bits_x, bits_y = bits_of("gx"), bits_of("gy")
+
+    def source(place):
+        device_x, device_y = own_x, own_y
+        for number, bit in enumerate(bits_x):
+            if place >> number & 1:
+                device_x = jnp.bitwise_xor(device_x, bit)
+        for number, bit in enumerate(bits_y):
+            if place >> (len(bits_x) + number) & 1:
+                device_y = jnp.bitwise_xor(device_y, bit)
+        return device_x * size_y + device_y
+
+    for group in range(gathered.shape[0] // in_row):
+        at_x = at_y = jnp.zeros((1, LANES), jnp.int32)
+        window = jnp.zeros((STEPS, LANES), jnp.float32)
+        for part in range(in_row):
+            place = group * in_row + part
+            device = source(place)
+            here = (lane >= part * samples) & (lane < (part + 1) * samples)
+            shift = lax.rem((part - lax.rem(device, in_row)) * samples + LANES, LANES)
+            table_row = pl.ds(lax.div(device, in_row), 1)
+            at_x = jnp.where(here, pltpu.roll(table_x[table_row, :], shift, 1), at_x)
+            at_y = jnp.where(here, pltpu.roll(table_y[table_row, :], shift, 1), at_y)
+            moved = gathered[place]
+            if part:
+                moved = pltpu.roll(moved, part * samples, 1)
+            window = jnp.where(here, moved, window)
+        span = slice(group * LANES, (group + 1) * LANES)
+        picks[:, span] = (at_x == x_global).astype(jnp.float32)
+        is_y = at_y == y_global
+        for sample in range(STEPS):
+            weights[sample * rows : (sample + 1) * rows, span] = jnp.where(
+                is_y, window[sample : sample + 1], 0.0
+            )
+    rest = weights[...]
+    pick = picks[...].astype(jnp.bfloat16)
+    total = None
+    for _ in range(3):
+        part = rest.astype(jnp.bfloat16)
+        rest = rest - part.astype(jnp.float32)
+        product = lax.dot_general(
+            part, pick, (((1,), (1,)), ((), ())), preferred_element_type=jnp.float32
+        )
+        total = product if total is None else total + product
+    planes[...] = jnp.zeros_like(planes)
+    for sample in range(STEPS):
+        for tile in range(tiles):
+            begin = sample * rows + tile * SUBLANES
+            planes[sample, tile, :, :wide_x] = total[begin : begin + SUBLANES]
+
+
+def injected(gathered, receiver_x, receiver_y, samples, cells_x, cells_y, depth):
+    rows = cells_y + 2 * RIM
+    receivers = receiver_x.shape[0]
+    wide_x = -(-(cells_x + 2 * RIM) // 32) * 32
+    return pl.pallas_call(
+        functools.partial(inject_kernel, samples, cells_x, cells_y),
+        out_shape=vmem_out(STEPS, rows // SUBLANES, SUBLANES, depth),
+        in_specs=in_vmem(3),
+        out_specs=in_vmem(1)[0],
+        scratch_shapes=[
+            pltpu.VMEM((STEPS * rows, receivers), jnp.float32),
+            pltpu.VMEM((wide_x, receivers), jnp.float32),
+        ],
+        compiler_params=PARAMS,
+        name="inject",
+    )(gathered, receiver_x.reshape(-1, LANES), receiver_y.reshape(-1, LANES))
 
 
 def per_device(

time: 43.1 us -> 37.4 us (0.87)
  local copies, waits for them, and re-layouts: 8.81 us -> 0.05 us
  waiting for transfers between devices: 2.74 us -> 6.19 us
  matrix products: 0.47 us -> 0 us
    unnamed x15 -> x7, local copies, waits for them, and re-layouts: 8.25 us -> 0.03 us
    ppermute x6, waiting for transfers between devices: 0.59 us -> 4.03 us  [swap(): return lax.ppermute(value, axis, pairs)]
    ppermute x3, starting transfers between devices: 7.08 us -> 8.29 us  [doubled(): lax.ppermute(windows, axis, pairs)]
    ppermute x6, starting transfers between devices: 11.2 us -> 10.1 us  [swap(): return lax.ppermute(value, axis, pairs)]
    dot_general x1 -> x0, matrix products: 0.47 us -> none  [injected(): jnp.einsum('kyr,xr->kyx', weighted, pick_x, precision=lax.Precision.HIGHEST)]
    pallas_call x0 -> x1, Pallas kernels: none -> 0.46 us  [injected(): pl.pallas_call(functools.partial(inject_kernel, samples, cells_x, cells_y...]
  transfers between devices with their start and end apart: 9 -> 9, of which waited for: 3 -> 3; matrix products, arithmetic and copies ran while one was open for 3% -> 0% of each run, Pallas kernels for 1% -> 2%
where the time goes in v5:
time: 37.4 us; the launch traced here: 36.8 us
  starting transfers between devices  18.4 us (49%)
  Pallas kernels  10.7 us (29%)
  waiting for transfers between devices  6.19 us (17%)
  between operations  1.43 us (4%)
    ppermute x6, starting transfers between devices, swap(): return lax.ppermute(value, axis, pairs)  10.1 us
    ppermute x3, starting transfers between devices, doubled(): lax.ppermute(windows, axis, pairs)  8.29 us
    pallas_call x1, Pallas kernels, migrate(): pl.pallas_call(main_kernel, out_shape=[vmem_out(*wide.shape)] + [out] * 3...  8.15 us
    ppermute x6, waiting for transfers between devices, swap(): return lax.ppermute(value, axis, pairs)  4.03 us
    ppermute x3, waiting for transfers between devices, doubled(): lax.ppermute(windows, axis, pairs)  2.15 us
    pallas_call x1, Pallas kernels, pack(): pl.pallas_call(functools.partial(pack_kernel, count), out_shape=[wide, ri...  1.8 us
  transfers between devices with their start and end apart: 9, of which 3 were waited for; matrix products, arithmetic and copies ran while one was open for 0% of the time, Pallas kernels for 2%

profile of v5, /device:TPU:1, one launch (start us, length us, event | category | flops | bytes accessed | tf_op | source)
XLA Modules:
  0.0 36.8 jit_solution(6393951900708741057)
XLA Ops:
  1.3 1.8 %pack_y_rims.1 = (f32[13,26,24,128]{3,2,1,0:T(8,128)S(1)}, f32[11,16,4,128]{3,2,1,0:T(4,128)S(1)}, f32[11,16,4,128]{3,2,1,0:T(4,128)S(1)}, f32[1,4,128]{2,1,0:T(4,128)S(1)}) custom-call(f32[16,16,128]{2,1,0:T(8,128)} %refs_0_.1, f32[16,16,128]{2,1,0:T(8,128)} %refs_1_.1, f32[16,16,128]{2,1,0:T(8,128)} %refs_2_.1, f32[16,16,128]{2,1,0:T(8,128)} %refs_3_.1, ...), custom_call_target="tpu_custom_call" | custom-call | tf_op jit(solution)/shard_map/pack_y_rims/pallas_call | solution.py:123
  3.1 0.0 copy-start
  3.1 0.0 copy-start.1
  3.1 0.1 pack_x_rims.1
  3.2 0.1 collective-permute-start.2
  3.3 2.8 %collective-permute-start = (f32[11,16,4,128]{3,2,1,0:T(4,128)S(1)}, f32[11,16,4,128]{3,2,1,0:T(4,128)S(1)}, u32[]{:S(2)}, u32[]{:S(2)}) collective-permute-start(f32[11,16,4,128]{3,2,1,0:T(4,128)S(1)} %get-tuple-element.19), channel_id=1, source_target_pairs={{0,1},{2,3},{1,0},{3,2},{4,5},{6,7},{5,4},{7,6},{8,9},{10,11},{9,8... | collective-permute-start | bytes 1081352 | tf_op jit(solution)/shard_map/ppermute | solution.py:32
  6.1 0.7 %collective-permute-start.1 = (f32[11,16,4,128]{3,2,1,0:T(4,128)S(1)}, f32[11,16,4,128]{3,2,1,0:T(4,128)S(1)}, u32[]{:S(2)}, u32[]{:S(2)}) collective-permute-start(f32[11,16,4,128]{3,2,1,0:T(4,128)S(1)} %get-tuple-element.20), channel_id=1, source_target_pairs={{1,2},{2,1},{5,6},{6,5},{9,10},{10,9},{13,14},{14,13},{17,18},{18,... | collective-permute-start | bytes 1081352 | tf_op jit(solution)/shard_map/ppermute | solution.py:32
  6.8 0.0 collective-permute-done.2.x_a
  6.8 1.3 %collective-permute-start.6 = (f32[2,4,128]{2,1,0:T(4,128)S(1)}, f32[2,4,128]{2,1,0:T(4,128)S(1)}, u32[]{:S(2)}, u32[]{:S(2)}) collective-permute-start(f32[2,4,128]{2,1,0:T(4,128)S(1)} %pad_maximum_fusion.2), channel_id=1, source_target_pairs={{0,8},{4,12},{8,0},{12,4},{1,9},{5,13},{9,1},{13,5},{2,10},{6,14},... | collective-permute-start | bytes 12296 | tf_op jit(solution)/shard_map/ppermute | solution.py:414
  8.1 2.7 %collective-permute-start.3 = (f32[43,16,128]{2,1,0:T(8,128)S(1)}, f32[43,16,128]{2,1,0:T(8,128)S(1)}, u32[]{:S(2)}, u32[]{:S(2)}) collective-permute-start(f32[43,16,128]{2,1,0:T(8,128)S(1)} %get-tuple-element.23), channel_id=1, source_target_pairs={{4,8},{8,4},{5,9},{9,5},{6,10},{10,6},{7,11},{11,7},{20,24},{24,20... | collective-permute-start | bytes 1056776 | tf_op jit(solution)/shard_map/ppermute | solution.py:32
  10.7 4.0 %collective-permute-done.y_a = f32[11,16,4,128]{3,2,1,0:T(4,128)S(1)} collective-permute-done((f32[11,16,4,128]{3,2,1,0:T(4,128)S(1)}, f32[11,16,4,128]{3,2,1,0:T(4,128)S(1)}, u32[]{:S(2)}, u32[]{:S(2)}) %collective-permute-start) | collective-permute-done | bytes 360480 | tf_op jit(solution)/shard_map/ppermute | solution.py:32
  14.8 0.0 collective-permute-done.1.y_b
  14.8 0.2 pack_corners.1
  15.0 0.7 %collective-permute-start.4 = (f32[43,8,128]{2,1,0:T(8,128)S(1)}, f32[43,8,128]{2,1,0:T(8,128)S(1)}, u32[]{:S(2)}, u32[]{:S(2)}) collective-permute-start(f32[43,8,128]{2,1,0:T(8,128)S(1)} %get-tuple-element.24), channel_id=1, source_target_pairs={{0,4},{8,12},{4,0},{12,8},{1,5},{9,13},{5,1},{13,9},{2,6},{10,14},... | collective-permute-start | bytes 528392 | tf_op jit(solution)/shard_map/ppermute | solution.py:32
  15.7 3.2 %collective-permute-start.5 = (f32[43,8,128]{2,1,0:T(8,128)S(1)}, f32[43,8,128]{2,1,0:T(8,128)S(1)}, u32[]{:S(2)}, u32[]{:S(2)}) collective-permute-start(f32[43,8,128]{2,1,0:T(8,128)S(1)} %get-tuple-element.25), channel_id=1, source_target_pairs={{4,8},{8,4},{5,9},{9,5},{6,10},{10,6},{7,11},{11,7},{20,24},{24,20... | collective-permute-start | bytes 528392 | tf_op jit(solution)/shard_map/ppermute | solution.py:32
  18.9 0.0 collective-permute-done.6
  18.9 4.4 %collective-permute-start.7 = (f32[4,4,128]{2,1,0:T(4,128)S(1)}, f32[4,4,128]{2,1,0:T(4,128)S(1)}, u32[]{:S(2)}, u32[]{:S(2)}) collective-permute-start(f32[4,4,128]{2,1,0:T(4,128)S(1)} %pad_maximum_fusion.1), channel_id=1, source_target_pairs={{0,1},{1,0},{2,3},{3,2},{4,5},{5,4},{6,7},{7,6},{8,9},{9,8},{10,11... | collective-permute-start | bytes 24584 | tf_op jit(solution)/shard_map/ppermute | solution.py:414
  23.3 1.0 %collective-permute-done.7 = f32[4,4,128]{2,1,0:T(4,128)S(1)} collective-permute-done((f32[4,4,128]{2,1,0:T(4,128)S(1)}, f32[4,4,128]{2,1,0:T(4,128)S(1)}, u32[]{:S(2)}, u32[]{:S(2)}) %collective-permute-start.7) | collective-permute-done | bytes 8224 | tf_op jit(solution)/shard_map/ppermute | solution.py:414
  24.4 2.6 %collective-permute-start.8 = (f32[8,4,128]{2,1,0:T(4,128)S(1)}, f32[8,4,128]{2,1,0:T(4,128)S(1)}, u32[]{:S(2)}, u32[]{:S(2)}) collective-permute-start(f32[8,4,128]{2,1,0:T(4,128)S(1)} %pad_maximum_fusion), channel_id=1, source_target_pairs={{0,2},{1,3},{2,0},{3,1},{4,6},{5,7},{6,4},{7,5},{8,10},{9,11},{10,... | collective-permute-start | bytes 49160 | tf_op jit(solution)/shard_map/ppermute | solution.py:414
  27.0 1.1 %collective-permute-done.8 = f32[8,4,128]{2,1,0:T(4,128)S(1)} collective-permute-done((f32[8,4,128]{2,1,0:T(4,128)S(1)}, f32[8,4,128]{2,1,0:T(4,128)S(1)}, u32[]{:S(2)}, u32[]{:S(2)}) %collective-permute-start.8) | collective-permute-done | bytes 16416 | tf_op jit(solution)/shard_map/ppermute | solution.py:414
  28.1 0.0 copy-done
  28.1 0.0 copy-done.1
  28.1 0.5 %inject.1.planes = f32[4,3,8,128]{3,2,1,0:T(8,128)S(1)} custom-call(f32[16,4,128]{2,1,0:T(4,128)S(1)} %constant_dynamic-update-slice_fusion.gathered, s32[8,128]{1,0:T(8,128)S(1)} %bitcast.2, s32[8,128]{1,0:T(8,128)S(1)} %bitcast.3), custom_call_target="tpu_custom_call" | custom-call | tf_op jit(solution)/shard_map/inject/pallas_call | solution.py:484
  28.6 0.0 collective-permute-done.3.x_b
  28.6 0.0 collective-permute-done.4.c_a
  28.6 0.0 collective-permute-done.5.c_b
  28.6 8.1 %migrate.1 = (f32[13,26,24,128]{3,2,1,0:T(8,128)S(1)}, f32[16,16,128]{2,1,0:T(8,128)}, f32[16,16,128]{2,1,0:T(8,128)}, f32[16,16,128]{2,1,0:T(8,128)}) custom-call(f32[13,26,24,128]{3,2,1,0:T(8,128)S(1)} %get-tuple-element.21._, f32[44,16,128]{2,1,0:T(8,128)S(1)} %collective-permute-done.2.x_a, ...), custom_call_target="tpu_custom_call", output_to_operand_aliasing={{0}: (0, {})} | custom-call | tf_op jit(solution)/shard_map/migrate/pallas_call | solution.py:391
  (8 shorter events, 0.1 us)
Async XLA Ops:
  3.1 25.0 %copy-start = (s32[1024]{0:T(1024)S(1)}, s32[1024]{0:T(1024)}, u32[]{:S(2)}) copy-start(s32[1024]{0:T(1024)} %param.31) | copy-start | bytes 12292
  3.1 25.0 %copy-start.1 = (s32[1024]{0:T(1024)S(1)}, s32[1024]{0:T(1024)}, u32[]{:S(2)}) copy-start(s32[1024]{0:T(1024)} %param.32) | copy-start | bytes 12292
  3.2 3.6 %collective-permute-start.2 = (f32[44,16,128]{2,1,0:T(8,128)S(1)}, f32[44,16,128]{2,1,0:T(8,128)S(1)}, u32[]{:S(2)}, u32[]{:S(2)}) collective-permute-start(f32[44,16,128]{2,1,0:T(8,128)S(1)} %get-tuple-element.22), channel_id=1, source_target_pairs={{0,4},{8,12},{4,0},{12,8},{1,5},{9,13},{5,1},{13,9},{2,6},{10,14},... | collective-permute-start | bytes 1081352 | tf_op jit(solution)/shard_map/ppermute | solution.py:32
  3.3 11.5 %collective-permute-start = (f32[11,16,4,128]{3,2,1,0:T(4,128)S(1)}, f32[11,16,4,128]{3,2,1,0:T(4,128)S(1)}, u32[]{:S(2)}, u32[]{:S(2)}) collective-permute-start(f32[11,16,4,128]{3,2,1,0:T(4,128)S(1)} %get-tuple-element.19), channel_id=1, source_target_pairs={{0,1},{2,3},{1,0},{3,2},{4,5},{6,7},{5,4},{7,6},{8,9},{10,11},{9,8... | collective-permute-start | bytes 1081352 | tf_op jit(solution)/shard_map/ppermute | solution.py:32
  6.1 8.7 %collective-permute-start.1 = (f32[11,16,4,128]{3,2,1,0:T(4,128)S(1)}, f32[11,16,4,128]{3,2,1,0:T(4,128)S(1)}, u32[]{:S(2)}, u32[]{:S(2)}) collective-permute-start(f32[11,16,4,128]{3,2,1,0:T(4,128)S(1)} %get-tuple-element.20), channel_id=1, source_target_pairs={{1,2},{2,1},{5,6},{6,5},{9,10},{10,9},{13,14},{14,13},{17,18},{18,... | collective-permute-start | bytes 1081352 | tf_op jit(solution)/shard_map/ppermute | solution.py:32
  6.8 12.1 %collective-permute-start.6 = (f32[2,4,128]{2,1,0:T(4,128)S(1)}, f32[2,4,128]{2,1,0:T(4,128)S(1)}, u32[]{:S(2)}, u32[]{:S(2)}) collective-permute-start(f32[2,4,128]{2,1,0:T(4,128)S(1)} %pad_maximum_fusion.2), channel_id=1, source_target_pairs={{0,8},{4,12},{8,0},{12,4},{1,9},{5,13},{9,1},{13,5},{2,10},{6,14},... | collective-permute-start | bytes 12296 | tf_op jit(solution)/shard_map/ppermute | solution.py:414
  8.1 20.5 %collective-permute-start.3 = (f32[43,16,128]{2,1,0:T(8,128)S(1)}, f32[43,16,128]{2,1,0:T(8,128)S(1)}, u32[]{:S(2)}, u32[]{:S(2)}) collective-permute-start(f32[43,16,128]{2,1,0:T(8,128)S(1)} %get-tuple-element.23), channel_id=1, source_target_pairs={{4,8},{8,4},{5,9},{9,5},{6,10},{10,6},{7,11},{11,7},{20,24},{24,20... | collective-permute-start | bytes 1056776 | tf_op jit(solution)/shard_map/ppermute | solution.py:32
  15.0 13.6 %collective-permute-start.4 = (f32[43,8,128]{2,1,0:T(8,128)S(1)}, f32[43,8,128]{2,1,0:T(8,128)S(1)}, u32[]{:S(2)}, u32[]{:S(2)}) collective-permute-start(f32[43,8,128]{2,1,0:T(8,128)S(1)} %get-tuple-element.24), channel_id=1, source_target_pairs={{0,4},{8,12},{4,0},{12,8},{1,5},{9,13},{5,1},{13,9},{2,6},{10,14},... | collective-permute-start | bytes 528392 | tf_op jit(solution)/shard_map/ppermute | solution.py:32
  15.7 12.9 %collective-permute-start.5 = (f32[43,8,128]{2,1,0:T(8,128)S(1)}, f32[43,8,128]{2,1,0:T(8,128)S(1)}, u32[]{:S(2)}, u32[]{:S(2)}) collective-permute-start(f32[43,8,128]{2,1,0:T(8,128)S(1)} %get-tuple-element.25), channel_id=1, source_target_pairs={{4,8},{8,4},{5,9},{9,5},{6,10},{10,6},{7,11},{11,7},{20,24},{24,20... | collective-permute-start | bytes 528392 | tf_op jit(solution)/shard_map/ppermute | solution.py:32
  18.9 5.4 %collective-permute-start.7 = (f32[4,4,128]{2,1,0:T(4,128)S(1)}, f32[4,4,128]{2,1,0:T(4,128)S(1)}, u32[]{:S(2)}, u32[]{:S(2)}) collective-permute-start(f32[4,4,128]{2,1,0:T(4,128)S(1)} %pad_maximum_fusion.1), channel_id=1, source_target_pairs={{0,1},{1,0},{2,3},{3,2},{4,5},{5,4},{6,7},{7,6},{8,9},{9,8},{10,11... | collective-permute-start | bytes 24584 | tf_op jit(solution)/shard_map/ppermute | solution.py:414
  24.4 3.8 %collective-permute-start.8 = (f32[8,4,128]{2,1,0:T(4,128)S(1)}, f32[8,4,128]{2,1,0:T(4,128)S(1)}, u32[]{:S(2)}, u32[]{:S(2)}) collective-permute-start(f32[8,4,128]{2,1,0:T(4,128)S(1)} %pad_maximum_fusion), channel_id=1, source_target_pairs={{0,2},{1,3},{2,0},{3,1},{4,6},{5,7},{6,4},{7,5},{8,10},{9,11},{10,... | collective-permute-start | bytes 49160 | tf_op jit(solution)/shard_map/ppermute | solution.py:414

commit v6 on v5

--- a/solution.py
+++ b/solution.py
@@ -165,7 +165,7 @@
     )(pinned(wide, pltpu.VMEM), window)
 
 
-def corner_kernel(_, y_a, y_b, wide, c_a, c_b):
+def corner_kernel(_, y_a, y_b, __, wide, c_a, c_b):
     cells_x = y_a.shape[1]
     cells_y = wide.shape[2] - 2 * RIM
     odd_x, odd_y = is_odd("gx"), is_odd("gy")
@@ -191,17 +191,17 @@
             out[place : place + width] = wide[number, pl.ds(begin, width), cells_y:, :]
 
 
-def corners(wide, y_a, y_b):
+def corners(wide, y_a, y_b, earlier):
     corner = vmem_out(x_parts()[1], 2 * RIM, wide.shape[-1])
     return pl.pallas_call(
         corner_kernel,
         out_shape=[vmem_out(*wide.shape), corner, corner],
-        in_specs=in_vmem(3),
+        in_specs=in_vmem(4),
         out_specs=in_vmem(3),
         input_output_aliases={0: 0},
         compiler_params=PARAMS,
         name="pack_corners",
-    )(pinned(wide, pltpu.VMEM), y_a, y_b)
+    )(pinned(wide, pltpu.VMEM), y_a, y_b, earlier)
 
 
 def sine_cosine(angle):
@@ -537,9 +537,11 @@
     windows = jnp.concatenate([window, x_a[x_parts()[1] :, :STEPS, :]], axis=0)
     for bit in bits_of("gx")[1:]:
         windows = doubled(windows, "gx", bit)
-    for bit in bits_of("gy"):
+    for bit in bits_of("gy")[:-1]:
         windows = doubled(windows, "gy", bit)
-    wide, c_a, c_b = corners(wide, y_a, y_b)
+    wide, c_a, c_b = corners(wide, y_a, y_b, windows)
+    for bit in bits_of("gy")[-1:]:
+        windows = doubled(windows, "gy", bit)
     c_a, c_b = swap(c_a, "gx", 0), swap(c_b, "gx", 1)
     planes = injected(
         windows, receiver_x, receiver_y, traces.shape[1], cells_x, cells_y, depth

time: 37.4 us -> 33.8 us (0.904); the launches traced: 36.8 us -> 33.6 us
  waiting for transfers between devices: 6.19 us -> 4.23 us
  starting transfers between devices: 18.4 us -> 17.1 us
    ppermute x3, starting transfers between devices: 8.29 us -> 6.79 us  [doubled(): lax.ppermute(windows, axis, pairs)]
    ppermute x3, waiting for transfers between devices: 2.15 us -> 1.04 us  [doubled(): lax.ppermute(windows, axis, pairs)]
    ppermute x6, waiting for transfers between devices: 4.03 us -> 3.19 us  [swap(): return lax.ppermute(value, axis, pairs)]
  transfers between devices with their start and end apart: 9 -> 9, of which waited for: 3 -> 2; matrix products, arithmetic and copies ran while one was open for 0% -> 0% of each run, Pallas kernels for 2% -> 2%
where the time goes in v6:
time: 33.8 us; the launch traced here: 33.6 us
  starting transfers between devices  17.1 us (51%)
  Pallas kernels  10.7 us (32%)
  waiting for transfers between devices  4.23 us (13%)
  between operations  1.45 us (4%)
    ppermute x6, starting transfers between devices, swap(): return lax.ppermute(value, axis, pairs)  10.3 us
    pallas_call x1, Pallas kernels, migrate(): pl.pallas_call(main_kernel, out_shape=[vmem_out(*wide.shape)] + [out] * 3...  8.14 us
    ppermute x3, starting transfers between devices, doubled(): lax.ppermute(windows, axis, pairs)  6.79 us
    ppermute x6, waiting for transfers between devices, swap(): return lax.ppermute(value, axis, pairs)  3.19 us
    pallas_call x1, Pallas kernels, pack(): pl.pallas_call(functools.partial(pack_kernel, count), out_shape=[wide, ri...  1.8 us
    ppermute x3, waiting for transfers between devices, doubled(): lax.ppermute(windows, axis, pairs)  1.04 us
  transfers between devices with their start and end apart: 9, of which 2 were waited for; matrix products, arithmetic and copies ran while one was open for 0% of the time, Pallas kernels for 2%

profile of v6, /device:TPU:1, one launch (start us, length us, event | category | flops | bytes accessed | tf_op | source)
XLA Modules:
  0.0 33.6 jit_solution(16885056856625401942)
XLA Ops:
  1.3 1.8 %pack_y_rims.1 = (f32[13,26,24,128]{3,2,1,0:T(8,128)S(1)}, f32[11,16,4,128]{3,2,1,0:T(4,128)S(1)}, f32[11,16,4,128]{3,2,1,0:T(4,128)S(1)}, f32[1,4,128]{2,1,0:T(4,128)S(1)}) custom-call(f32[16,16,128]{2,1,0:T(8,128)} %refs_0_.1, f32[16,16,128]{2,1,0:T(8,128)} %refs_1_.1, f32[16,16,128]{2,1,0:T(8,128)} %refs_2_.1, f32[16,16,128]{2,1,0:T(8,128)} %refs_3_.1, ...), custom_call_target="tpu_custom_call" | custom-call | tf_op jit(solution)/shard_map/pack_y_rims/pallas_call | solution.py:123
  3.1 0.0 copy-start
  3.1 0.0 copy-start.1
  3.1 0.1 pack_x_rims.1
  3.2 0.1 collective-permute-start.2
  3.3 2.8 %collective-permute-start = (f32[11,16,4,128]{3,2,1,0:T(4,128)S(1)}, f32[11,16,4,128]{3,2,1,0:T(4,128)S(1)}, u32[]{:S(2)}, u32[]{:S(2)}) collective-permute-start(f32[11,16,4,128]{3,2,1,0:T(4,128)S(1)} %get-tuple-element.19), channel_id=1, source_target_pairs={{0,1},{2,3},{1,0},{3,2},{4,5},{6,7},{5,4},{7,6},{8,9},{10,11},{9,8... | collective-permute-start | bytes 1081352 | tf_op jit(solution)/shard_map/ppermute | solution.py:32
  6.1 0.7 %collective-permute-start.1 = (f32[11,16,4,128]{3,2,1,0:T(4,128)S(1)}, f32[11,16,4,128]{3,2,1,0:T(4,128)S(1)}, u32[]{:S(2)}, u32[]{:S(2)}) collective-permute-start(f32[11,16,4,128]{3,2,1,0:T(4,128)S(1)} %get-tuple-element.20), channel_id=1, source_target_pairs={{1,2},{2,1},{5,6},{6,5},{9,10},{10,9},{13,14},{14,13},{17,18},{18,... | collective-permute-start | bytes 1081352 | tf_op jit(solution)/shard_map/ppermute | solution.py:32
  6.8 0.0 collective-permute-done.2.x_a
  6.8 1.3 %collective-permute-start.3 = (f32[2,4,128]{2,1,0:T(4,128)S(1)}, f32[2,4,128]{2,1,0:T(4,128)S(1)}, u32[]{:S(2)}, u32[]{:S(2)}) collective-permute-start(f32[2,4,128]{2,1,0:T(4,128)S(1)} %pad_maximum_fusion.2), channel_id=1, source_target_pairs={{0,8},{4,12},{8,0},{12,4},{1,9},{5,13},{9,1},{13,5},{2,10},{6,14},... | collective-permute-start | bytes 12296 | tf_op jit(solution)/shard_map/ppermute | solution.py:414
  8.1 2.7 %collective-permute-start.5 = (f32[43,16,128]{2,1,0:T(8,128)S(1)}, f32[43,16,128]{2,1,0:T(8,128)S(1)}, u32[]{:S(2)}, u32[]{:S(2)}) collective-permute-start(f32[43,16,128]{2,1,0:T(8,128)S(1)} %get-tuple-element.23), channel_id=1, source_target_pairs={{4,8},{8,4},{5,9},{9,5},{6,10},{10,6},{7,11},{11,7},{20,24},{24,20... | collective-permute-start | bytes 1056776 | tf_op jit(solution)/shard_map/ppermute | solution.py:32
  10.7 0.0 collective-permute-done.3
  10.8 4.2 %collective-permute-start.4 = (f32[4,4,128]{2,1,0:T(4,128)S(1)}, f32[4,4,128]{2,1,0:T(4,128)S(1)}, u32[]{:S(2)}, u32[]{:S(2)}) collective-permute-start(f32[4,4,128]{2,1,0:T(4,128)S(1)} %pad_maximum_fusion.1), channel_id=1, source_target_pairs={{0,1},{1,0},{2,3},{3,2},{4,5},{5,4},{6,7},{7,6},{8,9},{9,8},{10,11... | collective-permute-start | bytes 24584 | tf_op jit(solution)/shard_map/ppermute | solution.py:414
  14.9 1.0 %collective-permute-done.4 = f32[4,4,128]{2,1,0:T(4,128)S(1)} collective-permute-done((f32[4,4,128]{2,1,0:T(4,128)S(1)}, f32[4,4,128]{2,1,0:T(4,128)S(1)}, u32[]{:S(2)}, u32[]{:S(2)}) %collective-permute-start.4) | collective-permute-done | bytes 8224 | tf_op jit(solution)/shard_map/ppermute | solution.py:414
  16.0 1.4 %collective-permute-start.8 = (f32[8,4,128]{2,1,0:T(4,128)S(1)}, f32[8,4,128]{2,1,0:T(4,128)S(1)}, u32[]{:S(2)}, u32[]{:S(2)}) collective-permute-start(f32[8,4,128]{2,1,0:T(4,128)S(1)} %pad_maximum_fusion.__), channel_id=1, source_target_pairs={{0,2},{1,3},{2,0},{3,1},{4,6},{5,7},{6,4},{7,5},{8,10},{9,11},{10,... | collective-permute-start | bytes 49160 | tf_op jit(solution)/shard_map/ppermute | solution.py:414
  17.3 0.0 collective-permute-done.y_a
  17.3 0.0 collective-permute-done.1.y_b
  17.3 0.2 pack_corners.1
  17.6 1.1 %collective-permute-start.6 = (f32[43,8,128]{2,1,0:T(8,128)S(1)}, f32[43,8,128]{2,1,0:T(8,128)S(1)}, u32[]{:S(2)}, u32[]{:S(2)}) collective-permute-start(f32[43,8,128]{2,1,0:T(8,128)S(1)} %get-tuple-element.24), channel_id=1, source_target_pairs={{0,4},{8,12},{4,0},{12,8},{1,5},{9,13},{5,1},{13,9},{2,6},{10,14},... | collective-permute-start | bytes 528392 | tf_op jit(solution)/shard_map/ppermute | solution.py:32
  18.7 3.0 %collective-permute-start.7 = (f32[43,8,128]{2,1,0:T(8,128)S(1)}, f32[43,8,128]{2,1,0:T(8,128)S(1)}, u32[]{:S(2)}, u32[]{:S(2)}) collective-permute-start(f32[43,8,128]{2,1,0:T(8,128)S(1)} %get-tuple-element.25), channel_id=1, source_target_pairs={{4,8},{8,4},{5,9},{9,5},{6,10},{10,6},{7,11},{11,7},{20,24},{24,20... | collective-permute-start | bytes 528392 | tf_op jit(solution)/shard_map/ppermute | solution.py:32
  21.7 0.0 collective-permute-done.8
  21.7 0.0 copy-done
  21.7 0.0 copy-done.1
  21.7 0.5 %inject.1.planes = f32[4,3,8,128]{3,2,1,0:T(8,128)S(1)} custom-call(f32[16,4,128]{2,1,0:T(4,128)S(1)} %constant_dynamic-update-slice_fusion.gathered, s32[8,128]{1,0:T(8,128)S(1)} %bitcast.2, s32[8,128]{1,0:T(8,128)S(1)} %bitcast.3), custom_call_target="tpu_custom_call" | custom-call | tf_op jit(solution)/shard_map/inject/pallas_call | solution.py:484
  22.2 0.0 collective-permute-done.5.x_b
  22.2 0.0 collective-permute-done.6.c_a
  22.2 3.2 %collective-permute-done.7.c_b = f32[43,8,128]{2,1,0:T(8,128)S(1)} collective-permute-done((f32[43,8,128]{2,1,0:T(8,128)S(1)}, f32[43,8,128]{2,1,0:T(8,128)S(1)}, u32[]{:S(2)}, u32[]{:S(2)}) %collective-permute-start.7) | collective-permute-done | bytes 176160 | tf_op jit(solution)/shard_map/ppermute | solution.py:32
  25.4 8.1 %migrate.1 = (f32[13,26,24,128]{3,2,1,0:T(8,128)S(1)}, f32[16,16,128]{2,1,0:T(8,128)}, f32[16,16,128]{2,1,0:T(8,128)}, f32[16,16,128]{2,1,0:T(8,128)}) custom-call(f32[13,26,24,128]{3,2,1,0:T(8,128)S(1)} %get-tuple-element.22._, f32[44,16,128]{2,1,0:T(8,128)S(1)} %collective-permute-done.2.x_a, ...), custom_call_target="tpu_custom_call", output_to_operand_aliasing={{0}: (0, {})} | custom-call | tf_op jit(solution)/shard_map/migrate/pallas_call | solution.py:391
  (8 shorter events, 0.1 us)
Async XLA Ops:
  3.1 18.6 %copy-start = (s32[1024]{0:T(1024)S(1)}, s32[1024]{0:T(1024)}, u32[]{:S(2)}) copy-start(s32[1024]{0:T(1024)} %param.31) | copy-start | bytes 12292
  3.1 18.6 %copy-start.1 = (s32[1024]{0:T(1024)S(1)}, s32[1024]{0:T(1024)}, u32[]{:S(2)}) copy-start(s32[1024]{0:T(1024)} %param.32) | copy-start | bytes 12292
  3.2 3.6 %collective-permute-start.2 = (f32[44,16,128]{2,1,0:T(8,128)S(1)}, f32[44,16,128]{2,1,0:T(8,128)S(1)}, u32[]{:S(2)}, u32[]{:S(2)}) collective-permute-start(f32[44,16,128]{2,1,0:T(8,128)S(1)} %get-tuple-element.21), channel_id=1, source_target_pairs={{0,4},{8,12},{4,0},{12,8},{1,5},{9,13},{5,1},{13,9},{2,6},{10,14},... | collective-permute-start | bytes 1081352 | tf_op jit(solution)/shard_map/ppermute | solution.py:32
  3.3 14.0 %collective-permute-start = (f32[11,16,4,128]{3,2,1,0:T(4,128)S(1)}, f32[11,16,4,128]{3,2,1,0:T(4,128)S(1)}, u32[]{:S(2)}, u32[]{:S(2)}) collective-permute-start(f32[11,16,4,128]{3,2,1,0:T(4,128)S(1)} %get-tuple-element.19), channel_id=1, source_target_pairs={{0,1},{2,3},{1,0},{3,2},{4,5},{6,7},{5,4},{7,6},{8,9},{10,11},{9,8... | collective-permute-start | bytes 1081352 | tf_op jit(solution)/shard_map/ppermute | solution.py:32
  6.1 11.3 %collective-permute-start.1 = (f32[11,16,4,128]{3,2,1,0:T(4,128)S(1)}, f32[11,16,4,128]{3,2,1,0:T(4,128)S(1)}, u32[]{:S(2)}, u32[]{:S(2)}) collective-permute-start(f32[11,16,4,128]{3,2,1,0:T(4,128)S(1)} %get-tuple-element.20), channel_id=1, source_target_pairs={{1,2},{2,1},{5,6},{6,5},{9,10},{10,9},{13,14},{14,13},{17,18},{18,... | collective-permute-start | bytes 1081352 | tf_op jit(solution)/shard_map/ppermute | solution.py:32
  6.8 3.9 %collective-permute-start.3 = (f32[2,4,128]{2,1,0:T(4,128)S(1)}, f32[2,4,128]{2,1,0:T(4,128)S(1)}, u32[]{:S(2)}, u32[]{:S(2)}) collective-permute-start(f32[2,4,128]{2,1,0:T(4,128)S(1)} %pad_maximum_fusion.2), channel_id=1, source_target_pairs={{0,8},{4,12},{8,0},{12,4},{1,9},{5,13},{9,1},{13,5},{2,10},{6,14},... | collective-permute-start | bytes 12296 | tf_op jit(solution)/shard_map/ppermute | solution.py:414
  8.1 14.2 %collective-permute-start.5 = (f32[43,16,128]{2,1,0:T(8,128)S(1)}, f32[43,16,128]{2,1,0:T(8,128)S(1)}, u32[]{:S(2)}, u32[]{:S(2)}) collective-permute-start(f32[43,16,128]{2,1,0:T(8,128)S(1)} %get-tuple-element.23), channel_id=1, source_target_pairs={{4,8},{8,4},{5,9},{9,5},{6,10},{10,6},{7,11},{11,7},{20,24},{24,20... | collective-permute-start | bytes 1056776 | tf_op jit(solution)/shard_map/ppermute | solution.py:32
  10.8 5.2 %collective-permute-start.4 = (f32[4,4,128]{2,1,0:T(4,128)S(1)}, f32[4,4,128]{2,1,0:T(4,128)S(1)}, u32[]{:S(2)}, u32[]{:S(2)}) collective-permute-start(f32[4,4,128]{2,1,0:T(4,128)S(1)} %pad_maximum_fusion.1), channel_id=1, source_target_pairs={{0,1},{1,0},{2,3},{3,2},{4,5},{5,4},{6,7},{7,6},{8,9},{9,8},{10,11... | collective-permute-start | bytes 24584 | tf_op jit(solution)/shard_map/ppermute | solution.py:414
  16.0 5.7 %collective-permute-start.8 = (f32[8,4,128]{2,1,0:T(4,128)S(1)}, f32[8,4,128]{2,1,0:T(4,128)S(1)}, u32[]{:S(2)}, u32[]{:S(2)}) collective-permute-start(f32[8,4,128]{2,1,0:T(4,128)S(1)} %pad_maximum_fusion.__), channel_id=1, source_target_pairs={{0,2},{1,3},{2,0},{3,1},{4,6},{5,7},{6,4},{7,5},{8,10},{9,11},{10,... | collective-permute-start | bytes 49160 | tf_op jit(solution)/shard_map/ppermute | solution.py:414
  17.6 4.7 %collective-permute-start.6 = (f32[43,8,128]{2,1,0:T(8,128)S(1)}, f32[43,8,128]{2,1,0:T(8,128)S(1)}, u32[]{:S(2)}, u32[]{:S(2)}) collective-permute-start(f32[43,8,128]{2,1,0:T(8,128)S(1)} %get-tuple-element.24), channel_id=1, source_target_pairs={{0,4},{8,12},{4,0},{12,8},{1,5},{9,13},{5,1},{13,9},{2,6},{10,14},... | collective-permute-start | bytes 528392 | tf_op jit(solution)/shard_map/ppermute | solution.py:32
  18.7 6.8 %collective-permute-start.7 = (f32[43,8,128]{2,1,0:T(8,128)S(1)}, f32[43,8,128]{2,1,0:T(8,128)S(1)}, u32[]{:S(2)}, u32[]{:S(2)}) collective-permute-start(f32[43,8,128]{2,1,0:T(8,128)S(1)} %get-tuple-element.25), channel_id=1, source_target_pairs={{4,8},{8,4},{5,9},{9,5},{6,10},{10,6},{7,11},{11,7},{20,24},{24,20... | collective-permute-start | bytes 528392 | tf_op jit(solution)/shard_map/ppermute | solution.py:32

commit v7 on v6

--- a/solution.py
+++ b/solution.py
@@ -13,8 +13,8 @@
 FIELDS = 8
 SUBLANES = 8
 LANES = 128
-VMEM_LIMIT = 48 * 1024 * 1024
-PARAMS = pltpu.CompilerParams(vmem_limit_bytes=VMEM_LIMIT)
+PARAMS = pltpu.CompilerParams(vmem_limit_bytes=16 * 1024 * 1024)
+PACK_PARAMS = pltpu.CompilerParams(vmem_limit_bytes=48 * 1024 * 1024)
 
 
 def in_vmem(count):
@@ -130,7 +130,7 @@
             pltpu.VMEM(traces.shape, jnp.float32),
             pltpu.SemaphoreType.DMA((count + 1,)),
         ],
-        compiler_params=PARAMS,
+        compiler_params=PACK_PARAMS,
         name="pack_y_rims",
     )(*(pinned(value, pltpu.HBM) for value in (*blocks, traces)), segment_start)
 
@@ -215,104 +215,92 @@
     return sine * angle, cosine
 
 
-def main_kernel(_, x_a, x_b, c_a, c_b, planes, wide, image, p_last, q_last, waves, factors, local):
-    count = wide.shape[0]
-    cells_x, cells_y, depth = image.shape
-    span_x = cells_x + 2 * RIM
-    tiles = (cells_y + 2 * RIM) // SUBLANES
-    odd_x = is_odd("gx")
-    for number, width, place in x_parts()[0]:
-        low, high = RIM - width, RIM + cells_x
-        for begin, side, corner in (
-            (jnp.where(odd_x, low, high), x_a, c_a),
-            (jnp.where(odd_x, high, low), x_b, c_b),
-        ):
-            wide[number, pl.ds(begin, width), :cells_y, :] = side[place : place + width]
-            wide[number, pl.ds(begin, width), cells_y:, :] = corner[place : place + width]
-
-    def wide_tiles(number, x):
-        return [wide[number, x, pl.ds(tile, SUBLANES, stride=tiles), :] for tile in range(tiles)]
-
-    def wave_tiles(number, slot, x):
+class Steps:
+    def __init__(self, wide, planes, waves, factors, local):
+        self.wide, self.planes, self.waves, self.factors, self.local = wide, planes, waves, factors, local
+        self.count, _, rows, self.depth = wide.shape
+        self.tiles = rows // SUBLANES
+        self.cells_x = wide.shape[1] - 2 * RIM - 2
+        lane = lax.broadcasted_iota(jnp.int32, (SUBLANES, self.depth), 1)
+        self.not_last, self.not_first = lane < self.depth - 1, lane > 0
+        self.at_depth = lane == REC_DEPTH
+
+    def wide_tiles(self, number, x):
+        return [
+            self.wide[number, x, pl.ds(tile, SUBLANES, stride=self.tiles), :]
+            for tile in range(self.tiles)
+        ]
+
+    def wave_tiles(self, number, slot, x):
         if slot < 2:
-            return wide_tiles(2 * number + slot, x)
-        return [waves[number, slot - 2, x, tile] for tile in range(tiles)]
-
-    lane = lax.broadcasted_iota(jnp.int32, (SUBLANES, depth), 1)
-    not_last, not_first = lane < depth - 1, lane > 0
-    at_depth = lane == REC_DEPTH
-
-    def next_y(value):
+            return self.wide_tiles(2 * number + slot, x)
+        return [self.waves[slot - 2][number, x, tile] for tile in range(self.tiles)]
+
+    def next_y(self, value):
         return value[1:] + [pltpu.roll(value[0], SUBLANES - 1, 0)]
 
-    def previous_y(value):
+    def previous_y(self, value):
         return [pltpu.roll(value[-1], 1, 0)] + value[:-1]
 
-    def make_factors(i, carry):
-        stores = []
-        for x in (1 + 2 * i, 2 + 2 * i):
-            raw = [wide_tiles(FIELDS + number, x) for number in range(count - FIELDS)]
-            for tile in range(tiles):
-                velocity, epsilon, delta, tilt, azimuth = [value[tile] for value in raw]
-                f_e = 1.0 + 2.0 * epsilon
-                f_d = jnp.sqrt(1.0 + 2.0 * delta)
-                sin_tilt, cos_tilt = sine_cosine(tilt)
-                sin_half, cos_half = sine_cosine(0.5 * azimuth)
-                sin_azim = 2.0 * sin_half * cos_half
-                cos_azim = 1.0 - 2.0 * sin_half * sin_half
-                sin_square = sin_tilt * sin_tilt
-                half_tilt = 0.5 * sin_tilt * cos_tilt
-                along_x = sin_square * cos_azim
-                values = (
-                    velocity,
-                    velocity * f_e,
-                    velocity * f_d,
-                    along_x * cos_azim,
-                    sin_square * sin_azim * sin_azim,
-                    cos_tilt * cos_tilt,
-                    0.5 * along_x * sin_azim,
-                    half_tilt * cos_azim,
-                    half_tilt * sin_azim,
-                )
-                stores += [(number, x, tile, value) for number, value in enumerate(values)]
-        for number, x, tile, value in stores:
-            factors[number, x, tile] = value
-        return carry
-
-    lax.fori_loop(0, (span_x - 2) // 2, make_factors, 0)
-
-    def plane_part(turn, x, stores):
+    def make_factors(self, x):
+        raw = [self.wide_tiles(FIELDS + number, x) for number in range(self.count - FIELDS)]
+        for tile in range(self.tiles):
+            velocity, epsilon, delta, tilt, azimuth = [value[tile] for value in raw]
+            f_e = 1.0 + 2.0 * epsilon
+            f_d = jnp.sqrt(1.0 + 2.0 * delta)
+            sin_tilt, cos_tilt = sine_cosine(tilt)
+            sin_half, cos_half = sine_cosine(0.5 * azimuth)
+            sin_azim = 2.0 * sin_half * cos_half
+            cos_azim = 1.0 - 2.0 * sin_half * sin_half
+            sin_square = sin_tilt * sin_tilt
+            half_tilt = 0.5 * sin_tilt * cos_tilt
+            along_x = sin_square * cos_azim
+            values = (
+                velocity,
+                velocity * f_e,
+                velocity * f_d,
+                along_x * cos_azim,
+                sin_square * sin_azim * sin_azim,
+                cos_tilt * cos_tilt,
+                0.5 * along_x * sin_azim,
+                half_tilt * cos_azim,
+                half_tilt * sin_azim,
+            )
+            for number, value in enumerate(values):
+                self.factors[number, x, tile] = value
+
+    def plane_part(self, turn, x):
+        factors, local, tiles = self.factors, self.local[turn], self.tiles
         ayy = [factors[4, x, tile] for tile in range(tiles)]
         azz = [factors[5, x, tile] for tile in range(tiles)]
         ayz = [factors[8, x, tile] for tile in range(tiles)]
         for number in range(4):
-            now = wave_tiles(number, turn + 1, x)
-            above = [jnp.where(not_last, pltpu.roll(u, depth - 1, 1), 0.0) for u in now]
-            below = [jnp.where(not_first, pltpu.roll(u, 1, 1), 0.0) for u in now]
+            now = self.wave_tiles(number, turn + 1, x)
+            above = [jnp.where(self.not_last, pltpu.roll(u, self.depth - 1, 1), 0.0) for u in now]
+            below = [jnp.where(self.not_first, pltpu.roll(u, 1, 1), 0.0) for u in now]
             slope_z = [a - b for a, b in zip(above, below)]
-            after, before = next_y(now), previous_y(now)
-            slope_after, slope_before = next_y(slope_z), previous_y(slope_z)
+            after, before = self.next_y(now), self.previous_y(now)
+            slope_after, slope_before = self.next_y(slope_z), self.previous_y(slope_z)
             for tile in range(tiles):
                 double = now[tile] + now[tile]
                 sum_y = after[tile] + before[tile]
                 sum_z = above[tile] + below[tile]
-                part = (
+                local[number, 0, x, tile] = (
                     (ayy[tile] * sum_y + azz[tile] * sum_z)
                     + ayz[tile] * (slope_after[tile] - slope_before[tile])
                 ) - double
-                stores.append((local, (number, 0, x, tile), part))
-                stores.append((local, (number, 1, x, tile), after[tile] - before[tile]))
-                stores.append((local, (number, 2, x, tile), slope_z[tile]))
+                local[number, 1, x, tile] = after[tile] - before[tile]
+                local[number, 2, x, tile] = slope_z[tile]
                 if number % 2 == 0:
-                    rest = (sum_y + sum_z) - 3.0 * double
-                    stores.append((local, (number, 3, x, tile), rest))
-
-    def next_part(turn, x, stores):
-        held = [wave_tiles(number, turn, x) for number in range(4)]
-        now = [wave_tiles(number, turn + 1, x) for number in range(4)]
-        after = [wave_tiles(number, turn + 1, x + 1) for number in range(4)]
-        before = [wave_tiles(number, turn + 1, x - 1) for number in range(4)]
-        for tile in range(tiles):
+                    local[number, 3, x, tile] = (sum_y + sum_z) - 3.0 * double
+
+    def next_part(self, turn, x):
+        factors, local = self.factors, self.local[turn]
+        held = [self.wave_tiles(number, turn, x) for number in range(4)]
+        now = [self.wave_tiles(number, turn + 1, x) for number in range(4)]
+        after = [self.wave_tiles(number, turn + 1, x + 1) for number in range(4)]
+        before = [self.wave_tiles(number, turn + 1, x - 1) for number in range(4)]
+        for tile in range(self.tiles):
             velocity, with_e, with_d = [factors[number, x, tile] for number in range(3)]
             axx, axy, axz = [factors[number, x, tile] for number in (3, 6, 7)]
             for pair in range(2):
@@ -333,75 +321,139 @@
                     with_d * across + velocity * axis[1]
                 )
                 if pair == 1:
-                    shift = lax.rem(REC_DEPTH - x + depth, depth)
-                    moved = pltpu.roll(planes[STEPS - 1 - turn, tile], shift, 1)
-                    p_next = p_next + jnp.where(at_depth, moved, 0.0)
-                stores.append((waves, (p_number, turn, x, tile), p_next))
-                stores.append((waves, (q_number, turn, x, tile), q_next))
-
-    def write(stores):
-        for ref, index, value in stores:
-            ref[index] = value
-
+                    shift = lax.rem(REC_DEPTH - x + self.depth, self.depth)
+                    moved = pltpu.roll(self.planes[STEPS - 1 - turn, tile], shift, 1)
+                    p_next = p_next + jnp.where(self.at_depth, moved, 0.0)
+                self.waves[turn][p_number, x, tile] = p_next
+                self.waves[turn][q_number, x, tile] = q_next
+
+
+def repeat(count, body):
+    def run(i, carry):
+        body(i)
+        return carry
+
+    lax.fori_loop(0, count, run, 0)
+
+
+def inner_kernel(wide, planes, *refs):
+    waves, factors, local = refs[:STEPS], refs[STEPS], refs[STEPS + 1 :]
+    steps = Steps(wide, planes, waves, factors, local)
+    cells_x = steps.cells_x
+
+    def factor_pair(i):
+        steps.make_factors(RIM + 2 * i)
+        steps.make_factors(RIM + 2 * i + 1)
+
+    repeat(cells_x // 2, factor_pair)
     for turn in range(STEPS):
-        first, last = turn + 1, span_x - 1 - turn
+        first, last = RIM + 1 + turn, RIM + cells_x - 1 - turn
         for x in range(first - 1, first + 3):
-            stores = []
-            plane_part(turn, x, stores)
-            write(stores)
-
-        def body(i, carry, turn=turn, first=first):
+            steps.plane_part(turn, x)
+
+        def pair(i, turn=turn, first=first):
             x = first + 2 * i
-            stores = []
-            next_part(turn, x, stores)
-            next_part(turn, x + 1, stores)
-            plane_part(turn, x + 3, stores)
-            plane_part(turn, x + 4, stores)
-            write(stores)
-            return carry
-
-        lax.fori_loop(0, (last - first) // 2, body, 0)
-
-    def finish(i, carry):
+            steps.next_part(turn, x)
+            steps.next_part(turn, x + 1)
+            steps.plane_part(turn, x + 3)
+            steps.plane_part(turn, x + 4)
+
+        repeat((last - first) // 2, pair)
+
+
+def outer_kernel(*refs):
+    x_a, x_b, c_a, c_b, planes = refs[1:6]
+    refs = refs[6 + 2 * STEPS + 1 :]
+    wide, waves, factors, local = refs[0], refs[1 : 1 + STEPS], refs[1 + STEPS], refs[2 + STEPS : -3]
+    image, p_last, q_last = refs[-3:]
+    cells_x, cells_y, depth = image.shape
+    odd_x = is_odd("gx")
+    for number, width, place in x_parts()[0]:
+        low, high = RIM - width, RIM + cells_x
+        for begin, side, corner in (
+            (jnp.where(odd_x, low, high), x_a, c_a),
+            (jnp.where(odd_x, high, low), x_b, c_b),
+        ):
+            wide[number, pl.ds(begin, width), :cells_y, :] = side[place : place + width]
+            wide[number, pl.ds(begin, width), cells_y:, :] = corner[place : place + width]
+
+    steps = Steps(wide, planes, waves, factors, local)
+
+    def factor_pair(i):
+        steps.make_factors(RIM - SLIM + i)
+        steps.make_factors(RIM + cells_x + i)
+
+    repeat(SLIM, factor_pair)
+    for turn in range(STEPS):
+
+        def parts(i, turn=turn):
+            steps.plane_part(turn, turn + i)
+            steps.plane_part(turn, RIM + cells_x - turn + i)
+
+        def nexts(i, turn=turn):
+            steps.next_part(turn, turn + 1 + i)
+            steps.next_part(turn, RIM + cells_x - 1 - turn + i)
+
+        repeat(RIM, parts)
+        repeat(RIM, nexts)
+
+    tiles = steps.tiles
+
+    def finish(i):
         x = RIM + i
         total = None
         for back in range(STEPS + 1):
-            source = wave_tiles(0, 1 + STEPS - back, x)
-            receiver = wave_tiles(2, 1 + back, x)
+            source = steps.wave_tiles(0, 1 + STEPS - back, x)
+            receiver = steps.wave_tiles(2, 1 + back, x)
             product = [a * b for a, b in zip(source, receiver)]
             total = product if total is None else [a + b for a, b in zip(total, product)]
         for out, value in (
             (0, total),
-            (1, wave_tiles(2, 1 + STEPS, x)),
-            (2, wave_tiles(3, 1 + STEPS, x)),
+            (1, steps.wave_tiles(2, 1 + STEPS, x)),
+            (2, steps.wave_tiles(3, 1 + STEPS, x)),
         ):
             for tile in range(tiles):
                 wide[out, x, pl.ds(tile, SUBLANES, stride=tiles), :] = value[tile]
-        return carry
-
-    lax.fori_loop(0, cells_x, finish, 0)
+
+    repeat(cells_x, finish)
     for out, ref in enumerate((image, p_last, q_last)):
         ref[...] = wide[out, RIM : RIM + cells_x, :cells_y, :]
 
 
-def migrate(wide, rims, planes, cells_x, cells_y):
-    count, planes_x, rows, depth = wide.shape
-    tile = (rows // SUBLANES, SUBLANES, depth)
-    out = jax.ShapeDtypeStruct((cells_x, cells_y, depth), jnp.float32)
+def inner(wide, planes):
+    _, planes_x, rows, depth = wide.shape
+    tile = (planes_x, rows // SUBLANES, SUBLANES, depth)
     return pl.pallas_call(
-        main_kernel,
-        out_shape=[vmem_out(*wide.shape)] + [out] * 3,
-        in_specs=in_vmem(len(rims) + 2),
-        out_specs=in_vmem(4),
-        input_output_aliases={0: 0},
-        scratch_shapes=[
-            pltpu.VMEM((4, STEPS, planes_x) + tile, jnp.float32),
-            pltpu.VMEM((9, planes_x) + tile, jnp.float32),
-            pltpu.VMEM((4, 4, planes_x) + tile, jnp.float32),
-        ],
+        inner_kernel,
+        out_shape=[vmem_out(4, *tile)] * STEPS
+        + [vmem_out(9, *tile)]
+        + [vmem_out(4, 4, *tile)] * STEPS,
+        in_specs=in_vmem(2),
+        out_specs=in_vmem(2 * STEPS + 1),
         compiler_params=PARAMS,
-        name="migrate",
-    )(pinned(wide, pltpu.VMEM), *rims, planes)[1:]
+        name="inner_steps",
+    )(pinned(wide, pltpu.VMEM), planes)
+
+
+def outer(wide, rims, planes, state, cells_x, cells_y):
+    out = jax.ShapeDtypeStruct((cells_x, cells_y, wide.shape[-1]), jnp.float32)
+    kept = [vmem_out(*wide.shape)] + [vmem_out(*value.shape) for value in state]
+    first = len(rims) + 2
+    aliases = {0: 0} | {first + number: 1 + number for number in range(len(state))}
+    return pl.pallas_call(
+        outer_kernel,
+        out_shape=kept + [out] * 3,
+        in_specs=in_vmem(first + len(state)),
+        out_specs=in_vmem(len(kept) + 3),
+        input_output_aliases=aliases,
+        compiler_params=PARAMS,
+        name="outer_steps",
+    )(
+        pinned(wide, pltpu.VMEM),
+        *rims,
+        planes,
+        *(pinned(value, pltpu.VMEM) for value in state),
+    )[-3:]
 
 
 def bits_of(axis):
@@ -546,7 +598,8 @@
     planes = injected(
         windows, receiver_x, receiver_y, traces.shape[1], cells_x, cells_y, depth
     )
-    return tuple(migrate(wide, (x_a, x_b, c_a, c_b), planes, cells_x, cells_y))
+    state = inner(wide, planes)
+    return tuple(outer(wide, (x_a, x_b, c_a, c_b), planes, state, cells_x, cells_y))
 
 
 def solution(mesh):

time: 33.8 us -> 31.6 us (0.935)
  waiting for transfers between devices: 4.23 us -> 1.05 us
  Pallas kernels: 10.7 us -> 11.7 us
    ppermute x6, waiting for transfers between devices: 3.19 us -> 0.02 us  [swap(): return lax.ppermute(value, axis, pairs)]
    pallas_call x1 -> x2, Pallas kernels: 8.14 us -> 9.14 us  [the longest x1 4.58 us: outer(): pl.pallas_call(outer_kernel, out_shape=kept + [out] * 3, in_specs=in_vmem...]
  transfers between devices with their start and end apart: 9 -> 9, of which waited for: 2 -> 1; matrix products, arithmetic and copies ran while one was open for 0% -> 0% of each run, Pallas kernels for 2% -> 17%
where the time goes in v7:
time: 31.6 us; the launch traced here: 31.4 us
  starting transfers between devices  17.1 us (54%)
  Pallas kernels  11.7 us (37%)
  between operations  1.46 us (5%)
  waiting for transfers between devices  1.05 us (3%)
    ppermute x6, starting transfers between devices, swap(): return lax.ppermute(value, axis, pairs)  10.3 us
    ppermute x3, starting transfers between devices, doubled(): lax.ppermute(windows, axis, pairs)  6.79 us
    pallas_call x1, Pallas kernels, outer(): pl.pallas_call(outer_kernel, out_shape=kept + [out] * 3, in_specs=in_vmem...  4.58 us
    pallas_call x1, Pallas kernels, inner(): pl.pallas_call(inner_kernel, out_shape=[vmem_out(4, *tile)] * STEPS + [vm...  4.57 us
    pallas_call x1, Pallas kernels, pack(): pl.pallas_call(functools.partial(pack_kernel, count), out_shape=[wide, ri...  1.8 us
    ppermute x3, waiting for transfers between devices, doubled(): lax.ppermute(windows, axis, pairs)  1.04 us
  transfers between devices with their start and end apart: 9, of which 1 were waited for; matrix products, arithmetic and copies ran while one was open for 0% of the time, Pallas kernels for 17%

profile of v7, /device:TPU:1, one launch (start us, length us, event | category | flops | bytes accessed | tf_op | source)
XLA Modules:
  0.0 31.4 jit_solution(3008199520145753062)
XLA Ops:
  1.3 1.8 %pack_y_rims.1 = (f32[13,26,24,128]{3,2,1,0:T(8,128)S(1)}, f32[11,16,4,128]{3,2,1,0:T(4,128)S(1)}, f32[11,16,4,128]{3,2,1,0:T(4,128)S(1)}, f32[1,4,128]{2,1,0:T(4,128)S(1)}) custom-call(f32[16,16,128]{2,1,0:T(8,128)} %refs_0_.1, f32[16,16,128]{2,1,0:T(8,128)} %refs_1_.1, f32[16,16,128]{2,1,0:T(8,128)} %refs_2_.1, f32[16,16,128]{2,1,0:T(8,128)} %refs_3_.1, ...), custom_call_target="tpu_custom_call" | custom-call | tf_op jit(solution)/shard_map/pack_y_rims/pallas_call | solution.py:123
  3.1 0.0 copy-start
  3.1 0.0 copy-start.1
  3.1 0.1 pack_x_rims.1
  3.2 0.1 collective-permute-start.2
  3.3 2.8 %collective-permute-start = (f32[11,16,4,128]{3,2,1,0:T(4,128)S(1)}, f32[11,16,4,128]{3,2,1,0:T(4,128)S(1)}, u32[]{:S(2)}, u32[]{:S(2)}) collective-permute-start(f32[11,16,4,128]{3,2,1,0:T(4,128)S(1)} %get-tuple-element.28), channel_id=1, source_target_pairs={{0,1},{2,3},{1,0},{3,2},{4,5},{6,7},{5,4},{7,6},{8,9},{10,11},{9,8... | collective-permute-start | bytes 1081352 | tf_op jit(solution)/shard_map/ppermute | solution.py:32
  6.1 0.7 %collective-permute-start.1 = (f32[11,16,4,128]{3,2,1,0:T(4,128)S(1)}, f32[11,16,4,128]{3,2,1,0:T(4,128)S(1)}, u32[]{:S(2)}, u32[]{:S(2)}) collective-permute-start(f32[11,16,4,128]{3,2,1,0:T(4,128)S(1)} %get-tuple-element.29), channel_id=1, source_target_pairs={{1,2},{2,1},{5,6},{6,5},{9,10},{10,9},{13,14},{14,13},{17,18},{18,... | collective-permute-start | bytes 1081352 | tf_op jit(solution)/shard_map/ppermute | solution.py:32
  6.8 0.0 collective-permute-done.2.refs_1_
  6.8 1.3 %collective-permute-start.3 = (f32[2,4,128]{2,1,0:T(4,128)S(1)}, f32[2,4,128]{2,1,0:T(4,128)S(1)}, u32[]{:S(2)}, u32[]{:S(2)}) collective-permute-start(f32[2,4,128]{2,1,0:T(4,128)S(1)} %pad_maximum_fusion.2), channel_id=1, source_target_pairs={{0,8},{4,12},{8,0},{12,4},{1,9},{5,13},{9,1},{13,5},{2,10},{6,14},... | collective-permute-start | bytes 12296 | tf_op jit(solution)/shard_map/ppermute | solution.py:466
  8.1 2.7 %collective-permute-start.5 = (f32[43,16,128]{2,1,0:T(8,128)S(1)}, f32[43,16,128]{2,1,0:T(8,128)S(1)}, u32[]{:S(2)}, u32[]{:S(2)}) collective-permute-start(f32[43,16,128]{2,1,0:T(8,128)S(1)} %get-tuple-element.32), channel_id=1, source_target_pairs={{4,8},{8,4},{5,9},{9,5},{6,10},{10,6},{7,11},{11,7},{20,24},{24,20... | collective-permute-start | bytes 1056776 | tf_op jit(solution)/shard_map/ppermute | solution.py:32
  10.7 0.0 collective-permute-done.3
  10.8 4.2 %collective-permute-start.4 = (f32[4,4,128]{2,1,0:T(4,128)S(1)}, f32[4,4,128]{2,1,0:T(4,128)S(1)}, u32[]{:S(2)}, u32[]{:S(2)}) collective-permute-start(f32[4,4,128]{2,1,0:T(4,128)S(1)} %pad_maximum_fusion.1), channel_id=1, source_target_pairs={{0,1},{1,0},{2,3},{3,2},{4,5},{5,4},{6,7},{7,6},{8,9},{9,8},{10,11... | collective-permute-start | bytes 24584 | tf_op jit(solution)/shard_map/ppermute | solution.py:466
  14.9 1.0 %collective-permute-done.4 = f32[4,4,128]{2,1,0:T(4,128)S(1)} collective-permute-done((f32[4,4,128]{2,1,0:T(4,128)S(1)}, f32[4,4,128]{2,1,0:T(4,128)S(1)}, u32[]{:S(2)}, u32[]{:S(2)}) %collective-permute-start.4) | collective-permute-done | bytes 8224 | tf_op jit(solution)/shard_map/ppermute | solution.py:466
  16.0 1.4 %collective-permute-start.8 = (f32[8,4,128]{2,1,0:T(4,128)S(1)}, f32[8,4,128]{2,1,0:T(4,128)S(1)}, u32[]{:S(2)}, u32[]{:S(2)}) collective-permute-start(f32[8,4,128]{2,1,0:T(4,128)S(1)} %pad_maximum_fusion.__), channel_id=1, source_target_pairs={{0,2},{1,3},{2,0},{3,1},{4,6},{5,7},{6,4},{7,5},{8,10},{9,11},{10,... | collective-permute-start | bytes 49160 | tf_op jit(solution)/shard_map/ppermute | solution.py:466
  17.3 0.0 collective-permute-done.y_a
  17.3 0.0 collective-permute-done.1.y_b
  17.3 0.2 pack_corners.1
  17.6 1.1 %collective-permute-start.6 = (f32[43,8,128]{2,1,0:T(8,128)S(1)}, f32[43,8,128]{2,1,0:T(8,128)S(1)}, u32[]{:S(2)}, u32[]{:S(2)}) collective-permute-start(f32[43,8,128]{2,1,0:T(8,128)S(1)} %get-tuple-element.33), channel_id=1, source_target_pairs={{0,4},{8,12},{4,0},{12,8},{1,5},{9,13},{5,1},{13,9},{2,6},{10,14},... | collective-permute-start | bytes 528392 | tf_op jit(solution)/shard_map/ppermute | solution.py:32
  18.7 3.0 %collective-permute-start.7 = (f32[43,8,128]{2,1,0:T(8,128)S(1)}, f32[43,8,128]{2,1,0:T(8,128)S(1)}, u32[]{:S(2)}, u32[]{:S(2)}) collective-permute-start(f32[43,8,128]{2,1,0:T(8,128)S(1)} %get-tuple-element.34), channel_id=1, source_target_pairs={{4,8},{8,4},{5,9},{9,5},{6,10},{10,6},{7,11},{11,7},{20,24},{24,20... | collective-permute-start | bytes 528392 | tf_op jit(solution)/shard_map/ppermute | solution.py:32
  21.7 0.0 collective-permute-done.8
  21.7 0.0 copy-done
  21.7 0.0 copy-done.1
  21.8 0.5 %inject.1.planes.refs_5_ = f32[4,3,8,128]{3,2,1,0:T(8,128)S(1)} custom-call(f32[16,4,128]{2,1,0:T(4,128)S(1)} %constant_dynamic-update-slice_fusion.gathered, s32[8,128]{1,0:T(8,128)S(1)} %bitcast.2, s32[8,128]{1,0:T(8,128)S(1)} %bitcast.3), custom_call_target="tpu_custom_call" | custom-call | tf_op jit(solution)/shard_map/inject/pallas_call | solution.py:536
  22.2 4.6 %inner_steps.1 = (f32[4,26,3,8,128]{4,3,2,1,0:T(8,128)S(1)}, f32[4,26,3,8,128]{4,3,2,1,0:T(8,128)S(1)}, f32[4,26,3,8,128]{4,3,2,1,0:T(8,128)S(1)}, f32[4,26,3,8,...) custom-call(f32[13,26,24,128]{3,2,1,0:T(8,128)S(1)} %get-tuple-eleme, ...), custom_call_target="tpu_custom_call" | custom-call | tf_op jit(solution)/shard_map/inner_steps/pallas_call | solution.py:426
  26.8 0.0 collective-permute-done.5.refs_2_
  26.8 0.0 collective-permute-done.6.refs_3_
  26.8 0.0 collective-permute-done.7.refs_4_
  26.8 4.6 %outer_steps.1 = (f32[13,26,24,128]{3,2,1,0:T(8,128)S(1)}, f32[4,26,3,8,128]{4,3,2,1,0:T(8,128)S(1)}, f32[4,26,3,8,128]{4,3,2,1,0:T(8,128)S(1)}, f32[4,26,3,8,12...) custom-call(f32[13,26,24,128]{3,2,1,0:T(8,128)S(1)} %get-tuple-eleme, ...), custom_call_target="tpu_custom_call", output_to_operand_aliasing={{0}: (0, {}), {1}: (6, {}), {2}: (7, {}), {3}: (8, {}), {4}... | custom-call | tf_op jit(solution)/shard_map/outer_steps/pallas_call | solution.py:443
  (8 shorter events, 0.1 us)
Async XLA Ops:
  3.1 18.6 %copy-start = (s32[1024]{0:T(1024)S(1)}, s32[1024]{0:T(1024)}, u32[]{:S(2)}) copy-start(s32[1024]{0:T(1024)} %param.31) | copy-start | bytes 12292
  3.1 18.6 %copy-start.1 = (s32[1024]{0:T(1024)S(1)}, s32[1024]{0:T(1024)}, u32[]{:S(2)}) copy-start(s32[1024]{0:T(1024)} %param.32) | copy-start | bytes 12292
  3.2 3.6 %collective-permute-start.2 = (f32[44,16,128]{2,1,0:T(8,128)S(1)}, f32[44,16,128]{2,1,0:T(8,128)S(1)}, u32[]{:S(2)}, u32[]{:S(2)}) collective-permute-start(f32[44,16,128]{2,1,0:T(8,128)S(1)} %get-tuple-element.30), channel_id=1, source_target_pairs={{0,4},{8,12},{4,0},{12,8},{1,5},{9,13},{5,1},{13,9},{2,6},{10,14},... | collective-permute-start | bytes 1081352 | tf_op jit(solution)/shard_map/ppermute | solution.py:32
  3.3 14.0 %collective-permute-start = (f32[11,16,4,128]{3,2,1,0:T(4,128)S(1)}, f32[11,16,4,128]{3,2,1,0:T(4,128)S(1)}, u32[]{:S(2)}, u32[]{:S(2)}) collective-permute-start(f32[11,16,4,128]{3,2,1,0:T(4,128)S(1)} %get-tuple-element.28), channel_id=1, source_target_pairs={{0,1},{2,3},{1,0},{3,2},{4,5},{6,7},{5,4},{7,6},{8,9},{10,11},{9,8... | collective-permute-start | bytes 1081352 | tf_op jit(solution)/shard_map/ppermute | solution.py:32
  6.1 11.3 %collective-permute-start.1 = (f32[11,16,4,128]{3,2,1,0:T(4,128)S(1)}, f32[11,16,4,128]{3,2,1,0:T(4,128)S(1)}, u32[]{:S(2)}, u32[]{:S(2)}) collective-permute-start(f32[11,16,4,128]{3,2,1,0:T(4,128)S(1)} %get-tuple-element.29), channel_id=1, source_target_pairs={{1,2},{2,1},{5,6},{6,5},{9,10},{10,9},{13,14},{14,13},{17,18},{18,... | collective-permute-start | bytes 1081352 | tf_op jit(solution)/shard_map/ppermute | solution.py:32
  6.8 3.9 %collective-permute-start.3 = (f32[2,4,128]{2,1,0:T(4,128)S(1)}, f32[2,4,128]{2,1,0:T(4,128)S(1)}, u32[]{:S(2)}, u32[]{:S(2)}) collective-permute-start(f32[2,4,128]{2,1,0:T(4,128)S(1)} %pad_maximum_fusion.2), channel_id=1, source_target_pairs={{0,8},{4,12},{8,0},{12,4},{1,9},{5,13},{9,1},{13,5},{2,10},{6,14},... | collective-permute-start | bytes 12296 | tf_op jit(solution)/shard_map/ppermute | solution.py:466
  8.1 18.7 %collective-permute-start.5 = (f32[43,16,128]{2,1,0:T(8,128)S(1)}, f32[43,16,128]{2,1,0:T(8,128)S(1)}, u32[]{:S(2)}, u32[]{:S(2)}) collective-permute-start(f32[43,16,128]{2,1,0:T(8,128)S(1)} %get-tuple-element.32), channel_id=1, source_target_pairs={{4,8},{8,4},{5,9},{9,5},{6,10},{10,6},{7,11},{11,7},{20,24},{24,20... | collective-permute-start | bytes 1056776 | tf_op jit(solution)/shard_map/ppermute | solution.py:32
  10.8 5.2 %collective-permute-start.4 = (f32[4,4,128]{2,1,0:T(4,128)S(1)}, f32[4,4,128]{2,1,0:T(4,128)S(1)}, u32[]{:S(2)}, u32[]{:S(2)}) collective-permute-start(f32[4,4,128]{2,1,0:T(4,128)S(1)} %pad_maximum_fusion.1), channel_id=1, source_target_pairs={{0,1},{1,0},{2,3},{3,2},{4,5},{5,4},{6,7},{7,6},{8,9},{9,8},{10,11... | collective-permute-start | bytes 24584 | tf_op jit(solution)/shard_map/ppermute | solution.py:466
  16.0 5.7 %collective-permute-start.8 = (f32[8,4,128]{2,1,0:T(4,128)S(1)}, f32[8,4,128]{2,1,0:T(4,128)S(1)}, u32[]{:S(2)}, u32[]{:S(2)}) collective-permute-start(f32[8,4,128]{2,1,0:T(4,128)S(1)} %pad_maximum_fusion.__), channel_id=1, source_target_pairs={{0,2},{1,3},{2,0},{3,1},{4,6},{5,7},{6,4},{7,5},{8,10},{9,11},{10,... | collective-permute-start | bytes 49160 | tf_op jit(solution)/shard_map/ppermute | solution.py:466
  17.6 9.2 %collective-permute-start.6 = (f32[43,8,128]{2,1,0:T(8,128)S(1)}, f32[43,8,128]{2,1,0:T(8,128)S(1)}, u32[]{:S(2)}, u32[]{:S(2)}) collective-permute-start(f32[43,8,128]{2,1,0:T(8,128)S(1)} %get-tuple-element.33), channel_id=1, source_target_pairs={{0,4},{8,12},{4,0},{12,8},{1,5},{9,13},{5,1},{13,9},{2,6},{10,14},... | collective-permute-start | bytes 528392 | tf_op jit(solution)/shard_map/ppermute | solution.py:32
  18.7 8.2 %collective-permute-start.7 = (f32[43,8,128]{2,1,0:T(8,128)S(1)}, f32[43,8,128]{2,1,0:T(8,128)S(1)}, u32[]{:S(2)}, u32[]{:S(2)}) collective-permute-start(f32[43,8,128]{2,1,0:T(8,128)S(1)} %get-tuple-element.34), channel_id=1, source_target_pairs={{4,8},{8,4},{5,9},{9,5},{6,10},{10,6},{7,11},{11,7},{20,24},{24,20... | collective-permute-start | bytes 528392 | tf_op jit(solution)/shard_map/ppermute | solution.py:32

commit v8 on v7

--- a/solution.py
+++ b/solution.py
@@ -216,8 +216,8 @@
 
 
 class Steps:
-    def __init__(self, wide, planes, waves, factors, local):
-        self.wide, self.planes, self.waves, self.factors, self.local = wide, planes, waves, factors, local
+    def __init__(self, wide, planes, waves, factors):
+        self.wide, self.planes, self.waves, self.factors = wide, planes, waves, factors
         self.count, _, rows, self.depth = wide.shape
         self.tiles = rows // SUBLANES
         self.cells_x = wide.shape[1] - 2 * RIM - 2
@@ -269,63 +269,64 @@
             for number, value in enumerate(values):
                 self.factors[number, x, tile] = value
 
-    def plane_part(self, turn, x):
-        factors, local, tiles = self.factors, self.local[turn], self.tiles
-        ayy = [factors[4, x, tile] for tile in range(tiles)]
-        azz = [factors[5, x, tile] for tile in range(tiles)]
-        ayz = [factors[8, x, tile] for tile in range(tiles)]
-        for number in range(4):
-            now = self.wave_tiles(number, turn + 1, x)
-            above = [jnp.where(self.not_last, pltpu.roll(u, self.depth - 1, 1), 0.0) for u in now]
-            below = [jnp.where(self.not_first, pltpu.roll(u, 1, 1), 0.0) for u in now]
-            slope_z = [a - b for a, b in zip(above, below)]
-            after, before = self.next_y(now), self.previous_y(now)
-            slope_after, slope_before = self.next_y(slope_z), self.previous_y(slope_z)
-            for tile in range(tiles):
-                double = now[tile] + now[tile]
-                sum_y = after[tile] + before[tile]
-                sum_z = above[tile] + below[tile]
-                local[number, 0, x, tile] = (
-                    (ayy[tile] * sum_y + azz[tile] * sum_z)
-                    + ayz[tile] * (slope_after[tile] - slope_before[tile])
-                ) - double
-                local[number, 1, x, tile] = after[tile] - before[tile]
-                local[number, 2, x, tile] = slope_z[tile]
-                if number % 2 == 0:
-                    local[number, 3, x, tile] = (sum_y + sum_z) - 3.0 * double
-
-    def next_part(self, turn, x):
-        factors, local = self.factors, self.local[turn]
-        held = [self.wave_tiles(number, turn, x) for number in range(4)]
-        now = [self.wave_tiles(number, turn + 1, x) for number in range(4)]
-        after = [self.wave_tiles(number, turn + 1, x + 1) for number in range(4)]
-        before = [self.wave_tiles(number, turn + 1, x - 1) for number in range(4)]
+    def sides_z(self, value):
+        above = [jnp.where(self.not_last, pltpu.roll(u, self.depth - 1, 1), 0.0) for u in value]
+        below = [jnp.where(self.not_first, pltpu.roll(u, 1, 1), 0.0) for u in value]
+        return above, below
+
+    def stencil(self, factors, before, now, after, full):
+        slope_x = [a - b for a, b in zip(after, before)]
+        above, below = self.sides_z(now)
+        slope_z = [a - b for a, b in zip(above, below)]
+        next_now, previous_now = self.next_y(now), self.previous_y(now)
+        above_x, below_x = self.sides_z(slope_x)
+        next_x, previous_x = self.next_y(slope_x), self.previous_y(slope_x)
+        next_z, previous_z = self.next_y(slope_z), self.previous_y(slope_z)
+        axis, laplace = [], []
         for tile in range(self.tiles):
-            velocity, with_e, with_d = [factors[number, x, tile] for number in range(3)]
-            axx, axy, axz = [factors[number, x, tile] for number in (3, 6, 7)]
-            for pair in range(2):
-                sums, axis = [], []
-                for number in (2 * pair, 2 * pair + 1):
-                    sum_x = after[number][tile] + before[number][tile]
-                    d_xy = local[number, 1, x + 1, tile] - local[number, 1, x - 1, tile]
-                    d_xz = local[number, 2, x + 1, tile] - local[number, 2, x - 1, tile]
-                    sums.append(sum_x)
-                    axis.append((local[number, 0, x, tile] + axx * sum_x) + (axy * d_xy + axz * d_xz))
-                p_number, q_number = 2 * pair, 2 * pair + 1
-                across = (sums[0] + local[p_number, 3, x, tile]) - axis[0]
-                p_now, q_now = now[p_number][tile], now[q_number][tile]
-                p_next = ((p_now + p_now) - held[p_number][tile]) + (
-                    with_e * across + with_d * axis[1]
-                )
-                q_next = ((q_now + q_now) - held[q_number][tile]) + (
-                    with_d * across + velocity * axis[1]
-                )
-                if pair == 1:
-                    shift = lax.rem(REC_DEPTH - x + self.depth, self.depth)
-                    moved = pltpu.roll(self.planes[STEPS - 1 - turn, tile], shift, 1)
-                    p_next = p_next + jnp.where(self.at_depth, moved, 0.0)
-                self.waves[turn][p_number, x, tile] = p_next
-                self.waves[turn][q_number, x, tile] = q_next
+            axx, ayy, azz, axy, axz, ayz = [value[tile] for value in factors]
+            double = now[tile] + now[tile]
+            sum_x = after[tile] + before[tile]
+            sum_y = next_now[tile] + previous_now[tile]
+            sum_z = above[tile] + below[tile]
+            straight = ((axx * sum_x + ayy * sum_y) + azz * sum_z) - double
+            mixed = (
+                axy * (next_x[tile] - previous_x[tile]) + axz * (above_x[tile] - below_x[tile])
+            ) + ayz * (next_z[tile] - previous_z[tile])
+            axis.append(straight + mixed)
+            if full:
+                laplace.append(((sum_x + sum_y) + sum_z) - 3.0 * double)
+        return axis, laplace
+
+    def step(self, turn, x, count):
+        tiles, factors = range(self.tiles), self.factors
+        for pair in range(2):
+            p_number, q_number = 2 * pair, 2 * pair + 1
+            p = [self.wave_tiles(p_number, turn + 1, x - 1 + i) for i in range(count + 2)]
+            q = [self.wave_tiles(q_number, turn + 1, x - 1 + i) for i in range(count + 2)]
+            for i in range(count):
+                now = x + i
+                mixing = [[factors[number, now, tile] for tile in tiles] for number in range(3, 9)]
+                p_axis, p_laplace = self.stencil(mixing, p[i], p[i + 1], p[i + 2], True)
+                q_axis, _ = self.stencil(mixing, q[i], q[i + 1], q[i + 2], False)
+                p_held = self.wave_tiles(p_number, turn, now)
+                q_held = self.wave_tiles(q_number, turn, now)
+                for tile in tiles:
+                    velocity, with_e, with_d = [factors[number, now, tile] for number in range(3)]
+                    across = p_laplace[tile] - p_axis[tile]
+                    p_now, q_now = p[i + 1][tile], q[i + 1][tile]
+                    p_next = ((p_now + p_now) - p_held[tile]) + (
+                        with_e * across + with_d * q_axis[tile]
+                    )
+                    q_next = ((q_now + q_now) - q_held[tile]) + (
+                        with_d * across + velocity * q_axis[tile]
+                    )
+                    if pair == 1:
+                        shift = lax.rem(REC_DEPTH - now + self.depth, self.depth)
+                        moved = pltpu.roll(self.planes[STEPS - 1 - turn, tile], shift, 1)
+                        p_next = p_next + jnp.where(self.at_depth, moved, 0.0)
+                    self.waves[turn][p_number, now, tile] = p_next
+                    self.waves[turn][q_number, now, tile] = q_next
 
 
 def repeat(count, body):
@@ -337,8 +338,7 @@
 
 
 def inner_kernel(wide, planes, *refs):
-    waves, factors, local = refs[:STEPS], refs[STEPS], refs[STEPS + 1 :]
-    steps = Steps(wide, planes, waves, factors, local)
+    steps = Steps(wide, planes, refs[:STEPS], refs[STEPS])
     cells_x = steps.cells_x
 
     def factor_pair(i):
@@ -348,23 +348,13 @@
     repeat(cells_x // 2, factor_pair)
     for turn in range(STEPS):
         first, last = RIM + 1 + turn, RIM + cells_x - 1 - turn
-        for x in range(first - 1, first + 3):
-            steps.plane_part(turn, x)
-
-        def pair(i, turn=turn, first=first):
-            x = first + 2 * i
-            steps.next_part(turn, x)
-            steps.next_part(turn, x + 1)
-            steps.plane_part(turn, x + 3)
-            steps.plane_part(turn, x + 4)
-
-        repeat((last - first) // 2, pair)
+        repeat((last - first) // 2, lambda i, turn=turn, first=first: steps.step(turn, first + 2 * i, 2))
 
 
 def outer_kernel(*refs):
     x_a, x_b, c_a, c_b, planes = refs[1:6]
-    refs = refs[6 + 2 * STEPS + 1 :]
-    wide, waves, factors, local = refs[0], refs[1 : 1 + STEPS], refs[1 + STEPS], refs[2 + STEPS : -3]
+    refs = refs[6 + STEPS + 1 :]
+    wide, waves, factors = refs[0], refs[1 : 1 + STEPS], refs[1 + STEPS]
     image, p_last, q_last = refs[-3:]
     cells_x, cells_y, depth = image.shape
     odd_x = is_odd("gx")
@@ -377,7 +367,7 @@
             wide[number, pl.ds(begin, width), :cells_y, :] = side[place : place + width]
             wide[number, pl.ds(begin, width), cells_y:, :] = corner[place : place + width]
 
-    steps = Steps(wide, planes, waves, factors, local)
+    steps = Steps(wide, planes, waves, factors)
 
     def factor_pair(i):
         steps.make_factors(RIM - SLIM + i)
@@ -386,16 +376,11 @@
     repeat(SLIM, factor_pair)
     for turn in range(STEPS):
 
-        def parts(i, turn=turn):
-            steps.plane_part(turn, turn + i)
-            steps.plane_part(turn, RIM + cells_x - turn + i)
-
-        def nexts(i, turn=turn):
-            steps.next_part(turn, turn + 1 + i)
-            steps.next_part(turn, RIM + cells_x - 1 - turn + i)
-
-        repeat(RIM, parts)
-        repeat(RIM, nexts)
+        def both(i, turn=turn):
+            steps.step(turn, turn + 1 + 2 * i, 2)
+            steps.step(turn, RIM + cells_x - 1 - turn + 2 * i, 2)
+
+        repeat(RIM // 2, both)
 
     tiles = steps.tiles
 
@@ -425,11 +410,9 @@
     tile = (planes_x, rows // SUBLANES, SUBLANES, depth)
     return pl.pallas_call(
         inner_kernel,
-        out_shape=[vmem_out(4, *tile)] * STEPS
-        + [vmem_out(9, *tile)]
-        + [vmem_out(4, 4, *tile)] * STEPS,
+        out_shape=[vmem_out(4, *tile)] * STEPS + [vmem_out(9, *tile)],
         in_specs=in_vmem(2),
-        out_specs=in_vmem(2 * STEPS + 1),
+        out_specs=in_vmem(STEPS + 1),
         compiler_params=PARAMS,
         name="inner_steps",
     )(pinned(wide, pltpu.VMEM), planes)

time: 31.6 us -> 30.9 us (0.978)
  Pallas kernels: 11.7 us -> 10.9 us
    pallas_call x1, Pallas kernels: 4.58 us -> 3.74 us  [outer(): pl.pallas_call(outer_kernel, out_shape=kept + [out] * 3, in_specs=in_vmem...]
where the time goes in v8:
time: 30.9 us; the launch traced here: 30.6 us
  starting transfers between devices  17.1 us (55%)
  Pallas kernels  10.9 us (35%)
  between operations  1.46 us (5%)
  waiting for transfers between devices  1.05 us (3%)
    ppermute x6, starting transfers between devices, swap(): return lax.ppermute(value, axis, pairs)  10.3 us
    ppermute x3, starting transfers between devices, doubled(): lax.ppermute(windows, axis, pairs)  6.79 us
    pallas_call x1, Pallas kernels, inner(): pl.pallas_call(inner_kernel, out_shape=[vmem_out(4, *tile)] * STEPS + [vm...  4.63 us
    pallas_call x1, Pallas kernels, outer(): pl.pallas_call(outer_kernel, out_shape=kept + [out] * 3, in_specs=in_vmem...  3.74 us
    pallas_call x1, Pallas kernels, pack(): pl.pallas_call(functools.partial(pack_kernel, count), out_shape=[wide, ri...  1.8 us
    ppermute x3, waiting for transfers between devices, doubled(): lax.ppermute(windows, axis, pairs)  1.04 us
  transfers between devices with their start and end apart: 9, of which 1 were waited for; matrix products, arithmetic and copies ran while one was open for 0% of the time, Pallas kernels for 17%

profile of v8, /device:TPU:1, one launch (start us, length us, event | category | flops | bytes accessed | tf_op | source)
XLA Modules:
  0.0 30.6 jit_solution(5202607784988893242)
XLA Ops:
  1.3 1.8 %pack_y_rims.1 = (f32[13,26,24,128]{3,2,1,0:T(8,128)S(1)}, f32[11,16,4,128]{3,2,1,0:T(4,128)S(1)}, f32[11,16,4,128]{3,2,1,0:T(4,128)S(1)}, f32[1,4,128]{2,1,0:T(4,128)S(1)}) custom-call(f32[16,16,128]{2,1,0:T(8,128)} %refs_0_.1, f32[16,16,128]{2,1,0:T(8,128)} %refs_1_.1, f32[16,16,128]{2,1,0:T(8,128)} %refs_2_.1, f32[16,16,128]{2,1,0:T(8,128)} %refs_3_.1, ...), custom_call_target="tpu_custom_call" | custom-call | tf_op jit(solution)/shard_map/pack_y_rims/pallas_call | solution.py:123
  3.1 0.1 pack_x_rims.1
  3.2 0.1 collective-permute-start.2
  3.3 2.8 %collective-permute-start = (f32[11,16,4,128]{3,2,1,0:T(4,128)S(1)}, f32[11,16,4,128]{3,2,1,0:T(4,128)S(1)}, u32[]{:S(2)}, u32[]{:S(2)}) collective-permute-start(f32[11,16,4,128]{3,2,1,0:T(4,128)S(1)} %get-tuple-element.24), channel_id=1, source_target_pairs={{0,1},{2,3},{1,0},{3,2},{4,5},{6,7},{5,4},{7,6},{8,9},{10,11},{9,8... | collective-permute-start | bytes 1081352 | tf_op jit(solution)/shard_map/ppermute | solution.py:32
  6.0 0.7 %collective-permute-start.1 = (f32[11,16,4,128]{3,2,1,0:T(4,128)S(1)}, f32[11,16,4,128]{3,2,1,0:T(4,128)S(1)}, u32[]{:S(2)}, u32[]{:S(2)}) collective-permute-start(f32[11,16,4,128]{3,2,1,0:T(4,128)S(1)} %get-tuple-element.25), channel_id=1, source_target_pairs={{1,2},{2,1},{5,6},{6,5},{9,10},{10,9},{13,14},{14,13},{17,18},{18,... | collective-permute-start | bytes 1081352 | tf_op jit(solution)/shard_map/ppermute | solution.py:32
  6.7 0.0 collective-permute-done.2.refs_1_
  6.8 1.3 %collective-permute-start.3 = (f32[2,4,128]{2,1,0:T(4,128)S(1)}, f32[2,4,128]{2,1,0:T(4,128)S(1)}, u32[]{:S(2)}, u32[]{:S(2)}) collective-permute-start(f32[2,4,128]{2,1,0:T(4,128)S(1)} %pad_maximum_fusion.2), channel_id=1, source_target_pairs={{0,8},{4,12},{8,0},{12,4},{1,9},{5,13},{9,1},{13,5},{2,10},{6,14},... | collective-permute-start | bytes 12296 | tf_op jit(solution)/shard_map/ppermute | solution.py:449
  8.0 2.7 %collective-permute-start.5 = (f32[43,16,128]{2,1,0:T(8,128)S(1)}, f32[43,16,128]{2,1,0:T(8,128)S(1)}, u32[]{:S(2)}, u32[]{:S(2)}) collective-permute-start(f32[43,16,128]{2,1,0:T(8,128)S(1)} %get-tuple-element.28), channel_id=1, source_target_pairs={{4,8},{8,4},{5,9},{9,5},{6,10},{10,6},{7,11},{11,7},{20,24},{24,20... | collective-permute-start | bytes 1056776 | tf_op jit(solution)/shard_map/ppermute | solution.py:32
  10.7 0.0 collective-permute-done.3
  10.7 4.2 %collective-permute-start.4 = (f32[4,4,128]{2,1,0:T(4,128)S(1)}, f32[4,4,128]{2,1,0:T(4,128)S(1)}, u32[]{:S(2)}, u32[]{:S(2)}) collective-permute-start(f32[4,4,128]{2,1,0:T(4,128)S(1)} %pad_maximum_fusion.1), channel_id=1, source_target_pairs={{0,1},{1,0},{2,3},{3,2},{4,5},{5,4},{6,7},{7,6},{8,9},{9,8},{10,11... | collective-permute-start | bytes 24584 | tf_op jit(solution)/shard_map/ppermute | solution.py:449
  14.9 1.0 %collective-permute-done.4 = f32[4,4,128]{2,1,0:T(4,128)S(1)} collective-permute-done((f32[4,4,128]{2,1,0:T(4,128)S(1)}, f32[4,4,128]{2,1,0:T(4,128)S(1)}, u32[]{:S(2)}, u32[]{:S(2)}) %collective-permute-start.4) | collective-permute-done | bytes 8224 | tf_op jit(solution)/shard_map/ppermute | solution.py:449
  16.0 1.4 %collective-permute-start.8 = (f32[8,4,128]{2,1,0:T(4,128)S(1)}, f32[8,4,128]{2,1,0:T(4,128)S(1)}, u32[]{:S(2)}, u32[]{:S(2)}) collective-permute-start(f32[8,4,128]{2,1,0:T(4,128)S(1)} %pad_maximum_fusion.__), channel_id=1, source_target_pairs={{0,2},{1,3},{2,0},{3,1},{4,6},{5,7},{6,4},{7,5},{8,10},{9,11},{10,... | collective-permute-start | bytes 49160 | tf_op jit(solution)/shard_map/ppermute | solution.py:449
  17.3 0.0 collective-permute-done.y_a
  17.3 0.0 collective-permute-done.1.y_b
  17.3 0.0 copy-start
  17.3 0.0 copy-start.1
  17.3 0.2 pack_corners.1
  17.6 1.1 %collective-permute-start.6 = (f32[43,8,128]{2,1,0:T(8,128)S(1)}, f32[43,8,128]{2,1,0:T(8,128)S(1)}, u32[]{:S(2)}, u32[]{:S(2)}) collective-permute-start(f32[43,8,128]{2,1,0:T(8,128)S(1)} %get-tuple-element.29), channel_id=1, source_target_pairs={{0,4},{8,12},{4,0},{12,8},{1,5},{9,13},{5,1},{13,9},{2,6},{10,14},... | collective-permute-start | bytes 528392 | tf_op jit(solution)/shard_map/ppermute | solution.py:32
  18.7 3.0 %collective-permute-start.7 = (f32[43,8,128]{2,1,0:T(8,128)S(1)}, f32[43,8,128]{2,1,0:T(8,128)S(1)}, u32[]{:S(2)}, u32[]{:S(2)}) collective-permute-start(f32[43,8,128]{2,1,0:T(8,128)S(1)} %get-tuple-element.30), channel_id=1, source_target_pairs={{4,8},{8,4},{5,9},{9,5},{6,10},{10,6},{7,11},{11,7},{20,24},{24,20... | collective-permute-start | bytes 528392 | tf_op jit(solution)/shard_map/ppermute | solution.py:32
  21.7 0.0 collective-permute-done.8
  21.7 0.0 copy-done
  21.8 0.0 copy-done.1
  21.8 0.5 %inject.1.planes.refs_5_ = f32[4,3,8,128]{3,2,1,0:T(8,128)S(1)} custom-call(f32[16,4,128]{2,1,0:T(4,128)S(1)} %constant_dynamic-update-slice_fusion.gathered, s32[8,128]{1,0:T(8,128)S(1)} %bitcast.2, s32[8,128]{1,0:T(8,128)S(1)} %bitcast.3), custom_call_target="tpu_custom_call" | custom-call | tf_op jit(solution)/shard_map/inject/pallas_call | solution.py:519
  22.2 4.6 %inner_steps.1 = (f32[4,26,3,8,128]{4,3,2,1,0:T(8,128)S(1)}, f32[4,26,3,8,128]{4,3,2,1,0:T(8,128)S(1)}, f32[4,26,3,8,128]{4,3,2,1,0:T(8,128)S(1)}, f32[4,26,3,8,...) custom-call(f32[13,26,24,128]{3,2,1,0:T(8,128)S(1)} %get-tuple-element.27.wide.refs_0_, ...), custom_call_target="tpu_custom_call" | custom-call | tf_op jit(solution)/shard_map/inner_steps/pallas_call | solution.py:411
  26.9 0.0 collective-permute-done.5.refs_2_
  26.9 0.0 collective-permute-done.6.refs_3_
  26.9 0.0 collective-permute-done.7.refs_4_
  26.9 3.7 %outer_steps.1 = (f32[13,26,24,128]{3,2,1,0:T(8,128)S(1)}, f32[4,26,3,8,128]{4,3,2,1,0:T(8,128)S(1)}, f32[4,26,3,8,128]{4,3,2,1,0:T(8,128)S(1)}, f32[4,26,3,8,12...) custom-call(f32[13,26,24,128]{3,2,1,0:T(8,128)S(1)} %get-tuple-eleme, ...), custom_call_target="tpu_custom_call", output_to_operand_aliasing={{0}: (0, {}), {1}: (6, {}), {2}: (7, {}), {3}: (8, {}), {4}... | custom-call | tf_op jit(solution)/shard_map/outer_steps/pallas_call | solution.py:426
  (8 shorter events, 0.1 us)
Async XLA Ops:
  3.2 3.6 %collective-permute-start.2 = (f32[44,16,128]{2,1,0:T(8,128)S(1)}, f32[44,16,128]{2,1,0:T(8,128)S(1)}, u32[]{:S(2)}, u32[]{:S(2)}) collective-permute-start(f32[44,16,128]{2,1,0:T(8,128)S(1)} %get-tuple-element.26), channel_id=1, source_target_pairs={{0,4},{8,12},{4,0},{12,8},{1,5},{9,13},{5,1},{13,9},{2,6},{10,14},... | collective-permute-start | bytes 1081352 | tf_op jit(solution)/shard_map/ppermute | solution.py:32
  3.3 14.0 %collective-permute-start = (f32[11,16,4,128]{3,2,1,0:T(4,128)S(1)}, f32[11,16,4,128]{3,2,1,0:T(4,128)S(1)}, u32[]{:S(2)}, u32[]{:S(2)}) collective-permute-start(f32[11,16,4,128]{3,2,1,0:T(4,128)S(1)} %get-tuple-element.24), channel_id=1, source_target_pairs={{0,1},{2,3},{1,0},{3,2},{4,5},{6,7},{5,4},{7,6},{8,9},{10,11},{9,8... | collective-permute-start | bytes 1081352 | tf_op jit(solution)/shard_map/ppermute | solution.py:32
  6.0 11.3 %collective-permute-start.1 = (f32[11,16,4,128]{3,2,1,0:T(4,128)S(1)}, f32[11,16,4,128]{3,2,1,0:T(4,128)S(1)}, u32[]{:S(2)}, u32[]{:S(2)}) collective-permute-start(f32[11,16,4,128]{3,2,1,0:T(4,128)S(1)} %get-tuple-element.25), channel_id=1, source_target_pairs={{1,2},{2,1},{5,6},{6,5},{9,10},{10,9},{13,14},{14,13},{17,18},{18,... | collective-permute-start | bytes 1081352 | tf_op jit(solution)/shard_map/ppermute | solution.py:32
  6.8 3.9 %collective-permute-start.3 = (f32[2,4,128]{2,1,0:T(4,128)S(1)}, f32[2,4,128]{2,1,0:T(4,128)S(1)}, u32[]{:S(2)}, u32[]{:S(2)}) collective-permute-start(f32[2,4,128]{2,1,0:T(4,128)S(1)} %pad_maximum_fusion.2), channel_id=1, source_target_pairs={{0,8},{4,12},{8,0},{12,4},{1,9},{5,13},{9,1},{13,5},{2,10},{6,14},... | collective-permute-start | bytes 12296 | tf_op jit(solution)/shard_map/ppermute | solution.py:449
  8.0 18.8 %collective-permute-start.5 = (f32[43,16,128]{2,1,0:T(8,128)S(1)}, f32[43,16,128]{2,1,0:T(8,128)S(1)}, u32[]{:S(2)}, u32[]{:S(2)}) collective-permute-start(f32[43,16,128]{2,1,0:T(8,128)S(1)} %get-tuple-element.28), channel_id=1, source_target_pairs={{4,8},{8,4},{5,9},{9,5},{6,10},{10,6},{7,11},{11,7},{20,24},{24,20... | collective-permute-start | bytes 1056776 | tf_op jit(solution)/shard_map/ppermute | solution.py:32
  10.7 5.2 %collective-permute-start.4 = (f32[4,4,128]{2,1,0:T(4,128)S(1)}, f32[4,4,128]{2,1,0:T(4,128)S(1)}, u32[]{:S(2)}, u32[]{:S(2)}) collective-permute-start(f32[4,4,128]{2,1,0:T(4,128)S(1)} %pad_maximum_fusion.1), channel_id=1, source_target_pairs={{0,1},{1,0},{2,3},{3,2},{4,5},{5,4},{6,7},{7,6},{8,9},{9,8},{10,11... | collective-permute-start | bytes 24584 | tf_op jit(solution)/shard_map/ppermute | solution.py:449
  16.0 5.8 %collective-permute-start.8 = (f32[8,4,128]{2,1,0:T(4,128)S(1)}, f32[8,4,128]{2,1,0:T(4,128)S(1)}, u32[]{:S(2)}, u32[]{:S(2)}) collective-permute-start(f32[8,4,128]{2,1,0:T(4,128)S(1)} %pad_maximum_fusion.__), channel_id=1, source_target_pairs={{0,2},{1,3},{2,0},{3,1},{4,6},{5,7},{6,4},{7,5},{8,10},{9,11},{10,... | collective-permute-start | bytes 49160 | tf_op jit(solution)/shard_map/ppermute | solution.py:449
  17.3 4.4 %copy-start = (s32[1024]{0:T(1024)S(1)}, s32[1024]{0:T(1024)}, u32[]{:S(2)}) copy-start(s32[1024]{0:T(1024)} %param.31) | copy-start | bytes 12292
  17.3 4.4 %copy-start.1 = (s32[1024]{0:T(1024)S(1)}, s32[1024]{0:T(1024)}, u32[]{:S(2)}) copy-start(s32[1024]{0:T(1024)} %param.32) | copy-start | bytes 12292
  17.6 9.3 %collective-permute-start.6 = (f32[43,8,128]{2,1,0:T(8,128)S(1)}, f32[43,8,128]{2,1,0:T(8,128)S(1)}, u32[]{:S(2)}, u32[]{:S(2)}) collective-permute-start(f32[43,8,128]{2,1,0:T(8,128)S(1)} %get-tuple-element.29), channel_id=1, source_target_pairs={{0,4},{8,12},{4,0},{12,8},{1,5},{9,13},{5,1},{13,9},{2,6},{10,14},... | collective-permute-start | bytes 528392 | tf_op jit(solution)/shard_map/ppermute | solution.py:32
  18.7 8.2 %collective-permute-start.7 = (f32[43,8,128]{2,1,0:T(8,128)S(1)}, f32[43,8,128]{2,1,0:T(8,128)S(1)}, u32[]{:S(2)}, u32[]{:S(2)}) collective-permute-start(f32[43,8,128]{2,1,0:T(8,128)S(1)} %get-tuple-element.30), channel_id=1, source_target_pairs={{4,8},{8,4},{5,9},{9,5},{6,10},{10,6},{7,11},{11,7},{20,24},{24,20... | collective-permute-start | bytes 528392 | tf_op jit(solution)/shard_map/ppermute | solution.py:32

commit v9 on v8

--- a/solution.py
+++ b/solution.py
@@ -165,7 +165,7 @@
     )(pinned(wide, pltpu.VMEM), window)
 
 
-def corner_kernel(_, y_a, y_b, __, wide, c_a, c_b):
+def corner_kernel(_, y_a, y_b, __, ___, wide, c_a, c_b):
     cells_x = y_a.shape[1]
     cells_y = wide.shape[2] - 2 * RIM
     odd_x, odd_y = is_odd("gx"), is_odd("gy")
@@ -191,17 +191,17 @@
             out[place : place + width] = wide[number, pl.ds(begin, width), cells_y:, :]
 
 
-def corners(wide, y_a, y_b, earlier):
+def corners(wide, y_a, y_b, *earlier):
     corner = vmem_out(x_parts()[1], 2 * RIM, wide.shape[-1])
     return pl.pallas_call(
         corner_kernel,
         out_shape=[vmem_out(*wide.shape), corner, corner],
-        in_specs=in_vmem(4),
+        in_specs=in_vmem(5),
         out_specs=in_vmem(3),
         input_output_aliases={0: 0},
         compiler_params=PARAMS,
         name="pack_corners",
-    )(pinned(wide, pltpu.VMEM), y_a, y_b, earlier)
+    )(pinned(wide, pltpu.VMEM), y_a, y_b, *earlier)
 
 
 def sine_cosine(angle):
@@ -215,6 +215,57 @@
     return sine * angle, cosine
 
 
+def factors_of(velocity, epsilon, delta, tilt, azimuth):
+    f_e = 1.0 + 2.0 * epsilon
+    f_d = jnp.sqrt(1.0 + 2.0 * delta)
+    sin_tilt, cos_tilt = sine_cosine(tilt)
+    sin_half, cos_half = sine_cosine(0.5 * azimuth)
+    sin_azim = 2.0 * sin_half * cos_half
+    cos_azim = 1.0 - 2.0 * sin_half * sin_half
+    sin_square = sin_tilt * sin_tilt
+    half_tilt = 0.5 * sin_tilt * cos_tilt
+    along_x = sin_square * cos_azim
+    return (
+        velocity,
+        velocity * f_e,
+        velocity * f_d,
+        along_x * cos_azim,
+        sin_square * sin_azim * sin_azim,
+        cos_tilt * cos_tilt,
+        0.5 * along_x * sin_azim,
+        half_tilt * cos_azim,
+        half_tilt * sin_azim,
+    )
+
+
+FACTORS = 9
+
+
+def own_kernel(wide, _, own):
+    _, cells_x, cells_y, _ = own.shape
+
+    def body(i):
+        for x in [4 * i + k for k in range(4)]:
+            raw = [wide[FIELDS + number, RIM + x, :cells_y, :] for number in range(5)]
+            for number, value in enumerate(factors_of(*raw)):
+                own[number, x] = value
+
+    repeat(cells_x // 4, body)
+
+
+def own_factors(wide, earlier):
+    _, planes_x, rows, depth = wide.shape
+    cells_x, cells_y = planes_x - 2 * RIM - 2, rows - 2 * RIM
+    return pl.pallas_call(
+        own_kernel,
+        out_shape=vmem_out(FACTORS, cells_x, cells_y, depth),
+        in_specs=in_vmem(2),
+        out_specs=in_vmem(1)[0],
+        compiler_params=PARAMS,
+        name="own_factors",
+    )(pinned(wide, pltpu.VMEM), earlier)
+
+
 class Steps:
     def __init__(self, wide, planes, waves, factors):
         self.wide, self.planes, self.waves, self.factors = wide, planes, waves, factors
@@ -245,28 +296,7 @@
     def make_factors(self, x):
         raw = [self.wide_tiles(FIELDS + number, x) for number in range(self.count - FIELDS)]
         for tile in range(self.tiles):
-            velocity, epsilon, delta, tilt, azimuth = [value[tile] for value in raw]
-            f_e = 1.0 + 2.0 * epsilon
-            f_d = jnp.sqrt(1.0 + 2.0 * delta)
-            sin_tilt, cos_tilt = sine_cosine(tilt)
-            sin_half, cos_half = sine_cosine(0.5 * azimuth)
-            sin_azim = 2.0 * sin_half * cos_half
-            cos_azim = 1.0 - 2.0 * sin_half * sin_half
-            sin_square = sin_tilt * sin_tilt
-            half_tilt = 0.5 * sin_tilt * cos_tilt
-            along_x = sin_square * cos_azim
-            values = (
-                velocity,
-                velocity * f_e,
-                velocity * f_d,
-                along_x * cos_azim,
-                sin_square * sin_azim * sin_azim,
-                cos_tilt * cos_tilt,
-                0.5 * along_x * sin_azim,
-                half_tilt * cos_azim,
-                half_tilt * sin_azim,
-            )
-            for number, value in enumerate(values):
+            for number, value in enumerate(factors_of(*[value[tile] for value in raw])):
                 self.factors[number, x, tile] = value
 
     def sides_z(self, value):
@@ -337,15 +367,28 @@
     lax.fori_loop(0, count, run, 0)
 
 
-def inner_kernel(wide, planes, *refs):
+def inner_kernel(wide, planes, own, *refs):
     steps = Steps(wide, planes, refs[:STEPS], refs[STEPS])
-    cells_x = steps.cells_x
-
-    def factor_pair(i):
-        steps.make_factors(RIM + 2 * i)
-        steps.make_factors(RIM + 2 * i + 1)
-
-    repeat(cells_x // 2, factor_pair)
+    natural = refs[STEPS + 1]
+    cells_x, cells_y, tiles = steps.cells_x, own.shape[2], steps.tiles
+
+    def rim_rows(i):
+        for x in [4 * i + k for k in range(4)]:
+            raw = [wide[FIELDS + number, RIM + x, cells_y:, :] for number in range(5)]
+            for number, value in enumerate(factors_of(*raw)):
+                natural[number, x, cells_y:, :] = value
+                natural[number, x, :cells_y, :] = own[number, x]
+
+    def in_step_order(i):
+        for x in [2 * i + k for k in range(2)]:
+            for number in range(FACTORS):
+                for tile in range(tiles):
+                    steps.factors[number, RIM + x, tile] = natural[
+                        number, x, pl.ds(tile, SUBLANES, stride=tiles), :
+                    ]
+
+    repeat(cells_x // 4, rim_rows)
+    repeat(cells_x // 2, in_step_order)
     for turn in range(STEPS):
         first, last = RIM + 1 + turn, RIM + cells_x - 1 - turn
         repeat((last - first) // 2, lambda i, turn=turn, first=first: steps.step(turn, first + 2 * i, 2))
@@ -369,11 +412,9 @@
 
     steps = Steps(wide, planes, waves, factors)
 
-    def factor_pair(i):
-        steps.make_factors(RIM - SLIM + i)
-        steps.make_factors(RIM + cells_x + i)
-
-    repeat(SLIM, factor_pair)
+    for x in range(SLIM):
+        steps.make_factors(RIM - SLIM + x)
+        steps.make_factors(RIM + cells_x + x)
     for turn in range(STEPS):
 
         def both(i, turn=turn):
@@ -405,17 +446,18 @@
         ref[...] = wide[out, RIM : RIM + cells_x, :cells_y, :]
 
 
-def inner(wide, planes):
+def inner(wide, planes, own):
     _, planes_x, rows, depth = wide.shape
     tile = (planes_x, rows // SUBLANES, SUBLANES, depth)
     return pl.pallas_call(
         inner_kernel,
-        out_shape=[vmem_out(4, *tile)] * STEPS + [vmem_out(9, *tile)],
-        in_specs=in_vmem(2),
+        out_shape=[vmem_out(4, *tile)] * STEPS + [vmem_out(FACTORS, *tile)],
+        in_specs=in_vmem(3),
         out_specs=in_vmem(STEPS + 1),
+        scratch_shapes=[pltpu.VMEM((FACTORS, own.shape[1], rows, depth), jnp.float32)],
         compiler_params=PARAMS,
         name="inner_steps",
-    )(pinned(wide, pltpu.VMEM), planes)
+    )(pinned(wide, pltpu.VMEM), planes, pinned(own, pltpu.VMEM))
 
 
 def outer(wide, rims, planes, state, cells_x, cells_y):
@@ -572,16 +614,17 @@
     windows = jnp.concatenate([window, x_a[x_parts()[1] :, :STEPS, :]], axis=0)
     for bit in bits_of("gx")[1:]:
         windows = doubled(windows, "gx", bit)
+    own = own_factors(wide, windows)
     for bit in bits_of("gy")[:-1]:
         windows = doubled(windows, "gy", bit)
-    wide, c_a, c_b = corners(wide, y_a, y_b, windows)
+    wide, c_a, c_b = corners(wide, y_a, y_b, windows, pinned(own, pltpu.VMEM))
     for bit in bits_of("gy")[-1:]:
         windows = doubled(windows, "gy", bit)
     c_a, c_b = swap(c_a, "gx", 0), swap(c_b, "gx", 1)
     planes = injected(
         windows, receiver_x, receiver_y, traces.shape[1], cells_x, cells_y, depth
     )
-    state = inner(wide, planes)
+    state = inner(wide, planes, own)
     return tuple(outer(wide, (x_a, x_b, c_a, c_b), planes, state, cells_x, cells_y))
 
 

time: 30.9 us -> 30.7 us (level)
  waiting for transfers between devices: 1.05 us -> 0.68 us
    ppermute x3, waiting for transfers between devices: 1.04 us -> 0.66 us  [doubled(): lax.ppermute(windows, axis, pairs)]
    pallas_call x0 -> x1, Pallas kernels: none -> 0.37 us  [own_factors(): pl.pallas_call(own_kernel, out_shape=vmem_out(FACTORS, cells_x, cells_y,...]
  transfers between devices with their start and end apart: 9 -> 9, of which waited for: 1 -> 1; matrix products, arithmetic and copies ran while one was open for 0% -> 0% of each run, Pallas kernels for 17% -> 18%
where the time goes in v9:
time: 30.7 us; the launch traced here: 30.5 us
  starting transfers between devices  17.2 us (56%)
  Pallas kernels  11.1 us (36%)
  between operations  1.46 us (5%)
  waiting for transfers between devices  0.68 us (2%)
    ppermute x6, starting transfers between devices, swap(): return lax.ppermute(value, axis, pairs)  10.3 us
    ppermute x3, starting transfers between devices, doubled(): lax.ppermute(windows, axis, pairs)  6.86 us
    pallas_call x1, Pallas kernels, inner(): pl.pallas_call(inner_kernel, out_shape=[vmem_out(4, *tile)] * STEPS + [vm...  4.43 us
    pallas_call x1, Pallas kernels, outer(): pl.pallas_call(outer_kernel, out_shape=kept + [out] * 3, in_specs=in_vmem...  3.72 us
    pallas_call x1, Pallas kernels, pack(): pl.pallas_call(functools.partial(pack_kernel, count), out_shape=[wide, ri...  1.8 us
    ppermute x3, waiting for transfers between devices, doubled(): lax.ppermute(windows, axis, pairs)  0.66 us
  transfers between devices with their start and end apart: 9, of which 1 were waited for; matrix products, arithmetic and copies ran while one was open for 0% of the time, Pallas kernels for 18%

profile of v9, /device:TPU:1, one launch (start us, length us, event | category | flops | bytes accessed | tf_op | source)
XLA Modules:
  0.0 30.5 jit_solution(5972018873479288753)
XLA Ops:
  1.3 1.8 %pack_y_rims.1 = (f32[13,26,24,128]{3,2,1,0:T(8,128)S(1)}, f32[11,16,4,128]{3,2,1,0:T(4,128)S(1)}, f32[11,16,4,128]{3,2,1,0:T(4,128)S(1)}, f32[1,4,128]{2,1,0:T(4,128)S(1)}) custom-call(f32[16,16,128]{2,1,0:T(8,128)} %refs_0_.1, f32[16,16,128]{2,1,0:T(8,128)} %refs_1_.1, f32[16,16,128]{2,1,0:T(8,128)} %refs_2_.1, f32[16,16,128]{2,1,0:T(8,128)} %refs_3_.1, ...), custom_call_target="tpu_custom_call" | custom-call | tf_op jit(solution)/shard_map/pack_y_rims/pallas_call | solution.py:123
  3.1 0.1 pack_x_rims.1
  3.2 0.1 collective-permute-start.2
  3.3 2.8 %collective-permute-start = (f32[11,16,4,128]{3,2,1,0:T(4,128)S(1)}, f32[11,16,4,128]{3,2,1,0:T(4,128)S(1)}, u32[]{:S(2)}, u32[]{:S(2)}) collective-permute-start(f32[11,16,4,128]{3,2,1,0:T(4,128)S(1)} %get-tuple-element.24), channel_id=1, source_target_pairs={{0,1},{2,3},{1,0},{3,2},{4,5},{6,7},{5,4},{7,6},{8,9},{10,11},{9,8... | collective-permute-start | bytes 1081352 | tf_op jit(solution)/shard_map/ppermute | solution.py:32
  6.0 0.7 %collective-permute-start.1 = (f32[11,16,4,128]{3,2,1,0:T(4,128)S(1)}, f32[11,16,4,128]{3,2,1,0:T(4,128)S(1)}, u32[]{:S(2)}, u32[]{:S(2)}) collective-permute-start(f32[11,16,4,128]{3,2,1,0:T(4,128)S(1)} %get-tuple-element.25), channel_id=1, source_target_pairs={{1,2},{2,1},{5,6},{6,5},{9,10},{10,9},{13,14},{14,13},{17,18},{18,... | collective-permute-start | bytes 1081352 | tf_op jit(solution)/shard_map/ppermute | solution.py:32
  6.7 0.0 collective-permute-done.2.refs_1_
  6.8 1.3 %collective-permute-start.3 = (f32[2,4,128]{2,1,0:T(4,128)S(1)}, f32[2,4,128]{2,1,0:T(4,128)S(1)}, u32[]{:S(2)}, u32[]{:S(2)}) collective-permute-start(f32[2,4,128]{2,1,0:T(4,128)S(1)} %pad_maximum_fusion.2), channel_id=1, source_target_pairs={{0,8},{4,12},{8,0},{12,4},{1,9},{5,13},{9,1},{13,5},{2,10},{6,14},... | collective-permute-start | bytes 12296 | tf_op jit(solution)/shard_map/ppermute | solution.py:491
  8.0 2.7 %collective-permute-start.5 = (f32[43,16,128]{2,1,0:T(8,128)S(1)}, f32[43,16,128]{2,1,0:T(8,128)S(1)}, u32[]{:S(2)}, u32[]{:S(2)}) collective-permute-start(f32[43,16,128]{2,1,0:T(8,128)S(1)} %get-tuple-element.28), channel_id=1, source_target_pairs={{4,8},{8,4},{5,9},{9,5},{6,10},{10,6},{7,11},{11,7},{20,24},{24,20... | collective-permute-start | bytes 1056776 | tf_op jit(solution)/shard_map/ppermute | solution.py:32
  10.7 0.0 collective-permute-done.3
  10.7 4.2 %collective-permute-start.4 = (f32[4,4,128]{2,1,0:T(4,128)S(1)}, f32[4,4,128]{2,1,0:T(4,128)S(1)}, u32[]{:S(2)}, u32[]{:S(2)}) collective-permute-start(f32[4,4,128]{2,1,0:T(4,128)S(1)} %pad_maximum_fusion.1._), channel_id=1, source_target_pairs={{0,1},{1,0},{2,3},{3,2},{4,5},{5,4},{6,7},{7,6},{8,9},{9,8},{10,11... | collective-permute-start | bytes 24584 | tf_op jit(solution)/shard_map/ppermute | solution.py:491
  14.9 0.4 %own_factors.1.___.own = f32[9,16,16,128]{3,2,1,0:T(8,128)S(1)} custom-call(f32[13,26,24,128]{3,2,1,0:T(8,128)S(1)} %get-tuple-element.23.wide._, f32[4,4,128]{2,1,0:T(4,128)S(1)} %pad_maximum_fusion.1._), custom_call_target="tpu_custom_call" | custom-call | tf_op jit(solution)/shard_map/own_factors/pallas_call | solution.py:259
  15.3 0.7 %collective-permute-done.4 = f32[4,4,128]{2,1,0:T(4,128)S(1)} collective-permute-done((f32[4,4,128]{2,1,0:T(4,128)S(1)}, f32[4,4,128]{2,1,0:T(4,128)S(1)}, u32[]{:S(2)}, u32[]{:S(2)}) %collective-permute-start.4) | collective-permute-done | bytes 8224 | tf_op jit(solution)/shard_map/ppermute | solution.py:491
  16.0 0.0 copy-start
  16.0 0.0 copy-start.1
  16.0 1.4 %collective-permute-start.8 = (f32[8,4,128]{2,1,0:T(4,128)S(1)}, f32[8,4,128]{2,1,0:T(4,128)S(1)}, u32[]{:S(2)}, u32[]{:S(2)}) collective-permute-start(f32[8,4,128]{2,1,0:T(4,128)S(1)} %pad_maximum_fusion.__), channel_id=1, source_target_pairs={{0,2},{1,3},{2,0},{3,1},{4,6},{5,7},{6,4},{7,5},{8,10},{9,11},{10,... | collective-permute-start | bytes 49160 | tf_op jit(solution)/shard_map/ppermute | solution.py:491
  17.4 0.0 collective-permute-done.y_a
  17.4 0.0 collective-permute-done.1.y_b
  17.4 0.2 pack_corners.1
  17.6 1.1 %collective-permute-start.6 = (f32[43,8,128]{2,1,0:T(8,128)S(1)}, f32[43,8,128]{2,1,0:T(8,128)S(1)}, u32[]{:S(2)}, u32[]{:S(2)}) collective-permute-start(f32[43,8,128]{2,1,0:T(8,128)S(1)} %get-tuple-element.29), channel_id=1, source_target_pairs={{0,4},{8,12},{4,0},{12,8},{1,5},{9,13},{5,1},{13,9},{2,6},{10,14},... | collective-permute-start | bytes 528392 | tf_op jit(solution)/shard_map/ppermute | solution.py:32
  18.7 3.0 %collective-permute-start.7 = (f32[43,8,128]{2,1,0:T(8,128)S(1)}, f32[43,8,128]{2,1,0:T(8,128)S(1)}, u32[]{:S(2)}, u32[]{:S(2)}) collective-permute-start(f32[43,8,128]{2,1,0:T(8,128)S(1)} %get-tuple-element.30), channel_id=1, source_target_pairs={{4,8},{8,4},{5,9},{9,5},{6,10},{10,6},{7,11},{11,7},{20,24},{24,20... | collective-permute-start | bytes 528392 | tf_op jit(solution)/shard_map/ppermute | solution.py:32
  21.8 0.0 collective-permute-done.8
  21.8 0.0 copy-done
  21.8 0.0 copy-done.1
  21.8 0.5 %inject.1.planes.refs_5_ = f32[4,3,8,128]{3,2,1,0:T(8,128)S(1)} custom-call(f32[16,4,128]{2,1,0:T(4,128)S(1)} %constant_dynamic-update-slice_fusion.gathered, s32[8,128]{1,0:T(8,128)S(1)} %bitcast.2, s32[8,128]{1,0:T(8,128)S(1)} %bitcast.3), custom_call_target="tpu_custom_call" | custom-call | tf_op jit(solution)/shard_map/inject/pallas_call | solution.py:561
  22.3 4.4 %inner_steps.1 = (f32[4,26,3,8,128]{4,3,2,1,0:T(8,128)S(1)}, f32[4,26,3,8,128]{4,3,2,1,0:T(8,128)S(1)}, f32[4,26,3,8,128]{4,3,2,1,0:T(8,128)S(1)}, f32[4,26,3,8,...) custom-call(f32[13,26,24,128]{3,2,1,0:T(8,128)S(1)} %get-tuple-element.27.wide.refs_0_, ...), custom_call_target="tpu_custom_call" | custom-call | tf_op jit(solution)/shard_map/inner_steps/pallas_call | solution.py:452
  26.7 0.0 collective-permute-done.5.refs_2_
  26.7 0.0 collective-permute-done.6.refs_3_
  26.7 0.0 collective-permute-done.7.refs_4_
  26.8 3.7 %outer_steps.1 = (f32[13,26,24,128]{3,2,1,0:T(8,128)S(1)}, f32[4,26,3,8,128]{4,3,2,1,0:T(8,128)S(1)}, f32[4,26,3,8,128]{4,3,2,1,0:T(8,128)S(1)}, f32[4,26,3,8,12...) custom-call(f32[13,26,24,128]{3,2,1,0:T(8,128)S(1)} %get-tuple-eleme, ...), custom_call_target="tpu_custom_call", output_to_operand_aliasing={{0}: (0, {}), {1}: (6, {}), {2}: (7, {}), {3}: (8, {}), {4}... | custom-call | tf_op jit(solution)/shard_map/outer_steps/pallas_call | solution.py:468
  (8 shorter events, 0.1 us)
Async XLA Ops:
  3.2 3.6 %collective-permute-start.2 = (f32[44,16,128]{2,1,0:T(8,128)S(1)}, f32[44,16,128]{2,1,0:T(8,128)S(1)}, u32[]{:S(2)}, u32[]{:S(2)}) collective-permute-start(f32[44,16,128]{2,1,0:T(8,128)S(1)} %get-tuple-element.26), channel_id=1, source_target_pairs={{0,4},{8,12},{4,0},{12,8},{1,5},{9,13},{5,1},{13,9},{2,6},{10,14},... | collective-permute-start | bytes 1081352 | tf_op jit(solution)/shard_map/ppermute | solution.py:32
  3.3 14.1 %collective-permute-start = (f32[11,16,4,128]{3,2,1,0:T(4,128)S(1)}, f32[11,16,4,128]{3,2,1,0:T(4,128)S(1)}, u32[]{:S(2)}, u32[]{:S(2)}) collective-permute-start(f32[11,16,4,128]{3,2,1,0:T(4,128)S(1)} %get-tuple-element.24), channel_id=1, source_target_pairs={{0,1},{2,3},{1,0},{3,2},{4,5},{6,7},{5,4},{7,6},{8,9},{10,11},{9,8... | collective-permute-start | bytes 1081352 | tf_op jit(solution)/shard_map/ppermute | solution.py:32
  6.0 11.3 %collective-permute-start.1 = (f32[11,16,4,128]{3,2,1,0:T(4,128)S(1)}, f32[11,16,4,128]{3,2,1,0:T(4,128)S(1)}, u32[]{:S(2)}, u32[]{:S(2)}) collective-permute-start(f32[11,16,4,128]{3,2,1,0:T(4,128)S(1)} %get-tuple-element.25), channel_id=1, source_target_pairs={{1,2},{2,1},{5,6},{6,5},{9,10},{10,9},{13,14},{14,13},{17,18},{18,... | collective-permute-start | bytes 1081352 | tf_op jit(solution)/shard_map/ppermute | solution.py:32
  6.8 3.9 %collective-permute-start.3 = (f32[2,4,128]{2,1,0:T(4,128)S(1)}, f32[2,4,128]{2,1,0:T(4,128)S(1)}, u32[]{:S(2)}, u32[]{:S(2)}) collective-permute-start(f32[2,4,128]{2,1,0:T(4,128)S(1)} %pad_maximum_fusion.2), channel_id=1, source_target_pairs={{0,8},{4,12},{8,0},{12,4},{1,9},{5,13},{9,1},{13,5},{2,10},{6,14},... | collective-permute-start | bytes 12296 | tf_op jit(solution)/shard_map/ppermute | solution.py:491
  8.0 18.7 %collective-permute-start.5 = (f32[43,16,128]{2,1,0:T(8,128)S(1)}, f32[43,16,128]{2,1,0:T(8,128)S(1)}, u32[]{:S(2)}, u32[]{:S(2)}) collective-permute-start(f32[43,16,128]{2,1,0:T(8,128)S(1)} %get-tuple-element.28), channel_id=1, source_target_pairs={{4,8},{8,4},{5,9},{9,5},{6,10},{10,6},{7,11},{11,7},{20,24},{24,20... | collective-permute-start | bytes 1056776 | tf_op jit(solution)/shard_map/ppermute | solution.py:32
  10.7 5.2 %collective-permute-start.4 = (f32[4,4,128]{2,1,0:T(4,128)S(1)}, f32[4,4,128]{2,1,0:T(4,128)S(1)}, u32[]{:S(2)}, u32[]{:S(2)}) collective-permute-start(f32[4,4,128]{2,1,0:T(4,128)S(1)} %pad_maximum_fusion.1._), channel_id=1, source_target_pairs={{0,1},{1,0},{2,3},{3,2},{4,5},{5,4},{6,7},{7,6},{8,9},{9,8},{10,11... | collective-permute-start | bytes 24584 | tf_op jit(solution)/shard_map/ppermute | solution.py:491
  16.0 5.8 %copy-start = (s32[1024]{0:T(1024)S(1)}, s32[1024]{0:T(1024)}, u32[]{:S(2)}) copy-start(s32[1024]{0:T(1024)} %param.31) | copy-start | bytes 12292
  16.0 5.8 %copy-start.1 = (s32[1024]{0:T(1024)S(1)}, s32[1024]{0:T(1024)}, u32[]{:S(2)}) copy-start(s32[1024]{0:T(1024)} %param.32) | copy-start | bytes 12292
  16.0 5.8 %collective-permute-start.8 = (f32[8,4,128]{2,1,0:T(4,128)S(1)}, f32[8,4,128]{2,1,0:T(4,128)S(1)}, u32[]{:S(2)}, u32[]{:S(2)}) collective-permute-start(f32[8,4,128]{2,1,0:T(4,128)S(1)} %pad_maximum_fusion.__), channel_id=1, source_target_pairs={{0,2},{1,3},{2,0},{3,1},{4,6},{5,7},{6,4},{7,5},{8,10},{9,11},{10,... | collective-permute-start | bytes 49160 | tf_op jit(solution)/shard_map/ppermute | solution.py:491
  17.6 9.1 %collective-permute-start.6 = (f32[43,8,128]{2,1,0:T(8,128)S(1)}, f32[43,8,128]{2,1,0:T(8,128)S(1)}, u32[]{:S(2)}, u32[]{:S(2)}) collective-permute-start(f32[43,8,128]{2,1,0:T(8,128)S(1)} %get-tuple-element.29), channel_id=1, source_target_pairs={{0,4},{8,12},{4,0},{12,8},{1,5},{9,13},{5,1},{13,9},{2,6},{10,14},... | collective-permute-start | bytes 528392 | tf_op jit(solution)/shard_map/ppermute | solution.py:32
  18.7 8.0 %collective-permute-start.7 = (f32[43,8,128]{2,1,0:T(8,128)S(1)}, f32[43,8,128]{2,1,0:T(8,128)S(1)}, u32[]{:S(2)}, u32[]{:S(2)}) collective-permute-start(f32[43,8,128]{2,1,0:T(8,128)S(1)} %get-tuple-element.30), channel_id=1, source_target_pairs={{4,8},{8,4},{5,9},{9,5},{6,10},{10,6},{7,11},{11,7},{20,24},{24,20... | collective-permute-start | bytes 528392 | tf_op jit(solution)/shard_map/ppermute | solution.py:32

commit v10 on v9

--- a/solution.py
+++ b/solution.py
@@ -391,7 +391,8 @@
     repeat(cells_x // 2, in_step_order)
     for turn in range(STEPS):
         first, last = RIM + 1 + turn, RIM + cells_x - 1 - turn
-        repeat((last - first) // 2, lambda i, turn=turn, first=first: steps.step(turn, first + 2 * i, 2))
+        half = (last - first) // 2
+        repeat(2, lambda i, turn=turn, first=first, half=half: steps.step(turn, first + half * i, half))
 
 
 def outer_kernel(*refs):
@@ -416,12 +417,8 @@
         steps.make_factors(RIM - SLIM + x)
         steps.make_factors(RIM + cells_x + x)
     for turn in range(STEPS):
-
-        def both(i, turn=turn):
-            steps.step(turn, turn + 1 + 2 * i, 2)
-            steps.step(turn, RIM + cells_x - 1 - turn + 2 * i, 2)
-
-        repeat(RIM // 2, both)
+        steps.step(turn, turn + 1, RIM)
+        steps.step(turn, RIM + cells_x - 1 - turn, RIM)
 
     tiles = steps.tiles
 

time: 30.7 us -> 29.5 us (0.961)
  Pallas kernels: 11.1 us -> 9.89 us
    pallas_call x1, Pallas kernels: 4.43 us -> 3.72 us  [inner(): pl.pallas_call(inner_kernel, out_shape=[vmem_out(4, *tile)] * STEPS + [vm...]
    pallas_call x1, Pallas kernels: 3.72 us -> 3.25 us  [outer(): pl.pallas_call(outer_kernel, out_shape=kept + [out] * 3, in_specs=in_vmem...]
  transfers between devices with their start and end apart: 9 -> 9, of which waited for: 1 -> 1; matrix products, arithmetic and copies ran while one was open for 0% -> 0% of each run, Pallas kernels for 18% -> 16%
where the time goes in v10:
time: 29.5 us; the launch traced here: 29.3 us
  starting transfers between devices  17.2 us (58%)
  Pallas kernels  9.89 us (34%)
  between operations  1.46 us (5%)
  waiting for transfers between devices  0.68 us (2%)
    ppermute x6, starting transfers between devices, swap(): return lax.ppermute(value, axis, pairs)  10.3 us
    ppermute x3, starting transfers between devices, doubled(): lax.ppermute(windows, axis, pairs)  6.86 us
    pallas_call x1, Pallas kernels, inner(): pl.pallas_call(inner_kernel, out_shape=[vmem_out(4, *tile)] * STEPS + [vm...  3.72 us
    pallas_call x1, Pallas kernels, outer(): pl.pallas_call(outer_kernel, out_shape=kept + [out] * 3, in_specs=in_vmem...  3.25 us
    pallas_call x1, Pallas kernels, pack(): pl.pallas_call(functools.partial(pack_kernel, count), out_shape=[wide, ri...  1.8 us
    ppermute x3, waiting for transfers between devices, doubled(): lax.ppermute(windows, axis, pairs)  0.66 us
  transfers between devices with their start and end apart: 9, of which 1 were waited for; matrix products, arithmetic and copies ran while one was open for 0% of the time, Pallas kernels for 16%

profile of v10, /device:TPU:1, one launch (start us, length us, event | category | flops | bytes accessed | tf_op | source)
XLA Modules:
  0.0 29.3 jit_solution(3460316036075512004)
XLA Ops:
  1.3 1.8 %pack_y_rims.1 = (f32[13,26,24,128]{3,2,1,0:T(8,128)S(1)}, f32[11,16,4,128]{3,2,1,0:T(4,128)S(1)}, f32[11,16,4,128]{3,2,1,0:T(4,128)S(1)}, f32[1,4,128]{2,1,0:T(4,128)S(1)}) custom-call(f32[16,16,128]{2,1,0:T(8,128)} %refs_0_.1, f32[16,16,128]{2,1,0:T(8,128)} %refs_1_.1, f32[16,16,128]{2,1,0:T(8,128)} %refs_2_.1, f32[16,16,128]{2,1,0:T(8,128)} %refs_3_.1, ...), custom_call_target="tpu_custom_call" | custom-call | tf_op jit(solution)/shard_map/pack_y_rims/pallas_call | solution.py:123
  3.1 0.1 pack_x_rims.1
  3.2 0.1 collective-permute-start.2
  3.3 2.8 %collective-permute-start = (f32[11,16,4,128]{3,2,1,0:T(4,128)S(1)}, f32[11,16,4,128]{3,2,1,0:T(4,128)S(1)}, u32[]{:S(2)}, u32[]{:S(2)}) collective-permute-start(f32[11,16,4,128]{3,2,1,0:T(4,128)S(1)} %get-tuple-element.24), channel_id=1, source_target_pairs={{0,1},{2,3},{1,0},{3,2},{4,5},{6,7},{5,4},{7,6},{8,9},{10,11},{9,8... | collective-permute-start | bytes 1081352 | tf_op jit(solution)/shard_map/ppermute | solution.py:32
  6.0 0.7 %collective-permute-start.1 = (f32[11,16,4,128]{3,2,1,0:T(4,128)S(1)}, f32[11,16,4,128]{3,2,1,0:T(4,128)S(1)}, u32[]{:S(2)}, u32[]{:S(2)}) collective-permute-start(f32[11,16,4,128]{3,2,1,0:T(4,128)S(1)} %get-tuple-element.25), channel_id=1, source_target_pairs={{1,2},{2,1},{5,6},{6,5},{9,10},{10,9},{13,14},{14,13},{17,18},{18,... | collective-permute-start | bytes 1081352 | tf_op jit(solution)/shard_map/ppermute | solution.py:32
  6.7 0.0 collective-permute-done.2.refs_1_
  6.8 1.3 %collective-permute-start.3 = (f32[2,4,128]{2,1,0:T(4,128)S(1)}, f32[2,4,128]{2,1,0:T(4,128)S(1)}, u32[]{:S(2)}, u32[]{:S(2)}) collective-permute-start(f32[2,4,128]{2,1,0:T(4,128)S(1)} %pad_maximum_fusion.2), channel_id=1, source_target_pairs={{0,8},{4,12},{8,0},{12,4},{1,9},{5,13},{9,1},{13,5},{2,10},{6,14},... | collective-permute-start | bytes 12296 | tf_op jit(solution)/shard_map/ppermute | solution.py:488
  8.0 2.7 %collective-permute-start.5 = (f32[43,16,128]{2,1,0:T(8,128)S(1)}, f32[43,16,128]{2,1,0:T(8,128)S(1)}, u32[]{:S(2)}, u32[]{:S(2)}) collective-permute-start(f32[43,16,128]{2,1,0:T(8,128)S(1)} %get-tuple-element.28), channel_id=1, source_target_pairs={{4,8},{8,4},{5,9},{9,5},{6,10},{10,6},{7,11},{11,7},{20,24},{24,20... | collective-permute-start | bytes 1056776 | tf_op jit(solution)/shard_map/ppermute | solution.py:32
  10.7 0.0 collective-permute-done.3
  10.7 4.2 %collective-permute-start.4 = (f32[4,4,128]{2,1,0:T(4,128)S(1)}, f32[4,4,128]{2,1,0:T(4,128)S(1)}, u32[]{:S(2)}, u32[]{:S(2)}) collective-permute-start(f32[4,4,128]{2,1,0:T(4,128)S(1)} %pad_maximum_fusion.1._), channel_id=1, source_target_pairs={{0,1},{1,0},{2,3},{3,2},{4,5},{5,4},{6,7},{7,6},{8,9},{9,8},{10,11... | collective-permute-start | bytes 24584 | tf_op jit(solution)/shard_map/ppermute | solution.py:488
  14.9 0.4 %own_factors.1.___.own = f32[9,16,16,128]{3,2,1,0:T(8,128)S(1)} custom-call(f32[13,26,24,128]{3,2,1,0:T(8,128)S(1)} %get-tuple-element.23.wide._, f32[4,4,128]{2,1,0:T(4,128)S(1)} %pad_maximum_fusion.1._), custom_call_target="tpu_custom_call" | custom-call | tf_op jit(solution)/shard_map/own_factors/pallas_call | solution.py:259
  15.3 0.7 %collective-permute-done.4 = f32[4,4,128]{2,1,0:T(4,128)S(1)} collective-permute-done((f32[4,4,128]{2,1,0:T(4,128)S(1)}, f32[4,4,128]{2,1,0:T(4,128)S(1)}, u32[]{:S(2)}, u32[]{:S(2)}) %collective-permute-start.4) | collective-permute-done | bytes 8224 | tf_op jit(solution)/shard_map/ppermute | solution.py:488
  16.0 0.0 copy-start
  16.0 0.0 copy-start.1
  16.0 1.4 %collective-permute-start.8 = (f32[8,4,128]{2,1,0:T(4,128)S(1)}, f32[8,4,128]{2,1,0:T(4,128)S(1)}, u32[]{:S(2)}, u32[]{:S(2)}) collective-permute-start(f32[8,4,128]{2,1,0:T(4,128)S(1)} %pad_maximum_fusion.__), channel_id=1, source_target_pairs={{0,2},{1,3},{2,0},{3,1},{4,6},{5,7},{6,4},{7,5},{8,10},{9,11},{10,... | collective-permute-start | bytes 49160 | tf_op jit(solution)/shard_map/ppermute | solution.py:488
  17.4 0.0 collective-permute-done.y_a
  17.4 0.0 collective-permute-done.1.y_b
  17.4 0.2 pack_corners.1
  17.6 1.1 %collective-permute-start.6 = (f32[43,8,128]{2,1,0:T(8,128)S(1)}, f32[43,8,128]{2,1,0:T(8,128)S(1)}, u32[]{:S(2)}, u32[]{:S(2)}) collective-permute-start(f32[43,8,128]{2,1,0:T(8,128)S(1)} %get-tuple-element.29), channel_id=1, source_target_pairs={{0,4},{8,12},{4,0},{12,8},{1,5},{9,13},{5,1},{13,9},{2,6},{10,14},... | collective-permute-start | bytes 528392 | tf_op jit(solution)/shard_map/ppermute | solution.py:32
  18.7 3.0 %collective-permute-start.7 = (f32[43,8,128]{2,1,0:T(8,128)S(1)}, f32[43,8,128]{2,1,0:T(8,128)S(1)}, u32[]{:S(2)}, u32[]{:S(2)}) collective-permute-start(f32[43,8,128]{2,1,0:T(8,128)S(1)} %get-tuple-element.30), channel_id=1, source_target_pairs={{4,8},{8,4},{5,9},{9,5},{6,10},{10,6},{7,11},{11,7},{20,24},{24,20... | collective-permute-start | bytes 528392 | tf_op jit(solution)/shard_map/ppermute | solution.py:32
  21.8 0.0 collective-permute-done.8
  21.8 0.0 copy-done
  21.8 0.0 copy-done.1
  21.8 0.5 %inject.1.planes.refs_5_ = f32[4,3,8,128]{3,2,1,0:T(8,128)S(1)} custom-call(f32[16,4,128]{2,1,0:T(4,128)S(1)} %constant_dynamic-update-slice_fusion.gathered, s32[8,128]{1,0:T(8,128)S(1)} %bitcast.2, s32[8,128]{1,0:T(8,128)S(1)} %bitcast.3), custom_call_target="tpu_custom_call" | custom-call | tf_op jit(solution)/shard_map/inject/pallas_call | solution.py:558
  22.3 3.7 %inner_steps.1 = (f32[4,26,3,8,128]{4,3,2,1,0:T(8,128)S(1)}, f32[4,26,3,8,128]{4,3,2,1,0:T(8,128)S(1)}, f32[4,26,3,8,128]{4,3,2,1,0:T(8,128)S(1)}, f32[4,26,3,8,...) custom-call(f32[13,26,24,128]{3,2,1,0:T(8,128)S(1)} %get-tuple-element.27.wide.refs_0_, ...), custom_call_target="tpu_custom_call" | custom-call | tf_op jit(solution)/shard_map/inner_steps/pallas_call | solution.py:449
  26.0 0.0 collective-permute-done.5.refs_2_
  26.0 0.0 collective-permute-done.6.refs_3_
  26.0 0.0 collective-permute-done.7.refs_4_
  26.0 3.3 %outer_steps.1 = (f32[13,26,24,128]{3,2,1,0:T(8,128)S(1)}, f32[4,26,3,8,128]{4,3,2,1,0:T(8,128)S(1)}, f32[4,26,3,8,128]{4,3,2,1,0:T(8,128)S(1)}, f32[4,26,3,8,12...) custom-call(f32[13,26,24,128]{3,2,1,0:T(8,128)S(1)} %get-tuple-eleme, ...), custom_call_target="tpu_custom_call", output_to_operand_aliasing={{0}: (0, {}), {1}: (6, {}), {2}: (7, {}), {3}: (8, {}), {4}... | custom-call | tf_op jit(solution)/shard_map/outer_steps/pallas_call | solution.py:465
  (8 shorter events, 0.1 us)
Async XLA Ops:
  3.2 3.6 %collective-permute-start.2 = (f32[44,16,128]{2,1,0:T(8,128)S(1)}, f32[44,16,128]{2,1,0:T(8,128)S(1)}, u32[]{:S(2)}, u32[]{:S(2)}) collective-permute-start(f32[44,16,128]{2,1,0:T(8,128)S(1)} %get-tuple-element.26), channel_id=1, source_target_pairs={{0,4},{8,12},{4,0},{12,8},{1,5},{9,13},{5,1},{13,9},{2,6},{10,14},... | collective-permute-start | bytes 1081352 | tf_op jit(solution)/shard_map/ppermute | solution.py:32
  3.3 14.1 %collective-permute-start = (f32[11,16,4,128]{3,2,1,0:T(4,128)S(1)}, f32[11,16,4,128]{3,2,1,0:T(4,128)S(1)}, u32[]{:S(2)}, u32[]{:S(2)}) collective-permute-start(f32[11,16,4,128]{3,2,1,0:T(4,128)S(1)} %get-tuple-element.24), channel_id=1, source_target_pairs={{0,1},{2,3},{1,0},{3,2},{4,5},{6,7},{5,4},{7,6},{8,9},{10,11},{9,8... | collective-permute-start | bytes 1081352 | tf_op jit(solution)/shard_map/ppermute | solution.py:32
  6.0 11.3 %collective-permute-start.1 = (f32[11,16,4,128]{3,2,1,0:T(4,128)S(1)}, f32[11,16,4,128]{3,2,1,0:T(4,128)S(1)}, u32[]{:S(2)}, u32[]{:S(2)}) collective-permute-start(f32[11,16,4,128]{3,2,1,0:T(4,128)S(1)} %get-tuple-element.25), channel_id=1, source_target_pairs={{1,2},{2,1},{5,6},{6,5},{9,10},{10,9},{13,14},{14,13},{17,18},{18,... | collective-permute-start | bytes 1081352 | tf_op jit(solution)/shard_map/ppermute | solution.py:32
  6.8 3.9 %collective-permute-start.3 = (f32[2,4,128]{2,1,0:T(4,128)S(1)}, f32[2,4,128]{2,1,0:T(4,128)S(1)}, u32[]{:S(2)}, u32[]{:S(2)}) collective-permute-start(f32[2,4,128]{2,1,0:T(4,128)S(1)} %pad_maximum_fusion.2), channel_id=1, source_target_pairs={{0,8},{4,12},{8,0},{12,4},{1,9},{5,13},{9,1},{13,5},{2,10},{6,14},... | collective-permute-start | bytes 12296 | tf_op jit(solution)/shard_map/ppermute | solution.py:488
  8.0 18.0 %collective-permute-start.5 = (f32[43,16,128]{2,1,0:T(8,128)S(1)}, f32[43,16,128]{2,1,0:T(8,128)S(1)}, u32[]{:S(2)}, u32[]{:S(2)}) collective-permute-start(f32[43,16,128]{2,1,0:T(8,128)S(1)} %get-tuple-element.28), channel_id=1, source_target_pairs={{4,8},{8,4},{5,9},{9,5},{6,10},{10,6},{7,11},{11,7},{20,24},{24,20... | collective-permute-start | bytes 1056776 | tf_op jit(solution)/shard_map/ppermute | solution.py:32
  10.7 5.2 %collective-permute-start.4 = (f32[4,4,128]{2,1,0:T(4,128)S(1)}, f32[4,4,128]{2,1,0:T(4,128)S(1)}, u32[]{:S(2)}, u32[]{:S(2)}) collective-permute-start(f32[4,4,128]{2,1,0:T(4,128)S(1)} %pad_maximum_fusion.1._), channel_id=1, source_target_pairs={{0,1},{1,0},{2,3},{3,2},{4,5},{5,4},{6,7},{7,6},{8,9},{9,8},{10,11... | collective-permute-start | bytes 24584 | tf_op jit(solution)/shard_map/ppermute | solution.py:488
  16.0 5.8 %copy-start = (s32[1024]{0:T(1024)S(1)}, s32[1024]{0:T(1024)}, u32[]{:S(2)}) copy-start(s32[1024]{0:T(1024)} %param.31) | copy-start | bytes 12292
  16.0 5.8 %copy-start.1 = (s32[1024]{0:T(1024)S(1)}, s32[1024]{0:T(1024)}, u32[]{:S(2)}) copy-start(s32[1024]{0:T(1024)} %param.32) | copy-start | bytes 12292
  16.0 5.8 %collective-permute-start.8 = (f32[8,4,128]{2,1,0:T(4,128)S(1)}, f32[8,4,128]{2,1,0:T(4,128)S(1)}, u32[]{:S(2)}, u32[]{:S(2)}) collective-permute-start(f32[8,4,128]{2,1,0:T(4,128)S(1)} %pad_maximum_fusion.__), channel_id=1, source_target_pairs={{0,2},{1,3},{2,0},{3,1},{4,6},{5,7},{6,4},{7,5},{8,10},{9,11},{10,... | collective-permute-start | bytes 49160 | tf_op jit(solution)/shard_map/ppermute | solution.py:488
  17.6 8.4 %collective-permute-start.6 = (f32[43,8,128]{2,1,0:T(8,128)S(1)}, f32[43,8,128]{2,1,0:T(8,128)S(1)}, u32[]{:S(2)}, u32[]{:S(2)}) collective-permute-start(f32[43,8,128]{2,1,0:T(8,128)S(1)} %get-tuple-element.29), channel_id=1, source_target_pairs={{0,4},{8,12},{4,0},{12,8},{1,5},{9,13},{5,1},{13,9},{2,6},{10,14},... | collective-permute-start | bytes 528392 | tf_op jit(solution)/shard_map/ppermute | solution.py:32
  18.7 7.3 %collective-permute-start.7 = (f32[43,8,128]{2,1,0:T(8,128)S(1)}, f32[43,8,128]{2,1,0:T(8,128)S(1)}, u32[]{:S(2)}, u32[]{:S(2)}) collective-permute-start(f32[43,8,128]{2,1,0:T(8,128)S(1)} %get-tuple-element.30), channel_id=1, source_target_pairs={{4,8},{8,4},{5,9},{9,5},{6,10},{10,6},{7,11},{11,7},{20,24},{24,20... | collective-permute-start | bytes 528392 | tf_op jit(solution)/shard_map/ppermute | solution.py:32

commit v11 on v10

--- a/solution.py
+++ b/solution.py
@@ -76,6 +76,12 @@
 
 def vmem_out(*shape):
     return pltpu.VMEM(shape, jnp.float32)
+
+
+def swap_far(value, axis):
+    size = lax.axis_size(axis)
+    pairs = [(i, i + 2) for i in range(0, size - 2, 2)] + [(i, i - 2) for i in range(3, size, 2)]
+    return lax.ppermute(swap(value, axis, 0), axis, pairs)
 
 
 def pack_kernel(count, *refs):
@@ -605,9 +611,10 @@
     )
     cells_x, cells_y, depth = src_p_now.shape
     wide, y_a, y_b, window = pack(blocks, traces, segment_start)
-    y_a, y_b = swap(y_a, "gy", 0), swap(y_b, "gy", 1)
+    y_b = swap(y_b, "gy", 1)
+    y_a = swap(y_a, "gy", 0)
     wide, x_a, x_b = pack_x(wide, window)
-    x_a, x_b = swap(x_a, "gx", 0), swap(x_b, "gx", 1)
+    x_a, x_b = swap(x_a, "gx", 0), swap_far(x_b, "gx")
     windows = jnp.concatenate([window, x_a[x_parts()[1] :, :STEPS, :]], axis=0)
     for bit in bits_of("gx")[1:]:
         windows = doubled(windows, "gx", bit)
@@ -617,7 +624,7 @@
     wide, c_a, c_b = corners(wide, y_a, y_b, windows, pinned(own, pltpu.VMEM))
     for bit in bits_of("gy")[-1:]:
         windows = doubled(windows, "gy", bit)
-    c_a, c_b = swap(c_a, "gx", 0), swap(c_b, "gx", 1)
+    c_a, c_b = swap(c_a, "gx", 0), swap_far(c_b, "gx")
     planes = injected(
         windows, receiver_x, receiver_y, traces.shape[1], cells_x, cells_y, depth
     )

time: 29.5 us -> 35.2 us (1.19); the launches traced: 29.3 us -> 34.6 us
  starting transfers between devices: 17.2 us -> 20.3 us
  waiting for transfers between devices: 0.68 us -> 2.84 us
    ppermute x3, starting transfers between devices: 6.86 us -> 9.56 us  [doubled(): lax.ppermute(windows, axis, pairs)]
    ppermute x0 -> x2, starting transfers between devices: none -> 2.56 us  [swap_far(): return lax.ppermute(swap(value, axis, 0), axis, pairs)]
    ppermute x6, starting transfers between devices: 10.3 us -> 8.22 us  [swap(): return lax.ppermute(value, axis, pairs)]
    ppermute x3, waiting for transfers between devices: 0.66 us -> 2.2 us  [doubled(): lax.ppermute(windows, axis, pairs)]
    ppermute x0 -> x2, waiting for transfers between devices: none -> 0.62 us  [swap_far(): return lax.ppermute(swap(value, axis, 0), axis, pairs)]
  transfers between devices with their start and end apart: 9 -> 11, of which waited for: 1 -> 3; matrix products, arithmetic and copies ran while one was open for 0% -> 0% of each run, Pallas kernels for 16% -> 14%
where the time goes in v11:
time: 35.2 us; the launch traced here: 34.6 us
  starting transfers between devices  20.3 us (58%)
  Pallas kernels  9.9 us (28%)
  waiting for transfers between devices  2.84 us (8%)
  between operations  1.44 us (4%)
    ppermute x3, starting transfers between devices, doubled(): lax.ppermute(windows, axis, pairs)  9.56 us
    ppermute x6, starting transfers between devices, swap(): return lax.ppermute(value, axis, pairs)  8.22 us
    pallas_call x1, Pallas kernels, inner(): pl.pallas_call(inner_kernel, out_shape=[vmem_out(4, *tile)] * STEPS + [vm...  3.72 us
    pallas_call x1, Pallas kernels, outer(): pl.pallas_call(outer_kernel, out_shape=kept + [out] * 3, in_specs=in_vmem...  3.23 us
    ppermute x2, starting transfers between devices, swap_far(): return lax.ppermute(swap(value, axis, 0), axis, pairs)  2.56 us
    ppermute x3, waiting for transfers between devices, doubled(): lax.ppermute(windows, axis, pairs)  2.2 us
    pallas_call x1, Pallas kernels, pack(): pl.pallas_call(functools.partial(pack_kernel, count), out_shape=[wide, ri...  1.8 us
  transfers between devices with their start and end apart: 11, of which 3 were waited for; matrix products, arithmetic and copies ran while one was open for 0% of the time, Pallas kernels for 14%

profile of v11, /device:TPU:1, one launch (start us, length us, event | category | flops | bytes accessed | tf_op | source)
XLA Modules:
  0.0 34.6 jit_solution(8958218102596790404)
XLA Ops:
  1.3 1.8 %pack_y_rims.1 = (f32[13,26,24,128]{3,2,1,0:T(8,128)S(1)}, f32[11,16,4,128]{3,2,1,0:T(4,128)S(1)}, f32[11,16,4,128]{3,2,1,0:T(4,128)S(1)}, f32[1,4,128]{2,1,0:T(4,128)S(1)}) custom-call(f32[16,16,128]{2,1,0:T(8,128)} %refs_0_.1, f32[16,16,128]{2,1,0:T(8,128)} %refs_1_.1, f32[16,16,128]{2,1,0:T(8,128)} %refs_2_.1, f32[16,16,128]{2,1,0:T(8,128)} %refs_3_.1, ...), custom_call_target="tpu_custom_call" | custom-call | tf_op jit(solution)/shard_map/pack_y_rims/pallas_call | solution.py:129
  3.1 0.1 pack_x_rims.1
  3.2 0.1 collective-permute-start.2
  3.3 2.8 %collective-permute-start = (f32[11,16,4,128]{3,2,1,0:T(4,128)S(1)}, f32[11,16,4,128]{3,2,1,0:T(4,128)S(1)}, u32[]{:S(2)}, u32[]{:S(2)}) collective-permute-start(f32[11,16,4,128]{3,2,1,0:T(4,128)S(1)} %get-tuple-element.24), channel_id=1, source_target_pairs={{0,1},{2,3},{1,0},{3,2},{4,5},{6,7},{5,4},{7,6},{8,9},{10,11},{9,8... | collective-permute-start | bytes 1081352 | tf_op jit(solution)/shard_map/ppermute | solution.py:32
  6.0 0.7 %collective-permute-start.1 = (f32[11,16,4,128]{3,2,1,0:T(4,128)S(1)}, f32[11,16,4,128]{3,2,1,0:T(4,128)S(1)}, u32[]{:S(2)}, u32[]{:S(2)}) collective-permute-start(f32[11,16,4,128]{3,2,1,0:T(4,128)S(1)} %get-tuple-element.25), channel_id=1, source_target_pairs={{1,2},{2,1},{5,6},{6,5},{9,10},{10,9},{13,14},{14,13},{17,18},{18,... | collective-permute-start | bytes 1081352 | tf_op jit(solution)/shard_map/ppermute | solution.py:32
  6.7 0.4 %collective-permute-start.5 = (f32[43,16,128]{2,1,0:T(8,128)S(1)}, f32[43,16,128]{2,1,0:T(8,128)S(1)}, u32[]{:S(2)}, u32[]{:S(2)}) collective-permute-start(f32[43,16,128]{2,1,0:T(8,128)S(1)} %get-tuple-element.28), channel_id=1, source_target_pairs={{0,4},{8,12},{4,0},{12,8},{1,5},{9,13},{5,1},{13,9},{2,6},{10,14},... | collective-permute-start | bytes 1056776 | tf_op jit(solution)/shard_map/ppermute | solution.py:32
  7.1 0.0 collective-permute-done.2.refs_1_
  7.2 1.3 %collective-permute-start.3 = (f32[2,4,128]{2,1,0:T(4,128)S(1)}, f32[2,4,128]{2,1,0:T(4,128)S(1)}, u32[]{:S(2)}, u32[]{:S(2)}) collective-permute-start(f32[2,4,128]{2,1,0:T(4,128)S(1)} %pad_maximum_fusion.2), channel_id=1, source_target_pairs={{0,8},{4,12},{8,0},{12,4},{1,9},{5,13},{9,1},{13,5},{2,10},{6,14},... | collective-permute-start | bytes 12296 | tf_op jit(solution)/shard_map/ppermute | solution.py:494
  8.4 1.5 %collective-permute-done.3 = f32[2,4,128]{2,1,0:T(4,128)S(1)} collective-permute-done((f32[2,4,128]{2,1,0:T(4,128)S(1)}, f32[2,4,128]{2,1,0:T(4,128)S(1)}, u32[]{:S(2)}, u32[]{:S(2)}) %collective-permute-start.3) | collective-permute-done | bytes 4128 | tf_op jit(solution)/shard_map/ppermute | solution.py:494
  10.0 4.1 %collective-permute-start.4 = (f32[4,4,128]{2,1,0:T(4,128)S(1)}, f32[4,4,128]{2,1,0:T(4,128)S(1)}, u32[]{:S(2)}, u32[]{:S(2)}) collective-permute-start(f32[4,4,128]{2,1,0:T(4,128)S(1)} %pad_maximum_fusion.1._), channel_id=1, source_target_pairs={{0,1},{1,0},{2,3},{3,2},{4,5},{5,4},{6,7},{7,6},{8,9},{9,8},{10,11... | collective-permute-start | bytes 24584 | tf_op jit(solution)/shard_map/ppermute | solution.py:494
  14.1 0.4 %own_factors.1.___.own = f32[9,16,16,128]{3,2,1,0:T(8,128)S(1)} custom-call(f32[13,26,24,128]{3,2,1,0:T(8,128)S(1)} %get-tuple-element.23.wide._, f32[4,4,128]{2,1,0:T(4,128)S(1)} %pad_maximum_fusion.1._), custom_call_target="tpu_custom_call" | custom-call | tf_op jit(solution)/shard_map/own_factors/pallas_call | solution.py:265
  14.5 0.7 %collective-permute-done.4 = f32[4,4,128]{2,1,0:T(4,128)S(1)} collective-permute-done((f32[4,4,128]{2,1,0:T(4,128)S(1)}, f32[4,4,128]{2,1,0:T(4,128)S(1)}, u32[]{:S(2)}, u32[]{:S(2)}) %collective-permute-start.4) | collective-permute-done | bytes 8224 | tf_op jit(solution)/shard_map/ppermute | solution.py:494
  15.1 0.0 copy-start
  15.1 0.0 copy-start.1
  15.1 0.0 collective-permute-done.y_a
  15.2 0.0 collective-permute-done.1.y_b
  15.2 0.2 pack_corners.1
  15.4 1.8 %collective-permute-start.8 = (f32[43,8,128]{2,1,0:T(8,128)S(1)}, f32[43,8,128]{2,1,0:T(8,128)S(1)}, u32[]{:S(2)}, u32[]{:S(2)}) collective-permute-start(f32[43,8,128]{2,1,0:T(8,128)S(1)} %get-tuple-element.30), channel_id=1, source_target_pairs={{0,4},{8,12},{4,0},{12,8},{1,5},{9,13},{5,1},{13,9},{2,6},{10,14},... | collective-permute-start | bytes 528392 | tf_op jit(solution)/shard_map/ppermute | solution.py:32
  17.2 0.0 collective-permute-done.5
  17.2 1.3 %collective-permute-start.6 = (f32[43,16,128]{2,1,0:T(8,128)S(1)}, f32[43,16,128]{2,1,0:T(8,128)S(1)}, u32[]{:S(2)}, u32[]{:S(2)}) collective-permute-start(f32[43,16,128]{2,1,0:T(8,128)S(1)} %collective-permute-done.5), channel_id=1, source_target_pairs={{0,8},{12,4},{1,9},{13,5},{2,10},{14,6},{3,11},{15,7},{16,24},{28,... | collective-permute-start | bytes 1056776 | tf_op jit(solution)/shard_map/ppermute | solution.py:84
  18.5 4.2 %collective-permute-start.10 = (f32[8,4,128]{2,1,0:T(4,128)S(1)}, f32[8,4,128]{2,1,0:T(4,128)S(1)}, u32[]{:S(2)}, u32[]{:S(2)}) collective-permute-start(f32[8,4,128]{2,1,0:T(4,128)S(1)} %pad_maximum_fusion.__), channel_id=1, source_target_pairs={{0,2},{1,3},{2,0},{3,1},{4,6},{5,7},{6,4},{7,5},{8,10},{9,11},{10,... | collective-permute-start | bytes 49160 | tf_op jit(solution)/shard_map/ppermute | solution.py:494
  22.7 2.4 %collective-permute-start.7 = (f32[43,8,128]{2,1,0:T(8,128)S(1)}, f32[43,8,128]{2,1,0:T(8,128)S(1)}, u32[]{:S(2)}, u32[]{:S(2)}) collective-permute-start(f32[43,8,128]{2,1,0:T(8,128)S(1)} %get-tuple-element.29), channel_id=1, source_target_pairs={{0,4},{8,12},{4,0},{12,8},{1,5},{9,13},{5,1},{13,9},{2,6},{10,14},... | collective-permute-start | bytes 528392 | tf_op jit(solution)/shard_map/ppermute | solution.py:32
  25.2 0.0 collective-permute-done.8
  25.2 1.3 %collective-permute-start.9 = (f32[43,8,128]{2,1,0:T(8,128)S(1)}, f32[43,8,128]{2,1,0:T(8,128)S(1)}, u32[]{:S(2)}, u32[]{:S(2)}) collective-permute-start(f32[43,8,128]{2,1,0:T(8,128)S(1)} %collective-permute-done.8), channel_id=1, source_target_pairs={{0,8},{12,4},{1,9},{13,5},{2,10},{14,6},{3,11},{15,7},{16,24},{28,... | collective-permute-start | bytes 528392 | tf_op jit(solution)/shard_map/ppermute | solution.py:84
  26.5 0.0 collective-permute-done.10
  26.5 0.0 copy-done
  26.5 0.0 copy-done.1
  26.5 0.5 %inject.1.planes.refs_5_ = f32[4,3,8,128]{3,2,1,0:T(8,128)S(1)} custom-call(f32[16,4,128]{2,1,0:T(4,128)S(1)} %constant_dynamic-update-slice_fusion.gathered, s32[8,128]{1,0:T(8,128)S(1)} %bitcast.2, s32[8,128]{1,0:T(8,128)S(1)} %bitcast.3), custom_call_target="tpu_custom_call" | custom-call | tf_op jit(solution)/shard_map/inject/pallas_call | solution.py:564
  27.0 3.7 %inner_steps.1 = (f32[4,26,3,8,128]{4,3,2,1,0:T(8,128)S(1)}, f32[4,26,3,8,128]{4,3,2,1,0:T(8,128)S(1)}, f32[4,26,3,8,128]{4,3,2,1,0:T(8,128)S(1)}, f32[4,26,3,8,...) custom-call(f32[13,26,24,128]{3,2,1,0:T(8,128)S(1)} %get-tuple-element.27.wide.refs_0_, ...), custom_call_target="tpu_custom_call" | custom-call | tf_op jit(solution)/shard_map/inner_steps/pallas_call | solution.py:455
  30.7 0.0 collective-permute-done.7.refs_3_
  30.7 0.0 collective-permute-done.6.refs_2_
  30.7 0.6 %collective-permute-done.9.refs_4_ = f32[43,8,128]{2,1,0:T(8,128)S(1)} collective-permute-done((f32[43,8,128]{2,1,0:T(8,128)S(1)}, f32[43,8,128]{2,1,0:T(8,128)S(1)}, u32[]{:S(2)}, u32[]{:S(2)}) %collective-permute-start.9) | collective-permute-done | bytes 176160 | tf_op jit(solution)/shard_map/ppermute | solution.py:84
  31.3 3.2 %outer_steps.1 = (f32[13,26,24,128]{3,2,1,0:T(8,128)S(1)}, f32[4,26,3,8,128]{4,3,2,1,0:T(8,128)S(1)}, f32[4,26,3,8,128]{4,3,2,1,0:T(8,128)S(1)}, f32[4,26,3,8,12...) custom-call(f32[13,26,24,128]{3,2,1,0:T(8,128)S(1)} %get-tuple-eleme, ...), custom_call_target="tpu_custom_call", output_to_operand_aliasing={{0}: (0, {}), {1}: (6, {}), {2}: (7, {}), {3}: (8, {}), {4}... | custom-call | tf_op jit(solution)/shard_map/outer_steps/pallas_call | solution.py:471
  (8 shorter events, 0.1 us)
Async XLA Ops:
  3.2 4.0 %collective-permute-start.2 = (f32[44,16,128]{2,1,0:T(8,128)S(1)}, f32[44,16,128]{2,1,0:T(8,128)S(1)}, u32[]{:S(2)}, u32[]{:S(2)}) collective-permute-start(f32[44,16,128]{2,1,0:T(8,128)S(1)} %get-tuple-element.26), channel_id=1, source_target_pairs={{0,4},{8,12},{4,0},{12,8},{1,5},{9,13},{5,1},{13,9},{2,6},{10,14},... | collective-permute-start | bytes 1081352 | tf_op jit(solution)/shard_map/ppermute | solution.py:32
  3.3 11.9 %collective-permute-start = (f32[11,16,4,128]{3,2,1,0:T(4,128)S(1)}, f32[11,16,4,128]{3,2,1,0:T(4,128)S(1)}, u32[]{:S(2)}, u32[]{:S(2)}) collective-permute-start(f32[11,16,4,128]{3,2,1,0:T(4,128)S(1)} %get-tuple-element.24), channel_id=1, source_target_pairs={{0,1},{2,3},{1,0},{3,2},{4,5},{6,7},{5,4},{7,6},{8,9},{10,11},{9,8... | collective-permute-start | bytes 1081352 | tf_op jit(solution)/shard_map/ppermute | solution.py:32
  6.0 9.1 %collective-permute-start.1 = (f32[11,16,4,128]{3,2,1,0:T(4,128)S(1)}, f32[11,16,4,128]{3,2,1,0:T(4,128)S(1)}, u32[]{:S(2)}, u32[]{:S(2)}) collective-permute-start(f32[11,16,4,128]{3,2,1,0:T(4,128)S(1)} %get-tuple-element.25), channel_id=1, source_target_pairs={{1,2},{2,1},{5,6},{6,5},{9,10},{10,9},{13,14},{14,13},{17,18},{18,... | collective-permute-start | bytes 1081352 | tf_op jit(solution)/shard_map/ppermute | solution.py:32
  6.7 10.5 %collective-permute-start.5 = (f32[43,16,128]{2,1,0:T(8,128)S(1)}, f32[43,16,128]{2,1,0:T(8,128)S(1)}, u32[]{:S(2)}, u32[]{:S(2)}) collective-permute-start(f32[43,16,128]{2,1,0:T(8,128)S(1)} %get-tuple-element.28), channel_id=1, source_target_pairs={{0,4},{8,12},{4,0},{12,8},{1,5},{9,13},{5,1},{13,9},{2,6},{10,14},... | collective-permute-start | bytes 1056776 | tf_op jit(solution)/shard_map/ppermute | solution.py:32
  7.2 2.8 %collective-permute-start.3 = (f32[2,4,128]{2,1,0:T(4,128)S(1)}, f32[2,4,128]{2,1,0:T(4,128)S(1)}, u32[]{:S(2)}, u32[]{:S(2)}) collective-permute-start(f32[2,4,128]{2,1,0:T(4,128)S(1)} %pad_maximum_fusion.2), channel_id=1, source_target_pairs={{0,8},{4,12},{8,0},{12,4},{1,9},{5,13},{9,1},{13,5},{2,10},{6,14},... | collective-permute-start | bytes 12296 | tf_op jit(solution)/shard_map/ppermute | solution.py:494
  10.0 5.1 %collective-permute-start.4 = (f32[4,4,128]{2,1,0:T(4,128)S(1)}, f32[4,4,128]{2,1,0:T(4,128)S(1)}, u32[]{:S(2)}, u32[]{:S(2)}) collective-permute-start(f32[4,4,128]{2,1,0:T(4,128)S(1)} %pad_maximum_fusion.1._), channel_id=1, source_target_pairs={{0,1},{1,0},{2,3},{3,2},{4,5},{5,4},{6,7},{7,6},{8,9},{9,8},{10,11... | collective-permute-start | bytes 24584 | tf_op jit(solution)/shard_map/ppermute | solution.py:494
  15.1 11.4 %copy-start = (s32[1024]{0:T(1024)S(1)}, s32[1024]{0:T(1024)}, u32[]{:S(2)}) copy-start(s32[1024]{0:T(1024)} %param.31) | copy-start | bytes 12292
  15.1 11.4 %copy-start.1 = (s32[1024]{0:T(1024)S(1)}, s32[1024]{0:T(1024)}, u32[]{:S(2)}) copy-start(s32[1024]{0:T(1024)} %param.32) | copy-start | bytes 12292
  15.4 9.8 %collective-permute-start.8 = (f32[43,8,128]{2,1,0:T(8,128)S(1)}, f32[43,8,128]{2,1,0:T(8,128)S(1)}, u32[]{:S(2)}, u32[]{:S(2)}) collective-permute-start(f32[43,8,128]{2,1,0:T(8,128)S(1)} %get-tuple-element.30), channel_id=1, source_target_pairs={{0,4},{8,12},{4,0},{12,8},{1,5},{9,13},{5,1},{13,9},{2,6},{10,14},... | collective-permute-start | bytes 528392 | tf_op jit(solution)/shard_map/ppermute | solution.py:32
  17.2 13.5 %collective-permute-start.6 = (f32[43,16,128]{2,1,0:T(8,128)S(1)}, f32[43,16,128]{2,1,0:T(8,128)S(1)}, u32[]{:S(2)}, u32[]{:S(2)}) collective-permute-start(f32[43,16,128]{2,1,0:T(8,128)S(1)} %collective-permute-done.5), channel_id=1, source_target_pairs={{0,8},{12,4},{1,9},{13,5},{2,10},{14,6},{3,11},{15,7},{16,24},{28,... | collective-permute-start | bytes 1056776 | tf_op jit(solution)/shard_map/ppermute | solution.py:84
  18.5 7.9 %collective-permute-start.10 = (f32[8,4,128]{2,1,0:T(4,128)S(1)}, f32[8,4,128]{2,1,0:T(4,128)S(1)}, u32[]{:S(2)}, u32[]{:S(2)}) collective-permute-start(f32[8,4,128]{2,1,0:T(4,128)S(1)} %pad_maximum_fusion.__), channel_id=1, source_target_pairs={{0,2},{1,3},{2,0},{3,1},{4,6},{5,7},{6,4},{7,5},{8,10},{9,11},{10,... | collective-permute-start | bytes 49160 | tf_op jit(solution)/shard_map/ppermute | solution.py:494
  22.7 8.0 %collective-permute-start.7 = (f32[43,8,128]{2,1,0:T(8,128)S(1)}, f32[43,8,128]{2,1,0:T(8,128)S(1)}, u32[]{:S(2)}, u32[]{:S(2)}) collective-permute-start(f32[43,8,128]{2,1,0:T(8,128)S(1)} %get-tuple-element.29), channel_id=1, source_target_pairs={{0,4},{8,12},{4,0},{12,8},{1,5},{9,13},{5,1},{13,9},{2,6},{10,14},... | collective-permute-start | bytes 528392 | tf_op jit(solution)/shard_map/ppermute | solution.py:32
  25.2 6.2 %collective-permute-start.9 = (f32[43,8,128]{2,1,0:T(8,128)S(1)}, f32[43,8,128]{2,1,0:T(8,128)S(1)}, u32[]{:S(2)}, u32[]{:S(2)}) collective-permute-start(f32[43,8,128]{2,1,0:T(8,128)S(1)} %collective-permute-done.8), channel_id=1, source_target_pairs={{0,8},{12,4},{1,9},{13,5},{2,10},{14,6},{3,11},{15,7},{16,24},{28,... | collective-permute-start | bytes 528392 | tf_op jit(solution)/shard_map/ppermute | solution.py:84

commit v12 on v11

--- a/solution.py
+++ b/solution.py
@@ -611,10 +611,9 @@
     )
     cells_x, cells_y, depth = src_p_now.shape
     wide, y_a, y_b, window = pack(blocks, traces, segment_start)
-    y_b = swap(y_b, "gy", 1)
-    y_a = swap(y_a, "gy", 0)
+    y_a, y_b = swap(y_a, "gy", 0), swap(y_b, "gy", 1)
     wide, x_a, x_b = pack_x(wide, window)
-    x_a, x_b = swap(x_a, "gx", 0), swap_far(x_b, "gx")
+    x_a, x_b = swap(x_a, "gx", 0), swap(x_b, "gx", 1)
     windows = jnp.concatenate([window, x_a[x_parts()[1] :, :STEPS, :]], axis=0)
     for bit in bits_of("gx")[1:]:
         windows = doubled(windows, "gx", bit)

time: 35.2 us -> 35.4 us (level)
  the two profiles are of different devices: /device:TPU:1 before, /device:TPU:0 now
where the time goes in v12:
time: 35.4 us; the launch traced here: 35.2 us
  starting transfers between devices  20.3 us (57%)
  Pallas kernels  9.91 us (28%)
  waiting for transfers between devices  3.39 us (10%)
  between operations  1.48 us (4%)
    ppermute x3, starting transfers between devices, doubled(): lax.ppermute(windows, axis, pairs)  10.5 us
    ppermute x6, starting transfers between devices, swap(): return lax.ppermute(value, axis, pairs)  7.15 us
    pallas_call x1, Pallas kernels, inner(): pl.pallas_call(inner_kernel, out_shape=[vmem_out(4, *tile)] * STEPS + [vm...  3.72 us
    ppermute x3, waiting for transfers between devices, doubled(): lax.ppermute(windows, axis, pairs)  3.37 us
    pallas_call x1, Pallas kernels, outer(): pl.pallas_call(outer_kernel, out_shape=kept + [out] * 3, in_specs=in_vmem...  3.25 us
    ppermute x1, starting transfers between devices, swap_far(): return lax.ppermute(swap(value, axis, 0), axis, pairs)  2.7 us
    pallas_call x1, Pallas kernels, pack(): pl.pallas_call(functools.partial(pack_kernel, count), out_shape=[wide, ri...  1.8 us
  transfers between devices with their start and end apart: 10, of which 2 were waited for; matrix products, arithmetic and copies ran while one was open for 0% of the time, Pallas kernels for 13%

profile of v12, /device:TPU:0, one launch (start us, length us, event | category | flops | bytes accessed | tf_op | source)
XLA Modules:
  0.0 35.2 jit_solution(17459776565841442168)
XLA Ops:
  1.3 1.8 %pack_y_rims.1 = (f32[13,26,24,128]{3,2,1,0:T(8,128)S(1)}, f32[11,16,4,128]{3,2,1,0:T(4,128)S(1)}, f32[11,16,4,128]{3,2,1,0:T(4,128)S(1)}, f32[1,4,128]{2,1,0:T(4,128)S(1)}) custom-call(f32[16,16,128]{2,1,0:T(8,128)} %refs_0_.1, f32[16,16,128]{2,1,0:T(8,128)} %refs_1_.1, f32[16,16,128]{2,1,0:T(8,128)} %refs_2_.1, f32[16,16,128]{2,1,0:T(8,128)} %refs_3_.1, ...), custom_call_target="tpu_custom_call" | custom-call | tf_op jit(solution)/shard_map/pack_y_rims/pallas_call | solution.py:129
  3.1 0.1 pack_x_rims.1
  3.2 0.5 %collective-permute-start.2 = (f32[44,16,128]{2,1,0:T(8,128)S(1)}, f32[44,16,128]{2,1,0:T(8,128)S(1)}, u32[]{:S(2)}, u32[]{:S(2)}) collective-permute-start(f32[44,16,128]{2,1,0:T(8,128)S(1)} %get-tuple-element.26), channel_id=1, source_target_pairs={{0,4},{8,12},{4,0},{12,8},{1,5},{9,13},{5,1},{13,9},{2,6},{10,14},... | collective-permute-start | bytes 1081352 | tf_op jit(solution)/shard_map/ppermute | solution.py:32
  3.7 2.7 %collective-permute-start = (f32[11,16,4,128]{3,2,1,0:T(4,128)S(1)}, f32[11,16,4,128]{3,2,1,0:T(4,128)S(1)}, u32[]{:S(2)}, u32[]{:S(2)}) collective-permute-start(f32[11,16,4,128]{3,2,1,0:T(4,128)S(1)} %get-tuple-element.24), channel_id=1, source_target_pairs={{0,1},{2,3},{1,0},{3,2},{4,5},{6,7},{5,4},{7,6},{8,9},{10,11},{9,8... | collective-permute-start | bytes 1081352 | tf_op jit(solution)/shard_map/ppermute | solution.py:32
  6.3 0.7 %collective-permute-start.1 = (f32[11,16,4,128]{3,2,1,0:T(4,128)S(1)}, f32[11,16,4,128]{3,2,1,0:T(4,128)S(1)}, u32[]{:S(2)}, u32[]{:S(2)}) collective-permute-start(f32[11,16,4,128]{3,2,1,0:T(4,128)S(1)} %get-tuple-element.25), channel_id=1, source_target_pairs={{1,2},{2,1},{5,6},{6,5},{9,10},{10,9},{13,14},{14,13},{17,18},{18,... | collective-permute-start | bytes 1081352 | tf_op jit(solution)/shard_map/ppermute | solution.py:32
  7.0 0.0 collective-permute-done.2.refs_1_
  7.1 1.6 %collective-permute-start.3 = (f32[2,4,128]{2,1,0:T(4,128)S(1)}, f32[2,4,128]{2,1,0:T(4,128)S(1)}, u32[]{:S(2)}, u32[]{:S(2)}) collective-permute-start(f32[2,4,128]{2,1,0:T(4,128)S(1)} %pad_maximum_fusion.2), channel_id=1, source_target_pairs={{0,8},{4,12},{8,0},{12,4},{1,9},{5,13},{9,1},{13,5},{2,10},{6,14},... | collective-permute-start | bytes 12296 | tf_op jit(solution)/shard_map/ppermute | solution.py:494
  8.6 2.1 %collective-permute-done.3 = f32[2,4,128]{2,1,0:T(4,128)S(1)} collective-permute-done((f32[2,4,128]{2,1,0:T(4,128)S(1)}, f32[2,4,128]{2,1,0:T(4,128)S(1)}, u32[]{:S(2)}, u32[]{:S(2)}) %collective-permute-start.3) | collective-permute-done | bytes 4128 | tf_op jit(solution)/shard_map/ppermute | solution.py:494
  10.7 4.4 %collective-permute-start.4 = (f32[4,4,128]{2,1,0:T(4,128)S(1)}, f32[4,4,128]{2,1,0:T(4,128)S(1)}, u32[]{:S(2)}, u32[]{:S(2)}) collective-permute-start(f32[4,4,128]{2,1,0:T(4,128)S(1)} %pad_maximum_fusion.1._), channel_id=1, source_target_pairs={{0,1},{1,0},{2,3},{3,2},{4,5},{5,4},{6,7},{7,6},{8,9},{9,8},{10,11... | collective-permute-start | bytes 24584 | tf_op jit(solution)/shard_map/ppermute | solution.py:494
  15.1 0.4 %own_factors.1.___.own = f32[9,16,16,128]{3,2,1,0:T(8,128)S(1)} custom-call(f32[13,26,24,128]{3,2,1,0:T(8,128)S(1)} %get-tuple-element.23.wide._, f32[4,4,128]{2,1,0:T(4,128)S(1)} %pad_maximum_fusion.1._), custom_call_target="tpu_custom_call" | custom-call | tf_op jit(solution)/shard_map/own_factors/pallas_call | solution.py:265
  15.5 1.3 %collective-permute-done.4 = f32[4,4,128]{2,1,0:T(4,128)S(1)} collective-permute-done((f32[4,4,128]{2,1,0:T(4,128)S(1)}, f32[4,4,128]{2,1,0:T(4,128)S(1)}, u32[]{:S(2)}, u32[]{:S(2)}) %collective-permute-start.4) | collective-permute-done | bytes 8224 | tf_op jit(solution)/shard_map/ppermute | solution.py:494
  16.7 0.0 copy-start
  16.8 0.0 copy-start.1
  16.8 0.0 collective-permute-done.y_a
  16.8 0.0 collective-permute-done.1.y_b
  16.8 0.2 pack_corners.1
  17.0 0.1 collective-permute-start.7
  17.1 0.7 %collective-permute-start.5 = (f32[43,16,128]{2,1,0:T(8,128)S(1)}, f32[43,16,128]{2,1,0:T(8,128)S(1)}, u32[]{:S(2)}, u32[]{:S(2)}) collective-permute-start(f32[43,16,128]{2,1,0:T(8,128)S(1)} %get-tuple-element.28), channel_id=1, source_target_pairs={{4,8},{8,4},{5,9},{9,5},{6,10},{10,6},{7,11},{11,7},{20,24},{24,20... | collective-permute-start | bytes 1056776 | tf_op jit(solution)/shard_map/ppermute | solution.py:32
  17.8 4.5 %collective-permute-start.9 = (f32[8,4,128]{2,1,0:T(4,128)S(1)}, f32[8,4,128]{2,1,0:T(4,128)S(1)}, u32[]{:S(2)}, u32[]{:S(2)}) collective-permute-start(f32[8,4,128]{2,1,0:T(4,128)S(1)} %pad_maximum_fusion.__), channel_id=1, source_target_pairs={{0,2},{1,3},{2,0},{3,1},{4,6},{5,7},{6,4},{7,5},{8,10},{9,11},{10,... | collective-permute-start | bytes 49160 | tf_op jit(solution)/shard_map/ppermute | solution.py:494
  22.4 2.6 %collective-permute-start.6 = (f32[43,8,128]{2,1,0:T(8,128)S(1)}, f32[43,8,128]{2,1,0:T(8,128)S(1)}, u32[]{:S(2)}, u32[]{:S(2)}) collective-permute-start(f32[43,8,128]{2,1,0:T(8,128)S(1)} %get-tuple-element.29), channel_id=1, source_target_pairs={{0,4},{8,12},{4,0},{12,8},{1,5},{9,13},{5,1},{13,9},{2,6},{10,14},... | collective-permute-start | bytes 528392 | tf_op jit(solution)/shard_map/ppermute | solution.py:32
  24.9 0.0 collective-permute-done.7
  24.9 2.7 %collective-permute-start.8 = (f32[43,8,128]{2,1,0:T(8,128)S(1)}, f32[43,8,128]{2,1,0:T(8,128)S(1)}, u32[]{:S(2)}, u32[]{:S(2)}) collective-permute-start(f32[43,8,128]{2,1,0:T(8,128)S(1)} %collective-permute-done.7), channel_id=1, source_target_pairs={{0,8},{12,4},{1,9},{13,5},{2,10},{14,6},{3,11},{15,7},{16,24},{28,... | collective-permute-start | bytes 528392 | tf_op jit(solution)/shard_map/ppermute | solution.py:84
  27.6 0.0 collective-permute-done.9
  27.7 0.0 copy-done
  27.7 0.0 copy-done.1
  27.7 0.5 %inject.1.planes.refs_5_ = f32[4,3,8,128]{3,2,1,0:T(8,128)S(1)} custom-call(f32[16,4,128]{2,1,0:T(4,128)S(1)} %constant_dynamic-update-slice_fusion.gathered, s32[8,128]{1,0:T(8,128)S(1)} %bitcast.2, s32[8,128]{1,0:T(8,128)S(1)} %bitcast.3), custom_call_target="tpu_custom_call" | custom-call | tf_op jit(solution)/shard_map/inject/pallas_call | solution.py:564
  28.1 3.7 %inner_steps.1 = (f32[4,26,3,8,128]{4,3,2,1,0:T(8,128)S(1)}, f32[4,26,3,8,128]{4,3,2,1,0:T(8,128)S(1)}, f32[4,26,3,8,128]{4,3,2,1,0:T(8,128)S(1)}, f32[4,26,3,8,...) custom-call(f32[13,26,24,128]{3,2,1,0:T(8,128)S(1)} %get-tuple-element.27.wide.refs_0_, ...), custom_call_target="tpu_custom_call" | custom-call | tf_op jit(solution)/shard_map/inner_steps/pallas_call | solution.py:455
  31.9 0.0 collective-permute-done.5.refs_2_
  31.9 0.0 collective-permute-done.6.refs_3_
  31.9 0.0 collective-permute-done.8.refs_4_
  31.9 3.3 %outer_steps.1 = (f32[13,26,24,128]{3,2,1,0:T(8,128)S(1)}, f32[4,26,3,8,128]{4,3,2,1,0:T(8,128)S(1)}, f32[4,26,3,8,128]{4,3,2,1,0:T(8,128)S(1)}, f32[4,26,3,8,12...) custom-call(f32[13,26,24,128]{3,2,1,0:T(8,128)S(1)} %get-tuple-eleme, ...), custom_call_target="tpu_custom_call", output_to_operand_aliasing={{0}: (0, {}), {1}: (6, {}), {2}: (7, {}), {3}: (8, {}), {4}... | custom-call | tf_op jit(solution)/shard_map/outer_steps/pallas_call | solution.py:471
  (8 shorter events, 0.1 us)
Async XLA Ops:
  3.2 3.9 %collective-permute-start.2 = (f32[44,16,128]{2,1,0:T(8,128)S(1)}, f32[44,16,128]{2,1,0:T(8,128)S(1)}, u32[]{:S(2)}, u32[]{:S(2)}) collective-permute-start(f32[44,16,128]{2,1,0:T(8,128)S(1)} %get-tuple-element.26), channel_id=1, source_target_pairs={{0,4},{8,12},{4,0},{12,8},{1,5},{9,13},{5,1},{13,9},{2,6},{10,14},... | collective-permute-start | bytes 1081352 | tf_op jit(solution)/shard_map/ppermute | solution.py:32
  3.7 13.1 %collective-permute-start = (f32[11,16,4,128]{3,2,1,0:T(4,128)S(1)}, f32[11,16,4,128]{3,2,1,0:T(4,128)S(1)}, u32[]{:S(2)}, u32[]{:S(2)}) collective-permute-start(f32[11,16,4,128]{3,2,1,0:T(4,128)S(1)} %get-tuple-element.24), channel_id=1, source_target_pairs={{0,1},{2,3},{1,0},{3,2},{4,5},{6,7},{5,4},{7,6},{8,9},{10,11},{9,8... | collective-permute-start | bytes 1081352 | tf_op jit(solution)/shard_map/ppermute | solution.py:32
  6.3 10.4 %collective-permute-start.1 = (f32[11,16,4,128]{3,2,1,0:T(4,128)S(1)}, f32[11,16,4,128]{3,2,1,0:T(4,128)S(1)}, u32[]{:S(2)}, u32[]{:S(2)}) collective-permute-start(f32[11,16,4,128]{3,2,1,0:T(4,128)S(1)} %get-tuple-element.25), channel_id=1, source_target_pairs={{1,2},{2,1},{5,6},{6,5},{9,10},{10,9},{13,14},{14,13},{17,18},{18,... | collective-permute-start | bytes 1081352 | tf_op jit(solution)/shard_map/ppermute | solution.py:32
  7.1 3.7 %collective-permute-start.3 = (f32[2,4,128]{2,1,0:T(4,128)S(1)}, f32[2,4,128]{2,1,0:T(4,128)S(1)}, u32[]{:S(2)}, u32[]{:S(2)}) collective-permute-start(f32[2,4,128]{2,1,0:T(4,128)S(1)} %pad_maximum_fusion.2), channel_id=1, source_target_pairs={{0,8},{4,12},{8,0},{12,4},{1,9},{5,13},{9,1},{13,5},{2,10},{6,14},... | collective-permute-start | bytes 12296 | tf_op jit(solution)/shard_map/ppermute | solution.py:494
  10.7 6.0 %collective-permute-start.4 = (f32[4,4,128]{2,1,0:T(4,128)S(1)}, f32[4,4,128]{2,1,0:T(4,128)S(1)}, u32[]{:S(2)}, u32[]{:S(2)}) collective-permute-start(f32[4,4,128]{2,1,0:T(4,128)S(1)} %pad_maximum_fusion.1._), channel_id=1, source_target_pairs={{0,1},{1,0},{2,3},{3,2},{4,5},{5,4},{6,7},{7,6},{8,9},{9,8},{10,11... | collective-permute-start | bytes 24584 | tf_op jit(solution)/shard_map/ppermute | solution.py:494
  16.7 10.9 %copy-start = (s32[1024]{0:T(1024)S(1)}, s32[1024]{0:T(1024)}, u32[]{:S(2)}) copy-start(s32[1024]{0:T(1024)} %param.31) | copy-start | bytes 12292
  16.8 10.9 %copy-start.1 = (s32[1024]{0:T(1024)S(1)}, s32[1024]{0:T(1024)}, u32[]{:S(2)}) copy-start(s32[1024]{0:T(1024)} %param.32) | copy-start | bytes 12292
  17.0 7.9 %collective-permute-start.7 = (f32[43,8,128]{2,1,0:T(8,128)S(1)}, f32[43,8,128]{2,1,0:T(8,128)S(1)}, u32[]{:S(2)}, u32[]{:S(2)}) collective-permute-start(f32[43,8,128]{2,1,0:T(8,128)S(1)} %get-tuple-element.30), channel_id=1, source_target_pairs={{0,4},{8,12},{4,0},{12,8},{1,5},{9,13},{5,1},{13,9},{2,6},{10,14},... | collective-permute-start | bytes 528392 | tf_op jit(solution)/shard_map/ppermute | solution.py:32
  17.1 14.8 %collective-permute-start.5 = (f32[43,16,128]{2,1,0:T(8,128)S(1)}, f32[43,16,128]{2,1,0:T(8,128)S(1)}, u32[]{:S(2)}, u32[]{:S(2)}) collective-permute-start(f32[43,16,128]{2,1,0:T(8,128)S(1)} %get-tuple-element.28), channel_id=1, source_target_pairs={{4,8},{8,4},{5,9},{9,5},{6,10},{10,6},{7,11},{11,7},{20,24},{24,20... | collective-permute-start | bytes 1056776 | tf_op jit(solution)/shard_map/ppermute | solution.py:32
  17.8 9.8 %collective-permute-start.9 = (f32[8,4,128]{2,1,0:T(4,128)S(1)}, f32[8,4,128]{2,1,0:T(4,128)S(1)}, u32[]{:S(2)}, u32[]{:S(2)}) collective-permute-start(f32[8,4,128]{2,1,0:T(4,128)S(1)} %pad_maximum_fusion.__), channel_id=1, source_target_pairs={{0,2},{1,3},{2,0},{3,1},{4,6},{5,7},{6,4},{7,5},{8,10},{9,11},{10,... | collective-permute-start | bytes 49160 | tf_op jit(solution)/shard_map/ppermute | solution.py:494
  22.4 9.5 %collective-permute-start.6 = (f32[43,8,128]{2,1,0:T(8,128)S(1)}, f32[43,8,128]{2,1,0:T(8,128)S(1)}, u32[]{:S(2)}, u32[]{:S(2)}) collective-permute-start(f32[43,8,128]{2,1,0:T(8,128)S(1)} %get-tuple-element.29), channel_id=1, source_target_pairs={{0,4},{8,12},{4,0},{12,8},{1,5},{9,13},{5,1},{13,9},{2,6},{10,14},... | collective-permute-start | bytes 528392 | tf_op jit(solution)/shard_map/ppermute | solution.py:32
  24.9 7.0 %collective-permute-start.8 = (f32[43,8,128]{2,1,0:T(8,128)S(1)}, f32[43,8,128]{2,1,0:T(8,128)S(1)}, u32[]{:S(2)}, u32[]{:S(2)}) collective-permute-start(f32[43,8,128]{2,1,0:T(8,128)S(1)} %collective-permute-done.7), channel_id=1, source_target_pairs={{0,8},{12,4},{1,9},{13,5},{2,10},{14,6},{3,11},{15,7},{16,24},{28,... | collective-permute-start | bytes 528392 | tf_op jit(solution)/shard_map/ppermute | solution.py:84

commit v13 on v12

--- a/solution.py
+++ b/solution.py
@@ -78,10 +78,10 @@
     return pltpu.VMEM(shape, jnp.float32)
 
 
-def swap_far(value, axis):
+def hand_on(value, axis):
     size = lax.axis_size(axis)
     pairs = [(i, i + 2) for i in range(0, size - 2, 2)] + [(i, i - 2) for i in range(3, size, 2)]
-    return lax.ppermute(swap(value, axis, 0), axis, pairs)
+    return lax.ppermute(value, axis, pairs)
 
 
 def pack_kernel(count, *refs):
@@ -171,7 +171,7 @@
     )(pinned(wide, pltpu.VMEM), window)
 
 
-def corner_kernel(_, y_a, y_b, __, ___, wide, c_a, c_b):
+def corner_kernel(_, y_a, y_b, __, ___, ____, wide, c_a, c_b):
     cells_x = y_a.shape[1]
     cells_y = wide.shape[2] - 2 * RIM
     odd_x, odd_y = is_odd("gx"), is_odd("gy")
@@ -202,7 +202,7 @@
     return pl.pallas_call(
         corner_kernel,
         out_shape=[vmem_out(*wide.shape), corner, corner],
-        in_specs=in_vmem(5),
+        in_specs=in_vmem(6),
         out_specs=in_vmem(3),
         input_output_aliases={0: 0},
         compiler_params=PARAMS,
@@ -373,10 +373,9 @@
     lax.fori_loop(0, count, run, 0)
 
 
-def inner_kernel(wide, planes, own, *refs):
-    steps = Steps(wide, planes, refs[:STEPS], refs[STEPS])
-    natural = refs[STEPS + 1]
-    cells_x, cells_y, tiles = steps.cells_x, own.shape[2], steps.tiles
+def order_kernel(wide, own, factors, natural):
+    _, cells_x, cells_y, _ = own.shape
+    tiles = factors.shape[2]
 
     def rim_rows(i):
         for x in [4 * i + k for k in range(4)]:
@@ -389,12 +388,30 @@
         for x in [2 * i + k for k in range(2)]:
             for number in range(FACTORS):
                 for tile in range(tiles):
-                    steps.factors[number, RIM + x, tile] = natural[
+                    factors[number, RIM + x, tile] = natural[
                         number, x, pl.ds(tile, SUBLANES, stride=tiles), :
                     ]
 
     repeat(cells_x // 4, rim_rows)
     repeat(cells_x // 2, in_step_order)
+
+
+def ordered_factors(wide, own):
+    _, planes_x, rows, depth = wide.shape
+    return pl.pallas_call(
+        order_kernel,
+        out_shape=vmem_out(FACTORS, planes_x, rows // SUBLANES, SUBLANES, depth),
+        in_specs=in_vmem(2),
+        out_specs=in_vmem(1)[0],
+        scratch_shapes=[pltpu.VMEM((FACTORS, own.shape[1], rows, depth), jnp.float32)],
+        compiler_params=PARAMS,
+        name="order_factors",
+    )(pinned(wide, pltpu.VMEM), pinned(own, pltpu.VMEM))
+
+
+def inner_kernel(wide, planes, factors, *waves):
+    steps = Steps(wide, planes, waves, factors)
+    cells_x = steps.cells_x
     for turn in range(STEPS):
         first, last = RIM + 1 + turn, RIM + cells_x - 1 - turn
         half = (last - first) // 2
@@ -449,18 +466,16 @@
         ref[...] = wide[out, RIM : RIM + cells_x, :cells_y, :]
 
 
-def inner(wide, planes, own):
+def inner(wide, planes, factors):
     _, planes_x, rows, depth = wide.shape
-    tile = (planes_x, rows // SUBLANES, SUBLANES, depth)
     return pl.pallas_call(
         inner_kernel,
-        out_shape=[vmem_out(4, *tile)] * STEPS + [vmem_out(FACTORS, *tile)],
+        out_shape=[vmem_out(4, planes_x, rows // SUBLANES, SUBLANES, depth)] * STEPS,
         in_specs=in_vmem(3),
-        out_specs=in_vmem(STEPS + 1),
-        scratch_shapes=[pltpu.VMEM((FACTORS, own.shape[1], rows, depth), jnp.float32)],
+        out_specs=in_vmem(STEPS),
         compiler_params=PARAMS,
         name="inner_steps",
-    )(pinned(wide, pltpu.VMEM), planes, pinned(own, pltpu.VMEM))
+    )(pinned(wide, pltpu.VMEM), planes, pinned(factors, pltpu.VMEM))
 
 
 def outer(wide, rims, planes, state, cells_x, cells_y):
@@ -494,7 +509,7 @@
     return jnp.concatenate([windows, lax.ppermute(windows, axis, pairs)], axis=0)
 
 
-def inject_kernel(samples, cells_x, cells_y, gathered, table_x, table_y, planes, weights, picks):
+def inject_kernel(samples, cells_x, cells_y, gathered, table_x, table_y, _, planes, weights, picks):
     size_y = lax.axis_size("gy")
     own_x, own_y = lax.axis_index("gx"), lax.axis_index("gy")
     rows = cells_y + 2 * RIM
@@ -557,14 +572,14 @@
             planes[sample, tile, :, :wide_x] = total[begin : begin + SUBLANES]
 
 
-def injected(gathered, receiver_x, receiver_y, samples, cells_x, cells_y, depth):
+def injected(gathered, receiver_x, receiver_y, earlier, samples, cells_x, cells_y, depth):
     rows = cells_y + 2 * RIM
     receivers = receiver_x.shape[0]
     wide_x = -(-(cells_x + 2 * RIM) // 32) * 32
     return pl.pallas_call(
         functools.partial(inject_kernel, samples, cells_x, cells_y),
         out_shape=vmem_out(STEPS, rows // SUBLANES, SUBLANES, depth),
-        in_specs=in_vmem(3),
+        in_specs=in_vmem(4),
         out_specs=in_vmem(1)[0],
         scratch_shapes=[
             pltpu.VMEM((STEPS * rows, receivers), jnp.float32),
@@ -572,7 +587,12 @@
         ],
         compiler_params=PARAMS,
         name="inject",
-    )(gathered, receiver_x.reshape(-1, LANES), receiver_y.reshape(-1, LANES))
+    )(
+        gathered,
+        receiver_x.reshape(-1, LANES),
+        receiver_y.reshape(-1, LANES),
+        pinned(earlier, pltpu.VMEM),
+    )
 
 
 def per_device(
@@ -620,14 +640,17 @@
     own = own_factors(wide, windows)
     for bit in bits_of("gy")[:-1]:
         windows = doubled(windows, "gy", bit)
-    wide, c_a, c_b = corners(wide, y_a, y_b, windows, pinned(own, pltpu.VMEM))
+    wide, c_a, c_b = corners(wide, y_a, y_b, windows, pinned(own, pltpu.VMEM), x_b)
     for bit in bits_of("gy")[-1:]:
         windows = doubled(windows, "gy", bit)
-    c_a, c_b = swap(c_a, "gx", 0), swap_far(c_b, "gx")
+    c_a, c_b = swap(c_a, "gx", 0), swap(c_b, "gx", 0)
+    factors = ordered_factors(wide, own)
     planes = injected(
-        windows, receiver_x, receiver_y, traces.shape[1], cells_x, cells_y, depth
+        windows, receiver_x, receiver_y, factors, traces.shape[1], cells_x, cells_y, depth
     )
-    state = inner(wide, planes, own)
+    c_b, planes = lax.optimization_barrier((c_b, planes))
+    c_b = hand_on(c_b, "gx")
+    state = [*inner(wide, planes, factors), factors]
     return tuple(outer(wide, (x_a, x_b, c_a, c_b), planes, state, cells_x, cells_y))
 
 

time: 35.4 us -> 35.2 us (level)
  the two profiles are of different devices: /device:TPU:0 before, /device:TPU:1 now
where the time goes in v13:
time: 35.2 us; the launch traced here: 34.8 us
  starting transfers between devices  16.6 us (47%)
  Pallas kernels  9.8 us (28%)
  waiting for transfers between devices  6.66 us (19%)
  between operations  1.43 us (4%)
    ppermute x6, starting transfers between devices, swap(): return lax.ppermute(value, axis, pairs)  10 us
    ppermute x3, starting transfers between devices, doubled(): lax.ppermute(windows, axis, pairs)  5.27 us
    ppermute x3, waiting for transfers between devices, doubled(): lax.ppermute(windows, axis, pairs)  4.88 us
    pallas_call x1, Pallas kernels, inner(): pl.pallas_call(inner_kernel, out_shape=[vmem_out(4, planes_x, rows // SUB...  3.27 us
    pallas_call x1, Pallas kernels, outer(): pl.pallas_call(outer_kernel, out_shape=kept + [out] * 3, in_specs=in_vmem...  3.21 us
    pallas_call x1, Pallas kernels, pack(): pl.pallas_call(functools.partial(pack_kernel, count), out_shape=[wide, ri...  1.8 us
    ppermute x1, waiting for transfers between devices, hand_on(): return lax.ppermute(value, axis, pairs)  1.61 us
    ppermute x1, starting transfers between devices, hand_on(): return lax.ppermute(value, axis, pairs)  1.28 us
  transfers between devices with their start and end apart: 10, of which 4 were waited for; matrix products, arithmetic and copies ran while one was open for 0% of the time, Pallas kernels for 14%

profile of v13, /device:TPU:1, one launch (start us, length us, event | category | flops | bytes accessed | tf_op | source)
XLA Modules:
  0.0 34.8 jit_solution(4211097469914317980)
XLA Ops:
  1.3 1.8 %pack_y_rims.1 = (f32[13,26,24,128]{3,2,1,0:T(8,128)S(1)}, f32[11,16,4,128]{3,2,1,0:T(4,128)S(1)}, f32[11,16,4,128]{3,2,1,0:T(4,128)S(1)}, f32[1,4,128]{2,1,0:T(4,128)S(1)}) custom-call(f32[16,16,128]{2,1,0:T(8,128)} %refs_0_.1, f32[16,16,128]{2,1,0:T(8,128)} %refs_1_.1, f32[16,16,128]{2,1,0:T(8,128)} %refs_2_.1, f32[16,16,128]{2,1,0:T(8,128)} %refs_3_.1, ...), custom_call_target="tpu_custom_call" | custom-call | tf_op jit(solution)/shard_map/pack_y_rims/pallas_call | solution.py:129
  3.1 0.1 pack_x_rims.1
  3.2 0.1 collective-permute-start.2
  3.3 2.8 %collective-permute-start = (f32[11,16,4,128]{3,2,1,0:T(4,128)S(1)}, f32[11,16,4,128]{3,2,1,0:T(4,128)S(1)}, u32[]{:S(2)}, u32[]{:S(2)}) collective-permute-start(f32[11,16,4,128]{3,2,1,0:T(4,128)S(1)} %get-tuple-element.25), channel_id=1, source_target_pairs={{0,1},{2,3},{1,0},{3,2},{4,5},{6,7},{5,4},{7,6},{8,9},{10,11},{9,8... | collective-permute-start | bytes 1081352 | tf_op jit(solution)/shard_map/ppermute | solution.py:32
  6.0 0.7 %collective-permute-start.1 = (f32[11,16,4,128]{3,2,1,0:T(4,128)S(1)}, f32[11,16,4,128]{3,2,1,0:T(4,128)S(1)}, u32[]{:S(2)}, u32[]{:S(2)}) collective-permute-start(f32[11,16,4,128]{3,2,1,0:T(4,128)S(1)} %get-tuple-element.26), channel_id=1, source_target_pairs={{1,2},{2,1},{5,6},{6,5},{9,10},{10,9},{13,14},{14,13},{17,18},{18,... | collective-permute-start | bytes 1081352 | tf_op jit(solution)/shard_map/ppermute | solution.py:32
  6.7 3.3 %collective-permute-start.5 = (f32[43,16,128]{2,1,0:T(8,128)S(1)}, f32[43,16,128]{2,1,0:T(8,128)S(1)}, u32[]{:S(2)}, u32[]{:S(2)}) collective-permute-start(f32[43,16,128]{2,1,0:T(8,128)S(1)} %get-tuple-element.28), channel_id=1, source_target_pairs={{4,8},{8,4},{5,9},{9,5},{6,10},{10,6},{7,11},{11,7},{20,24},{24,20... | collective-permute-start | bytes 1056776 | tf_op jit(solution)/shard_map/ppermute | solution.py:32
  10.1 0.0 collective-permute-done.2.refs_1_
  10.1 0.1 collective-permute-start.3
  10.2 4.2 %collective-permute-done.3 = f32[2,4,128]{2,1,0:T(4,128)S(1)} collective-permute-done((f32[2,4,128]{2,1,0:T(4,128)S(1)}, f32[2,4,128]{2,1,0:T(4,128)S(1)}, u32[]{:S(2)}, u32[]{:S(2)}) %collective-permute-start.3) | collective-permute-done | bytes 4128 | tf_op jit(solution)/shard_map/ppermute | solution.py:509
  14.4 4.1 %collective-permute-start.4 = (f32[4,4,128]{2,1,0:T(4,128)S(1)}, f32[4,4,128]{2,1,0:T(4,128)S(1)}, u32[]{:S(2)}, u32[]{:S(2)}) collective-permute-start(f32[4,4,128]{2,1,0:T(4,128)S(1)} %pad_maximum_fusion.1._), channel_id=1, source_target_pairs={{0,1},{1,0},{2,3},{3,2},{4,5},{5,4},{6,7},{7,6},{8,9},{9,8},{10,11... | collective-permute-start | bytes 24584 | tf_op jit(solution)/shard_map/ppermute | solution.py:509
  18.5 0.4 %own_factors.1.___.own = f32[9,16,16,128]{3,2,1,0:T(8,128)S(1)} custom-call(f32[13,26,24,128]{3,2,1,0:T(8,128)S(1)} %get-tuple-element.24.wide._, f32[4,4,128]{2,1,0:T(4,128)S(1)} %pad_maximum_fusion.1._), custom_call_target="tpu_custom_call" | custom-call | tf_op jit(solution)/shard_map/own_factors/pallas_call | solution.py:265
  18.9 0.7 %collective-permute-done.4 = f32[4,4,128]{2,1,0:T(4,128)S(1)} collective-permute-done((f32[4,4,128]{2,1,0:T(4,128)S(1)}, f32[4,4,128]{2,1,0:T(4,128)S(1)}, u32[]{:S(2)}, u32[]{:S(2)}) %collective-permute-start.4) | collective-permute-done | bytes 8224 | tf_op jit(solution)/shard_map/ppermute | solution.py:509
  19.6 1.1 %collective-permute-start.8 = (f32[8,4,128]{2,1,0:T(4,128)S(1)}, f32[8,4,128]{2,1,0:T(4,128)S(1)}, u32[]{:S(2)}, u32[]{:S(2)}) collective-permute-start(f32[8,4,128]{2,1,0:T(4,128)S(1)} %pad_maximum_fusion.__), channel_id=1, source_target_pairs={{0,2},{1,3},{2,0},{3,1},{4,6},{5,7},{6,4},{7,5},{8,10},{9,11},{10,... | collective-permute-start | bytes 49160 | tf_op jit(solution)/shard_map/ppermute | solution.py:509
  20.7 0.0 collective-permute-done.5.____.refs_2_
  20.7 0.0 collective-permute-done.y_a
  20.7 0.0 collective-permute-done.1.y_b
  20.7 0.2 pack_corners.1
  20.9 3.0 %collective-permute-start.6 = (f32[43,8,128]{2,1,0:T(8,128)S(1)}, f32[43,8,128]{2,1,0:T(8,128)S(1)}, u32[]{:S(2)}, u32[]{:S(2)}) collective-permute-start(f32[43,8,128]{2,1,0:T(8,128)S(1)} %get-tuple-element.30), channel_id=1, source_target_pairs={{0,4},{8,12},{4,0},{12,8},{1,5},{9,13},{5,1},{13,9},{2,6},{10,14},... | collective-permute-start | bytes 528392 | tf_op jit(solution)/shard_map/ppermute | solution.py:32
  24.0 0.1 collective-permute-start.7
  24.1 0.0 copy-start
  24.1 0.0 copy-start.1
  24.1 0.4 %order_factors.1._.factors.refs_10_ = f32[9,26,3,8,128]{4,3,2,1,0:T(8,128)S(1)} custom-call(f32[13,26,24,128]{3,2,1,0:T(8,128)S(1)} %get-tuple-element.29.wide.refs_0_, f32[9,16,16,128]{3,2,1,0:T(8,128)S(1)} %own_factors.1.___.own), custom_call_target="tpu_custom_call" | custom-call | tf_op jit(solution)/shard_map/order_factors/pallas_call | solution.py:401
  24.5 0.0 collective-permute-done.8
  24.5 0.3 copy-done
  24.7 0.0 copy-done.1
  24.8 0.5 %inject.1.planes.refs_5_ = f32[4,3,8,128]{3,2,1,0:T(8,128)S(1)} custom-call(f32[16,4,128]{2,1,0:T(4,128)S(1)} %constant_dynamic-update-slice_fusion.gathered, s32[8,128]{1,0:T(8,128)S(1)} %bitcast.2, s32[8,128]{1,0:T(8,128)S(1)} %bitcast.3, f32[9,26,3,8,128]{4,3,2,1,0:T(8,128)S(1)} %order_factors.1._.factors.refs_10_), custom_call_target="tpu_custom_call" | custom-call | tf_op jit(solution)/shard_map/inject/pallas_call | solution.py:579
  25.2 0.2 collective-permute-done.7
  25.4 1.3 %collective-permute-start.9 = (f32[43,8,128]{2,1,0:T(8,128)S(1)}, f32[43,8,128]{2,1,0:T(8,128)S(1)}, u32[]{:S(2)}, u32[]{:S(2)}) collective-permute-start(f32[43,8,128]{2,1,0:T(8,128)S(1)} %collective-permute-done.7), channel_id=1, source_target_pairs={{0,8},{12,4},{1,9},{13,5},{2,10},{14,6},{3,11},{15,7},{16,24},{28,... | collective-permute-start | bytes 528392 | tf_op jit(solution)/shard_map/ppermute | solution.py:84
  26.7 3.3 %inner_steps.1 = (f32[4,26,3,8,128]{4,3,2,1,0:T(8,128)S(1)}, f32[4,26,3,8,128]{4,3,2,1,0:T(8,128)S(1)}, f32[4,26,3,8,128]{4,3,2,1,0:T(8,128)S(1)}, f32[4,26,3,8,128]{4,3,2,1,0:T(8,128)S(1)}) custom-call(f32[13,26,24,128]{3,2,1,0:T(8,128)S(1)} %get-tuple-element.29.wide.refs_0_, f32[4,3,8,128]{3,2,1,0:T(8,128)S(1)} %inject.1.planes.refs_5_, ...), custom_call_target="tpu_custom_call" | custom-call | tf_op jit(solution)/shard_map/inner_steps/pallas_call | solution.py:471
  30.0 0.0 collective-permute-done.6.refs_3_
  30.0 1.6 %collective-permute-done.9.refs_4_ = f32[43,8,128]{2,1,0:T(8,128)S(1)} collective-permute-done((f32[43,8,128]{2,1,0:T(8,128)S(1)}, f32[43,8,128]{2,1,0:T(8,128)S(1)}, u32[]{:S(2)}, u32[]{:S(2)}) %collective-permute-start.9) | collective-permute-done | bytes 176160 | tf_op jit(solution)/shard_map/ppermute | solution.py:84
  31.6 3.2 %outer_steps.1 = (f32[13,26,24,128]{3,2,1,0:T(8,128)S(1)}, f32[4,26,3,8,128]{4,3,2,1,0:T(8,128)S(1)}, f32[4,26,3,8,128]{4,3,2,1,0:T(8,128)S(1)}, f32[4,26,3,8,12...) custom-call(f32[13,26,24,128]{3,2,1,0:T(8,128)S(1)} %get-tuple-eleme, ...), custom_call_target="tpu_custom_call", output_to_operand_aliasing={{0}: (0, {}), {1}: (6, {}), {2}: (7, {}), {3}: (8, {}), {4}... | custom-call | tf_op jit(solution)/shard_map/outer_steps/pallas_call | solution.py:486
  (8 shorter events, 0.1 us)
Async XLA Ops:
  3.2 6.9 %collective-permute-start.2 = (f32[44,16,128]{2,1,0:T(8,128)S(1)}, f32[44,16,128]{2,1,0:T(8,128)S(1)}, u32[]{:S(2)}, u32[]{:S(2)}) collective-permute-start(f32[44,16,128]{2,1,0:T(8,128)S(1)} %get-tuple-element.27), channel_id=1, source_target_pairs={{0,4},{8,12},{4,0},{12,8},{1,5},{9,13},{5,1},{13,9},{2,6},{10,14},... | collective-permute-start | bytes 1081352 | tf_op jit(solution)/shard_map/ppermute | solution.py:32
  3.3 17.4 %collective-permute-start = (f32[11,16,4,128]{3,2,1,0:T(4,128)S(1)}, f32[11,16,4,128]{3,2,1,0:T(4,128)S(1)}, u32[]{:S(2)}, u32[]{:S(2)}) collective-permute-start(f32[11,16,4,128]{3,2,1,0:T(4,128)S(1)} %get-tuple-element.25), channel_id=1, source_target_pairs={{0,1},{2,3},{1,0},{3,2},{4,5},{6,7},{5,4},{7,6},{8,9},{10,11},{9,8... | collective-permute-start | bytes 1081352 | tf_op jit(solution)/shard_map/ppermute | solution.py:32
  6.0 14.6 %collective-permute-start.1 = (f32[11,16,4,128]{3,2,1,0:T(4,128)S(1)}, f32[11,16,4,128]{3,2,1,0:T(4,128)S(1)}, u32[]{:S(2)}, u32[]{:S(2)}) collective-permute-start(f32[11,16,4,128]{3,2,1,0:T(4,128)S(1)} %get-tuple-element.26), channel_id=1, source_target_pairs={{1,2},{2,1},{5,6},{6,5},{9,10},{10,9},{13,14},{14,13},{17,18},{18,... | collective-permute-start | bytes 1081352 | tf_op jit(solution)/shard_map/ppermute | solution.py:32
  6.7 14.0 %collective-permute-start.5 = (f32[43,16,128]{2,1,0:T(8,128)S(1)}, f32[43,16,128]{2,1,0:T(8,128)S(1)}, u32[]{:S(2)}, u32[]{:S(2)}) collective-permute-start(f32[43,16,128]{2,1,0:T(8,128)S(1)} %get-tuple-element.28), channel_id=1, source_target_pairs={{4,8},{8,4},{5,9},{9,5},{6,10},{10,6},{7,11},{11,7},{20,24},{24,20... | collective-permute-start | bytes 1056776 | tf_op jit(solution)/shard_map/ppermute | solution.py:32
  10.1 4.3 %collective-permute-start.3 = (f32[2,4,128]{2,1,0:T(4,128)S(1)}, f32[2,4,128]{2,1,0:T(4,128)S(1)}, u32[]{:S(2)}, u32[]{:S(2)}) collective-permute-start(f32[2,4,128]{2,1,0:T(4,128)S(1)} %pad_maximum_fusion.2), channel_id=1, source_target_pairs={{0,8},{4,12},{8,0},{12,4},{1,9},{5,13},{9,1},{13,5},{2,10},{6,14},... | collective-permute-start | bytes 12296 | tf_op jit(solution)/shard_map/ppermute | solution.py:509
  14.4 5.1 %collective-permute-start.4 = (f32[4,4,128]{2,1,0:T(4,128)S(1)}, f32[4,4,128]{2,1,0:T(4,128)S(1)}, u32[]{:S(2)}, u32[]{:S(2)}) collective-permute-start(f32[4,4,128]{2,1,0:T(4,128)S(1)} %pad_maximum_fusion.1._), channel_id=1, source_target_pairs={{0,1},{1,0},{2,3},{3,2},{4,5},{5,4},{6,7},{7,6},{8,9},{9,8},{10,11... | collective-permute-start | bytes 24584 | tf_op jit(solution)/shard_map/ppermute | solution.py:509
  19.6 4.9 %collective-permute-start.8 = (f32[8,4,128]{2,1,0:T(4,128)S(1)}, f32[8,4,128]{2,1,0:T(4,128)S(1)}, u32[]{:S(2)}, u32[]{:S(2)}) collective-permute-start(f32[8,4,128]{2,1,0:T(4,128)S(1)} %pad_maximum_fusion.__), channel_id=1, source_target_pairs={{0,2},{1,3},{2,0},{3,1},{4,6},{5,7},{6,4},{7,5},{8,10},{9,11},{10,... | collective-permute-start | bytes 49160 | tf_op jit(solution)/shard_map/ppermute | solution.py:509
  20.9 9.0 %collective-permute-start.6 = (f32[43,8,128]{2,1,0:T(8,128)S(1)}, f32[43,8,128]{2,1,0:T(8,128)S(1)}, u32[]{:S(2)}, u32[]{:S(2)}) collective-permute-start(f32[43,8,128]{2,1,0:T(8,128)S(1)} %get-tuple-element.30), channel_id=1, source_target_pairs={{0,4},{8,12},{4,0},{12,8},{1,5},{9,13},{5,1},{13,9},{2,6},{10,14},... | collective-permute-start | bytes 528392 | tf_op jit(solution)/shard_map/ppermute | solution.py:32
  24.0 1.4 %collective-permute-start.7 = (f32[43,8,128]{2,1,0:T(8,128)S(1)}, f32[43,8,128]{2,1,0:T(8,128)S(1)}, u32[]{:S(2)}, u32[]{:S(2)}) collective-permute-start(f32[43,8,128]{2,1,0:T(8,128)S(1)} %get-tuple-element.31), channel_id=1, source_target_pairs={{0,4},{8,12},{4,0},{12,8},{1,5},{9,13},{5,1},{13,9},{2,6},{10,14},... | collective-permute-start | bytes 528392 | tf_op jit(solution)/shard_map/ppermute | solution.py:32
  24.1 0.7 %copy-start = (s32[1024]{0:T(1024)S(1)}, s32[1024]{0:T(1024)}, u32[]{:S(2)}) copy-start(s32[1024]{0:T(1024)} %param.31) | copy-start | bytes 12292
  24.1 0.7 %copy-start.1 = (s32[1024]{0:T(1024)S(1)}, s32[1024]{0:T(1024)}, u32[]{:S(2)}) copy-start(s32[1024]{0:T(1024)} %param.32) | copy-start | bytes 12292
  25.4 6.2 %collective-permute-start.9 = (f32[43,8,128]{2,1,0:T(8,128)S(1)}, f32[43,8,128]{2,1,0:T(8,128)S(1)}, u32[]{:S(2)}, u32[]{:S(2)}) collective-permute-start(f32[43,8,128]{2,1,0:T(8,128)S(1)} %collective-permute-done.7), channel_id=1, source_target_pairs={{0,8},{12,4},{1,9},{13,5},{2,10},{14,6},{3,11},{15,7},{16,24},{28,... | collective-permute-start | bytes 528392 | tf_op jit(solution)/shard_map/ppermute | solution.py:84

commit v14 on v10

--- a/solution.py
+++ b/solution.py
@@ -94,25 +94,28 @@
     begin = start[0]
     samples = traces.shape[1]
     window[...] = jnp.zeros_like(window)
-    for move in moves:
-        move.wait()
+    for number in range(count):
+        moves[number].wait()
+
+        def put_y(low, high, number=number):
+            for out, is_high, base in ((low, False, 0), (high, True, cells_y - RIM)):
+                for slot, part, row, place, length in each_y_part(y_slots(), is_high):
+                    if part == number:
+                        out[slot, :, place : place + length, :] = wide[
+                            number, RIM : RIM + cells_x, base + row : base + row + length, :
+                        ]
+
+        @pl.when(odd_y)
+        def _(put_y=put_y):
+            put_y(y_a, y_b)
+
+        @pl.when(jnp.logical_not(odd_y))
+        def _(put_y=put_y):
+            put_y(y_b, y_a)
+
+    moves[count].wait()
     for sample in range(STEPS):
         window[0, sample : sample + 1, :samples] = held[pl.ds(begin + sample, 1), :]
-
-    def put_y(low, high):
-        for out, is_high, base in ((low, False, 0), (high, True, cells_y - RIM)):
-            for slot, number, row, place, length in each_y_part(y_slots(), is_high):
-                out[slot, :, place : place + length, :] = wide[
-                    number, RIM : RIM + cells_x, base + row : base + row + length, :
-                ]
-
-    @pl.when(odd_y)
-    def _():
-        put_y(y_a, y_b)
-
-    @pl.when(jnp.logical_not(odd_y))
-    def _():
-        put_y(y_b, y_a)
 
 
 def pack(blocks, traces, segment_start):
@@ -304,51 +307,64 @@
         below = [jnp.where(self.not_first, pltpu.roll(u, 1, 1), 0.0) for u in value]
         return above, below
 
-    def stencil(self, factors, before, now, after, full):
-        slope_x = [a - b for a, b in zip(after, before)]
+    def plane_part(self, now):
         above, below = self.sides_z(now)
-        slope_z = [a - b for a, b in zip(above, below)]
-        next_now, previous_now = self.next_y(now), self.previous_y(now)
-        above_x, below_x = self.sides_z(slope_x)
-        next_x, previous_x = self.next_y(slope_x), self.previous_y(slope_x)
-        next_z, previous_z = self.next_y(slope_z), self.previous_y(slope_z)
-        axis, laplace = [], []
-        for tile in range(self.tiles):
-            axx, ayy, azz, axy, axz, ayz = [value[tile] for value in factors]
-            double = now[tile] + now[tile]
-            sum_x = after[tile] + before[tile]
-            sum_y = next_now[tile] + previous_now[tile]
-            sum_z = above[tile] + below[tile]
-            straight = ((axx * sum_x + ayy * sum_y) + azz * sum_z) - double
-            mixed = (
-                axy * (next_x[tile] - previous_x[tile]) + axz * (above_x[tile] - below_x[tile])
-            ) + ayz * (next_z[tile] - previous_z[tile])
-            axis.append(straight + mixed)
-            if full:
-                laplace.append(((sum_x + sum_y) + sum_z) - 3.0 * double)
-        return axis, laplace
+        after, before = self.next_y(now), self.previous_y(now)
+        pairs_z, pairs_y = list(zip(above, below)), list(zip(after, before))
+        return (
+            [a - b for a, b in pairs_y],
+            [a - b for a, b in pairs_z],
+            [a + b for a, b in pairs_y],
+            [a + b for a, b in pairs_z],
+        )
+
+    def stencil(self, number, turn, x, count, full):
+        planes = [self.wave_tiles(number, turn + 1, x - 1 + i) for i in range(count + 2)]
+        parts = [self.plane_part(planes[0]), self.plane_part(planes[1])]
+        result = []
+        for i in range(1, count + 1):
+            parts.append(self.plane_part(planes[i + 1]))
+            slope_y, slope_z, sums_y, sums_z = parts[i]
+            next_z, previous_z = self.next_y(slope_z), self.previous_y(slope_z)
+            axis, laplace = [], []
+            for tile in range(self.tiles):
+                axx, ayy, azz, axy, axz, ayz = [
+                    self.factors[factor, x - 1 + i, tile] for factor in range(3, 9)
+                ]
+                now = planes[i][tile]
+                double = now + now
+                sum_x = planes[i + 1][tile] + planes[i - 1][tile]
+                sum_y, sum_z = sums_y[tile], sums_z[tile]
+                straight = ((axx * sum_x + ayy * sum_y) + azz * sum_z) - double
+                mixed = (
+                    axy * (parts[i + 1][0][tile] - parts[i - 1][0][tile])
+                    + axz * (parts[i + 1][1][tile] - parts[i - 1][1][tile])
+                ) + ayz * (next_z[tile] - previous_z[tile])
+                axis.append(straight + mixed)
+                if full:
+                    laplace.append(((sum_x + sum_y) + sum_z) - 3.0 * double)
+            result.append((planes[i], axis, laplace))
+        return result
 
     def step(self, turn, x, count):
         tiles, factors = range(self.tiles), self.factors
         for pair in range(2):
             p_number, q_number = 2 * pair, 2 * pair + 1
-            p = [self.wave_tiles(p_number, turn + 1, x - 1 + i) for i in range(count + 2)]
-            q = [self.wave_tiles(q_number, turn + 1, x - 1 + i) for i in range(count + 2)]
+            of_q = self.stencil(q_number, turn, x, count, False)
+            of_p = self.stencil(p_number, turn, x, count, True)
             for i in range(count):
                 now = x + i
-                mixing = [[factors[number, now, tile] for tile in tiles] for number in range(3, 9)]
-                p_axis, p_laplace = self.stencil(mixing, p[i], p[i + 1], p[i + 2], True)
-                q_axis, _ = self.stencil(mixing, q[i], q[i + 1], q[i + 2], False)
+                q, q_axis, _ = of_q[i]
+                p, p_axis, p_laplace = of_p[i]
                 p_held = self.wave_tiles(p_number, turn, now)
                 q_held = self.wave_tiles(q_number, turn, now)
                 for tile in tiles:
                     velocity, with_e, with_d = [factors[number, now, tile] for number in range(3)]
                     across = p_laplace[tile] - p_axis[tile]
-                    p_now, q_now = p[i + 1][tile], q[i + 1][tile]
-                    p_next = ((p_now + p_now) - p_held[tile]) + (
+                    p_next = ((p[tile] + p[tile]) - p_held[tile]) + (
                         with_e * across + with_d * q_axis[tile]
                     )
-                    q_next = ((q_now + q_now) - q_held[tile]) + (
+                    q_next = ((q[tile] + q[tile]) - q_held[tile]) + (
                         with_d * across + velocity * q_axis[tile]
                     )
                     if pair == 1:

time: 29.5 us -> 29.5 us (level)
    pallas_call x1, Pallas kernels: 3.25 us -> 3.58 us  [outer(): pl.pallas_call(outer_kernel, out_shape=kept + [out] * 3, in_specs=in_vmem...]
where the time goes in v14:
time: 29.5 us; the launch traced here: 29.3 us
  starting transfers between devices  17.2 us (58%)
  Pallas kernels  9.94 us (34%)
  between operations  1.46 us (5%)
  waiting for transfers between devices  0.68 us (2%)
    ppermute x6, starting transfers between devices, swap(): return lax.ppermute(value, axis, pairs)  10.3 us
    ppermute x3, starting transfers between devices, doubled(): lax.ppermute(windows, axis, pairs)  6.86 us
    pallas_call x1, Pallas kernels, inner(): pl.pallas_call(inner_kernel, out_shape=[vmem_out(4, *tile)] * STEPS + [vm...  3.6 us
    pallas_call x1, Pallas kernels, outer(): pl.pallas_call(outer_kernel, out_shape=kept + [out] * 3, in_specs=in_vmem...  3.58 us
    pallas_call x1, Pallas kernels, pack(): pl.pallas_call(functools.partial(pack_kernel, count), out_shape=[wide, ri...  1.64 us
    ppermute x3, waiting for transfers between devices, doubled(): lax.ppermute(windows, axis, pairs)  0.66 us
  transfers between devices with their start and end apart: 9, of which 1 were waited for; matrix products, arithmetic and copies ran while one was open for 0% of the time, Pallas kernels for 16%

profile of v14, /device:TPU:1, one launch (start us, length us, event | category | flops | bytes accessed | tf_op | source)
XLA Modules:
  0.0 29.3 jit_solution(18299123715215104590)
XLA Ops:
  1.3 1.6 %pack_y_rims.1 = (f32[13,26,24,128]{3,2,1,0:T(8,128)S(1)}, f32[11,16,4,128]{3,2,1,0:T(4,128)S(1)}, f32[11,16,4,128]{3,2,1,0:T(4,128)S(1)}, f32[1,4,128]{2,1,0:T(4,128)S(1)}) custom-call(f32[16,16,128]{2,1,0:T(8,128)} %refs_0_.1, f32[16,16,128]{2,1,0:T(8,128)} %refs_1_.1, f32[16,16,128]{2,1,0:T(8,128)} %refs_2_.1, f32[16,16,128]{2,1,0:T(8,128)} %refs_3_.1, ...), custom_call_target="tpu_custom_call" | custom-call | tf_op jit(solution)/shard_map/pack_y_rims/pallas_call | solution.py:126
  2.9 0.1 pack_x_rims.1
  3.0 0.1 collective-permute-start.2
  3.1 2.8 %collective-permute-start = (f32[11,16,4,128]{3,2,1,0:T(4,128)S(1)}, f32[11,16,4,128]{3,2,1,0:T(4,128)S(1)}, u32[]{:S(2)}, u32[]{:S(2)}) collective-permute-start(f32[11,16,4,128]{3,2,1,0:T(4,128)S(1)} %get-tuple-element.24), channel_id=1, source_target_pairs={{0,1},{2,3},{1,0},{3,2},{4,5},{6,7},{5,4},{7,6},{8,9},{10,11},{9,8... | collective-permute-start | bytes 1081352 | tf_op jit(solution)/shard_map/ppermute | solution.py:32
  5.9 0.7 %collective-permute-start.1 = (f32[11,16,4,128]{3,2,1,0:T(4,128)S(1)}, f32[11,16,4,128]{3,2,1,0:T(4,128)S(1)}, u32[]{:S(2)}, u32[]{:S(2)}) collective-permute-start(f32[11,16,4,128]{3,2,1,0:T(4,128)S(1)} %get-tuple-element.25), channel_id=1, source_target_pairs={{1,2},{2,1},{5,6},{6,5},{9,10},{10,9},{13,14},{14,13},{17,18},{18,... | collective-permute-start | bytes 1081352 | tf_op jit(solution)/shard_map/ppermute | solution.py:32
  6.6 0.0 collective-permute-done.2.refs_1_
  6.6 1.3 %collective-permute-start.3 = (f32[2,4,128]{2,1,0:T(4,128)S(1)}, f32[2,4,128]{2,1,0:T(4,128)S(1)}, u32[]{:S(2)}, u32[]{:S(2)}) collective-permute-start(f32[2,4,128]{2,1,0:T(4,128)S(1)} %pad_maximum_fusion.2), channel_id=1, source_target_pairs={{0,8},{4,12},{8,0},{12,4},{1,9},{5,13},{9,1},{13,5},{2,10},{6,14},... | collective-permute-start | bytes 12296 | tf_op jit(solution)/shard_map/ppermute | solution.py:504
  7.9 2.7 %collective-permute-start.5 = (f32[43,16,128]{2,1,0:T(8,128)S(1)}, f32[43,16,128]{2,1,0:T(8,128)S(1)}, u32[]{:S(2)}, u32[]{:S(2)}) collective-permute-start(f32[43,16,128]{2,1,0:T(8,128)S(1)} %get-tuple-element.28), channel_id=1, source_target_pairs={{4,8},{8,4},{5,9},{9,5},{6,10},{10,6},{7,11},{11,7},{20,24},{24,20... | collective-permute-start | bytes 1056776 | tf_op jit(solution)/shard_map/ppermute | solution.py:32
  10.6 0.0 collective-permute-done.3
  10.6 4.2 %collective-permute-start.4 = (f32[4,4,128]{2,1,0:T(4,128)S(1)}, f32[4,4,128]{2,1,0:T(4,128)S(1)}, u32[]{:S(2)}, u32[]{:S(2)}) collective-permute-start(f32[4,4,128]{2,1,0:T(4,128)S(1)} %pad_maximum_fusion.1._), channel_id=1, source_target_pairs={{0,1},{1,0},{2,3},{3,2},{4,5},{5,4},{6,7},{7,6},{8,9},{9,8},{10,11... | collective-permute-start | bytes 24584 | tf_op jit(solution)/shard_map/ppermute | solution.py:504
  14.8 0.4 %own_factors.1.___.own = f32[9,16,16,128]{3,2,1,0:T(8,128)S(1)} custom-call(f32[13,26,24,128]{3,2,1,0:T(8,128)S(1)} %get-tuple-element.23.wide._, f32[4,4,128]{2,1,0:T(4,128)S(1)} %pad_maximum_fusion.1._), custom_call_target="tpu_custom_call" | custom-call | tf_op jit(solution)/shard_map/own_factors/pallas_call | solution.py:262
  15.1 0.7 %collective-permute-done.4 = f32[4,4,128]{2,1,0:T(4,128)S(1)} collective-permute-done((f32[4,4,128]{2,1,0:T(4,128)S(1)}, f32[4,4,128]{2,1,0:T(4,128)S(1)}, u32[]{:S(2)}, u32[]{:S(2)}) %collective-permute-start.4) | collective-permute-done | bytes 8224 | tf_op jit(solution)/shard_map/ppermute | solution.py:504
  15.8 0.0 copy-start
  15.8 0.0 copy-start.1
  15.8 1.4 %collective-permute-start.8 = (f32[8,4,128]{2,1,0:T(4,128)S(1)}, f32[8,4,128]{2,1,0:T(4,128)S(1)}, u32[]{:S(2)}, u32[]{:S(2)}) collective-permute-start(f32[8,4,128]{2,1,0:T(4,128)S(1)} %pad_maximum_fusion.__), channel_id=1, source_target_pairs={{0,2},{1,3},{2,0},{3,1},{4,6},{5,7},{6,4},{7,5},{8,10},{9,11},{10,... | collective-permute-start | bytes 49160 | tf_op jit(solution)/shard_map/ppermute | solution.py:504
  17.2 0.0 collective-permute-done.y_a
  17.2 0.0 collective-permute-done.1.y_b
  17.2 0.2 pack_corners.1
  17.5 1.1 %collective-permute-start.6 = (f32[43,8,128]{2,1,0:T(8,128)S(1)}, f32[43,8,128]{2,1,0:T(8,128)S(1)}, u32[]{:S(2)}, u32[]{:S(2)}) collective-permute-start(f32[43,8,128]{2,1,0:T(8,128)S(1)} %get-tuple-element.29), channel_id=1, source_target_pairs={{0,4},{8,12},{4,0},{12,8},{1,5},{9,13},{5,1},{13,9},{2,6},{10,14},... | collective-permute-start | bytes 528392 | tf_op jit(solution)/shard_map/ppermute | solution.py:32
  18.6 3.0 %collective-permute-start.7 = (f32[43,8,128]{2,1,0:T(8,128)S(1)}, f32[43,8,128]{2,1,0:T(8,128)S(1)}, u32[]{:S(2)}, u32[]{:S(2)}) collective-permute-start(f32[43,8,128]{2,1,0:T(8,128)S(1)} %get-tuple-element.30), channel_id=1, source_target_pairs={{4,8},{8,4},{5,9},{9,5},{6,10},{10,6},{7,11},{11,7},{20,24},{24,20... | collective-permute-start | bytes 528392 | tf_op jit(solution)/shard_map/ppermute | solution.py:32
  21.6 0.0 collective-permute-done.8
  21.6 0.0 copy-done
  21.6 0.0 copy-done.1
  21.7 0.5 %inject.1.planes.refs_5_ = f32[4,3,8,128]{3,2,1,0:T(8,128)S(1)} custom-call(f32[16,4,128]{2,1,0:T(4,128)S(1)} %constant_dynamic-update-slice_fusion.gathered, s32[8,128]{1,0:T(8,128)S(1)} %bitcast.2, s32[8,128]{1,0:T(8,128)S(1)} %bitcast.3), custom_call_target="tpu_custom_call" | custom-call | tf_op jit(solution)/shard_map/inject/pallas_call | solution.py:574
  22.1 3.6 %inner_steps.1 = (f32[4,26,3,8,128]{4,3,2,1,0:T(8,128)S(1)}, f32[4,26,3,8,128]{4,3,2,1,0:T(8,128)S(1)}, f32[4,26,3,8,128]{4,3,2,1,0:T(8,128)S(1)}, f32[4,26,3,8,...) custom-call(f32[13,26,24,128]{3,2,1,0:T(8,128)S(1)} %get-tuple-element.27.wide.refs_0_, ...), custom_call_target="tpu_custom_call" | custom-call | tf_op jit(solution)/shard_map/inner_steps/pallas_call | solution.py:465
  25.7 0.0 collective-permute-done.5.refs_2_
  25.7 0.0 collective-permute-done.6.refs_3_
  25.7 0.0 collective-permute-done.7.refs_4_
  25.8 3.6 %outer_steps.1 = (f32[13,26,24,128]{3,2,1,0:T(8,128)S(1)}, f32[4,26,3,8,128]{4,3,2,1,0:T(8,128)S(1)}, f32[4,26,3,8,128]{4,3,2,1,0:T(8,128)S(1)}, f32[4,26,3,8,12...) custom-call(f32[13,26,24,128]{3,2,1,0:T(8,128)S(1)} %get-tuple-eleme, ...), custom_call_target="tpu_custom_call", output_to_operand_aliasing={{0}: (0, {}), {1}: (6, {}), {2}: (7, {}), {3}: (8, {}), {4}... | custom-call | tf_op jit(solution)/shard_map/outer_steps/pallas_call | solution.py:481
  (8 shorter events, 0.1 us)
Async XLA Ops:
  3.0 3.6 %collective-permute-start.2 = (f32[44,16,128]{2,1,0:T(8,128)S(1)}, f32[44,16,128]{2,1,0:T(8,128)S(1)}, u32[]{:S(2)}, u32[]{:S(2)}) collective-permute-start(f32[44,16,128]{2,1,0:T(8,128)S(1)} %get-tuple-element.26), channel_id=1, source_target_pairs={{0,4},{8,12},{4,0},{12,8},{1,5},{9,13},{5,1},{13,9},{2,6},{10,14},... | collective-permute-start | bytes 1081352 | tf_op jit(solution)/shard_map/ppermute | solution.py:32
  3.1 14.1 %collective-permute-start = (f32[11,16,4,128]{3,2,1,0:T(4,128)S(1)}, f32[11,16,4,128]{3,2,1,0:T(4,128)S(1)}, u32[]{:S(2)}, u32[]{:S(2)}) collective-permute-start(f32[11,16,4,128]{3,2,1,0:T(4,128)S(1)} %get-tuple-element.24), channel_id=1, source_target_pairs={{0,1},{2,3},{1,0},{3,2},{4,5},{6,7},{5,4},{7,6},{8,9},{10,11},{9,8... | collective-permute-start | bytes 1081352 | tf_op jit(solution)/shard_map/ppermute | solution.py:32
  5.9 11.3 %collective-permute-start.1 = (f32[11,16,4,128]{3,2,1,0:T(4,128)S(1)}, f32[11,16,4,128]{3,2,1,0:T(4,128)S(1)}, u32[]{:S(2)}, u32[]{:S(2)}) collective-permute-start(f32[11,16,4,128]{3,2,1,0:T(4,128)S(1)} %get-tuple-element.25), channel_id=1, source_target_pairs={{1,2},{2,1},{5,6},{6,5},{9,10},{10,9},{13,14},{14,13},{17,18},{18,... | collective-permute-start | bytes 1081352 | tf_op jit(solution)/shard_map/ppermute | solution.py:32
  6.6 3.9 %collective-permute-start.3 = (f32[2,4,128]{2,1,0:T(4,128)S(1)}, f32[2,4,128]{2,1,0:T(4,128)S(1)}, u32[]{:S(2)}, u32[]{:S(2)}) collective-permute-start(f32[2,4,128]{2,1,0:T(4,128)S(1)} %pad_maximum_fusion.2), channel_id=1, source_target_pairs={{0,8},{4,12},{8,0},{12,4},{1,9},{5,13},{9,1},{13,5},{2,10},{6,14},... | collective-permute-start | bytes 12296 | tf_op jit(solution)/shard_map/ppermute | solution.py:504
  7.9 17.8 %collective-permute-start.5 = (f32[43,16,128]{2,1,0:T(8,128)S(1)}, f32[43,16,128]{2,1,0:T(8,128)S(1)}, u32[]{:S(2)}, u32[]{:S(2)}) collective-permute-start(f32[43,16,128]{2,1,0:T(8,128)S(1)} %get-tuple-element.28), channel_id=1, source_target_pairs={{4,8},{8,4},{5,9},{9,5},{6,10},{10,6},{7,11},{11,7},{20,24},{24,20... | collective-permute-start | bytes 1056776 | tf_op jit(solution)/shard_map/ppermute | solution.py:32
  10.6 5.2 %collective-permute-start.4 = (f32[4,4,128]{2,1,0:T(4,128)S(1)}, f32[4,4,128]{2,1,0:T(4,128)S(1)}, u32[]{:S(2)}, u32[]{:S(2)}) collective-permute-start(f32[4,4,128]{2,1,0:T(4,128)S(1)} %pad_maximum_fusion.1._), channel_id=1, source_target_pairs={{0,1},{1,0},{2,3},{3,2},{4,5},{5,4},{6,7},{7,6},{8,9},{9,8},{10,11... | collective-permute-start | bytes 24584 | tf_op jit(solution)/shard_map/ppermute | solution.py:504
  15.8 5.8 %copy-start = (s32[1024]{0:T(1024)S(1)}, s32[1024]{0:T(1024)}, u32[]{:S(2)}) copy-start(s32[1024]{0:T(1024)} %param.31) | copy-start | bytes 12292
  15.8 5.8 %copy-start.1 = (s32[1024]{0:T(1024)S(1)}, s32[1024]{0:T(1024)}, u32[]{:S(2)}) copy-start(s32[1024]{0:T(1024)} %param.32) | copy-start | bytes 12292
  15.8 5.8 %collective-permute-start.8 = (f32[8,4,128]{2,1,0:T(4,128)S(1)}, f32[8,4,128]{2,1,0:T(4,128)S(1)}, u32[]{:S(2)}, u32[]{:S(2)}) collective-permute-start(f32[8,4,128]{2,1,0:T(4,128)S(1)} %pad_maximum_fusion.__), channel_id=1, source_target_pairs={{0,2},{1,3},{2,0},{3,1},{4,6},{5,7},{6,4},{7,5},{8,10},{9,11},{10,... | collective-permute-start | bytes 49160 | tf_op jit(solution)/shard_map/ppermute | solution.py:504
  17.5 8.3 %collective-permute-start.6 = (f32[43,8,128]{2,1,0:T(8,128)S(1)}, f32[43,8,128]{2,1,0:T(8,128)S(1)}, u32[]{:S(2)}, u32[]{:S(2)}) collective-permute-start(f32[43,8,128]{2,1,0:T(8,128)S(1)} %get-tuple-element.29), channel_id=1, source_target_pairs={{0,4},{8,12},{4,0},{12,8},{1,5},{9,13},{5,1},{13,9},{2,6},{10,14},... | collective-permute-start | bytes 528392 | tf_op jit(solution)/shard_map/ppermute | solution.py:32
  18.6 7.2 %collective-permute-start.7 = (f32[43,8,128]{2,1,0:T(8,128)S(1)}, f32[43,8,128]{2,1,0:T(8,128)S(1)}, u32[]{:S(2)}, u32[]{:S(2)}) collective-permute-start(f32[43,8,128]{2,1,0:T(8,128)S(1)} %get-tuple-element.30), channel_id=1, source_target_pairs={{4,8},{8,4},{5,9},{9,5},{6,10},{10,6},{7,11},{11,7},{20,24},{24,20... | collective-permute-start | bytes 528392 | tf_op jit(solution)/shard_map/ppermute | solution.py:32

commit v15 on v14

--- a/solution.py
+++ b/solution.py
@@ -10,6 +10,7 @@
 STEPS = 4
 REC_DEPTH = 4
 RIM = STEPS
+QUARTERS = 4
 FIELDS = 8
 SUBLANES = 8
 LANES = 128
@@ -346,12 +347,40 @@
             result.append((planes[i], axis, laplace))
         return result
 
+    def short_stencil(self, number, turn, x, count, full):
+        planes = [self.wave_tiles(number, turn + 1, x - 1 + i) for i in range(count + 2)]
+        result = []
+        for i in range(1, count + 1):
+            before, now, after = planes[i - 1 : i + 2]
+            slope_x = [a - b for a, b in zip(after, before)]
+            _, slope_z, sums_y, sums_z = self.plane_part(now)
+            slope_xy, slope_xz, _, _ = self.plane_part(slope_x)
+            next_z, previous_z = self.next_y(slope_z), self.previous_y(slope_z)
+            axis, laplace = [], []
+            for tile in range(self.tiles):
+                axx, ayy, azz, axy, axz, ayz = [
+                    self.factors[factor, x - 1 + i, tile] for factor in range(3, 9)
+                ]
+                double = now[tile] + now[tile]
+                sum_x = after[tile] + before[tile]
+                sum_y, sum_z = sums_y[tile], sums_z[tile]
+                straight = ((axx * sum_x + ayy * sum_y) + azz * sum_z) - double
+                mixed = (axy * slope_xy[tile] + axz * slope_xz[tile]) + ayz * (
+                    next_z[tile] - previous_z[tile]
+                )
+                axis.append(straight + mixed)
+                if full:
+                    laplace.append(((sum_x + sum_y) + sum_z) - 3.0 * double)
+            result.append((now, axis, laplace))
+        return result
+
     def step(self, turn, x, count):
         tiles, factors = range(self.tiles), self.factors
         for pair in range(2):
             p_number, q_number = 2 * pair, 2 * pair + 1
-            of_q = self.stencil(q_number, turn, x, count, False)
-            of_p = self.stencil(p_number, turn, x, count, True)
+            stencil = self.stencil if count > RIM else self.short_stencil
+            of_q = stencil(q_number, turn, x, count, False)
+            of_p = stencil(p_number, turn, x, count, True)
             for i in range(count):
                 now = x + i
                 q, q_axis, _ = of_q[i]
@@ -372,7 +401,8 @@
                         moved = pltpu.roll(self.planes[STEPS - 1 - turn, tile], shift, 1)
                         p_next = p_next + jnp.where(self.at_depth, moved, 0.0)
                     self.waves[turn][p_number, now, tile] = p_next
-                    self.waves[turn][q_number, now, tile] = q_next
+                    if pair == 1 or turn < STEPS - 1:
+                        self.waves[turn][q_number, now, tile] = q_next
 
 
 def repeat(count, body):
@@ -415,8 +445,8 @@
     x_a, x_b, c_a, c_b, planes = refs[1:6]
     refs = refs[6 + STEPS + 1 :]
     wide, waves, factors = refs[0], refs[1 : 1 + STEPS], refs[1 + STEPS]
-    image, p_last, q_last = refs[-3:]
-    cells_x, cells_y, depth = image.shape
+    outputs, sems = refs[-4:-1], refs[-1]
+    cells_x, cells_y, depth = outputs[0].shape
     odd_x = is_odd("gx")
     for number, width, place in x_parts()[0]:
         low, high = RIM - width, RIM + cells_x
@@ -454,9 +484,18 @@
             for tile in range(tiles):
                 wide[out, x, pl.ds(tile, SUBLANES, stride=tiles), :] = value[tile]
 
-    repeat(cells_x, finish)
-    for out, ref in enumerate((image, p_last, q_last)):
-        ref[...] = wide[out, RIM : RIM + cells_x, :cells_y, :]
+    moves = []
+    quarter = cells_x // QUARTERS
+    for part in range(QUARTERS):
+        begin = part * quarter
+        repeat(quarter, lambda i, begin=begin: finish(begin + i))
+        for out, ref in enumerate(outputs):
+            source = wide.at[out, pl.ds(RIM + begin, quarter), pl.ds(0, cells_y)]
+            move = pltpu.make_async_copy(source, ref.at[pl.ds(begin, quarter)], sems.at[out, part])
+            move.start()
+            moves.append(move)
+    for move in moves:
+        move.wait()
 
 
 def inner(wide, planes, own):
@@ -474,7 +513,7 @@
 
 
 def outer(wide, rims, planes, state, cells_x, cells_y):
-    out = jax.ShapeDtypeStruct((cells_x, cells_y, wide.shape[-1]), jnp.float32)
+    out = pltpu.HBM((cells_x, cells_y, wide.shape[-1]), jnp.float32)
     kept = [vmem_out(*wide.shape)] + [vmem_out(*value.shape) for value in state]
     first = len(rims) + 2
     aliases = {0: 0} | {first + number: 1 + number for number in range(len(state))}
@@ -482,8 +521,9 @@
         outer_kernel,
         out_shape=kept + [out] * 3,
         in_specs=in_vmem(first + len(state)),
-        out_specs=in_vmem(len(kept) + 3),
+        out_specs=in_vmem(len(kept)) + [pl.BlockSpec(memory_space=pltpu.HBM)] * 3,
         input_output_aliases=aliases,
+        scratch_shapes=[pltpu.SemaphoreType.DMA((3, QUARTERS))],
         compiler_params=PARAMS,
         name="outer_steps",
     )(

time: 29.5 us -> 29.3 us (level)
  no operation moved by 1% of the time
where the time goes in v15:
time: 29.3 us; the launch traced here: 29.1 us
  starting transfers between devices  17.2 us (59%)
  Pallas kernels  9.73 us (33%)
  between operations  1.46 us (5%)
  waiting for transfers between devices  0.68 us (2%)
    ppermute x6, starting transfers between devices, swap(): return lax.ppermute(value, axis, pairs)  10.3 us
    ppermute x3, starting transfers between devices, doubled(): lax.ppermute(windows, axis, pairs)  6.86 us
    pallas_call x1, Pallas kernels, inner(): pl.pallas_call(inner_kernel, out_shape=[vmem_out(4, *tile)] * STEPS + [vm...  3.65 us
    pallas_call x1, Pallas kernels, outer(): pl.pallas_call(outer_kernel, out_shape=kept + [out] * 3, in_specs=in_vmem...  3.32 us
    pallas_call x1, Pallas kernels, pack(): pl.pallas_call(functools.partial(pack_kernel, count), out_shape=[wide, ri...  1.64 us
    ppermute x3, waiting for transfers between devices, doubled(): lax.ppermute(windows, axis, pairs)  0.66 us
  transfers between devices with their start and end apart: 9, of which 1 were waited for; matrix products, arithmetic and copies ran while one was open for 0% of the time, Pallas kernels for 16%

profile of v15, /device:TPU:1, one launch (start us, length us, event | category | flops | bytes accessed | tf_op | source)
XLA Modules:
  0.0 29.1 jit_solution(2662006136548809610)
XLA Ops:
  1.3 1.6 %pack_y_rims.1 = (f32[13,26,24,128]{3,2,1,0:T(8,128)S(1)}, f32[11,16,4,128]{3,2,1,0:T(4,128)S(1)}, f32[11,16,4,128]{3,2,1,0:T(4,128)S(1)}, f32[1,4,128]{2,1,0:T(4,128)S(1)}) custom-call(f32[16,16,128]{2,1,0:T(8,128)} %refs_0_.1, f32[16,16,128]{2,1,0:T(8,128)} %refs_1_.1, f32[16,16,128]{2,1,0:T(8,128)} %refs_2_.1, f32[16,16,128]{2,1,0:T(8,128)} %refs_3_.1, ...), custom_call_target="tpu_custom_call" | custom-call | tf_op jit(solution)/shard_map/pack_y_rims/pallas_call | solution.py:127
  2.9 0.1 pack_x_rims.1
  3.0 0.1 collective-permute-start.2
  3.1 2.8 %collective-permute-start = (f32[11,16,4,128]{3,2,1,0:T(4,128)S(1)}, f32[11,16,4,128]{3,2,1,0:T(4,128)S(1)}, u32[]{:S(2)}, u32[]{:S(2)}) collective-permute-start(f32[11,16,4,128]{3,2,1,0:T(4,128)S(1)} %get-tuple-element.24), channel_id=1, source_target_pairs={{0,1},{2,3},{1,0},{3,2},{4,5},{6,7},{5,4},{7,6},{8,9},{10,11},{9,8... | collective-permute-start | bytes 1081352 | tf_op jit(solution)/shard_map/ppermute | solution.py:33
  5.9 0.7 %collective-permute-start.1 = (f32[11,16,4,128]{3,2,1,0:T(4,128)S(1)}, f32[11,16,4,128]{3,2,1,0:T(4,128)S(1)}, u32[]{:S(2)}, u32[]{:S(2)}) collective-permute-start(f32[11,16,4,128]{3,2,1,0:T(4,128)S(1)} %get-tuple-element.25), channel_id=1, source_target_pairs={{1,2},{2,1},{5,6},{6,5},{9,10},{10,9},{13,14},{14,13},{17,18},{18,... | collective-permute-start | bytes 1081352 | tf_op jit(solution)/shard_map/ppermute | solution.py:33
  6.6 0.0 collective-permute-done.2.refs_1_
  6.6 1.3 %collective-permute-start.3 = (f32[2,4,128]{2,1,0:T(4,128)S(1)}, f32[2,4,128]{2,1,0:T(4,128)S(1)}, u32[]{:S(2)}, u32[]{:S(2)}) collective-permute-start(f32[2,4,128]{2,1,0:T(4,128)S(1)} %pad_maximum_fusion.2), channel_id=1, source_target_pairs={{0,8},{4,12},{8,0},{12,4},{1,9},{5,13},{9,1},{13,5},{2,10},{6,14},... | collective-permute-start | bytes 12296 | tf_op jit(solution)/shard_map/ppermute | solution.py:544
  7.9 2.7 %collective-permute-start.5 = (f32[43,16,128]{2,1,0:T(8,128)S(1)}, f32[43,16,128]{2,1,0:T(8,128)S(1)}, u32[]{:S(2)}, u32[]{:S(2)}) collective-permute-start(f32[43,16,128]{2,1,0:T(8,128)S(1)} %get-tuple-element.28), channel_id=1, source_target_pairs={{4,8},{8,4},{5,9},{9,5},{6,10},{10,6},{7,11},{11,7},{20,24},{24,20... | collective-permute-start | bytes 1056776 | tf_op jit(solution)/shard_map/ppermute | solution.py:33
  10.6 0.0 collective-permute-done.3
  10.6 4.2 %collective-permute-start.4 = (f32[4,4,128]{2,1,0:T(4,128)S(1)}, f32[4,4,128]{2,1,0:T(4,128)S(1)}, u32[]{:S(2)}, u32[]{:S(2)}) collective-permute-start(f32[4,4,128]{2,1,0:T(4,128)S(1)} %pad_maximum_fusion.1._), channel_id=1, source_target_pairs={{0,1},{1,0},{2,3},{3,2},{4,5},{5,4},{6,7},{7,6},{8,9},{9,8},{10,11... | collective-permute-start | bytes 24584 | tf_op jit(solution)/shard_map/ppermute | solution.py:544
  14.8 0.4 %own_factors.1.___.own = f32[9,16,16,128]{3,2,1,0:T(8,128)S(1)} custom-call(f32[13,26,24,128]{3,2,1,0:T(8,128)S(1)} %get-tuple-element.23.wide._, f32[4,4,128]{2,1,0:T(4,128)S(1)} %pad_maximum_fusion.1._), custom_call_target="tpu_custom_call" | custom-call | tf_op jit(solution)/shard_map/own_factors/pallas_call | solution.py:263
  15.1 0.7 %collective-permute-done.4 = f32[4,4,128]{2,1,0:T(4,128)S(1)} collective-permute-done((f32[4,4,128]{2,1,0:T(4,128)S(1)}, f32[4,4,128]{2,1,0:T(4,128)S(1)}, u32[]{:S(2)}, u32[]{:S(2)}) %collective-permute-start.4) | collective-permute-done | bytes 8224 | tf_op jit(solution)/shard_map/ppermute | solution.py:544
  15.8 0.0 copy-start
  15.8 0.0 copy-start.1
  15.8 1.4 %collective-permute-start.8 = (f32[8,4,128]{2,1,0:T(4,128)S(1)}, f32[8,4,128]{2,1,0:T(4,128)S(1)}, u32[]{:S(2)}, u32[]{:S(2)}) collective-permute-start(f32[8,4,128]{2,1,0:T(4,128)S(1)} %pad_maximum_fusion.__), channel_id=1, source_target_pairs={{0,2},{1,3},{2,0},{3,1},{4,6},{5,7},{6,4},{7,5},{8,10},{9,11},{10,... | collective-permute-start | bytes 49160 | tf_op jit(solution)/shard_map/ppermute | solution.py:544
  17.2 0.0 collective-permute-done.y_a
  17.2 0.0 collective-permute-done.1.y_b
  17.2 0.2 pack_corners.1
  17.5 1.1 %collective-permute-start.6 = (f32[43,8,128]{2,1,0:T(8,128)S(1)}, f32[43,8,128]{2,1,0:T(8,128)S(1)}, u32[]{:S(2)}, u32[]{:S(2)}) collective-permute-start(f32[43,8,128]{2,1,0:T(8,128)S(1)} %get-tuple-element.29), channel_id=1, source_target_pairs={{0,4},{8,12},{4,0},{12,8},{1,5},{9,13},{5,1},{13,9},{2,6},{10,14},... | collective-permute-start | bytes 528392 | tf_op jit(solution)/shard_map/ppermute | solution.py:33
  18.6 3.0 %collective-permute-start.7 = (f32[43,8,128]{2,1,0:T(8,128)S(1)}, f32[43,8,128]{2,1,0:T(8,128)S(1)}, u32[]{:S(2)}, u32[]{:S(2)}) collective-permute-start(f32[43,8,128]{2,1,0:T(8,128)S(1)} %get-tuple-element.30), channel_id=1, source_target_pairs={{4,8},{8,4},{5,9},{9,5},{6,10},{10,6},{7,11},{11,7},{20,24},{24,20... | collective-permute-start | bytes 528392 | tf_op jit(solution)/shard_map/ppermute | solution.py:33
  21.6 0.0 collective-permute-done.8
  21.6 0.0 copy-done
  21.6 0.0 copy-done.1
  21.7 0.5 %inject.1.planes.refs_5_ = f32[4,3,8,128]{3,2,1,0:T(8,128)S(1)} custom-call(f32[16,4,128]{2,1,0:T(4,128)S(1)} %constant_dynamic-update-slice_fusion.gathered, s32[8,128]{1,0:T(8,128)S(1)} %bitcast.2, s32[8,128]{1,0:T(8,128)S(1)} %bitcast.3), custom_call_target="tpu_custom_call" | custom-call | tf_op jit(solution)/shard_map/inject/pallas_call | solution.py:614
  22.1 3.6 %inner_steps.1 = (f32[4,26,3,8,128]{4,3,2,1,0:T(8,128)S(1)}, f32[4,26,3,8,128]{4,3,2,1,0:T(8,128)S(1)}, f32[4,26,3,8,128]{4,3,2,1,0:T(8,128)S(1)}, f32[4,26,3,8,...) custom-call(f32[13,26,24,128]{3,2,1,0:T(8,128)S(1)} %get-tuple-element.27.wide.refs_0_, ...), custom_call_target="tpu_custom_call" | custom-call | tf_op jit(solution)/shard_map/inner_steps/pallas_call | solution.py:504
  25.8 0.0 collective-permute-done.5.refs_2_
  25.8 0.0 collective-permute-done.6.refs_3_
  25.8 0.0 collective-permute-done.7.refs_4_
  25.8 3.3 %outer_steps.1 = (f32[13,26,24,128]{3,2,1,0:T(8,128)S(1)}, f32[4,26,3,8,128]{4,3,2,1,0:T(8,128)S(1)}, f32[4,26,3,8,128]{4,3,2,1,0:T(8,128)S(1)}, f32[4,26,3,8,12...) custom-call(f32[13,26,24,128]{3,2,1,0:T(8,128)S(1)} %get-tuple-eleme, ...), custom_call_target="tpu_custom_call", output_to_operand_aliasing={{0}: (0, {}), {1}: (6, {}), {2}: (7, {}), {3}: (8, {}), {4}... | custom-call | tf_op jit(solution)/shard_map/outer_steps/pallas_call | solution.py:520
  (8 shorter events, 0.1 us)
Async XLA Ops:
  3.0 3.6 %collective-permute-start.2 = (f32[44,16,128]{2,1,0:T(8,128)S(1)}, f32[44,16,128]{2,1,0:T(8,128)S(1)}, u32[]{:S(2)}, u32[]{:S(2)}) collective-permute-start(f32[44,16,128]{2,1,0:T(8,128)S(1)} %get-tuple-element.26), channel_id=1, source_target_pairs={{0,4},{8,12},{4,0},{12,8},{1,5},{9,13},{5,1},{13,9},{2,6},{10,14},... | collective-permute-start | bytes 1081352 | tf_op jit(solution)/shard_map/ppermute | solution.py:33
  3.1 14.1 %collective-permute-start = (f32[11,16,4,128]{3,2,1,0:T(4,128)S(1)}, f32[11,16,4,128]{3,2,1,0:T(4,128)S(1)}, u32[]{:S(2)}, u32[]{:S(2)}) collective-permute-start(f32[11,16,4,128]{3,2,1,0:T(4,128)S(1)} %get-tuple-element.24), channel_id=1, source_target_pairs={{0,1},{2,3},{1,0},{3,2},{4,5},{6,7},{5,4},{7,6},{8,9},{10,11},{9,8... | collective-permute-start | bytes 1081352 | tf_op jit(solution)/shard_map/ppermute | solution.py:33
  5.9 11.3 %collective-permute-start.1 = (f32[11,16,4,128]{3,2,1,0:T(4,128)S(1)}, f32[11,16,4,128]{3,2,1,0:T(4,128)S(1)}, u32[]{:S(2)}, u32[]{:S(2)}) collective-permute-start(f32[11,16,4,128]{3,2,1,0:T(4,128)S(1)} %get-tuple-element.25), channel_id=1, source_target_pairs={{1,2},{2,1},{5,6},{6,5},{9,10},{10,9},{13,14},{14,13},{17,18},{18,... | collective-permute-start | bytes 1081352 | tf_op jit(solution)/shard_map/ppermute | solution.py:33
  6.6 3.9 %collective-permute-start.3 = (f32[2,4,128]{2,1,0:T(4,128)S(1)}, f32[2,4,128]{2,1,0:T(4,128)S(1)}, u32[]{:S(2)}, u32[]{:S(2)}) collective-permute-start(f32[2,4,128]{2,1,0:T(4,128)S(1)} %pad_maximum_fusion.2), channel_id=1, source_target_pairs={{0,8},{4,12},{8,0},{12,4},{1,9},{5,13},{9,1},{13,5},{2,10},{6,14},... | collective-permute-start | bytes 12296 | tf_op jit(solution)/shard_map/ppermute | solution.py:544
  7.9 17.9 %collective-permute-start.5 = (f32[43,16,128]{2,1,0:T(8,128)S(1)}, f32[43,16,128]{2,1,0:T(8,128)S(1)}, u32[]{:S(2)}, u32[]{:S(2)}) collective-permute-start(f32[43,16,128]{2,1,0:T(8,128)S(1)} %get-tuple-element.28), channel_id=1, source_target_pairs={{4,8},{8,4},{5,9},{9,5},{6,10},{10,6},{7,11},{11,7},{20,24},{24,20... | collective-permute-start | bytes 1056776 | tf_op jit(solution)/shard_map/ppermute | solution.py:33
  10.6 5.2 %collective-permute-start.4 = (f32[4,4,128]{2,1,0:T(4,128)S(1)}, f32[4,4,128]{2,1,0:T(4,128)S(1)}, u32[]{:S(2)}, u32[]{:S(2)}) collective-permute-start(f32[4,4,128]{2,1,0:T(4,128)S(1)} %pad_maximum_fusion.1._), channel_id=1, source_target_pairs={{0,1},{1,0},{2,3},{3,2},{4,5},{5,4},{6,7},{7,6},{8,9},{9,8},{10,11... | collective-permute-start | bytes 24584 | tf_op jit(solution)/shard_map/ppermute | solution.py:544
  15.8 5.8 %copy-start = (s32[1024]{0:T(1024)S(1)}, s32[1024]{0:T(1024)}, u32[]{:S(2)}) copy-start(s32[1024]{0:T(1024)} %param.31) | copy-start | bytes 12292
  15.8 5.8 %copy-start.1 = (s32[1024]{0:T(1024)S(1)}, s32[1024]{0:T(1024)}, u32[]{:S(2)}) copy-start(s32[1024]{0:T(1024)} %param.32) | copy-start | bytes 12292
  15.8 5.8 %collective-permute-start.8 = (f32[8,4,128]{2,1,0:T(4,128)S(1)}, f32[8,4,128]{2,1,0:T(4,128)S(1)}, u32[]{:S(2)}, u32[]{:S(2)}) collective-permute-start(f32[8,4,128]{2,1,0:T(4,128)S(1)} %pad_maximum_fusion.__), channel_id=1, source_target_pairs={{0,2},{1,3},{2,0},{3,1},{4,6},{5,7},{6,4},{7,5},{8,10},{9,11},{10,... | collective-permute-start | bytes 49160 | tf_op jit(solution)/shard_map/ppermute | solution.py:544
  17.5 8.3 %collective-permute-start.6 = (f32[43,8,128]{2,1,0:T(8,128)S(1)}, f32[43,8,128]{2,1,0:T(8,128)S(1)}, u32[]{:S(2)}, u32[]{:S(2)}) collective-permute-start(f32[43,8,128]{2,1,0:T(8,128)S(1)} %get-tuple-element.29), channel_id=1, source_target_pairs={{0,4},{8,12},{4,0},{12,8},{1,5},{9,13},{5,1},{13,9},{2,6},{10,14},... | collective-permute-start | bytes 528392 | tf_op jit(solution)/shard_map/ppermute | solution.py:33
  18.6 7.2 %collective-permute-start.7 = (f32[43,8,128]{2,1,0:T(8,128)S(1)}, f32[43,8,128]{2,1,0:T(8,128)S(1)}, u32[]{:S(2)}, u32[]{:S(2)}) collective-permute-start(f32[43,8,128]{2,1,0:T(8,128)S(1)} %get-tuple-element.30), channel_id=1, source_target_pairs={{4,8},{8,4},{5,9},{9,5},{6,10},{10,6},{7,11},{11,7},{20,24},{24,20... | collective-permute-start | bytes 528392 | tf_op jit(solution)/shard_map/ppermute | solution.py:33

commit v16 on v15

--- a/solution.py
+++ b/solution.py
@@ -169,7 +169,7 @@
     )(pinned(wide, pltpu.VMEM), window)
 
 
-def corner_kernel(_, y_a, y_b, __, ___, wide, c_a, c_b):
+def corner_kernel(_, y_a, y_b, __, ___, ____, wide, c_a, c_b):
     cells_x = y_a.shape[1]
     cells_y = wide.shape[2] - 2 * RIM
     odd_x, odd_y = is_odd("gx"), is_odd("gy")
@@ -200,7 +200,7 @@
     return pl.pallas_call(
         corner_kernel,
         out_shape=[vmem_out(*wide.shape), corner, corner],
-        in_specs=in_vmem(5),
+        in_specs=in_vmem(6),
         out_specs=in_vmem(3),
         input_output_aliases={0: 0},
         compiler_params=PARAMS,
@@ -246,23 +246,23 @@
 
 
 def own_kernel(wide, _, own):
-    _, cells_x, cells_y, _ = own.shape
+    _, cells_x, rows, _ = own.shape
+    cells_y = rows - 2 * RIM
 
     def body(i):
         for x in [4 * i + k for k in range(4)]:
             raw = [wide[FIELDS + number, RIM + x, :cells_y, :] for number in range(5)]
             for number, value in enumerate(factors_of(*raw)):
-                own[number, x] = value
+                own[number, x, :cells_y, :] = value
 
     repeat(cells_x // 4, body)
 
 
 def own_factors(wide, earlier):
     _, planes_x, rows, depth = wide.shape
-    cells_x, cells_y = planes_x - 2 * RIM - 2, rows - 2 * RIM
     return pl.pallas_call(
         own_kernel,
-        out_shape=vmem_out(FACTORS, cells_x, cells_y, depth),
+        out_shape=vmem_out(FACTORS, planes_x - 2 * RIM - 2, rows, depth),
         in_specs=in_vmem(2),
         out_specs=in_vmem(1)[0],
         compiler_params=PARAMS,
@@ -413,17 +413,16 @@
     lax.fori_loop(0, count, run, 0)
 
 
-def inner_kernel(wide, planes, own, *refs):
+def inner_kernel(wide, planes, _, *refs):
     steps = Steps(wide, planes, refs[:STEPS], refs[STEPS])
     natural = refs[STEPS + 1]
-    cells_x, cells_y, tiles = steps.cells_x, own.shape[2], steps.tiles
+    cells_x, cells_y, tiles = steps.cells_x, natural.shape[2] - 2 * RIM, steps.tiles
 
     def rim_rows(i):
         for x in [4 * i + k for k in range(4)]:
             raw = [wide[FIELDS + number, RIM + x, cells_y:, :] for number in range(5)]
             for number, value in enumerate(factors_of(*raw)):
                 natural[number, x, cells_y:, :] = value
-                natural[number, x, :cells_y, :] = own[number, x]
 
     def in_step_order(i):
         for x in [2 * i + k for k in range(2)]:
@@ -503,13 +502,14 @@
     tile = (planes_x, rows // SUBLANES, SUBLANES, depth)
     return pl.pallas_call(
         inner_kernel,
-        out_shape=[vmem_out(4, *tile)] * STEPS + [vmem_out(FACTORS, *tile)],
+        out_shape=[vmem_out(4, *tile)] * STEPS
+        + [vmem_out(FACTORS, *tile), vmem_out(*own.shape)],
         in_specs=in_vmem(3),
-        out_specs=in_vmem(STEPS + 1),
-        scratch_shapes=[pltpu.VMEM((FACTORS, own.shape[1], rows, depth), jnp.float32)],
+        out_specs=in_vmem(STEPS + 2),
+        input_output_aliases={2: STEPS + 1},
         compiler_params=PARAMS,
         name="inner_steps",
-    )(pinned(wide, pltpu.VMEM), planes, pinned(own, pltpu.VMEM))
+    )(pinned(wide, pltpu.VMEM), planes, pinned(own, pltpu.VMEM))[:-1]
 
 
 def outer(wide, rims, planes, state, cells_x, cells_y):
@@ -544,16 +544,11 @@
     return jnp.concatenate([windows, lax.ppermute(windows, axis, pairs)], axis=0)
 
 
-def inject_kernel(samples, cells_x, cells_y, gathered, table_x, table_y, planes, weights, picks):
+def table_kernel(samples, cells_x, table_x, table_y, picks, rows_y):
     size_y = lax.axis_size("gy")
     own_x, own_y = lax.axis_index("gx"), lax.axis_index("gy")
-    rows = cells_y + 2 * RIM
-    tiles = rows // SUBLANES
     wide_x = picks.shape[0]
     in_row = LANES // samples
-    place = lax.broadcasted_iota(jnp.int32, (rows, LANES), 0)
-    row = tiles * lax.rem(place, SUBLANES) + lax.div(place, SUBLANES)
-    y_global = own_y * cells_y + jnp.where(row < cells_y + RIM, row, row - rows)
     x_global = own_x * cells_x - RIM + lax.broadcasted_iota(jnp.int32, (wide_x, LANES), 0)
     lane = lax.broadcasted_iota(jnp.int32, (1, LANES), 1)
     bits_x, bits_y = bits_of("gx"), bits_of("gy")
@@ -568,24 +563,54 @@
                 device_y = jnp.bitwise_xor(device_y, bit)
         return device_x * size_y + device_y
 
-    for group in range(gathered.shape[0] // in_row):
+    for group in range(rows_y.shape[0]):
         at_x = at_y = jnp.zeros((1, LANES), jnp.int32)
-        window = jnp.zeros((STEPS, LANES), jnp.float32)
         for part in range(in_row):
-            place = group * in_row + part
-            device = source(place)
+            device = source(group * in_row + part)
             here = (lane >= part * samples) & (lane < (part + 1) * samples)
             shift = lax.rem((part - lax.rem(device, in_row)) * samples + LANES, LANES)
             table_row = pl.ds(lax.div(device, in_row), 1)
             at_x = jnp.where(here, pltpu.roll(table_x[table_row, :], shift, 1), at_x)
             at_y = jnp.where(here, pltpu.roll(table_y[table_row, :], shift, 1), at_y)
-            moved = gathered[place]
-            if part:
-                moved = pltpu.roll(moved, part * samples, 1)
+        span = slice(group * LANES, (group + 1) * LANES)
+        picks[:, span] = (at_x == x_global).astype(jnp.float32)
+        rows_y[group : group + 1, :] = at_y
+
+
+def receiver_tables(receiver_x, receiver_y, samples, cells_x):
+    receivers = receiver_x.shape[0]
+    wide_x = -(-(cells_x + 2 * RIM) // 32) * 32
+    return pl.pallas_call(
+        functools.partial(table_kernel, samples, cells_x),
+        out_shape=[
+            vmem_out(wide_x, receivers),
+            pltpu.VMEM((receivers // LANES, LANES), jnp.int32),
+        ],
+        in_specs=in_vmem(2),
+        out_specs=in_vmem(2),
+        compiler_params=PARAMS,
+        name="receiver_tables",
+    )(receiver_x.reshape(-1, LANES), receiver_y.reshape(-1, LANES))
+
+
+def inject_kernel(samples, cells_y, gathered, picks, rows_y, planes, weights):
+    own_y = lax.axis_index("gy")
+    rows = cells_y + 2 * RIM
+    tiles = rows // SUBLANES
+    wide_x = picks.shape[0]
+    in_row = LANES // samples
+    place = lax.broadcasted_iota(jnp.int32, (rows, LANES), 0)
+    row = tiles * lax.rem(place, SUBLANES) + lax.div(place, SUBLANES)
+    y_global = own_y * cells_y + jnp.where(row < cells_y + RIM, row, row - rows)
+    lane = lax.broadcasted_iota(jnp.int32, (1, LANES), 1)
+    for group in range(rows_y.shape[0]):
+        window = gathered[group * in_row]
+        for part in range(1, in_row):
+            here = (lane >= part * samples) & (lane < (part + 1) * samples)
+            moved = pltpu.roll(gathered[group * in_row + part], part * samples, 1)
             window = jnp.where(here, moved, window)
         span = slice(group * LANES, (group + 1) * LANES)
-        picks[:, span] = (at_x == x_global).astype(jnp.float32)
-        is_y = at_y == y_global
+        is_y = rows_y[group : group + 1, :] == y_global
         for sample in range(STEPS):
             weights[sample * rows : (sample + 1) * rows, span] = jnp.where(
                 is_y, window[sample : sample + 1], 0.0
@@ -607,22 +632,17 @@
             planes[sample, tile, :, :wide_x] = total[begin : begin + SUBLANES]
 
 
-def injected(gathered, receiver_x, receiver_y, samples, cells_x, cells_y, depth):
+def injected(gathered, picks, rows_y, samples, cells_y, depth):
     rows = cells_y + 2 * RIM
-    receivers = receiver_x.shape[0]
-    wide_x = -(-(cells_x + 2 * RIM) // 32) * 32
     return pl.pallas_call(
-        functools.partial(inject_kernel, samples, cells_x, cells_y),
+        functools.partial(inject_kernel, samples, cells_y),
         out_shape=vmem_out(STEPS, rows // SUBLANES, SUBLANES, depth),
         in_specs=in_vmem(3),
         out_specs=in_vmem(1)[0],
-        scratch_shapes=[
-            pltpu.VMEM((STEPS * rows, receivers), jnp.float32),
-            pltpu.VMEM((wide_x, receivers), jnp.float32),
-        ],
+        scratch_shapes=[pltpu.VMEM((STEPS * rows, picks.shape[1]), jnp.float32)],
         compiler_params=PARAMS,
         name="inject",
-    )(gathered, receiver_x.reshape(-1, LANES), receiver_y.reshape(-1, LANES))
+    )(gathered, pinned(picks, pltpu.VMEM), pinned(rows_y, pltpu.VMEM))
 
 
 def per_device(
@@ -670,13 +690,14 @@
     own = own_factors(wide, windows)
     for bit in bits_of("gy")[:-1]:
         windows = doubled(windows, "gy", bit)
-    wide, c_a, c_b = corners(wide, y_a, y_b, windows, pinned(own, pltpu.VMEM))
+    picks, rows_y = receiver_tables(receiver_x, receiver_y, traces.shape[1], cells_x)
+    wide, c_a, c_b = corners(
+        wide, y_a, y_b, windows, pinned(own, pltpu.VMEM), pinned(rows_y, pltpu.VMEM)
+    )
     for bit in bits_of("gy")[-1:]:
         windows = doubled(windows, "gy", bit)
     c_a, c_b = swap(c_a, "gx", 0), swap(c_b, "gx", 1)
-    planes = injected(
-        windows, receiver_x, receiver_y, traces.shape[1], cells_x, cells_y, depth
-    )
+    planes = injected(windows, picks, rows_y, traces.shape[1], cells_y, depth)
     state = inner(wide, planes, own)
     return tuple(outer(wide, (x_a, x_b, c_a, c_b), planes, state, cells_x, cells_y))
 

time: 29.3 us -> 29 us (0.990)
  starting transfers between devices: 17.2 us -> 16.6 us
  waiting for transfers between devices: 0.68 us -> 0.99 us
    ppermute x3, starting transfers between devices: 6.86 us -> 6.48 us  [doubled(): lax.ppermute(windows, axis, pairs)]
    ppermute x3, waiting for transfers between devices: 0.66 us -> 0.98 us  [doubled(): lax.ppermute(windows, axis, pairs)]
    pallas_call x2 -> x3, Pallas kernels: 0.84 us -> 0.91 us  [the longest x1 0.37 us: own_factors(): pl.pallas_call(own_kernel, out_shape=vmem_out(FACTORS, planes_x - 2 * RIM...]
where the time goes in v16:
time: 29 us; the launch traced here: 28.8 us
  starting transfers between devices  16.6 us (57%)
  Pallas kernels  9.62 us (33%)
  between operations  1.48 us (5%)
  waiting for transfers between devices  0.99 us (3%)
    ppermute x6, starting transfers between devices, swap(): return lax.ppermute(value, axis, pairs)  10.2 us
    ppermute x3, starting transfers between devices, doubled(): lax.ppermute(windows, axis, pairs)  6.48 us
    pallas_call x1, Pallas kernels, inner(): pl.pallas_call(inner_kernel, out_shape=[vmem_out(4, *tile)] * STEPS + [vm...  3.5 us
    pallas_call x1, Pallas kernels, outer(): pl.pallas_call(outer_kernel, out_shape=kept + [out] * 3, in_specs=in_vmem...  3.28 us
    pallas_call x1, Pallas kernels, pack(): pl.pallas_call(functools.partial(pack_kernel, count), out_shape=[wide, ri...  1.64 us
    ppermute x3, waiting for transfers between devices, doubled(): lax.ppermute(windows, axis, pairs)  0.98 us
  transfers between devices with their start and end apart: 9, of which 1 were waited for; matrix products, arithmetic and copies ran while one was open for 0% of the time, Pallas kernels for 16%

profile of v16, /device:TPU:1, one launch (start us, length us, event | category | flops | bytes accessed | tf_op | source)
XLA Modules:
  0.0 28.8 jit_solution(1630929237357944920)
XLA Ops:
  1.3 1.6 %pack_y_rims.1 = (f32[13,26,24,128]{3,2,1,0:T(8,128)S(1)}, f32[11,16,4,128]{3,2,1,0:T(4,128)S(1)}, f32[11,16,4,128]{3,2,1,0:T(4,128)S(1)}, f32[1,4,128]{2,1,0:T(4,128)S(1)}) custom-call(f32[16,16,128]{2,1,0:T(8,128)} %refs_0_.1, f32[16,16,128]{2,1,0:T(8,128)} %refs_1_.1, f32[16,16,128]{2,1,0:T(8,128)} %refs_2_.1, f32[16,16,128]{2,1,0:T(8,128)} %refs_3_.1, ...), custom_call_target="tpu_custom_call" | custom-call | tf_op jit(solution)/shard_map/pack_y_rims/pallas_call | solution.py:127
  2.9 0.0 copy-start
  2.9 0.0 copy-start.1
  3.0 0.1 pack_x_rims.1
  3.0 0.1 collective-permute-start.2
  3.2 2.8 %collective-permute-start = (f32[11,16,4,128]{3,2,1,0:T(4,128)S(1)}, f32[11,16,4,128]{3,2,1,0:T(4,128)S(1)}, u32[]{:S(2)}, u32[]{:S(2)}) collective-permute-start(f32[11,16,4,128]{3,2,1,0:T(4,128)S(1)} %get-tuple-element.26), channel_id=1, source_target_pairs={{0,1},{2,3},{1,0},{3,2},{4,5},{6,7},{5,4},{7,6},{8,9},{10,11},{9,8... | collective-permute-start | bytes 1081352 | tf_op jit(solution)/shard_map/ppermute | solution.py:33
  5.9 0.7 %collective-permute-start.1 = (f32[11,16,4,128]{3,2,1,0:T(4,128)S(1)}, f32[11,16,4,128]{3,2,1,0:T(4,128)S(1)}, u32[]{:S(2)}, u32[]{:S(2)}) collective-permute-start(f32[11,16,4,128]{3,2,1,0:T(4,128)S(1)} %get-tuple-element.27), channel_id=1, source_target_pairs={{1,2},{2,1},{5,6},{6,5},{9,10},{10,9},{13,14},{14,13},{17,18},{18,... | collective-permute-start | bytes 1081352 | tf_op jit(solution)/shard_map/ppermute | solution.py:33
  6.6 0.0 collective-permute-done.2.refs_1_
  6.6 1.3 %collective-permute-start.3 = (f32[2,4,128]{2,1,0:T(4,128)S(1)}, f32[2,4,128]{2,1,0:T(4,128)S(1)}, u32[]{:S(2)}, u32[]{:S(2)}) collective-permute-start(f32[2,4,128]{2,1,0:T(4,128)S(1)} %pad_maximum_fusion.2), channel_id=1, source_target_pairs={{0,8},{4,12},{8,0},{12,4},{1,9},{5,13},{9,1},{13,5},{2,10},{6,14},... | collective-permute-start | bytes 12296 | tf_op jit(solution)/shard_map/ppermute | solution.py:544
  7.9 2.7 %collective-permute-start.5 = (f32[43,16,128]{2,1,0:T(8,128)S(1)}, f32[43,16,128]{2,1,0:T(8,128)S(1)}, u32[]{:S(2)}, u32[]{:S(2)}) collective-permute-start(f32[43,16,128]{2,1,0:T(8,128)S(1)} %get-tuple-element.31), channel_id=1, source_target_pairs={{4,8},{8,4},{5,9},{9,5},{6,10},{10,6},{7,11},{11,7},{20,24},{24,20... | collective-permute-start | bytes 1056776 | tf_op jit(solution)/shard_map/ppermute | solution.py:33
  10.6 0.0 copy-done
  10.6 0.0 copy-done.1
  10.6 0.2 receiver_tables.1
  10.8 0.0 collective-permute-done.3
  10.8 4.2 %collective-permute-start.4 = (f32[4,4,128]{2,1,0:T(4,128)S(1)}, f32[4,4,128]{2,1,0:T(4,128)S(1)}, u32[]{:S(2)}, u32[]{:S(2)}) collective-permute-start(f32[4,4,128]{2,1,0:T(4,128)S(1)} %pad_maximum_fusion.1._), channel_id=1, source_target_pairs={{0,1},{1,0},{2,3},{3,2},{4,5},{5,4},{6,7},{7,6},{8,9},{9,8},{10,11... | collective-permute-start | bytes 24584 | tf_op jit(solution)/shard_map/ppermute | solution.py:544
  15.0 0.4 %own_factors.1.___._ = f32[9,16,24,128]{3,2,1,0:T(8,128)S(1)} custom-call(f32[13,26,24,128]{3,2,1,0:T(8,128)S(1)} %get-tuple-element.25.wide._, f32[4,4,128]{2,1,0:T(4,128)S(1)} %pad_maximum_fusion.1._), custom_call_target="tpu_custom_call" | custom-call | tf_op jit(solution)/shard_map/own_factors/pallas_call | solution.py:263
  15.4 1.0 %collective-permute-done.4 = f32[4,4,128]{2,1,0:T(4,128)S(1)} collective-permute-done((f32[4,4,128]{2,1,0:T(4,128)S(1)}, f32[4,4,128]{2,1,0:T(4,128)S(1)}, u32[]{:S(2)}, u32[]{:S(2)}) %collective-permute-start.4) | collective-permute-done | bytes 8224 | tf_op jit(solution)/shard_map/ppermute | solution.py:544
  16.3 1.0 %collective-permute-start.8 = (f32[8,4,128]{2,1,0:T(4,128)S(1)}, f32[8,4,128]{2,1,0:T(4,128)S(1)}, u32[]{:S(2)}, u32[]{:S(2)}) collective-permute-start(f32[8,4,128]{2,1,0:T(4,128)S(1)} %pad_maximum_fusion.__), channel_id=1, source_target_pairs={{0,2},{1,3},{2,0},{3,1},{4,6},{5,7},{6,4},{7,5},{8,10},{9,11},{10,... | collective-permute-start | bytes 49160 | tf_op jit(solution)/shard_map/ppermute | solution.py:544
  17.4 0.0 collective-permute-done.y_a
  17.4 0.0 collective-permute-done.1.y_b
  17.4 0.2 pack_corners.1
  17.6 0.9 %collective-permute-start.6 = (f32[43,8,128]{2,1,0:T(8,128)S(1)}, f32[43,8,128]{2,1,0:T(8,128)S(1)}, u32[]{:S(2)}, u32[]{:S(2)}) collective-permute-start(f32[43,8,128]{2,1,0:T(8,128)S(1)} %get-tuple-element.32), channel_id=1, source_target_pairs={{0,4},{8,12},{4,0},{12,8},{1,5},{9,13},{5,1},{13,9},{2,6},{10,14},... | collective-permute-start | bytes 528392 | tf_op jit(solution)/shard_map/ppermute | solution.py:33
  18.5 3.0 %collective-permute-start.7 = (f32[43,8,128]{2,1,0:T(8,128)S(1)}, f32[43,8,128]{2,1,0:T(8,128)S(1)}, u32[]{:S(2)}, u32[]{:S(2)}) collective-permute-start(f32[43,8,128]{2,1,0:T(8,128)S(1)} %get-tuple-element.33), channel_id=1, source_target_pairs={{4,8},{8,4},{5,9},{9,5},{6,10},{10,6},{7,11},{11,7},{20,24},{24,20... | collective-permute-start | bytes 528392 | tf_op jit(solution)/shard_map/ppermute | solution.py:33
  21.6 0.0 collective-permute-done.8
  21.6 0.4 %inject.1.planes.refs_5_ = f32[4,3,8,128]{3,2,1,0:T(8,128)S(1)} custom-call(f32[16,4,128]{2,1,0:T(4,128)S(1)} %constant_dynamic-update-slice_fusion.gathered, f32[32,1024]{1,0:T(8,128)S(1)} %get-tuple-element.34.picks, s32[8,128]{1,0:T(8,128)S(1)} %get-tuple-element.29.____.rows_y), custom_call_target="tpu_custom_call" | custom-call | tf_op jit(solution)/shard_map/inject/pallas_call | solution.py:637
  22.0 3.5 %inner_steps.1 = (f32[4,26,3,8,128]{4,3,2,1,0:T(8,128)S(1)}, f32[4,26,3,8,128]{4,3,2,1,0:T(8,128)S(1)}, f32[4,26,3,8,128]{4,3,2,1,0:T(8,128)S(1)}, f32[4,26,3,8,...) custom-call(f32[13,26,24,128]{3,2,1,0:T(8,128)S(1)} %get-tuple-eleme, ...), custom_call_target="tpu_custom_call", output_to_operand_aliasing={{5}: (2, {})} | custom-call | tf_op jit(solution)/shard_map/inner_steps/pallas_call | solution.py:503
  25.5 0.0 collective-permute-done.5.refs_2_
  25.5 0.0 collective-permute-done.6.refs_3_
  25.5 0.0 collective-permute-done.7.refs_4_
  25.5 3.3 %outer_steps.1 = (f32[13,26,24,128]{3,2,1,0:T(8,128)S(1)}, f32[4,26,3,8,128]{4,3,2,1,0:T(8,128)S(1)}, f32[4,26,3,8,128]{4,3,2,1,0:T(8,128)S(1)}, f32[4,26,3,8,12...) custom-call(f32[13,26,24,128]{3,2,1,0:T(8,128)S(1)} %get-tuple-eleme, ...), custom_call_target="tpu_custom_call", output_to_operand_aliasing={{0}: (0, {}), {1}: (6, {}), {2}: (7, {}), {3}: (8, {}), {4}... | custom-call | tf_op jit(solution)/shard_map/outer_steps/pallas_call | solution.py:520
  (8 shorter events, 0.1 us)
Async XLA Ops:
  2.9 7.7 %copy-start = (s32[1024]{0:T(1024)S(1)}, s32[1024]{0:T(1024)}, u32[]{:S(2)}) copy-start(s32[1024]{0:T(1024)} %param.31) | copy-start | bytes 12292
  2.9 7.7 %copy-start.1 = (s32[1024]{0:T(1024)S(1)}, s32[1024]{0:T(1024)}, u32[]{:S(2)}) copy-start(s32[1024]{0:T(1024)} %param.32) | copy-start | bytes 12292
  3.0 3.6 %collective-permute-start.2 = (f32[44,16,128]{2,1,0:T(8,128)S(1)}, f32[44,16,128]{2,1,0:T(8,128)S(1)}, u32[]{:S(2)}, u32[]{:S(2)}) collective-permute-start(f32[44,16,128]{2,1,0:T(8,128)S(1)} %get-tuple-element.28), channel_id=1, source_target_pairs={{0,4},{8,12},{4,0},{12,8},{1,5},{9,13},{5,1},{13,9},{2,6},{10,14},... | collective-permute-start | bytes 1081352 | tf_op jit(solution)/shard_map/ppermute | solution.py:33
  3.2 14.2 %collective-permute-start = (f32[11,16,4,128]{3,2,1,0:T(4,128)S(1)}, f32[11,16,4,128]{3,2,1,0:T(4,128)S(1)}, u32[]{:S(2)}, u32[]{:S(2)}) collective-permute-start(f32[11,16,4,128]{3,2,1,0:T(4,128)S(1)} %get-tuple-element.26), channel_id=1, source_target_pairs={{0,1},{2,3},{1,0},{3,2},{4,5},{6,7},{5,4},{7,6},{8,9},{10,11},{9,8... | collective-permute-start | bytes 1081352 | tf_op jit(solution)/shard_map/ppermute | solution.py:33
  5.9 11.5 %collective-permute-start.1 = (f32[11,16,4,128]{3,2,1,0:T(4,128)S(1)}, f32[11,16,4,128]{3,2,1,0:T(4,128)S(1)}, u32[]{:S(2)}, u32[]{:S(2)}) collective-permute-start(f32[11,16,4,128]{3,2,1,0:T(4,128)S(1)} %get-tuple-element.27), channel_id=1, source_target_pairs={{1,2},{2,1},{5,6},{6,5},{9,10},{10,9},{13,14},{14,13},{17,18},{18,... | collective-permute-start | bytes 1081352 | tf_op jit(solution)/shard_map/ppermute | solution.py:33
  6.6 4.1 %collective-permute-start.3 = (f32[2,4,128]{2,1,0:T(4,128)S(1)}, f32[2,4,128]{2,1,0:T(4,128)S(1)}, u32[]{:S(2)}, u32[]{:S(2)}) collective-permute-start(f32[2,4,128]{2,1,0:T(4,128)S(1)} %pad_maximum_fusion.2), channel_id=1, source_target_pairs={{0,8},{4,12},{8,0},{12,4},{1,9},{5,13},{9,1},{13,5},{2,10},{6,14},... | collective-permute-start | bytes 12296 | tf_op jit(solution)/shard_map/ppermute | solution.py:544
  7.9 17.6 %collective-permute-start.5 = (f32[43,16,128]{2,1,0:T(8,128)S(1)}, f32[43,16,128]{2,1,0:T(8,128)S(1)}, u32[]{:S(2)}, u32[]{:S(2)}) collective-permute-start(f32[43,16,128]{2,1,0:T(8,128)S(1)} %get-tuple-element.31), channel_id=1, source_target_pairs={{4,8},{8,4},{5,9},{9,5},{6,10},{10,6},{7,11},{11,7},{20,24},{24,20... | collective-permute-start | bytes 1056776 | tf_op jit(solution)/shard_map/ppermute | solution.py:33
  10.8 5.5 %collective-permute-start.4 = (f32[4,4,128]{2,1,0:T(4,128)S(1)}, f32[4,4,128]{2,1,0:T(4,128)S(1)}, u32[]{:S(2)}, u32[]{:S(2)}) collective-permute-start(f32[4,4,128]{2,1,0:T(4,128)S(1)} %pad_maximum_fusion.1._), channel_id=1, source_target_pairs={{0,1},{1,0},{2,3},{3,2},{4,5},{5,4},{6,7},{7,6},{8,9},{9,8},{10,11... | collective-permute-start | bytes 24584 | tf_op jit(solution)/shard_map/ppermute | solution.py:544
  16.3 5.2 %collective-permute-start.8 = (f32[8,4,128]{2,1,0:T(4,128)S(1)}, f32[8,4,128]{2,1,0:T(4,128)S(1)}, u32[]{:S(2)}, u32[]{:S(2)}) collective-permute-start(f32[8,4,128]{2,1,0:T(4,128)S(1)} %pad_maximum_fusion.__), channel_id=1, source_target_pairs={{0,2},{1,3},{2,0},{3,1},{4,6},{5,7},{6,4},{7,5},{8,10},{9,11},{10,... | collective-permute-start | bytes 49160 | tf_op jit(solution)/shard_map/ppermute | solution.py:544
  17.6 7.9 %collective-permute-start.6 = (f32[43,8,128]{2,1,0:T(8,128)S(1)}, f32[43,8,128]{2,1,0:T(8,128)S(1)}, u32[]{:S(2)}, u32[]{:S(2)}) collective-permute-start(f32[43,8,128]{2,1,0:T(8,128)S(1)} %get-tuple-element.32), channel_id=1, source_target_pairs={{0,4},{8,12},{4,0},{12,8},{1,5},{9,13},{5,1},{13,9},{2,6},{10,14},... | collective-permute-start | bytes 528392 | tf_op jit(solution)/shard_map/ppermute | solution.py:33
  18.5 7.0 %collective-permute-start.7 = (f32[43,8,128]{2,1,0:T(8,128)S(1)}, f32[43,8,128]{2,1,0:T(8,128)S(1)}, u32[]{:S(2)}, u32[]{:S(2)}) collective-permute-start(f32[43,8,128]{2,1,0:T(8,128)S(1)} %get-tuple-element.33), channel_id=1, source_target_pairs={{4,8},{8,4},{5,9},{9,5},{6,10},{10,6},{7,11},{11,7},{20,24},{24,20... | collective-permute-start | bytes 528392 | tf_op jit(solution)/shard_map/ppermute | solution.py:33

commit v17 on v16

--- a/solution.py
+++ b/solution.py
@@ -437,7 +437,8 @@
     for turn in range(STEPS):
         first, last = RIM + 1 + turn, RIM + cells_x - 1 - turn
         half = (last - first) // 2
-        repeat(2, lambda i, turn=turn, first=first, half=half: steps.step(turn, first + half * i, half))
+        steps.step(turn, first, half)
+        steps.step(turn, first + half, half)
 
 
 def outer_kernel(*refs):

time: 29 us -> 28.7 us (0.990)
  Pallas kernels: 9.62 us -> 9.28 us
    pallas_call x1, Pallas kernels: 3.5 us -> 3.17 us  [inner(): pl.pallas_call(inner_kernel, out_shape=[vmem_out(4, *tile)] * STEPS + [vm...]
  transfers between devices with their start and end apart: 9 -> 9, of which waited for: 1 -> 2; matrix products, arithmetic and copies ran while one was open for 0% -> 0% of each run, Pallas kernels for 16% -> 15%
where the time goes in v17:
time: 28.7 us; the launch traced here: 28.5 us
  starting transfers between devices  16.6 us (58%)
  Pallas kernels  9.28 us (32%)
  between operations  1.47 us (5%)
  waiting for transfers between devices  1.08 us (4%)
    ppermute x6, starting transfers between devices, swap(): return lax.ppermute(value, axis, pairs)  10.2 us
    ppermute x3, starting transfers between devices, doubled(): lax.ppermute(windows, axis, pairs)  6.48 us
    pallas_call x1, Pallas kernels, outer(): pl.pallas_call(outer_kernel, out_shape=kept + [out] * 3, in_specs=in_vmem...  3.27 us
    pallas_call x1, Pallas kernels, inner(): pl.pallas_call(inner_kernel, out_shape=[vmem_out(4, *tile)] * STEPS + [vm...  3.17 us
    pallas_call x1, Pallas kernels, pack(): pl.pallas_call(functools.partial(pack_kernel, count), out_shape=[wide, ri...  1.64 us
    ppermute x3, waiting for transfers between devices, doubled(): lax.ppermute(windows, axis, pairs)  0.98 us
  transfers between devices with their start and end apart: 9, of which 2 were waited for; matrix products, arithmetic and copies ran while one was open for 0% of the time, Pallas kernels for 15%

profile of v17, /device:TPU:1, one launch (start us, length us, event | category | flops | bytes accessed | tf_op | source)
XLA Modules:
  0.0 28.5 jit_solution(14821426210563079913)
XLA Ops:
  1.3 1.6 %pack_y_rims.1 = (f32[13,26,24,128]{3,2,1,0:T(8,128)S(1)}, f32[11,16,4,128]{3,2,1,0:T(4,128)S(1)}, f32[11,16,4,128]{3,2,1,0:T(4,128)S(1)}, f32[1,4,128]{2,1,0:T(4,128)S(1)}) custom-call(f32[16,16,128]{2,1,0:T(8,128)} %refs_0_.1, f32[16,16,128]{2,1,0:T(8,128)} %refs_1_.1, f32[16,16,128]{2,1,0:T(8,128)} %refs_2_.1, f32[16,16,128]{2,1,0:T(8,128)} %refs_3_.1, ...), custom_call_target="tpu_custom_call" | custom-call | tf_op jit(solution)/shard_map/pack_y_rims/pallas_call | solution.py:127
  2.9 0.0 copy-start
  2.9 0.0 copy-start.1
  3.0 0.1 pack_x_rims.1
  3.0 0.1 collective-permute-start.2
  3.2 2.8 %collective-permute-start = (f32[11,16,4,128]{3,2,1,0:T(4,128)S(1)}, f32[11,16,4,128]{3,2,1,0:T(4,128)S(1)}, u32[]{:S(2)}, u32[]{:S(2)}) collective-permute-start(f32[11,16,4,128]{3,2,1,0:T(4,128)S(1)} %get-tuple-element.26), channel_id=1, source_target_pairs={{0,1},{2,3},{1,0},{3,2},{4,5},{6,7},{5,4},{7,6},{8,9},{10,11},{9,8... | collective-permute-start | bytes 1081352 | tf_op jit(solution)/shard_map/ppermute | solution.py:33
  5.9 0.7 %collective-permute-start.1 = (f32[11,16,4,128]{3,2,1,0:T(4,128)S(1)}, f32[11,16,4,128]{3,2,1,0:T(4,128)S(1)}, u32[]{:S(2)}, u32[]{:S(2)}) collective-permute-start(f32[11,16,4,128]{3,2,1,0:T(4,128)S(1)} %get-tuple-element.27), channel_id=1, source_target_pairs={{1,2},{2,1},{5,6},{6,5},{9,10},{10,9},{13,14},{14,13},{17,18},{18,... | collective-permute-start | bytes 1081352 | tf_op jit(solution)/shard_map/ppermute | solution.py:33
  6.6 0.0 collective-permute-done.2.refs_1_
  6.6 1.3 %collective-permute-start.3 = (f32[2,4,128]{2,1,0:T(4,128)S(1)}, f32[2,4,128]{2,1,0:T(4,128)S(1)}, u32[]{:S(2)}, u32[]{:S(2)}) collective-permute-start(f32[2,4,128]{2,1,0:T(4,128)S(1)} %pad_maximum_fusion.2), channel_id=1, source_target_pairs={{0,8},{4,12},{8,0},{12,4},{1,9},{5,13},{9,1},{13,5},{2,10},{6,14},... | collective-permute-start | bytes 12296 | tf_op jit(solution)/shard_map/ppermute | solution.py:545
  7.9 2.7 %collective-permute-start.5 = (f32[43,16,128]{2,1,0:T(8,128)S(1)}, f32[43,16,128]{2,1,0:T(8,128)S(1)}, u32[]{:S(2)}, u32[]{:S(2)}) collective-permute-start(f32[43,16,128]{2,1,0:T(8,128)S(1)} %get-tuple-element.31), channel_id=1, source_target_pairs={{4,8},{8,4},{5,9},{9,5},{6,10},{10,6},{7,11},{11,7},{20,24},{24,20... | collective-permute-start | bytes 1056776 | tf_op jit(solution)/shard_map/ppermute | solution.py:33
  10.6 0.0 copy-done
  10.6 0.0 copy-done.1
  10.6 0.2 receiver_tables.1
  10.8 0.0 collective-permute-done.3
  10.8 4.2 %collective-permute-start.4 = (f32[4,4,128]{2,1,0:T(4,128)S(1)}, f32[4,4,128]{2,1,0:T(4,128)S(1)}, u32[]{:S(2)}, u32[]{:S(2)}) collective-permute-start(f32[4,4,128]{2,1,0:T(4,128)S(1)} %pad_maximum_fusion.1._), channel_id=1, source_target_pairs={{0,1},{1,0},{2,3},{3,2},{4,5},{5,4},{6,7},{7,6},{8,9},{9,8},{10,11... | collective-permute-start | bytes 24584 | tf_op jit(solution)/shard_map/ppermute | solution.py:545
  15.0 0.4 %own_factors.1.___._ = f32[9,16,24,128]{3,2,1,0:T(8,128)S(1)} custom-call(f32[13,26,24,128]{3,2,1,0:T(8,128)S(1)} %get-tuple-element.25.wide._, f32[4,4,128]{2,1,0:T(4,128)S(1)} %pad_maximum_fusion.1._), custom_call_target="tpu_custom_call" | custom-call | tf_op jit(solution)/shard_map/own_factors/pallas_call | solution.py:263
  15.4 1.0 %collective-permute-done.4 = f32[4,4,128]{2,1,0:T(4,128)S(1)} collective-permute-done((f32[4,4,128]{2,1,0:T(4,128)S(1)}, f32[4,4,128]{2,1,0:T(4,128)S(1)}, u32[]{:S(2)}, u32[]{:S(2)}) %collective-permute-start.4) | collective-permute-done | bytes 8224 | tf_op jit(solution)/shard_map/ppermute | solution.py:545
  16.3 1.0 %collective-permute-start.8 = (f32[8,4,128]{2,1,0:T(4,128)S(1)}, f32[8,4,128]{2,1,0:T(4,128)S(1)}, u32[]{:S(2)}, u32[]{:S(2)}) collective-permute-start(f32[8,4,128]{2,1,0:T(4,128)S(1)} %pad_maximum_fusion.__), channel_id=1, source_target_pairs={{0,2},{1,3},{2,0},{3,1},{4,6},{5,7},{6,4},{7,5},{8,10},{9,11},{10,... | collective-permute-start | bytes 49160 | tf_op jit(solution)/shard_map/ppermute | solution.py:545
  17.4 0.0 collective-permute-done.y_a
  17.4 0.0 collective-permute-done.1.y_b
  17.4 0.2 pack_corners.1
  17.6 0.9 %collective-permute-start.6 = (f32[43,8,128]{2,1,0:T(8,128)S(1)}, f32[43,8,128]{2,1,0:T(8,128)S(1)}, u32[]{:S(2)}, u32[]{:S(2)}) collective-permute-start(f32[43,8,128]{2,1,0:T(8,128)S(1)} %get-tuple-element.32), channel_id=1, source_target_pairs={{0,4},{8,12},{4,0},{12,8},{1,5},{9,13},{5,1},{13,9},{2,6},{10,14},... | collective-permute-start | bytes 528392 | tf_op jit(solution)/shard_map/ppermute | solution.py:33
  18.5 3.0 %collective-permute-start.7 = (f32[43,8,128]{2,1,0:T(8,128)S(1)}, f32[43,8,128]{2,1,0:T(8,128)S(1)}, u32[]{:S(2)}, u32[]{:S(2)}) collective-permute-start(f32[43,8,128]{2,1,0:T(8,128)S(1)} %get-tuple-element.33), channel_id=1, source_target_pairs={{4,8},{8,4},{5,9},{9,5},{6,10},{10,6},{7,11},{11,7},{20,24},{24,20... | collective-permute-start | bytes 528392 | tf_op jit(solution)/shard_map/ppermute | solution.py:33
  21.6 0.0 collective-permute-done.8
  21.6 0.4 %inject.1.planes.refs_5_ = f32[4,3,8,128]{3,2,1,0:T(8,128)S(1)} custom-call(f32[16,4,128]{2,1,0:T(4,128)S(1)} %constant_dynamic-update-slice_fusion.gathered, f32[32,1024]{1,0:T(8,128)S(1)} %get-tuple-element.34.picks, s32[8,128]{1,0:T(8,128)S(1)} %get-tuple-element.29.____.rows_y), custom_call_target="tpu_custom_call" | custom-call | tf_op jit(solution)/shard_map/inject/pallas_call | solution.py:638
  22.0 3.2 %inner_steps.1 = (f32[4,26,3,8,128]{4,3,2,1,0:T(8,128)S(1)}, f32[4,26,3,8,128]{4,3,2,1,0:T(8,128)S(1)}, f32[4,26,3,8,128]{4,3,2,1,0:T(8,128)S(1)}, f32[4,26,3,8,...) custom-call(f32[13,26,24,128]{3,2,1,0:T(8,128)S(1)} %get-tuple-eleme, ...), custom_call_target="tpu_custom_call", output_to_operand_aliasing={{5}: (2, {})} | custom-call | tf_op jit(solution)/shard_map/inner_steps/pallas_call | solution.py:504
  25.2 0.0 collective-permute-done.5.refs_2_
  25.2 0.0 collective-permute-done.6.refs_3_
  25.2 0.1 collective-permute-done.7.refs_4_
  25.3 3.3 %outer_steps.1 = (f32[13,26,24,128]{3,2,1,0:T(8,128)S(1)}, f32[4,26,3,8,128]{4,3,2,1,0:T(8,128)S(1)}, f32[4,26,3,8,128]{4,3,2,1,0:T(8,128)S(1)}, f32[4,26,3,8,12...) custom-call(f32[13,26,24,128]{3,2,1,0:T(8,128)S(1)} %get-tuple-eleme, ...), custom_call_target="tpu_custom_call", output_to_operand_aliasing={{0}: (0, {}), {1}: (6, {}), {2}: (7, {}), {3}: (8, {}), {4}... | custom-call | tf_op jit(solution)/shard_map/outer_steps/pallas_call | solution.py:521
  (8 shorter events, 0.1 us)
Async XLA Ops:
  2.9 7.7 %copy-start = (s32[1024]{0:T(1024)S(1)}, s32[1024]{0:T(1024)}, u32[]{:S(2)}) copy-start(s32[1024]{0:T(1024)} %param.31) | copy-start | bytes 12292
  2.9 7.7 %copy-start.1 = (s32[1024]{0:T(1024)S(1)}, s32[1024]{0:T(1024)}, u32[]{:S(2)}) copy-start(s32[1024]{0:T(1024)} %param.32) | copy-start | bytes 12292
  3.0 3.6 %collective-permute-start.2 = (f32[44,16,128]{2,1,0:T(8,128)S(1)}, f32[44,16,128]{2,1,0:T(8,128)S(1)}, u32[]{:S(2)}, u32[]{:S(2)}) collective-permute-start(f32[44,16,128]{2,1,0:T(8,128)S(1)} %get-tuple-element.28), channel_id=1, source_target_pairs={{0,4},{8,12},{4,0},{12,8},{1,5},{9,13},{5,1},{13,9},{2,6},{10,14},... | collective-permute-start | bytes 1081352 | tf_op jit(solution)/shard_map/ppermute | solution.py:33
  3.2 14.2 %collective-permute-start = (f32[11,16,4,128]{3,2,1,0:T(4,128)S(1)}, f32[11,16,4,128]{3,2,1,0:T(4,128)S(1)}, u32[]{:S(2)}, u32[]{:S(2)}) collective-permute-start(f32[11,16,4,128]{3,2,1,0:T(4,128)S(1)} %get-tuple-element.26), channel_id=1, source_target_pairs={{0,1},{2,3},{1,0},{3,2},{4,5},{6,7},{5,4},{7,6},{8,9},{10,11},{9,8... | collective-permute-start | bytes 1081352 | tf_op jit(solution)/shard_map/ppermute | solution.py:33
  5.9 11.5 %collective-permute-start.1 = (f32[11,16,4,128]{3,2,1,0:T(4,128)S(1)}, f32[11,16,4,128]{3,2,1,0:T(4,128)S(1)}, u32[]{:S(2)}, u32[]{:S(2)}) collective-permute-start(f32[11,16,4,128]{3,2,1,0:T(4,128)S(1)} %get-tuple-element.27), channel_id=1, source_target_pairs={{1,2},{2,1},{5,6},{6,5},{9,10},{10,9},{13,14},{14,13},{17,18},{18,... | collective-permute-start | bytes 1081352 | tf_op jit(solution)/shard_map/ppermute | solution.py:33
  6.6 4.1 %collective-permute-start.3 = (f32[2,4,128]{2,1,0:T(4,128)S(1)}, f32[2,4,128]{2,1,0:T(4,128)S(1)}, u32[]{:S(2)}, u32[]{:S(2)}) collective-permute-start(f32[2,4,128]{2,1,0:T(4,128)S(1)} %pad_maximum_fusion.2), channel_id=1, source_target_pairs={{0,8},{4,12},{8,0},{12,4},{1,9},{5,13},{9,1},{13,5},{2,10},{6,14},... | collective-permute-start | bytes 12296 | tf_op jit(solution)/shard_map/ppermute | solution.py:545
  7.9 17.2 %collective-permute-start.5 = (f32[43,16,128]{2,1,0:T(8,128)S(1)}, f32[43,16,128]{2,1,0:T(8,128)S(1)}, u32[]{:S(2)}, u32[]{:S(2)}) collective-permute-start(f32[43,16,128]{2,1,0:T(8,128)S(1)} %get-tuple-element.31), channel_id=1, source_target_pairs={{4,8},{8,4},{5,9},{9,5},{6,10},{10,6},{7,11},{11,7},{20,24},{24,20... | collective-permute-start | bytes 1056776 | tf_op jit(solution)/shard_map/ppermute | solution.py:33
  10.8 5.5 %collective-permute-start.4 = (f32[4,4,128]{2,1,0:T(4,128)S(1)}, f32[4,4,128]{2,1,0:T(4,128)S(1)}, u32[]{:S(2)}, u32[]{:S(2)}) collective-permute-start(f32[4,4,128]{2,1,0:T(4,128)S(1)} %pad_maximum_fusion.1._), channel_id=1, source_target_pairs={{0,1},{1,0},{2,3},{3,2},{4,5},{5,4},{6,7},{7,6},{8,9},{9,8},{10,11... | collective-permute-start | bytes 24584 | tf_op jit(solution)/shard_map/ppermute | solution.py:545
  16.3 5.2 %collective-permute-start.8 = (f32[8,4,128]{2,1,0:T(4,128)S(1)}, f32[8,4,128]{2,1,0:T(4,128)S(1)}, u32[]{:S(2)}, u32[]{:S(2)}) collective-permute-start(f32[8,4,128]{2,1,0:T(4,128)S(1)} %pad_maximum_fusion.__), channel_id=1, source_target_pairs={{0,2},{1,3},{2,0},{3,1},{4,6},{5,7},{6,4},{7,5},{8,10},{9,11},{10,... | collective-permute-start | bytes 49160 | tf_op jit(solution)/shard_map/ppermute | solution.py:545
  17.6 7.6 %collective-permute-start.6 = (f32[43,8,128]{2,1,0:T(8,128)S(1)}, f32[43,8,128]{2,1,0:T(8,128)S(1)}, u32[]{:S(2)}, u32[]{:S(2)}) collective-permute-start(f32[43,8,128]{2,1,0:T(8,128)S(1)} %get-tuple-element.32), channel_id=1, source_target_pairs={{0,4},{8,12},{4,0},{12,8},{1,5},{9,13},{5,1},{13,9},{2,6},{10,14},... | collective-permute-start | bytes 528392 | tf_op jit(solution)/shard_map/ppermute | solution.py:33
  18.5 6.8 %collective-permute-start.7 = (f32[43,8,128]{2,1,0:T(8,128)S(1)}, f32[43,8,128]{2,1,0:T(8,128)S(1)}, u32[]{:S(2)}, u32[]{:S(2)}) collective-permute-start(f32[43,8,128]{2,1,0:T(8,128)S(1)} %get-tuple-element.33), channel_id=1, source_target_pairs={{4,8},{8,4},{5,9},{9,5},{6,10},{10,6},{7,11},{11,7},{20,24},{24,20... | collective-permute-start | bytes 528392 | tf_op jit(solution)/shard_map/ppermute | solution.py:33
